TPU v7x, 32 devices: a whole 2x2x4 slice. The times are simulated.
32 devices in a mesh: parts: 2 (over y), slab: 16 (over z, x, core).
Axes of the slice: x: 2, y: 2, z: 4, core: 2. Of those that a mesh axis runs over, the one named last changes fastest.
Arguments:
- volume: bfloat16 [32, 32, 512], P(('parts', 'slab')), parts along dimension 0, may hold values from -6 to 6
- tiles: bfloat16 [8, 512, 256], replicated, may hold values from -0.09375 to 0.09375
- slab_ids: int32 [512, 8], P(('parts', 'slab')), parts along dimension 0, may hold values from 0 to 15, all different within a row; in each aligned block of 16 rows (0 to 15, 16 to 31, ...) at most 16 rows name the same one
- tile_ids: int32 [512, 8], P(('parts', 'slab')), parts along dimension 0, may hold values from 0 to 7
- batch_block: int32 [512], P(('parts', 'slab')), parts along dimension 0, may hold values from 0 to 15
- images: bfloat16 [4096, 32, 256], P(('parts', 'slab')), parts along dimension 0, may hold values from -6 to 6
- defocus: float32 [4096], P(('parts', 'slab')), parts along dimension 0, may hold values from 2 to 12
- inv_sigma2: float32 [64, 256], P('parts'), parts along dimension 0, may hold values from 0.3 to 3
Outputs:
- scores: float32 [4096], P(('parts', 'slab')), parts along dimension 0
- data_volume: float32 [32, 32, 512], P(('parts', 'slab')), parts along dimension 0
- weight_volume: float32 [32, 32, 512], P(('parts', 'slab')), parts along dimension 0
There are 2 independent parts, one for each index of `parts`. A program takes and returns all parts, laid end to end along the dimension named above; an argument that names none is the same for every part. Nothing has to cross between parts.
Inputs may be any that keep to these rules, and one draw needn't show every extreme that they name: `slab_ids`: each orientation block names 8 different slabs; among the blocks of one device no slab is named more than 16 times, a bound that some block reaches.
All inputs are finite; a program needn't handle non-finite values.
Results may differ from a plain program's by a relative error of at most 0.0041.
Values may be sent and summed in bfloat16 or wider, within the bound.
No kernel may reach another device: no remote copies, remote signals or barrier semaphores. Data moves between devices by JAX's collectives and lax.ppermute only.
A program may use at most 128 MiB of HBM per device.

v0:
```python
import jax
import jax.numpy as jnp
from jax import lax
from jax.sharding import PartitionSpec as P


def wave_factor(defocus_row, height, pixels):
    line_pos = (jnp.arange(height) // 2 + 1).astype(jnp.float32) / (height // 2)
    pixel_pos = (jnp.arange(pixels) + 1).astype(jnp.float32) / pixels
    radius = line_pos[:, None] ** 2 + pixel_pos[None, :] ** 2
    return jnp.sin(defocus_row[:, None, None] * radius[None] + 0.3)


def on_device(volume, tiles, slab_ids, tile_ids, batch_block, images, defocus, inv_sigma2):
    blocks, crossed = slab_ids.shape
    item_count = blocks * crossed
    height, line_length = (volume.shape[1], volume.shape[2])
    pixels = images.shape[2]
    slab_flat = slab_ids.reshape(item_count)
    devices = lax.axis_size("slab")
    capacity = max(2, 2 * item_count // devices)
    numbers = jnp.arange(item_count, dtype=jnp.int32)
    same_slab = slab_flat[:, None] == slab_flat[None, :]
    earlier = numbers[None, :] < numbers[:, None]
    slot_rank = jnp.sum(same_slab & earlier, axis=1)
    slot_index = slab_flat * capacity + slot_rank
    source = jnp.full((devices * capacity,), item_count, jnp.int32).at[slot_index].set(numbers)
    gathered = lax.all_gather(volume, "slab", axis=0, tiled=True)
    chosen = jnp.take(gathered, slab_flat, axis=0)
    chosen = chosen.reshape(blocks, crossed, height, line_length)

    def project(inputs):
        slab_rows, tile_kinds = inputs
        kernels = jnp.take(tiles, tile_kinds, axis=0)
        return jnp.einsum("rcl,rlp->cp", slab_rows, kernels, preferred_element_type=jnp.float32)

    contrast = wave_factor(defocus, height, pixels)
    owners = jnp.repeat(batch_block, images.shape[0] // batch_block.shape[0])
    pictures = images.astype(jnp.float32)
    member = (owners[:, None] == jnp.arange(blocks)[None, :]).astype(jnp.float32)
    data_sums = jnp.einsum(
        "io,icp->ocp", member, contrast * pictures * inv_sigma2, precision=lax.Precision.HIGHEST
    ).astype(jnp.bfloat16)
    weight_sums = jnp.einsum(
        "io,icp->ocp", member, contrast * contrast * inv_sigma2, precision=lax.Precision.HIGHEST
    ).astype(jnp.bfloat16)
    stacked = jnp.stack([data_sums, weight_sums], axis=1)
    projection = lax.map(project, (chosen, tile_ids))
    residual = pictures - contrast * jnp.take(projection, owners, axis=0)
    scores = jnp.mean(residual * residual * inv_sigma2, axis=(1, 2))

    def insert(inputs):
        block_sums, tile_kinds = inputs
        kernels = jnp.take(tiles, tile_kinds, axis=0)
        return jnp.einsum(
            "kcp,rlp->rkcl", block_sums, kernels, preferred_element_type=jnp.float32
        ).astype(jnp.bfloat16)

    partials = lax.map(insert, (stacked, tile_ids)).reshape(item_count, 2, height, line_length)
    padded = jnp.concatenate(
        [partials, jnp.zeros((1, 2, height, line_length), jnp.bfloat16)], axis=0
    )
    outgoing = jnp.take(padded, source, axis=0).reshape(devices, capacity, 2, height, line_length)
    incoming = lax.all_to_all(outgoing, "slab", split_axis=0, concat_axis=0, tiled=True)
    totals = jnp.sum(incoming, axis=(0, 1), dtype=jnp.float32)
    data_volume = totals[0][None]
    weight_volume = totals[1][None]
    return (scores, data_volume, weight_volume)


def solution(mesh):
    placed = (
        P(("parts", "slab"), None, None),
        P(),
        P(("parts", "slab"), None),
        P(("parts", "slab"), None),
        P(("parts", "slab")),
        P(("parts", "slab"), None, None),
        P(("parts", "slab")),
        P("parts", None),
    )
    return jax.shard_map(
        on_device,
        mesh=mesh,
        in_specs=placed,
        out_specs=(
            P(("parts", "slab")),
            P(("parts", "slab"), None, None),
            P(("parts", "slab"), None, None),
        ),
        check_vma=False,
    )
```

profile of v0, /device:TPU:15, one launch (start us, length us, event | category | flops | bytes accessed | tf_op | source)
XLA Modules:
  0.0 629.1 jit_solution(650293325230081274)
XLA Ops:
  5.4 17.3 %all_gather.3 = bf16[16,32,512]{2,1,0:T(8,128)(2,1)S(1)} all-gather(bf16[1,32,512]{2,1,0:T(8,128)(2,1)} %param.14), channel_id=1, replica_groups=mesh['parts'=2,'slab'=16] {'slab'}, dimensions={0}, use_global_device_ids=true | all-gather | bytes 557056 | tf_op jit(solution)/shard_map/all_gather | solution.py:28
  22.7 2.8 gather_fusion.2
  25.5 4.7 broadcast_select_fusion.1
  30.2 68.1 %while.20 = (s32[]{:T(128)}, f32[16,32,256]{2,1,0:T(8,128)S(1)}, bf16[16,8,32,512]{3,2,1,0:T(8,128)(2,1)}, s32[16,8]{1,0:T(8,128)S(1)}, bf16[8,512,256]{2,1,0:T(8,128)(2,1)S(1)}, /*index=5*/s32[]{:T(128)}) while((s32[]{:T(128)}, f32[16,32,256]{2,1,0:T(8,128)S(1)}, bf16[16,8,32,512]{3,2,1,0:T(8,128)(2,1)}, s32[16,8]{1,0:T(8,128)S(1)}, ...), condition=%wide.region_1.3_spmd, body=%wide.region_0.2_spmd.sunk | while | flops 68158512 | bytes 6592217 | solution.py:48
  87.6 2.2 fusion.78
  98.4 2.8 gather_fusion.3
  101.2 18.6 %fusion.37 = (f32[128,32,256]{2,1,0:T(8,128)S(1)}, f32[128]{0:T(128)S(1)}, f32[128,32,256]{2,1,0:T(8,128)S(1)}) fusion(bf16[128,32,256]{2,1,0:T(8,128)(2,1)} %param.19, f32[32,256]{1,0:T(8,128)S(1)} %copy-done.1, f32[32,256]{1,0:T(8,128)S(1)} %broadcast_add_fusion, f32[128]{0:T(128)S(1)} %copy-done.2, f32[128,32,256]{2,1,0:T(8,128)} %gather_fusion.3, ...), kind=kLoop, calls=%fused_computation.45 | loop fusion | flops 13631360 | bytes 14746752 | tf_op jit(solution)/shard_map/mul | solution.py:42
  119.9 3.8 fusion.51
  123.7 3.8 fusion.48
  127.7 84.8 %while.21 = (s32[]{:T(128)}, bf16[16,8,2,32,512]{4,3,2,1,0:T(8,128)(2,1)}, s32[16,8]{1,0:T(8,128)S(1)}, bf16[8,512,256]{2,1,0:T(8,128)(2,1)S(1)}, bf16[16,2,32,256]{3,2,1,0:T(8,128)(2,1)S(1)}, /*index=5*/s32[]{:T(128)}) while((s32[]{:T(128)}, bf16[16,8,2,32,512]{4,3,2,1,0:T(8,128)(2,1)}, s32[16,8]{1,0:T(8,128)S(1)}, ...), condition=%wide.region_6.8_spmd, body=%wide.region_5.7_spmd.sunk | while | flops 135529520 | bytes 6854361 | solution.py:59
  129.8 3.2 fusion.81
  135.1 3.2 fusion.81
  140.4 3.2 fusion.81
  145.7 3.2 fusion.81
  151.0 3.2 fusion.81
  156.3 3.2 fusion.81
  161.6 3.2 fusion.81
  166.9 3.2 fusion.81
  172.2 3.2 fusion.81
  177.5 3.2 fusion.81
  182.8 3.2 fusion.81
  188.1 3.2 fusion.81
  193.4 3.2 fusion.81
  198.7 3.2 fusion.81
  204.0 3.2 fusion.81
  209.3 3.2 fusion.81
  212.5 8.3 %concatenate.3 = bf16[129,2,32,512]{3,2,1,0:T(8,128)(2,1)} pad(bf16[128,2,32,512]{3,2,1,0:T(8,128)(2,1)} %bitcast.73, bf16[]{:T(256)} %constant.113.clone.1), padding=0_1x0_0x0_0x0_0 | pad | bytes 16842754 | tf_op jit(solution)/shard_map/concatenate | solution.py:60
  220.8 12.9 %gather_fusion.4 = bf16[256,2,32,512]{3,2,1,0:T(8,128)(2,1)} fusion(bf16[129,2,32,512]{3,2,1,0:T(8,128)(2,1)} %concatenate.3, s32[1024]{0:T(1024)S(1)} %pad_clamp_fusion.2), kind=kCustom, calls=%fused_computation.4 | custom fusion | bytes 33555456 | tf_op jit(solution)/shard_map/jit(_take)/gather | solution.py:63
  233.7 14.1 %broadcast_select_fusion = bf16[16,16,2,32,512]{4,3,2,1,0:T(8,128)(2,1)} fusion(bf16[16,16,2,32,512]{4,3,2,1,0:T(8,128)(2,1)} %bitcast.71, pred[16,16]{1,0:T(8,128)(4,1)S(1)} %broadcast_in_dim.82), kind=kLoop, calls=%fused_computation.39 | loop fusion | flops 8388608 | bytes 33554688 | tf_op jit(solution)/shard_map/jit(_take)/select_n | solution.py:63
  247.8 11.7 %all-to-all-start = ((bf16[16,16,2,32,512]{4,3,2,1,0:T(8,128)(2,1)}), bf16[16,16,2,32,512]{4,3,2,1,0:T(8,128)(2,1)}, u32[]{:S(2)}, u32[]{:S(2)}) async-start(bf16[16,16,2,32,512]{4,3,2,1,0:T(8,128)(2,1)} %broadcast_select_fusion), calls=%async_computation | async-start | bytes 33554432 | tf_op jit(solution)/shard_map/all_to_all | solution.py:64
  260.0 361.6 %all-to-all-done = bf16[16,16,2,32,512]{4,3,2,1,0:T(8,128)(2,1)} async-done(((bf16[16,16,2,32,512]{4,3,2,1,0:T(8,128)(2,1)}), bf16[16,16,2,32,512]{4,3,2,1,0:T(8,128)(2,1)}, u32[]{:S(2)}, u32[]{:S(2)}) %all-to-all-start) | async-done | bytes 16777248 | tf_op jit(solution)/shard_map/all_to_all | solution.py:64
  621.6 6.8 %convert_reduce_fusion = f32[2,32,512]{2,1,0:T(8,128)S(1)} fusion(bf16[16,16,2,32,512]{4,3,2,1,0:T(8,128)(2,1)} %all-to-all-done), kind=kLoop, calls=%fused_computation.38 | loop fusion | flops 16744448 | bytes 16908288 | tf_op jit(solution)/shard_map/reduce_sum | solution.py:65
  (147 shorter events, 104.7 us)
Async XLA Ops:
  25.5 4.7 copy-start
  98.4 2.8 copy-start.1
  98.4 2.8 copy-start.2
  247.8 373.8 %all-to-all-start = ((bf16[16,16,2,32,512]{4,3,2,1,0:T(8,128)(2,1)}), bf16[16,16,2,32,512]{4,3,2,1,0:T(8,128)(2,1)}, u32[]{:S(2)}, u32[]{:S(2)}) async-start(bf16[16,16,2,32,512]{4,3,2,1,0:T(8,128)(2,1)} %broadcast_select_fusion), calls=%async_computation | async-start | bytes 33554432 | tf_op jit(solution)/shard_map/all_to_all | solution.py:64
where the time goes:
time: 631 us; the launch traced here: 629 us
  waiting for transfers between devices  362 us (57%)
  local copies, waits for them, and re-layouts  96.4 us (15%)
  matrix products  94.1 us (15%)
  other arithmetic  46.5 us (7%)
  blocking collectives  17.3 us (3%)
  starting transfers between devices  11.7 us (2%)
    all_to_all x1, waiting for transfers between devices, on_device(): lax.all_to_all(outgoing, 'slab', split_axis=0, concat_axis=0, tiled=True)  362 us
    dot_general x16, matrix products, insert(): jnp.einsum('kcp,rlp->rkcl', block_sums, kernels, preferred_element_type=j...  51.5 us
    dot_general x16, matrix products, project(): jnp.einsum('rcl,rlp->cp', slab_rows, kernels, preferred_element_type=jnp....  34.9 us
    gather x16, local copies, waits for them, and re-layouts, insert(): kernels = jnp.take(tiles, tile_kinds, axis=0)  32.9 us
    gather x16, local copies, waits for them, and re-layouts, project(): kernels = jnp.take(tiles, tile_kinds, axis=0)  32.3 us
    mul x1, other arithmetic, on_device(): contrast * pictures * inv_sigma2  18.6 us
    all_gather x1, blocking collectives, on_device(): gathered = lax.all_gather(volume, 'slab', axis=0, tiled=True)  17.3 us
    select_n x2, other arithmetic, on_device(): jnp.take(padded, source, axis=0)  14.1 us
  transfers between devices with their start and end apart: 1, of which 1 were waited for; matrix products, arithmetic and copies ran while one was open for 0% of the time, Pallas kernels for 0%

commit v1 on v0

v1 whole, which is shorter than its diff:
```python
import functools

import jax
import jax.numpy as jnp
from jax import lax
from jax.experimental import pallas as pl
from jax.experimental.pallas import tpu as pltpu
from jax.sharding import PartitionSpec as P

LANES = 128
CHUNKS = 4
VMEM_BYTES = 48 * 1024 * 1024


def grid_of(devices):
    cores = 2 if devices % 2 == 0 else 1
    chips = devices // cores
    wide = 1
    while (2 * wide) ** 3 <= chips:
        wide *= 2
    return chips // wide, wide, cores


def sin_cos(angle):
    turns = jnp.floor(angle * 0.3183098861837907 + 0.5)
    rest = angle - turns * 3.140625
    rest = rest - turns * 9.675025939941406e-4
    rest = rest - turns * 1.5099580252808664e-7
    half = turns * 0.5
    sign = 1.0 - 4.0 * (half - jnp.floor(half))
    sq = rest * rest
    sin = rest * (1.0 + sq * (-1.0 / 6 + sq * (1.0 / 120 + sq * (-1.0 / 5040 + sq * (1.0 / 362880 + sq * (-1.0 / 39916800))))))
    cos = 1.0 + sq * (-0.5 + sq * (1.0 / 24 + sq * (-1.0 / 720 + sq * (1.0 / 40320 + sq * (-1.0 / 3628800 + sq * (1.0 / 479001600))))))
    return sign * sin, sign * cos


def tables(defocus_ref, height, repeat, pixels, line_ref, pixel_ref):
    images = defocus_ref.shape[1]
    defocus = defocus_ref[...]
    rows = lax.broadcasted_iota(jnp.int32, (height * repeat, images), 0)
    line = ((rows // repeat + 1).astype(jnp.float32) / height) ** 2
    line_ref[0], line_ref[1] = sin_cos(defocus * line + 0.3)
    column = jnp.transpose(jnp.broadcast_to(defocus, (LANES, images)))
    column = jnp.concatenate([column] * (pixels // LANES), axis=1)
    lanes = lax.broadcasted_iota(jnp.int32, (images, pixels), 1)
    pixel = ((lanes + 1).astype(jnp.float32) / pixels) ** 2
    pixel_ref[0], pixel_ref[1] = sin_cos(column * pixel)


def lines_of(line_ref, batch, size):
    images = line_ref.shape[2]
    shift = lax.rem(images - batch * size, images)
    return pltpu.roll(line_ref[0], shift, 1), pltpu.roll(line_ref[1], shift, 1)


def contrast_of(lines, pixel_ref, batch, size, j):
    sin_line, cos_line = lines
    row = pl.ds(batch * size + j, 1)
    return sin_line[:, j : j + 1] * pixel_ref[1, row, :] + cos_line[:, j : j + 1] * pixel_ref[0, row, :]


def clear_lists(count_ref):
    def clear(s, carry):
        count_ref[s] = 0
        return carry

    lax.fori_loop(0, count_ref.shape[0], clear, 0)


def list_block(k, slab_ref, tile_ref, count_ref, list_ref):
    crossed, blocks = slab_ref.shape
    for r in range(crossed):
        s = slab_ref[r, k]
        at = count_ref[s]
        list_ref[s * blocks + at] = k * 256 + tile_ref[r, k]
        count_ref[s] = at + 1


def insert(sums, tiles_ref, parts_ref, count_ref, list_ref, keep_ref, send_ref, height, shape):
    far, wide, cores = shape
    blocks = sums.shape[0] // height
    devices = count_ref.shape[0]
    for t in range(tiles_ref.shape[0]):
        parts_ref[t] = lax.dot_general(
            sums, tiles_ref[t], (((1,), (1,)), ((), ())), preferred_element_type=jnp.float32
        ).astype(jnp.bfloat16)
    me = lax.axis_index("slab")

    def total(slot, core):
        x, z = slot // far, lax.rem(slot, far)
        s = me ^ ((z * wide + x) * cores + core)

        def add(m, acc):
            item = list_ref[s * blocks + m]
            k, t = item // 256, lax.rem(item, 256)
            rows = pl.ds(pl.multiple_of(k * height, height), height)
            return acc + parts_ref[t, rows, :].astype(jnp.float32)

        zero = jnp.zeros((height, parts_ref.shape[2]), jnp.float32)
        return lax.fori_loop(0, count_ref[s], add, zero)

    def send(slot, carry):
        send_ref[slot] = total(slot, 1).astype(jnp.bfloat16)
        return carry

    def keep(slot, carry):
        keep_ref[slot] = total(slot, 0)
        return carry

    half = devices // 2
    lax.fori_loop(0, half, send, 0)
    lax.fori_loop(0, half, keep, 0)


def weight_kernel(shape, slab_ref, tile_ref, block_ref, defocus_ref, noise_ref, tiles_hbm, keep_ref, send_ref,
                  tiles_ref, line_ref, pixel_ref, sums_ref, wide_ref, parts_ref, count_ref, list_ref, sem):
    copy = pltpu.make_async_copy(tiles_hbm, tiles_ref, sem)
    copy.start()
    height, pixels = noise_ref.shape
    blocks = sums_ref.shape[0]
    batches = block_ref.shape[0]
    size = defocus_ref.shape[1] // batches
    tables(defocus_ref, height // 2, 1, pixels, line_ref, pixel_ref)
    sums_ref[...] = jnp.zeros_like(sums_ref)
    clear_lists(count_ref)

    def batch_step(b, carry):
        lines = lines_of(line_ref, b, size)
        acc = jnp.zeros((height // 2, pixels), jnp.float32)
        for j in range(size):
            wave = contrast_of(lines, pixel_ref, b, size, j)
            acc = acc + wave * wave
        k = block_ref[b]
        sums_ref[k] = sums_ref[k] + acc
        return carry

    def list_step(k, carry):
        list_block(k, slab_ref, tile_ref, count_ref, list_ref)
        return carry

    if blocks == batches:
        lax.fori_loop(0, batches, lambda b, c: list_step(b, batch_step(b, c)), 0)
    else:
        lax.fori_loop(0, batches, batch_step, 0)
        lax.fori_loop(0, blocks, list_step, 0)

    noise = noise_ref[...]
    for k in range(blocks):
        block = sums_ref[k]
        for n in range(pixels // LANES):
            for odd in range(2):
                wide_ref[k, n, pl.ds(odd, height // 2, 2), :] = block[:, n * LANES : (n + 1) * LANES]
    sums = jnp.concatenate([wide_ref[:, n] for n in range(pixels // LANES)], axis=2) * noise[None]
    sums = sums.astype(jnp.bfloat16).reshape(blocks * height, pixels)
    copy.wait()
    insert(sums, tiles_ref, parts_ref, count_ref, list_ref, keep_ref, send_ref, height, shape)


def data_kernel(shape, slab_ref, tile_ref, block_ref, defocus_ref, noise_ref, images_hbm, tiles_hbm, keep_ref, send_ref,
                images_ref, tiles_ref, line_ref, pixel_ref, sums_ref, parts_ref, count_ref, list_ref, sem, chunk_sem):
    height, pixels = noise_ref.shape
    blocks = sums_ref.shape[0]
    batches = block_ref.shape[0]
    size = defocus_ref.shape[1] // batches
    part = images_ref.shape[0] // CHUNKS
    chunk = [
        pltpu.make_async_copy(images_hbm.at[pl.ds(n * part, part)], images_ref.at[pl.ds(n * part, part)], chunk_sem.at[n])
        for n in range(CHUNKS)
    ]
    for c in chunk:
        c.start()
    copy = pltpu.make_async_copy(tiles_hbm, tiles_ref, sem)
    copy.start()
    tables(defocus_ref, height // 2, 2, pixels, line_ref, pixel_ref)
    sums_ref[...] = jnp.zeros_like(sums_ref)
    clear_lists(count_ref)

    def batch_step(b, carry):
        lines = lines_of(line_ref, b, size)
        acc = jnp.zeros((height, pixels), jnp.float32)
        for j in range(size):
            wave = contrast_of(lines, pixel_ref, b, size, j)
            acc = acc + wave * images_ref[b * size + j].astype(jnp.float32)
        k = block_ref[b]
        sums_ref[k] = sums_ref[k] + acc
        return carry

    def list_step(k, carry):
        list_block(k, slab_ref, tile_ref, count_ref, list_ref)
        return carry

    each = batches // CHUNKS
    for n in range(CHUNKS):
        chunk[n].wait()
        if blocks == batches:
            lax.fori_loop(n * each, (n + 1) * each, lambda b, c: list_step(b, batch_step(b, c)), 0)
        else:
            lax.fori_loop(n * each, (n + 1) * each, batch_step, 0)
    if blocks != batches:
        lax.fori_loop(0, blocks, list_step, 0)

    sums = (sums_ref[...] * noise_ref[...][None]).astype(jnp.bfloat16).reshape(blocks * height, pixels)
    copy.wait()
    insert(sums, tiles_ref, parts_ref, count_ref, list_ref, keep_ref, send_ref, height, shape)


def score_kernel(shape, slab_ref, tile_ref, block_ref, defocus_ref, noise_ref, near_ref, other_ref, images_hbm, tiles_hbm,
                 score_ref, images_ref, tiles_ref, line_ref, pixel_ref, flat_ref, proj_ref, part_ref, sem, chunk_sem):
    far, wide, cores = shape
    height, pixels = noise_ref.shape
    crossed, blocks = slab_ref.shape
    batches = block_ref.shape[0]
    size = defocus_ref.shape[1] // batches
    half = near_ref.shape[0]
    copy = pltpu.make_async_copy(tiles_hbm, tiles_ref, sem)
    copy.start()
    load = pltpu.make_async_copy(images_hbm, images_ref, chunk_sem)
    load.start()
    tables(defocus_ref, height // 2, 2, pixels, line_ref, pixel_ref)
    me = lax.axis_index("slab")
    copy.wait()
    dense = 2 * half * tiles_ref.shape[0] <= crossed * blocks

    def slot_of(s):
        away = me ^ s
        core, chip = lax.rem(away, cores), away // cores
        return core * half + lax.rem(chip, wide) * far + chip // wide

    if dense:
        for n, ref in enumerate((near_ref, other_ref)):
            lines = ref[...].reshape(half * height, ref.shape[2])
            for t in range(tiles_ref.shape[0]):
                flat_ref[t, n * half * height : (n + 1) * half * height, :] = jnp.dot(
                    lines, tiles_ref[t], preferred_element_type=jnp.float32
                )
    else:
        flat_ref[0:half] = near_ref[...]
        flat_ref[half : 2 * half] = other_ref[...]

    def project(k, carry):
        acc = jnp.zeros((height, pixels), jnp.float32)
        for r in range(crossed):
            slot, t = slot_of(slab_ref[r, k]), tile_ref[r, k]
            if dense:
                acc = acc + flat_ref[t, pl.ds(pl.multiple_of(slot * height, height), height), :]
            else:
                acc = acc + jnp.dot(flat_ref[slot], tiles_ref[t], preferred_element_type=jnp.float32)
        proj_ref[k] = acc
        return carry

    lax.fori_loop(0, blocks, project, 0)
    load.wait()

    def batch_step(b, carry):
        lines = lines_of(line_ref, b, size)
        k = block_ref[b]
        for j in range(size):
            wave = contrast_of(lines, pixel_ref, b, size, j)
            residual = images_ref[b * size + j].astype(jnp.float32) - wave * proj_ref[k]
            power = jnp.sum(residual * residual * noise_ref[...], axis=0, keepdims=True)
            part_ref[pl.ds(b * size + j, 1), :] = sum(
                power[:, n * LANES : (n + 1) * LANES] for n in range(pixels // LANES)
            )
        return carry

    lax.fori_loop(0, batches, batch_step, 0)
    total = jnp.sum(jnp.transpose(part_ref[...]), axis=0, keepdims=True)
    score_ref[...] = total * (1.0 / (height * pixels))


def on_device(volume, tiles, slab_ids, tile_ids, batch_block, images, defocus, inv_sigma2):
    blocks, crossed = slab_ids.shape
    height, length = volume.shape[1:]
    count, _, pixels = images.shape
    kinds = tiles.shape[0]
    devices = lax.axis_size("slab")
    shape = far, wide, cores = grid_of(devices)
    half = devices // 2
    slabs, kind_rows, row = slab_ids.T, tile_ids.T, defocus.reshape(1, count)

    def swap(array, offset):
        return lax.ppermute(array, "slab", [(i, i ^ offset) for i in range(devices)])

    smem = pl.BlockSpec(memory_space=pltpu.SMEM)
    vmem = pl.BlockSpec(memory_space=pltpu.VMEM)
    hbm = pl.BlockSpec(memory_space=pl.ANY)
    params = pltpu.CompilerParams(vmem_limit_bytes=VMEM_BYTES)
    tiles_scratch = pltpu.VMEM(tiles.shape, jnp.bfloat16)
    pixel_scratch = pltpu.VMEM((2, count, pixels), jnp.float32)
    parts_scratch = pltpu.VMEM((kinds, blocks * height, length), jnp.bfloat16)
    lists = [pltpu.SMEM((devices,), jnp.int32), pltpu.SMEM((devices * blocks,), jnp.int32)]
    sums_out = (
        jax.ShapeDtypeStruct((half, height, length), jnp.float32),
        jax.ShapeDtypeStruct((half, height, length), jnp.bfloat16),
    )
    insert_flops = 2 * blocks * height * pixels * kinds * length

    weight_keep, weight_send = pl.pallas_call(
        functools.partial(weight_kernel, shape),
        out_shape=sums_out,
        in_specs=[smem, smem, smem, vmem, vmem, hbm],
        out_specs=(vmem, vmem),
        scratch_shapes=[
            tiles_scratch,
            pltpu.VMEM((2, height // 2, count), jnp.float32),
            pixel_scratch,
            pltpu.VMEM((blocks, height // 2, pixels), jnp.float32),
            pltpu.VMEM((blocks, pixels // LANES, height, LANES), jnp.float32),
            parts_scratch,
            *lists,
            pltpu.SemaphoreType.DMA,
        ],
        compiler_params=params,
        cost_estimate=pl.CostEstimate(flops=insert_flops, bytes_accessed=4 << 20, transcendentals=0),
        name="weights",
    )(slabs, kind_rows, batch_block, row, inv_sigma2, tiles)

    data_keep, data_send = pl.pallas_call(
        functools.partial(data_kernel, shape),
        out_shape=sums_out,
        in_specs=[smem, smem, smem, vmem, vmem, hbm, hbm],
        out_specs=(vmem, vmem),
        scratch_shapes=[
            pltpu.VMEM(images.shape, jnp.bfloat16),
            tiles_scratch,
            pltpu.VMEM((2, height, count), jnp.float32),
            pixel_scratch,
            pltpu.VMEM((blocks, height, pixels), jnp.float32),
            parts_scratch,
            *lists,
            pltpu.SemaphoreType.DMA,
            pltpu.SemaphoreType.DMA((CHUNKS,)),
        ],
        compiler_params=params,
        cost_estimate=pl.CostEstimate(flops=insert_flops, bytes_accessed=6 << 20, transcendentals=0),
        name="data",
    )(slabs, kind_rows, batch_block, row, inv_sigma2, images, tiles)

    def reduce(keep, send):
        if cores == 2:
            other = swap(send, 1).astype(jnp.float32)
        else:
            other = send.astype(jnp.float32)
        sums = (keep + other).reshape(wide, far, height, length)
        outgoing = (keep + other).reshape(wide, far, height, length)[1:].astype(jnp.bfloat16)
        line = sums[0]
        for x in range(1, wide):
            line = line + swap(outgoing[x - 1], x * cores).astype(jnp.float32)
        total = line[0]
        for z in range(1, far):
            total = total + swap(line[z].astype(jnp.bfloat16), z * wide * cores).astype(jnp.float32)
        return total[None]

    column = jnp.concatenate([volume] + [swap(volume, z * wide * cores) for z in range(1, far)], axis=0)
    near = jnp.concatenate([column] + [swap(column, x * cores) for x in range(1, wide)], axis=0)
    other = swap(near, 1)

    if devices * kinds <= blocks * crossed:
        flat = pltpu.VMEM((kinds, devices * height, pixels), jnp.float32)
    else:
        flat = pltpu.VMEM((devices, height, length), jnp.bfloat16)
    scores = pl.pallas_call(
        functools.partial(score_kernel, shape),
        out_shape=jax.ShapeDtypeStruct((1, count), jnp.float32),
        in_specs=[smem, smem, smem, vmem, vmem, vmem, vmem, hbm, hbm],
        out_specs=vmem,
        scratch_shapes=[
            pltpu.VMEM(images.shape, jnp.bfloat16),
            tiles_scratch,
            pltpu.VMEM((2, height, count), jnp.float32),
            pixel_scratch,
            flat,
            pltpu.VMEM((blocks, height, pixels), jnp.float32),
            pltpu.VMEM((count, LANES), jnp.float32),
            pltpu.SemaphoreType.DMA,
            pltpu.SemaphoreType.DMA,
        ],
        compiler_params=params,
        cost_estimate=pl.CostEstimate(flops=insert_flops // 2, bytes_accessed=5 << 20, transcendentals=0),
        name="scores",
    )(slabs, kind_rows, batch_block, row, inv_sigma2, near, other, images, tiles)

    weight_volume = reduce(weight_keep, weight_send)
    data_volume = reduce(data_keep, data_send)
    return scores.reshape(count), data_volume, weight_volume


def solution(mesh):
    placed = (
        P(("parts", "slab"), None, None),
        P(),
        P(("parts", "slab"), None),
        P(("parts", "slab"), None),
        P(("parts", "slab")),
        P(("parts", "slab"), None, None),
        P(("parts", "slab")),
        P("parts", None),
    )
    return jax.shard_map(
        on_device,
        mesh=mesh,
        in_specs=placed,
        out_specs=(
            P(("parts", "slab")),
            P(("parts", "slab"), None, None),
            P(("parts", "slab"), None, None),
        ),
        check_vma=False,
    )
```

time: 631 us -> 62.3 us (0.10)
  the two profiles are of different devices: /device:TPU:15 before, /device:TPU:0 now
where the time goes in v1:
time: 62.3 us; the launch traced here: 62 us
  Pallas kernels  26.3 us (42%)
  starting transfers between devices  19.2 us (31%)
  waiting for transfers between devices  9.01 us (14%)
  local copies, waits for them, and re-layouts  5.13 us (8%)
  other arithmetic  1.54 us (2%)
  between operations  0.85 us (1%)
    ppermute x15, starting transfers between devices, swap(): lax.ppermute(array, 'slab', [(i, i ^ offset) for i in range(devices)])  19.2 us
    pallas_call x1, Pallas kernels, on_device(): pl.pallas_call(functools.partial(data_kernel, shape), out_shape=sums_out,...  9.16 us
    ppermute x15, waiting for transfers between devices, swap(): lax.ppermute(array, 'slab', [(i, i ^ offset) for i in range(devices)])  9.01 us
    pallas_call x1, Pallas kernels, on_device(): pl.pallas_call(functools.partial(score_kernel, shape), out_shape=jax.Shap...  8.69 us
    pallas_call x1, Pallas kernels, on_device(): pl.pallas_call(functools.partial(weight_kernel, shape), out_shape=sums_ou...  8.43 us
    unnamed x22, local copies, waits for them, and re-layouts  5.06 us
    broadcast_in_dim x2, other arithmetic, reduce(): return total[None]  1.29 us
  transfers between devices with their start and end apart: 15, of which 3 were waited for; matrix products, arithmetic and copies ran while one was open for 2% of the time, Pallas kernels for 42%

profile of v1, /device:TPU:0, one launch (start us, length us, event | category | flops | bytes accessed | tf_op | source)
XLA Modules:
  0.0 62.0 jit_solution(1394355455044116844)
XLA Ops:
  0.6 3.1 %collective-permute-start = (bf16[1,32,512]{2,1,0:T(8,128)(2,1)}, bf16[1,32,512]{2,1,0:T(8,128)(2,1)S(1)}, u32[]{:S(2)}, u32[]{:S(2)}) collective-permute-start(bf16[1,32,512]{2,1,0:T(8,128)(2,1)} %param.8), channel_id=1, source_target_pairs={{0,4},{1,5},{2,6},{3,7},{4,0},{5,1},{6,2},{7,3},{8,12},{9,13},{10,... | collective-permute-start | bytes 98312 | tf_op jit(solution)/shard_map/ppermute | solution.py:282
  3.7 2.6 %collective-permute-start.1 = (bf16[1,32,512]{2,1,0:T(8,128)(2,1)}, bf16[1,32,512]{2,1,0:T(8,128)(2,1)S(1)}, u32[]{:S(2)}, u32[]{:S(2)}) collective-permute-start(bf16[1,32,512]{2,1,0:T(8,128)(2,1)} %param.8), channel_id=1, source_target_pairs={{0,8},{1,9},{2,10},{3,11},{4,12},{5,13},{6,14},{7,15},{8,0},{9,1},... | collective-permute-start | bytes 98312 | tf_op jit(solution)/shard_map/ppermute | solution.py:282
  6.3 1.6 %copy-done.1 = bf16[8,512,256]{2,1,0:T(8,128)(2,1)S(1)} copy-done((bf16[8,512,256]{2,1,0:T(8,128)(2,1)S(1)}, bf16[8,512,256]{2,1,0:T(8,128)(2,1)}, u32[]{:S(2)}) %copy-start.1) | copy-done | bytes 2097176
  7.9 0.8 %copy-done.3 = f32[32,256]{1,0:T(8,128)S(1)} copy-done((f32[32,256]{1,0:T(8,128)S(1)}, f32[32,256]{1,0:T(8,128)}, u32[]{:S(2)}) %copy-start.3) | copy-done | bytes 32792
  8.7 0.7 %copy-done.4 = s32[16,8]{0,1:T(8,128)S(1)} copy-done((s32[16,8]{0,1:T(8,128)S(1)}, s32[16,8]{0,1:T(8,128)}, u32[]{:S(2)}) %copy-start.4) | copy-done | bytes 536
  9.4 0.7 %copy-done.5 = s32[16,8]{0,1:T(8,128)S(1)} copy-done((s32[16,8]{0,1:T(8,128)S(1)}, s32[16,8]{0,1:T(8,128)}, u32[]{:S(2)}) %copy-start.5) | copy-done | bytes 536
  10.1 0.7 %copy-done.6 = s32[16]{0:T(128)S(1)} copy-done((s32[16]{0:T(128)S(1)}, s32[16]{0:T(128)}, u32[]{:S(2)}) %copy-start.6) | copy-done | bytes 88
  10.7 0.7 %copy-done.7 = f32[128]{0:T(128)S(1)} copy-done((f32[128]{0:T(128)S(1)}, f32[128]{0:T(128)}, u32[]{:S(2)}) %copy-start.7) | copy-done | bytes 536
  11.4 8.4 %weights.1 = (f32[8,32,512]{2,1,0:T(8,128)S(1)}, bf16[8,32,512]{2,1,0:T(8,128)(2,1)S(1)}) custom-call(s32[8,16]{1,0:T(8,128)S(1)} %bitcast.40, s32[8,16]{1,0:T(8,128)S(1)} %bitcast.43, s32[16]{0:T(128)S(1)} %copy-done.6, f32[1,128]{1,0:T(1,128)S(1)} %bitcast.46, f32[32,256]{1,0:T(8,128)S(1)} %copy-done.3, bf16[8,512,256]{2,1,0:T(8,128)(2,1)S(1)} %copy-done.1), custom_call_target="tpu_custom_call" | custom-call | flops 1073741824 | bytes 4194304 | tf_op jit(solution)/shard_map/weights/pallas_call | solution.py:298
  19.8 0.0 copy-start.8
  19.8 0.1 collective-permute-start.10
  19.9 9.2 %data.1 = (f32[8,32,512]{2,1,0:T(8,128)S(1)}, bf16[8,32,512]{2,1,0:T(8,128)(2,1)S(1)}) custom-call(s32[8,16]{1,0:T(8,128)S(1)} %bitcast.41, s32[8,16]{1,0:T(8,128)S(1)} %bitcast.44, s32[16]{0:T(128)S(1)} %copy-done.6, f32[1,128]{1,0:T(1,128)S(1)} %bitcast.47, f32[32,256]{1,0:T(8,128)S(1)} %copy-done.3, bf16[128,32,256]{2,1,0:T(8,128)(2,1)S(1)} %copy-done, ...), custom_call_target="tpu_custom_call" | custom-call | flops 1073741824 | bytes 6291456 | tf_op jit(solution)/shard_map/data/pallas_call | solution.py:318
  29.1 0.6 collective-permute-start.5
  29.7 1.8 %collective-permute-start.3 = (bf16[4,32,512]{2,1,0:T(8,128)(2,1)S(1)}, bf16[4,32,512]{2,1,0:T(8,128)(2,1)S(1)}, u32[]{:S(2)}, u32[]{:S(2)}) collective-permute-start(bf16[4,32,512]{2,1,0:T(8,128)(2,1)S(1)} %pad_maximum_fusion), channel_id=1, source_target_pairs={{0,2},{1,3},{2,0},{3,1},{4,6},{5,7},{6,4},{7,5},{8,10},{9,11},{10,... | collective-permute-start | bytes 393224 | tf_op jit(solution)/shard_map/ppermute | solution.py:282
  31.5 3.7 %collective-permute-done.3 = bf16[4,32,512]{2,1,0:T(8,128)(2,1)S(1)} collective-permute-done((bf16[4,32,512]{2,1,0:T(8,128)(2,1)S(1)}, bf16[4,32,512]{2,1,0:T(8,128)(2,1)S(1)}, u32[]{:S(2)}, u32[]{:S(2)}) %collective-permute-start.3) | collective-permute-done | bytes 131104 | tf_op jit(solution)/shard_map/ppermute | solution.py:282
  35.2 0.1 collective-permute-start.4
  35.3 0.1 convert_add_fusion
  35.4 0.0 copy-start.2
  35.4 1.8 %collective-permute-start.11 = (bf16[4,32,512]{2,1,0:T(8,128)(2,1)S(1)}, bf16[4,32,512]{2,1,0:T(8,128)(2,1)S(1)}, u32[]{:S(2)}, u32[]{:S(2)}) collective-permute-start(bf16[4,32,512]{2,1,0:T(8,128)(2,1)S(1)} %slice.100), channel_id=1, source_target_pairs={{0,2},{1,3},{2,0},{3,1},{4,6},{5,7},{6,4},{7,5},{8,10},{9,11},{10,... | collective-permute-start | bytes 393224 | tf_op jit(solution)/shard_map/ppermute | solution.py:282
  37.2 0.1 convert_add_fusion.1
  37.3 0.4 collective-permute-start.6
  37.7 4.1 %collective-permute-done.11 = bf16[4,32,512]{2,1,0:T(8,128)(2,1)S(1)} collective-permute-done((bf16[4,32,512]{2,1,0:T(8,128)(2,1)S(1)}, bf16[4,32,512]{2,1,0:T(8,128)(2,1)S(1)}, u32[]{:S(2)}, u32[]{:S(2)}) %collective-permute-start.11) | collective-permute-done | bytes 131104 | tf_op jit(solution)/shard_map/ppermute | solution.py:282
  41.8 1.0 %collective-permute-start.12 = (bf16[32,512]{1,0:T(8,128)(2,1)S(1)}, bf16[32,512]{1,0:T(8,128)(2,1)S(1)}, u32[]{:S(2)}, u32[]{:S(2)}) collective-permute-start(bf16[32,512]{1,0:T(8,128)(2,1)S(1)} %get-tuple-element.15), channel_id=1, source_target_pairs={{0,4},{1,5},{2,6},{3,7},{4,0},{5,1},{6,2},{7,3},{8,12},{9,13},{10,... | collective-permute-start | bytes 98312 | tf_op jit(solution)/shard_map/ppermute | solution.py:282
  42.8 3.5 %collective-permute-start.13 = (bf16[32,512]{1,0:T(8,128)(2,1)S(1)}, bf16[32,512]{1,0:T(8,128)(2,1)S(1)}, u32[]{:S(2)}, u32[]{:S(2)}) collective-permute-start(bf16[32,512]{1,0:T(8,128)(2,1)S(1)} %get-tuple-element.17), channel_id=1, source_target_pairs={{0,8},{1,9},{2,10},{3,11},{4,12},{5,13},{6,14},{7,15},{8,0},{9,1},... | collective-permute-start | bytes 98312 | tf_op jit(solution)/shard_map/ppermute | solution.py:282
  46.3 0.0 collective-permute-start.14
  46.3 0.6 %collective-permute-start.7 = (bf16[32,512]{1,0:T(8,128)(2,1)S(1)}, bf16[32,512]{1,0:T(8,128)(2,1)S(1)}, u32[]{:S(2)}, u32[]{:S(2)}) collective-permute-start(bf16[32,512]{1,0:T(8,128)(2,1)S(1)} %get-tuple-element.18), channel_id=1, source_target_pairs={{0,4},{1,5},{2,6},{3,7},{4,0},{5,1},{6,2},{7,3},{8,12},{9,13},{10,... | collective-permute-start | bytes 98312 | tf_op jit(solution)/shard_map/ppermute | solution.py:282
  47.0 3.8 %collective-permute-start.8 = (bf16[32,512]{1,0:T(8,128)(2,1)S(1)}, bf16[32,512]{1,0:T(8,128)(2,1)S(1)}, u32[]{:S(2)}, u32[]{:S(2)}) collective-permute-start(bf16[32,512]{1,0:T(8,128)(2,1)S(1)} %get-tuple-element.20), channel_id=1, source_target_pairs={{0,8},{1,9},{2,10},{3,11},{4,12},{5,13},{6,14},{7,15},{8,0},{9,1},... | collective-permute-start | bytes 98312 | tf_op jit(solution)/shard_map/ppermute | solution.py:282
  50.8 0.0 collective-permute-start.9
  50.8 1.2 %collective-permute-done.14 = bf16[32,512]{1,0:T(8,128)(2,1)S(1)} collective-permute-done((bf16[32,512]{1,0:T(8,128)(2,1)S(1)}, bf16[32,512]{1,0:T(8,128)(2,1)S(1)}, u32[]{:S(2)}, u32[]{:S(2)}) %collective-permute-start.14) | collective-permute-done | bytes 32800 | tf_op jit(solution)/shard_map/ppermute | solution.py:282
  52.0 0.6 %fusion.3 = f32[1,32,512]{2,1,0:T(8,128)} fusion(f32[4,32,512]{2,1,0:T(8,128)S(1)} %get-tuple-element.12, bf16[32,512]{1,0:T(8,128)(2,1)S(1)} %collective-permute-done.14, bf16[32,512]{1,0:T(8,128)(2,1)S(1)} %collective-permute-done.13, bf16[32,512]{1,0:T(8,128)(2,1)S(1)} %collective-permute-done.12), kind=kLoop, calls=%fused_computation.11 | loop fusion | flops 98304 | bytes 229376 | tf_op jit(solution)/shard_map/broadcast_in_dim | solution.py:352
  52.6 8.7 %scores.1 = f32[1,128]{1,0:T(1,128)} custom-call(s32[8,16]{1,0:T(8,128)S(1)} %bitcast.42, s32[8,16]{1,0:T(8,128)S(1)} %bitcast.45, s32[16]{0:T(128)S(1)} %copy-done.6, f32[1,128]{1,0:T(1,128)S(1)} %bitcast.48, f32[32,256]{1,0:T(8,128)S(1)} %copy-done.3, bf16[8,32,512]{2,1,0:T(8,128)(2,1)S(1)} %constant_dynamic-update-slice_fusion.near_ref, ...), custom_call_target="tpu_custom_call" | custom-call | flops 536870912 | bytes 5242880 | tf_op jit(solution)/shard_map/scores/pallas_call | solution.py:362
  61.4 0.6 %fusion.7 = f32[1,32,512]{2,1,0:T(8,128)} fusion(f32[4,32,512]{2,1,0:T(8,128)S(1)} %get-tuple-element.14, bf16[32,512]{1,0:T(8,128)(2,1)S(1)} %collective-permute-done.9, bf16[32,512]{1,0:T(8,128)(2,1)S(1)} %collective-permute-done.8, bf16[32,512]{1,0:T(8,128)(2,1)S(1)} %collective-permute-done.7), kind=kLoop, calls=%fused_computation.16 | loop fusion | flops 98304 | bytes 229376 | tf_op jit(solution)/shard_map/broadcast_in_dim | solution.py:352
  (35 shorter events, 0.2 us)
Async XLA Ops:
  0.6 19.3 %copy-start = (bf16[128,32,256]{2,1,0:T(8,128)(2,1)S(1)}, bf16[128,32,256]{2,1,0:T(8,128)(2,1)}, u32[]{:S(2)}) copy-start(bf16[128,32,256]{2,1,0:T(8,128)(2,1)} %images_hbm.3) | copy-start | bytes 6291460
  0.6 29.0 %collective-permute-start = (bf16[1,32,512]{2,1,0:T(8,128)(2,1)}, bf16[1,32,512]{2,1,0:T(8,128)(2,1)S(1)}, u32[]{:S(2)}, u32[]{:S(2)}) collective-permute-start(bf16[1,32,512]{2,1,0:T(8,128)(2,1)} %param.8), channel_id=1, source_target_pairs={{0,4},{1,5},{2,6},{3,7},{4,0},{5,1},{6,2},{7,3},{8,12},{9,13},{10,... | collective-permute-start | bytes 98312 | tf_op jit(solution)/shard_map/ppermute | solution.py:282
  3.7 25.9 %collective-permute-start.1 = (bf16[1,32,512]{2,1,0:T(8,128)(2,1)}, bf16[1,32,512]{2,1,0:T(8,128)(2,1)S(1)}, u32[]{:S(2)}, u32[]{:S(2)}) collective-permute-start(bf16[1,32,512]{2,1,0:T(8,128)(2,1)} %param.8), channel_id=1, source_target_pairs={{0,8},{1,9},{2,10},{3,11},{4,12},{5,13},{6,14},{7,15},{8,0},{9,1},... | collective-permute-start | bytes 98312 | tf_op jit(solution)/shard_map/ppermute | solution.py:282
  6.3 23.3 %collective-permute-start.2 = (bf16[1,32,512]{2,1,0:T(8,128)(2,1)}, bf16[1,32,512]{2,1,0:T(8,128)(2,1)S(1)}, u32[]{:S(2)}, u32[]{:S(2)}) collective-permute-start(bf16[1,32,512]{2,1,0:T(8,128)(2,1)} %param.8), channel_id=1, source_target_pairs={{0,12},{1,13},{2,14},{3,15},{4,8},{5,9},{6,10},{7,11},{8,4},{9,5},... | collective-permute-start | bytes 98312 | tf_op jit(solution)/shard_map/ppermute | solution.py:282
  6.3 1.6 %copy-start.1 = (bf16[8,512,256]{2,1,0:T(8,128)(2,1)S(1)}, bf16[8,512,256]{2,1,0:T(8,128)(2,1)}, u32[]{:S(2)}) copy-start(bf16[8,512,256]{2,1,0:T(8,128)(2,1)} %tiles_hbm.5) | copy-start | bytes 6291460
  7.9 0.8 %copy-start.3 = (f32[32,256]{1,0:T(8,128)S(1)}, f32[32,256]{1,0:T(8,128)}, u32[]{:S(2)}) copy-start(f32[32,256]{1,0:T(8,128)} %noise_ref.5) | copy-start | bytes 98308
  8.7 0.7 %copy-start.4 = (s32[16,8]{0,1:T(8,128)S(1)}, s32[16,8]{0,1:T(8,128)}, u32[]{:S(2)}) copy-start(s32[16,8]{0,1:T(8,128)} %param.10) | copy-start | bytes 1540
  9.4 0.7 %copy-start.5 = (s32[16,8]{0,1:T(8,128)S(1)}, s32[16,8]{0,1:T(8,128)}, u32[]{:S(2)}) copy-start(s32[16,8]{0,1:T(8,128)} %param.11) | copy-start | bytes 1540
  10.0 0.7 %copy-start.6 = (s32[16]{0:T(128)S(1)}, s32[16]{0:T(128)}, u32[]{:S(2)}) copy-start(s32[16]{0:T(128)} %block_ref.5) | copy-start | bytes 196
  10.7 0.7 %copy-start.7 = (f32[128]{0:T(128)S(1)}, f32[128]{0:T(128)}, u32[]{:S(2)}) copy-start(f32[128]{0:T(128)} %param.14) | copy-start | bytes 1540
  19.8 9.8 %copy-start.8 = (bf16[1,32,512]{2,1,0:T(8,128)(2,1)S(1)}, bf16[1,32,512]{2,1,0:T(8,128)(2,1)}, u32[]{:S(2)}) copy-start(bf16[1,32,512]{2,1,0:T(8,128)(2,1)} %param.8) | copy-start | bytes 98308
  19.8 15.5 %collective-permute-start.10 = (bf16[8,32,512]{2,1,0:T(8,128)(2,1)S(1)}, bf16[8,32,512]{2,1,0:T(8,128)(2,1)S(1)}, u32[]{:S(2)}, u32[]{:S(2)}) collective-permute-start(bf16[8,32,512]{2,1,0:T(8,128)(2,1)S(1)} %get-tuple-element.10), channel_id=1, source_target_pairs={{0,1},{1,0},{2,3},{3,2},{4,5},{5,4},{6,7},{7,6},{8,9},{9,8},{10,11... | collective-permute-start | bytes 786440 | tf_op jit(solution)/shard_map/ppermute | solution.py:282
  29.1 8.1 %collective-permute-start.5 = (bf16[8,32,512]{2,1,0:T(8,128)(2,1)S(1)}, bf16[8,32,512]{2,1,0:T(8,128)(2,1)S(1)}, u32[]{:S(2)}, u32[]{:S(2)}) collective-permute-start(bf16[8,32,512]{2,1,0:T(8,128)(2,1)S(1)} %get-tuple-element.8), channel_id=1, source_target_pairs={{0,1},{1,0},{2,3},{3,2},{4,5},{5,4},{6,7},{7,6},{8,9},{9,8},{10,11... | collective-permute-start | bytes 786440 | tf_op jit(solution)/shard_map/ppermute | solution.py:282
  29.7 5.5 %collective-permute-start.3 = (bf16[4,32,512]{2,1,0:T(8,128)(2,1)S(1)}, bf16[4,32,512]{2,1,0:T(8,128)(2,1)S(1)}, u32[]{:S(2)}, u32[]{:S(2)}) collective-permute-start(bf16[4,32,512]{2,1,0:T(8,128)(2,1)S(1)} %pad_maximum_fusion), channel_id=1, source_target_pairs={{0,2},{1,3},{2,0},{3,1},{4,6},{5,7},{6,4},{7,5},{8,10},{9,11},{10,... | collective-permute-start | bytes 393224 | tf_op jit(solution)/shard_map/ppermute | solution.py:282
  35.2 17.4 %collective-permute-start.4 = (bf16[8,32,512]{2,1,0:T(8,128)(2,1)S(1)}, bf16[8,32,512]{2,1,0:T(8,128)(2,1)S(1)}, u32[]{:S(2)}, u32[]{:S(2)}) collective-permute-start(bf16[8,32,512]{2,1,0:T(8,128)(2,1)S(1)} %constant_dynamic-update-slice_fusion.near_ref), channel_id=1, source_target_pairs={{0,1},{1,0},{2,3},{3,2},{4,5},{5,4},{6,7},{7,6},{8,9},{9,8},{10,11... | collective-permute-start | bytes 786440 | tf_op jit(solution)/shard_map/ppermute | solution.py:282
  35.4 17.3 %copy-start.2 = (bf16[8,512,256]{2,1,0:T(8,128)(2,1)S(1)}, bf16[8,512,256]{2,1,0:T(8,128)(2,1)}, u32[]{:S(2)}) copy-start(bf16[8,512,256]{2,1,0:T(8,128)(2,1)} %tiles_hbm.5) | copy-start | bytes 6291460
  35.4 6.4 %collective-permute-start.11 = (bf16[4,32,512]{2,1,0:T(8,128)(2,1)S(1)}, bf16[4,32,512]{2,1,0:T(8,128)(2,1)S(1)}, u32[]{:S(2)}, u32[]{:S(2)}) collective-permute-start(bf16[4,32,512]{2,1,0:T(8,128)(2,1)S(1)} %slice.100), channel_id=1, source_target_pairs={{0,2},{1,3},{2,0},{3,1},{4,6},{5,7},{6,4},{7,5},{8,10},{9,11},{10,... | collective-permute-start | bytes 393224 | tf_op jit(solution)/shard_map/ppermute | solution.py:282
  37.3 9.0 %collective-permute-start.6 = (bf16[4,32,512]{2,1,0:T(8,128)(2,1)S(1)}, bf16[4,32,512]{2,1,0:T(8,128)(2,1)S(1)}, u32[]{:S(2)}, u32[]{:S(2)}) collective-permute-start(bf16[4,32,512]{2,1,0:T(8,128)(2,1)S(1)} %slice.101), channel_id=1, source_target_pairs={{0,2},{1,3},{2,0},{3,1},{4,6},{5,7},{6,4},{7,5},{8,10},{9,11},{10,... | collective-permute-start | bytes 393224 | tf_op jit(solution)/shard_map/ppermute | solution.py:282
  41.8 5.1 %collective-permute-start.12 = (bf16[32,512]{1,0:T(8,128)(2,1)S(1)}, bf16[32,512]{1,0:T(8,128)(2,1)S(1)}, u32[]{:S(2)}, u32[]{:S(2)}) collective-permute-start(bf16[32,512]{1,0:T(8,128)(2,1)S(1)} %get-tuple-element.15), channel_id=1, source_target_pairs={{0,4},{1,5},{2,6},{3,7},{4,0},{5,1},{6,2},{7,3},{8,12},{9,13},{10,... | collective-permute-start | bytes 98312 | tf_op jit(solution)/shard_map/ppermute | solution.py:282
  42.8 8.0 %collective-permute-start.13 = (bf16[32,512]{1,0:T(8,128)(2,1)S(1)}, bf16[32,512]{1,0:T(8,128)(2,1)S(1)}, u32[]{:S(2)}, u32[]{:S(2)}) collective-permute-start(bf16[32,512]{1,0:T(8,128)(2,1)S(1)} %get-tuple-element.17), channel_id=1, source_target_pairs={{0,8},{1,9},{2,10},{3,11},{4,12},{5,13},{6,14},{7,15},{8,0},{9,1},... | collective-permute-start | bytes 98312 | tf_op jit(solution)/shard_map/ppermute | solution.py:282
  46.3 5.7 %collective-permute-start.14 = (bf16[32,512]{1,0:T(8,128)(2,1)S(1)}, bf16[32,512]{1,0:T(8,128)(2,1)S(1)}, u32[]{:S(2)}, u32[]{:S(2)}) collective-permute-start(bf16[32,512]{1,0:T(8,128)(2,1)S(1)} %get-tuple-element.16), channel_id=1, source_target_pairs={{0,12},{1,13},{2,14},{3,15},{4,8},{5,9},{6,10},{7,11},{8,4},{9,5},... | collective-permute-start | bytes 98312 | tf_op jit(solution)/shard_map/ppermute | solution.py:282
  46.3 15.0 %collective-permute-start.7 = (bf16[32,512]{1,0:T(8,128)(2,1)S(1)}, bf16[32,512]{1,0:T(8,128)(2,1)S(1)}, u32[]{:S(2)}, u32[]{:S(2)}) collective-permute-start(bf16[32,512]{1,0:T(8,128)(2,1)S(1)} %get-tuple-element.18), channel_id=1, source_target_pairs={{0,4},{1,5},{2,6},{3,7},{4,0},{5,1},{6,2},{7,3},{8,12},{9,13},{10,... | collective-permute-start | bytes 98312 | tf_op jit(solution)/shard_map/ppermute | solution.py:282
  47.0 14.4 %collective-permute-start.8 = (bf16[32,512]{1,0:T(8,128)(2,1)S(1)}, bf16[32,512]{1,0:T(8,128)(2,1)S(1)}, u32[]{:S(2)}, u32[]{:S(2)}) collective-permute-start(bf16[32,512]{1,0:T(8,128)(2,1)S(1)} %get-tuple-element.20), channel_id=1, source_target_pairs={{0,8},{1,9},{2,10},{3,11},{4,12},{5,13},{6,14},{7,15},{8,0},{9,1},... | collective-permute-start | bytes 98312 | tf_op jit(solution)/shard_map/ppermute | solution.py:282
  50.8 10.6 %collective-permute-start.9 = (bf16[32,512]{1,0:T(8,128)(2,1)S(1)}, bf16[32,512]{1,0:T(8,128)(2,1)S(1)}, u32[]{:S(2)}, u32[]{:S(2)}) collective-permute-start(bf16[32,512]{1,0:T(8,128)(2,1)S(1)} %get-tuple-element.19), channel_id=1, source_target_pairs={{0,12},{1,13},{2,14},{3,15},{4,8},{5,9},{6,10},{7,11},{8,4},{9,5},... | collective-permute-start | bytes 98312 | tf_op jit(solution)/shard_map/ppermute | solution.py:282

commit v2 on v0

v2 whole, which is shorter than its diff:
```python
import functools

import jax
import jax.numpy as jnp
from jax import lax
from jax.experimental import pallas as pl
from jax.experimental.pallas import tpu as pltpu
from jax.sharding import PartitionSpec as P

LANES = 128
CHUNKS = 4
VMEM_BYTES = 62 * 1024 * 1024


def grid_of(devices):
    cores = 2 if devices % 2 == 0 else 1
    chips = devices // cores
    wide = 1
    while (2 * wide) ** 3 <= chips:
        wide *= 2
    return chips // wide, wide, cores


def sin_cos(angle):
    turns = jnp.floor(angle * 0.3183098861837907 + 0.5)
    rest = angle - turns * 3.140625
    rest = rest - turns * 9.675025939941406e-4
    rest = rest - turns * 1.5099580252808664e-7
    half = turns * 0.5
    sign = 1.0 - 4.0 * (half - jnp.floor(half))
    sq = rest * rest
    sin = rest * (1.0 + sq * (-1.0 / 6 + sq * (1.0 / 120 + sq * (-1.0 / 5040 + sq * (1.0 / 362880 + sq * (-1.0 / 39916800))))))
    cos = 1.0 + sq * (-0.5 + sq * (1.0 / 24 + sq * (-1.0 / 720 + sq * (1.0 / 40320 + sq * (-1.0 / 3628800 + sq * (1.0 / 479001600))))))
    return sign * sin, sign * cos


def tables(defocus_ref, height, pixels, line_ref, pixel_ref):
    images = defocus_ref.shape[1]
    defocus = defocus_ref[...]
    rows = lax.broadcasted_iota(jnp.int32, (height, images), 0)
    line = ((rows // 2 + 1).astype(jnp.float32) / (height // 2)) ** 2
    line_ref[0], line_ref[1] = sin_cos(defocus * line + 0.3)
    column = jnp.transpose(jnp.broadcast_to(defocus, (LANES, images)))
    part = 32
    lanes = lax.broadcasted_iota(jnp.int32, (part, LANES), 1)
    for n in range(images // part):
        rows = slice(n * part, (n + 1) * part)
        for m in range(pixels // LANES):
            pixel = ((lanes + (m * LANES + 1)).astype(jnp.float32) / pixels) ** 2
            at = slice(m * LANES, (m + 1) * LANES)
            pixel_ref[0, rows, at], pixel_ref[1, rows, at] = sin_cos(column[rows] * pixel)


def contrast_of(line_ref, pixel_ref, i):
    sin_line, cos_line = line_ref[0, :, i : i + 1], line_ref[1, :, i : i + 1]
    return sin_line * pixel_ref[1, i : i + 1, :] + cos_line * pixel_ref[0, i : i + 1, :]


def copies(pairs, sems):
    started = [pltpu.make_async_copy(source, target, sems.at[n]) for n, (source, target) in enumerate(pairs)]
    for copy in started:
        copy.start()
    return started


def image_parts(images_hbm, images_ref):
    part = images_ref.shape[0] // CHUNKS
    return [(images_hbm.at[pl.ds(n * part, part)], images_ref.at[pl.ds(n * part, part)]) for n in range(CHUNKS)]


def insert_kernel(shape, slab_hbm, tile_hbm, block_hbm, defocus_hbm, noise_hbm, tiles_hbm, images_hbm,
                  send_ref, keep_ref, line_ref, pixel_ref,
                  slab_ref, tile_ref, block_ref, defocus_ref, noise_ref, tiles_ref, images_ref,
                  sums_ref, parts_ref, place_ref, sems):
    far, wide, cores = shape
    small = [(defocus_hbm, defocus_ref), (block_hbm, block_ref), (noise_hbm, noise_ref), (slab_hbm, slab_ref), (tile_hbm, tile_ref)]
    started = copies(small + image_parts(images_hbm, images_ref) + [(tiles_hbm, tiles_ref)], sems)
    height, pixels = noise_ref.shape
    crossed, blocks = slab_ref.shape
    kinds = tiles_ref.shape[0]
    rows = blocks * 2 * height
    devices = place_ref.shape[0] // blocks
    batches = block_ref.shape[0]
    size = images_ref.shape[0] // batches
    for copy in started[: len(small)]:
        copy.wait()
    tables(defocus_ref, height, pixels, line_ref, pixel_ref)

    def clear(n, carry):
        for m in range(blocks):
            place_ref[n * blocks + m] = kinds * rows
        return carry

    lax.fori_loop(0, devices, clear, 0, unroll=devices <= 16)
    for k in range(blocks):
        for r in range(crossed):
            place_ref[slab_ref[r, k] * blocks + k] = tile_ref[r, k] * rows + k * 2 * height
    parts_ref[pl.ds(kinds * rows, 2 * height), :] = jnp.zeros((2 * height, parts_ref.shape[1]), jnp.float32)
    sums_ref[...] = jnp.zeros_like(sums_ref)

    for b in range(batches):
        if b % (batches // CHUNKS) == 0:
            started[len(small) + b // (batches // CHUNKS)].wait()
        data = jnp.zeros((height, pixels), jnp.float32)
        weight = jnp.zeros((height, pixels), jnp.float32)
        for j in range(size):
            wave = contrast_of(line_ref, pixel_ref, b * size + j)
            data = data + wave * images_ref[b * size + j].astype(jnp.float32)
            weight = weight + wave * wave
        k = block_ref[b]
        sums_ref[k, 0] = sums_ref[k, 0] + data
        sums_ref[k, 1] = sums_ref[k, 1] + weight

    sums = (sums_ref[...] * noise_ref[...][None, None]).astype(jnp.bfloat16).reshape(rows, pixels)
    started[-1].wait()
    for t in range(kinds):
        parts_ref[t * rows : (t + 1) * rows, :] = lax.dot_general(
            sums, tiles_ref[t], (((1,), (1,)), ((), ())), preferred_element_type=jnp.float32
        )
    me = lax.axis_index("slab")

    def total(slot, core, kind):
        x, z = slot // far, lax.rem(slot, far)
        s = me ^ ((z * wide + x) * cores + core)
        acc = None
        for k in range(blocks):
            at = pl.multiple_of(place_ref[s * blocks + k] + kind * height, height)
            part = parts_ref[pl.ds(at, height), :]
            acc = part if acc is None else acc + part
        return acc

    def send(slot, carry):
        for kind in range(2):
            send_ref[slot, kind] = total(slot, 1, kind).astype(jnp.bfloat16)
        return carry

    def keep(slot, carry):
        for kind in range(2):
            keep_ref[slot, kind] = total(slot, 0, kind)
        return carry

    half = devices // 2
    lax.fori_loop(0, half, send, 0)
    lax.fori_loop(0, half, keep, 0)


def score_kernel(shape, slab_hbm, tile_hbm, block_hbm, noise_hbm, line_hbm, pixel_hbm, near_hbm, other_hbm, images_hbm, tiles_hbm,
                 score_ref,
                 slab_ref, tile_ref, block_ref, noise_ref, line_ref, pixel_ref, slabs_ref, tiles_ref, images_ref,
                 flat_ref, proj_ref, part_ref, sems):
    far, wide, cores = shape
    height, pixels = noise_ref.shape
    crossed, blocks = slab_ref.shape
    batches = block_ref.shape[0]
    size = images_ref.shape[0] // batches
    half = near_hbm.shape[0]
    first = [(near_hbm, slabs_ref.at[pl.ds(0, half)]), (tiles_hbm, tiles_ref), (other_hbm, slabs_ref.at[pl.ds(half, half)]),
             (slab_hbm, slab_ref), (tile_hbm, tile_ref)]
    last = [(block_hbm, block_ref), (noise_hbm, noise_ref), (line_hbm, line_ref), (pixel_hbm, pixel_ref), (images_hbm, images_ref)]
    started = copies(first + last, sems)
    me = lax.axis_index("slab")
    dense = 2 * half * tiles_ref.shape[0] <= crossed * blocks
    for copy in started[: len(first)]:
        copy.wait()

    def slot_of(s):
        away = me ^ s
        core, chip = lax.rem(away, cores), away // cores
        return core * half + lax.rem(chip, wide) * far + chip // wide

    if dense:
        lines = slabs_ref[...].reshape(2 * half * height, slabs_ref.shape[2])
        for t in range(tiles_ref.shape[0]):
            flat_ref[t] = jnp.dot(lines, tiles_ref[t], preferred_element_type=jnp.float32)

    def project(k, carry):
        acc = None
        for r in range(crossed):
            slot, t = slot_of(slab_ref[r, k]), tile_ref[r, k]
            if dense:
                part = flat_ref[t, pl.ds(pl.multiple_of(slot * height, height), height), :]
            else:
                part = jnp.dot(slabs_ref[slot], tiles_ref[t], preferred_element_type=jnp.float32)
            acc = part if acc is None else acc + part
        proj_ref[k] = acc
        return carry

    lax.fori_loop(0, blocks, project, 0, unroll=dense)
    for copy in started[len(first) :]:
        copy.wait()

    for b in range(batches):
        k = block_ref[b]
        for j in range(size):
            i = b * size + j
            residual = images_ref[i].astype(jnp.float32) - contrast_of(line_ref, pixel_ref, i) * proj_ref[k]
            power = jnp.sum(residual * residual * noise_ref[...], axis=0, keepdims=True)
            part_ref[i : i + 1, :] = sum(power[:, n * LANES : (n + 1) * LANES] for n in range(pixels // LANES))
    total = jnp.sum(jnp.transpose(part_ref[...]), axis=0, keepdims=True)
    score_ref[...] = total * (1.0 / (height * pixels))


def on_device(volume, tiles, slab_ids, tile_ids, batch_block, images, defocus, inv_sigma2):
    blocks, crossed = slab_ids.shape
    height, length = volume.shape[1:]
    count, _, pixels = images.shape
    kinds = tiles.shape[0]
    devices = lax.axis_size("slab")
    shape = far, wide, cores = grid_of(devices)
    half = devices // 2
    slabs, kind_rows, row = slab_ids.T, tile_ids.T, defocus.reshape(1, count)

    def swap(array, offset):
        return lax.ppermute(array, "slab", [(i, i ^ offset) for i in range(devices)])

    vmem = pl.BlockSpec(memory_space=pltpu.VMEM)
    hbm = pl.BlockSpec(memory_space=pl.ANY)
    params = pltpu.CompilerParams(vmem_limit_bytes=VMEM_BYTES)
    line_shape, pixel_shape = (2, height, count), (2, count, pixels)
    index_scratch = [pltpu.SMEM((crossed, blocks), jnp.int32), pltpu.SMEM((crossed, blocks), jnp.int32), pltpu.SMEM(batch_block.shape, jnp.int32)]
    noise_scratch = pltpu.VMEM((height, pixels), jnp.float32)
    tiles_scratch = pltpu.VMEM(tiles.shape, jnp.bfloat16)
    images_scratch = pltpu.VMEM(images.shape, jnp.bfloat16)
    insert_flops = 4 * blocks * height * pixels * kinds * length

    send, keep, line, pixel = pl.pallas_call(
        functools.partial(insert_kernel, shape),
        out_shape=(
            jax.ShapeDtypeStruct((half, 2, height, length), jnp.bfloat16),
            jax.ShapeDtypeStruct((half, 2, height, length), jnp.float32),
            jax.ShapeDtypeStruct(line_shape, jnp.float32),
            jax.ShapeDtypeStruct(pixel_shape, jnp.float32),
        ),
        in_specs=[hbm] * 7,
        out_specs=(vmem, vmem, vmem, vmem),
        scratch_shapes=[
            *index_scratch,
            pltpu.VMEM((1, count), jnp.float32),
            noise_scratch,
            tiles_scratch,
            images_scratch,
            pltpu.VMEM((blocks, 2, height, pixels), jnp.float32),
            pltpu.VMEM((kinds * blocks * 2 * height + 2 * height, length), jnp.float32),
            pltpu.SMEM((devices * blocks,), jnp.int32),
            pltpu.SemaphoreType.DMA((CHUNKS + 6,)),
        ],
        compiler_params=params,
        cost_estimate=pl.CostEstimate(flops=insert_flops, bytes_accessed=6 << 20, transcendentals=0),
        name="insert",
    )(slabs, kind_rows, batch_block, row, inv_sigma2, tiles, images)

    column = jnp.concatenate([volume] + [swap(volume, z * wide * cores) for z in range(1, far)], axis=0)
    near = jnp.concatenate([column] + [swap(column, x * cores) for x in range(1, wide)], axis=0)
    other = swap(near, 1)

    if devices * kinds <= blocks * crossed:
        flat = pltpu.VMEM((kinds, devices * height, pixels), jnp.float32)
    else:
        flat = pltpu.VMEM((8, LANES), jnp.float32)
    scores = pl.pallas_call(
        functools.partial(score_kernel, shape),
        out_shape=jax.ShapeDtypeStruct((1, count), jnp.float32),
        in_specs=[hbm] * 10,
        out_specs=vmem,
        scratch_shapes=[
            *index_scratch,
            noise_scratch,
            pltpu.VMEM(line_shape, jnp.float32),
            pltpu.VMEM(pixel_shape, jnp.float32),
            pltpu.VMEM((devices, height, length), jnp.bfloat16),
            tiles_scratch,
            images_scratch,
            flat,
            pltpu.VMEM((blocks, height, pixels), jnp.float32),
            pltpu.VMEM((count, LANES), jnp.float32),
            pltpu.SemaphoreType.DMA((10,)),
        ],
        compiler_params=params,
        cost_estimate=pl.CostEstimate(flops=insert_flops // 4, bytes_accessed=5 << 20, transcendentals=0),
        name="scores",
    )(slabs, kind_rows, batch_block, inv_sigma2, line, pixel, near, other, images, tiles)

    sums = (keep + swap(send, 1).astype(jnp.float32)).reshape(wide, far, 2, height, length)
    mine = sums[0]
    for x in range(1, wide):
        mine = mine + swap(sums[x].astype(jnp.bfloat16), x * cores).astype(jnp.float32)
    total = mine[0]
    for z in range(1, far):
        total = total + swap(mine[z].astype(jnp.bfloat16), z * wide * cores).astype(jnp.float32)
    return scores.reshape(count), total[0:1], total[1:2]


def solution(mesh):
    placed = (
        P(("parts", "slab"), None, None),
        P(),
        P(("parts", "slab"), None),
        P(("parts", "slab"), None),
        P(("parts", "slab")),
        P(("parts", "slab"), None, None),
        P(("parts", "slab")),
        P("parts", None),
    )
    return jax.shard_map(
        on_device,
        mesh=mesh,
        in_specs=placed,
        out_specs=(
            P(("parts", "slab")),
            P(("parts", "slab"), None, None),
            P(("parts", "slab"), None, None),
        ),
        check_vma=False,
    )
```

time: 631 us -> 41.8 us (0.07)
  the two profiles are of different devices: /device:TPU:15 before, /device:TPU:0 now
where the time goes in v2:
time: 41.8 us; the launch traced here: 41.7 us
  Pallas kernels  15.2 us (36%)
  starting transfers between devices  11.6 us (28%)
  waiting for transfers between devices  11.1 us (27%)
  other arithmetic  1.57 us (4%)
  local copies, waits for them, and re-layouts  1.42 us (3%)
  between operations  0.76 us (2%)
    ppermute x10, starting transfers between devices, swap(): lax.ppermute(array, 'slab', [(i, i ^ offset) for i in range(devices)])  11.6 us
    ppermute x10, waiting for transfers between devices, swap(): lax.ppermute(array, 'slab', [(i, i ^ offset) for i in range(devices)])  11.1 us
    pallas_call x1, Pallas kernels, on_device(): pl.pallas_call(functools.partial(insert_kernel, shape), out_shape=(jax.Sh...  8.61 us
    pallas_call x1, Pallas kernels, on_device(): pl.pallas_call(functools.partial(score_kernel, shape), out_shape=jax.Shap...  6.6 us
    add x1, other arithmetic, on_device(): keep + swap(send, 1).astype(jnp.float32)  1.42 us
  transfers between devices with their start and end apart: 10, of which 4 were waited for; matrix products, arithmetic and copies ran while one was open for 4% of the time, Pallas kernels for 16%

profile of v2, /device:TPU:0, one launch (start us, length us, event | category | flops | bytes accessed | tf_op | source)
XLA Modules:
  0.0 41.7 jit_solution(14468302656930487438)
XLA Ops:
  0.6 0.0 copy-start.2
  0.6 8.6 %insert.1 = (bf16[8,2,32,512]{3,2,1,0:T(8,128)(2,1)}, f32[8,2,32,512]{3,2,1,0:T(8,128)}, f32[2,32,128]{2,1,0:T(8,128)}, f32[2,128,256]{2,1,0:T(8,128)}) custom-call(s32[8,16]{1,0:T(8,128)} %bitcast.18, s32[8,16]{1,0:T(8,128)} %bitcast.20, s32[16]{0:T(128)} %block_hbm.3, f32[1,128]{1,0:T(1,128)} %bitcast.23, f32[32,256]{1,0:T(8,128)} %noise_hbm.3, ...), custom_call_target="tpu_custom_call" | custom-call | flops 2147483648 | bytes 6291456 | tf_op jit(solution)/shard_map/insert/pallas_call | solution.py:226
  9.3 0.5 %collective-permute-start.5 = (bf16[8,2,32,512]{3,2,1,0:T(8,128)(2,1)}, bf16[8,2,32,512]{3,2,1,0:T(8,128)(2,1)S(1)}, u32[]{:S(2)}, u32[]{:S(2)}) collective-permute-start(bf16[8,2,32,512]{3,2,1,0:T(8,128)(2,1)} %get-tuple-element.10), channel_id=1, source_target_pairs={{0,1},{1,0},{2,3},{3,2},{4,5},{5,4},{6,7},{7,6},{8,9},{9,8},{10,11... | collective-permute-start | bytes 1572872 | tf_op jit(solution)/shard_map/ppermute | solution.py:214
  9.8 0.0 copy-done.2
  9.8 4.7 %collective-permute-start.2 = (bf16[1,32,512]{2,1,0:T(8,128)(2,1)S(1)}, bf16[1,32,512]{2,1,0:T(8,128)(2,1)S(1)}, u32[]{:S(2)}, u32[]{:S(2)}) collective-permute-start(bf16[1,32,512]{2,1,0:T(8,128)(2,1)S(1)} %copy-done.2), channel_id=1, source_target_pairs={{0,12},{1,13},{2,14},{3,15},{4,8},{5,9},{6,10},{7,11},{8,4},{9,5},... | collective-permute-start | bytes 98312 | tf_op jit(solution)/shard_map/ppermute | solution.py:214
  14.5 0.0 collective-permute-start.1
  14.5 0.6 %collective-permute-start = (bf16[1,32,512]{2,1,0:T(8,128)(2,1)S(1)}, bf16[1,32,512]{2,1,0:T(8,128)(2,1)S(1)}, u32[]{:S(2)}, u32[]{:S(2)}) collective-permute-start(bf16[1,32,512]{2,1,0:T(8,128)(2,1)S(1)} %copy-done.2), channel_id=1, source_target_pairs={{0,4},{1,5},{2,6},{3,7},{4,0},{5,1},{6,2},{7,3},{8,12},{9,13},{10,... | collective-permute-start | bytes 98312 | tf_op jit(solution)/shard_map/ppermute | solution.py:214
  15.1 1.4 %collective-permute-done.2 = bf16[1,32,512]{2,1,0:T(8,128)(2,1)S(1)} collective-permute-done((bf16[1,32,512]{2,1,0:T(8,128)(2,1)S(1)}, bf16[1,32,512]{2,1,0:T(8,128)(2,1)S(1)}, u32[]{:S(2)}, u32[]{:S(2)}) %collective-permute-start.2) | collective-permute-done | bytes 32800 | tf_op jit(solution)/shard_map/ppermute | solution.py:214
  16.5 2.8 %collective-permute-done.1 = bf16[1,32,512]{2,1,0:T(8,128)(2,1)S(1)} collective-permute-done((bf16[1,32,512]{2,1,0:T(8,128)(2,1)S(1)}, bf16[1,32,512]{2,1,0:T(8,128)(2,1)S(1)}, u32[]{:S(2)}, u32[]{:S(2)}) %collective-permute-start.1) | collective-permute-done | bytes 32800 | tf_op jit(solution)/shard_map/ppermute | solution.py:214
  19.3 0.0 collective-permute-done
  19.3 1.6 %collective-permute-start.3 = (bf16[4,32,512]{2,1,0:T(8,128)(2,1)S(1)}, bf16[4,32,512]{2,1,0:T(8,128)(2,1)S(1)}, u32[]{:S(2)}, u32[]{:S(2)}) collective-permute-start(bf16[4,32,512]{2,1,0:T(8,128)(2,1)S(1)} %pad_maximum_fusion), channel_id=1, source_target_pairs={{0,2},{1,3},{2,0},{3,1},{4,6},{5,7},{6,4},{7,5},{8,10},{9,11},{10,... | collective-permute-start | bytes 393224 | tf_op jit(solution)/shard_map/ppermute | solution.py:214
  20.9 0.0 collective-permute-done.5
  20.9 1.4 %convert_add_fusion = f32[8,2,32,512]{3,2,1,0:T(8,128)S(1)} fusion(f32[8,2,32,512]{3,2,1,0:T(8,128)} %get-tuple-element.9, bf16[8,2,32,512]{3,2,1,0:T(8,128)(2,1)S(1)} %collective-permute-done.5), kind=kLoop, calls=%fused_computation | loop fusion | flops 524288 | bytes 2621440 | tf_op jit(solution)/shard_map/add | solution.py:283
  22.3 0.6 %collective-permute-start.6 = (bf16[4,2,32,512]{3,2,1,0:T(8,128)(2,1)S(1)}, bf16[4,2,32,512]{3,2,1,0:T(8,128)(2,1)S(1)}, u32[]{:S(2)}, u32[]{:S(2)}) collective-permute-start(bf16[4,2,32,512]{3,2,1,0:T(8,128)(2,1)S(1)} %slice.58), channel_id=1, source_target_pairs={{0,2},{1,3},{2,0},{3,1},{4,6},{5,7},{6,4},{7,5},{8,10},{9,11},{10,... | collective-permute-start | bytes 786440 | tf_op jit(solution)/shard_map/ppermute | solution.py:214
  22.9 1.7 %collective-permute-done.3 = bf16[4,32,512]{2,1,0:T(8,128)(2,1)S(1)} collective-permute-done((bf16[4,32,512]{2,1,0:T(8,128)(2,1)S(1)}, bf16[4,32,512]{2,1,0:T(8,128)(2,1)S(1)}, u32[]{:S(2)}, u32[]{:S(2)}) %collective-permute-start.3) | collective-permute-done | bytes 131104 | tf_op jit(solution)/shard_map/ppermute | solution.py:214
  24.7 0.0 copy-start
  24.7 0.1 collective-permute-start.4
  24.8 5.2 %collective-permute-done.6 = bf16[4,2,32,512]{3,2,1,0:T(8,128)(2,1)S(1)} collective-permute-done((bf16[4,2,32,512]{3,2,1,0:T(8,128)(2,1)S(1)}, bf16[4,2,32,512]{3,2,1,0:T(8,128)(2,1)S(1)}, u32[]{:S(2)}, u32[]{:S(2)}) %collective-permute-start.6) | collective-permute-done | bytes 262176 | tf_op jit(solution)/shard_map/ppermute | solution.py:214
  29.9 0.1 fusion.3
  30.1 0.4 collective-permute-start.7
  30.5 3.2 %collective-permute-start.9 = (bf16[2,32,512]{2,1,0:T(8,128)(2,1)S(1)}, bf16[2,32,512]{2,1,0:T(8,128)(2,1)S(1)}, u32[]{:S(2)}, u32[]{:S(2)}) collective-permute-start(bf16[2,32,512]{2,1,0:T(8,128)(2,1)S(1)} %get-tuple-element.14), channel_id=1, source_target_pairs={{0,12},{1,13},{2,14},{3,15},{4,8},{5,9},{6,10},{7,11},{8,4},{9,5},... | collective-permute-start | bytes 196616 | tf_op jit(solution)/shard_map/ppermute | solution.py:214
  33.6 0.0 collective-permute-start.8
  33.6 0.0 collective-permute-done.4.other_hbm
  33.6 0.0 copy-start.1
  33.6 0.0 copy-done
  33.6 0.7 %copy-done.1 = bf16[8,32,512]{2,1,0:T(8,128)(2,1)} copy-done((bf16[8,32,512]{2,1,0:T(8,128)(2,1)}, bf16[8,32,512]{2,1,0:T(8,128)(2,1)S(1)}, u32[]{:S(2)}) %copy-start.1) | copy-done | bytes 262168
  34.3 6.6 %scores.1 = f32[1,128]{1,0:T(1,128)} custom-call(s32[8,16]{1,0:T(8,128)} %bitcast.19, s32[8,16]{1,0:T(8,128)} %bitcast.21, s32[16]{0:T(128)} %block_hbm.3, f32[32,256]{1,0:T(8,128)} %noise_hbm.3, f32[2,32,128]{2,1,0:T(8,128)} %get-tuple-element.7.line_hbm, f32[2,128,256]{2,1,0:T(8,128)} %get-tuple-element.8.pixel_hbm, bf16[8,32,512]{2,1,0:T(8,128)(2,1)} %copy-done, ...), custom_call_target="tpu_custom_call" | custom-call | flops 536870912 | bytes 5242880 | tf_op jit(solution)/shard_map/scores/pallas_call | solution.py:260
  40.9 0.0 collective-permute-done.7
  41.0 0.0 collective-permute-done.9
  41.0 0.0 collective-permute-done.8
  41.0 0.7 %fusion.4 = (f32[1,32,512]{2,1,0:T(8,128)}, f32[1,32,512]{2,1,0:T(8,128)}) fusion(f32[2,32,512]{2,1,0:T(8,128)S(1)} %fusion.2), kind=kLoop, calls=%fused_computation.17 | loop fusion | bytes 262144 | tf_op jit(solution)/shard_map/slice | solution.py:290
  (9 shorter events, 0.1 us)
Async XLA Ops:
  0.6 9.1 %copy-start.2 = (bf16[1,32,512]{2,1,0:T(8,128)(2,1)S(1)}, bf16[1,32,512]{2,1,0:T(8,128)(2,1)}, u32[]{:S(2)}) copy-start(bf16[1,32,512]{2,1,0:T(8,128)(2,1)} %param.8) | copy-start | bytes 98308
  9.3 11.6 %collective-permute-start.5 = (bf16[8,2,32,512]{3,2,1,0:T(8,128)(2,1)}, bf16[8,2,32,512]{3,2,1,0:T(8,128)(2,1)S(1)}, u32[]{:S(2)}, u32[]{:S(2)}) collective-permute-start(bf16[8,2,32,512]{3,2,1,0:T(8,128)(2,1)} %get-tuple-element.10), channel_id=1, source_target_pairs={{0,1},{1,0},{2,3},{3,2},{4,5},{5,4},{6,7},{7,6},{8,9},{9,8},{10,11... | collective-permute-start | bytes 1572872 | tf_op jit(solution)/shard_map/ppermute | solution.py:214
  9.8 6.7 %collective-permute-start.2 = (bf16[1,32,512]{2,1,0:T(8,128)(2,1)S(1)}, bf16[1,32,512]{2,1,0:T(8,128)(2,1)S(1)}, u32[]{:S(2)}, u32[]{:S(2)}) collective-permute-start(bf16[1,32,512]{2,1,0:T(8,128)(2,1)S(1)} %copy-done.2), channel_id=1, source_target_pairs={{0,12},{1,13},{2,14},{3,15},{4,8},{5,9},{6,10},{7,11},{8,4},{9,5},... | collective-permute-start | bytes 98312 | tf_op jit(solution)/shard_map/ppermute | solution.py:214
  14.5 4.8 %collective-permute-start.1 = (bf16[1,32,512]{2,1,0:T(8,128)(2,1)S(1)}, bf16[1,32,512]{2,1,0:T(8,128)(2,1)S(1)}, u32[]{:S(2)}, u32[]{:S(2)}) collective-permute-start(bf16[1,32,512]{2,1,0:T(8,128)(2,1)S(1)} %copy-done.2), channel_id=1, source_target_pairs={{0,8},{1,9},{2,10},{3,11},{4,12},{5,13},{6,14},{7,15},{8,0},{9,1},... | collective-permute-start | bytes 98312 | tf_op jit(solution)/shard_map/ppermute | solution.py:214
  14.5 4.8 %collective-permute-start = (bf16[1,32,512]{2,1,0:T(8,128)(2,1)S(1)}, bf16[1,32,512]{2,1,0:T(8,128)(2,1)S(1)}, u32[]{:S(2)}, u32[]{:S(2)}) collective-permute-start(bf16[1,32,512]{2,1,0:T(8,128)(2,1)S(1)} %copy-done.2), channel_id=1, source_target_pairs={{0,4},{1,5},{2,6},{3,7},{4,0},{5,1},{6,2},{7,3},{8,12},{9,13},{10,... | collective-permute-start | bytes 98312 | tf_op jit(solution)/shard_map/ppermute | solution.py:214
  19.3 5.4 %collective-permute-start.3 = (bf16[4,32,512]{2,1,0:T(8,128)(2,1)S(1)}, bf16[4,32,512]{2,1,0:T(8,128)(2,1)S(1)}, u32[]{:S(2)}, u32[]{:S(2)}) collective-permute-start(bf16[4,32,512]{2,1,0:T(8,128)(2,1)S(1)} %pad_maximum_fusion), channel_id=1, source_target_pairs={{0,2},{1,3},{2,0},{3,1},{4,6},{5,7},{6,4},{7,5},{8,10},{9,11},{10,... | collective-permute-start | bytes 393224 | tf_op jit(solution)/shard_map/ppermute | solution.py:214
  22.3 7.6 %collective-permute-start.6 = (bf16[4,2,32,512]{3,2,1,0:T(8,128)(2,1)S(1)}, bf16[4,2,32,512]{3,2,1,0:T(8,128)(2,1)S(1)}, u32[]{:S(2)}, u32[]{:S(2)}) collective-permute-start(bf16[4,2,32,512]{3,2,1,0:T(8,128)(2,1)S(1)} %slice.58), channel_id=1, source_target_pairs={{0,2},{1,3},{2,0},{3,1},{4,6},{5,7},{6,4},{7,5},{8,10},{9,11},{10,... | collective-permute-start | bytes 786440 | tf_op jit(solution)/shard_map/ppermute | solution.py:214
  24.7 9.0 %copy-start = (bf16[8,32,512]{2,1,0:T(8,128)(2,1)}, bf16[8,32,512]{2,1,0:T(8,128)(2,1)S(1)}, u32[]{:S(2)}) copy-start(bf16[8,32,512]{2,1,0:T(8,128)(2,1)S(1)} %constant_dynamic-update-slice_fusion.near_hbm) | copy-start | bytes 786436
  24.7 8.9 %collective-permute-start.4 = (bf16[8,32,512]{2,1,0:T(8,128)(2,1)S(1)}, bf16[8,32,512]{2,1,0:T(8,128)(2,1)S(1)}, u32[]{:S(2)}, u32[]{:S(2)}) collective-permute-start(bf16[8,32,512]{2,1,0:T(8,128)(2,1)S(1)} %constant_dynamic-update-slice_fusion.near_hbm), channel_id=1, source_target_pairs={{0,1},{1,0},{2,3},{3,2},{4,5},{5,4},{6,7},{7,6},{8,9},{9,8},{10,11... | collective-permute-start | bytes 786440 | tf_op jit(solution)/shard_map/ppermute | solution.py:214
  30.1 10.9 %collective-permute-start.7 = (bf16[2,32,512]{2,1,0:T(8,128)(2,1)S(1)}, bf16[2,32,512]{2,1,0:T(8,128)(2,1)S(1)}, u32[]{:S(2)}, u32[]{:S(2)}) collective-permute-start(bf16[2,32,512]{2,1,0:T(8,128)(2,1)S(1)} %get-tuple-element.13), channel_id=1, source_target_pairs={{0,4},{1,5},{2,6},{3,7},{4,0},{5,1},{6,2},{7,3},{8,12},{9,13},{10,... | collective-permute-start | bytes 196616 | tf_op jit(solution)/shard_map/ppermute | solution.py:214
  30.5 10.5 %collective-permute-start.9 = (bf16[2,32,512]{2,1,0:T(8,128)(2,1)S(1)}, bf16[2,32,512]{2,1,0:T(8,128)(2,1)S(1)}, u32[]{:S(2)}, u32[]{:S(2)}) collective-permute-start(bf16[2,32,512]{2,1,0:T(8,128)(2,1)S(1)} %get-tuple-element.14), channel_id=1, source_target_pairs={{0,12},{1,13},{2,14},{3,15},{4,8},{5,9},{6,10},{7,11},{8,4},{9,5},... | collective-permute-start | bytes 196616 | tf_op jit(solution)/shard_map/ppermute | solution.py:214
  33.6 7.3 %collective-permute-start.8 = (bf16[2,32,512]{2,1,0:T(8,128)(2,1)S(1)}, bf16[2,32,512]{2,1,0:T(8,128)(2,1)S(1)}, u32[]{:S(2)}, u32[]{:S(2)}) collective-permute-start(bf16[2,32,512]{2,1,0:T(8,128)(2,1)S(1)} %get-tuple-element.15), channel_id=1, source_target_pairs={{0,8},{1,9},{2,10},{3,11},{4,12},{5,13},{6,14},{7,15},{8,0},{9,1},... | collective-permute-start | bytes 196616 | tf_op jit(solution)/shard_map/ppermute | solution.py:214
  33.6 0.7 %copy-start.1 = (bf16[8,32,512]{2,1,0:T(8,128)(2,1)}, bf16[8,32,512]{2,1,0:T(8,128)(2,1)S(1)}, u32[]{:S(2)}) copy-start(bf16[8,32,512]{2,1,0:T(8,128)(2,1)S(1)} %collective-permute-done.4.other_hbm) | copy-start | bytes 786436

commit v3 on v2

v3 whole, which is shorter than its diff:
```python
import functools

import jax
import jax.numpy as jnp
from jax import lax
from jax.experimental import pallas as pl
from jax.experimental.pallas import tpu as pltpu
from jax.sharding import PartitionSpec as P

LANES = 128
CHUNKS = 4
VMEM_BYTES = 32 * 1024 * 1024


def grid_of(devices):
    cores = 2 if devices % 2 == 0 else 1
    chips = devices // cores
    wide = 1
    while (2 * wide) ** 3 <= chips:
        wide *= 2
    return chips // wide, wide, cores


def sin_cos(angle):
    turns = jnp.floor(angle * 0.3183098861837907 + 0.5)
    rest = angle - turns * 3.140625
    rest = rest - turns * 9.675025939941406e-4
    rest = rest - turns * 1.5099580252808664e-7
    half = turns * 0.5
    sign = 1.0 - 4.0 * (half - jnp.floor(half))
    sq = rest * rest
    sin = rest * (1.0 + sq * (-1.0 / 6 + sq * (1.0 / 120 + sq * (-1.0 / 5040 + sq * (1.0 / 362880 + sq * (-1.0 / 39916800))))))
    cos = 1.0 + sq * (-0.5 + sq * (1.0 / 24 + sq * (-1.0 / 720 + sq * (1.0 / 40320 + sq * (-1.0 / 3628800 + sq * (1.0 / 479001600))))))
    return sign * sin, sign * cos


def tables(defocus_ref, height, pixels, line_ref, pixel_ref):
    images = defocus_ref.shape[1]
    defocus = defocus_ref[...]
    rows = lax.broadcasted_iota(jnp.int32, (height, images), 0)
    line = ((rows // 2 + 1).astype(jnp.float32) / (height // 2)) ** 2
    line_ref[0], line_ref[1] = sin_cos(defocus * line + 0.3)
    column = jnp.transpose(jnp.broadcast_to(defocus, (LANES, images)))
    part = 32
    lanes = lax.broadcasted_iota(jnp.int32, (part, LANES), 1)
    for n in range(images // part):
        rows = slice(n * part, (n + 1) * part)
        for m in range(pixels // LANES):
            pixel = ((lanes + (m * LANES + 1)).astype(jnp.float32) / pixels) ** 2
            at = slice(m * LANES, (m + 1) * LANES)
            pixel_ref[0, rows, at], pixel_ref[1, rows, at] = sin_cos(column[rows] * pixel)


def contrast_of(line_ref, pixel_ref, i):
    sin_line, cos_line = line_ref[0, :, i : i + 1], line_ref[1, :, i : i + 1]
    return sin_line * pixel_ref[1, i : i + 1, :] + cos_line * pixel_ref[0, i : i + 1, :]


def copies(pairs, sems):
    started = [pltpu.make_async_copy(source, target, sems.at[n]) for n, (source, target) in enumerate(pairs)]
    for copy in started:
        copy.start()
    return started


def sum_kernel(block_hbm, defocus_hbm, noise_hbm, tiles_hbm, images_hbm,
               sums_ref, wave_ref, tiles_ref, images_ref,
               block_ref, defocus_ref, noise_ref, line_ref, pixel_ref, acc_ref, sems):
    count = images_ref.shape[0]
    part = count // CHUNKS
    small = [(defocus_hbm, defocus_ref), (block_hbm, block_ref), (noise_hbm, noise_ref)]
    large = [(images_hbm.at[pl.ds(n * part, part)], images_ref.at[pl.ds(n * part, part)]) for n in range(CHUNKS)]
    started = copies(small + large + [(tiles_hbm, tiles_ref)], sems)
    height, pixels = noise_ref.shape
    batches = block_ref.shape[0]
    size = count // batches
    acc_ref[...] = jnp.zeros_like(acc_ref)
    for copy in started[: len(small)]:
        copy.wait()
    tables(defocus_ref, height, pixels, line_ref, pixel_ref)
    for b in range(batches):
        if b % (batches // CHUNKS) == 0:
            started[len(small) + b // (batches // CHUNKS)].wait()
        data = jnp.zeros((height, pixels), jnp.float32)
        weight = jnp.zeros((height, pixels), jnp.float32)
        for j in range(size):
            i = b * size + j
            wave = contrast_of(line_ref, pixel_ref, i)
            wave_ref[i] = wave
            data = data + wave * images_ref[i].astype(jnp.float32)
            weight = weight + wave * wave
        k = block_ref[b]
        acc_ref[k, 0] = acc_ref[k, 0] + data
        acc_ref[k, 1] = acc_ref[k, 1] + weight
    sums = (acc_ref[...] * noise_ref[...][None, None]).astype(jnp.bfloat16)
    sums_ref[...] = sums.reshape(sums_ref.shape)
    started[-1].wait()


def insert_kernel(shape, slab_hbm, tile_hbm, sums_ref, tiles_ref, send_ref, far_ref, near_ref,
                  slab_ref, tile_ref, parts_ref, place_ref, sems):
    far, wide, cores = shape
    started = copies([(slab_hbm, slab_ref), (tile_hbm, tile_ref)], sems)
    crossed, blocks = slab_ref.shape
    kinds = tiles_ref.shape[0]
    rows = sums_ref.shape[0]
    height = rows // (2 * blocks)
    devices = place_ref.shape[0] // blocks

    def clear(n, carry):
        for m in range(blocks):
            place_ref[n * blocks + m] = kinds * rows
        return carry

    lax.fori_loop(0, devices, clear, 0, unroll=devices <= 16)
    for copy in started:
        copy.wait()
    for k in range(blocks):
        for r in range(crossed):
            place_ref[slab_ref[r, k] * blocks + k] = tile_ref[r, k] * rows + k * 2 * height
    parts_ref[pl.ds(kinds * rows, 2 * height), :] = jnp.zeros((2 * height, parts_ref.shape[1]), jnp.float32)
    for t in range(kinds):
        parts_ref[t * rows : (t + 1) * rows, :] = lax.dot_general(
            sums_ref[...], tiles_ref[t], (((1,), (1,)), ((), ())), preferred_element_type=jnp.float32
        )
    me = lax.axis_index("slab")

    def total(x, z, core, kind):
        s = me ^ ((z * wide + x) * cores + core)
        acc = None
        for k in range(blocks):
            at = pl.multiple_of(place_ref[s * blocks + k] + kind * height, height)
            part = parts_ref[pl.ds(at, height), :]
            acc = part if acc is None else acc + part
        return acc

    def fill(ref, start, core):
        def step(slot, carry):
            x, z = start + slot // far, lax.rem(slot, far)
            for kind in range(2):
                ref[slot, kind] = total(x, z, core, kind).astype(ref.dtype)
            return carry

        lax.fori_loop(0, ref.shape[0], step, 0)

    fill(send_ref, 0, 1)
    fill(far_ref, 1, 0)
    fill(near_ref, 0, 0)


def score_kernel(shape, slab_hbm, tile_hbm, block_hbm, noise_hbm, wave_ref, near_ref, other_ref, images_ref, tiles_ref,
                 score_ref, slab_ref, tile_ref, block_ref, noise_ref, flat_ref, proj_ref, part_ref, sems):
    far, wide, cores = shape
    started = copies([(slab_hbm, slab_ref), (tile_hbm, tile_ref), (block_hbm, block_ref), (noise_hbm, noise_ref)], sems)
    height, pixels = noise_ref.shape
    crossed, blocks = slab_ref.shape
    batches = block_ref.shape[0]
    count = images_ref.shape[0]
    size = count // batches
    half = near_ref.shape[0]
    me = lax.axis_index("slab")
    dense = 2 * half * tiles_ref.shape[0] <= crossed * blocks

    def slot_of(s):
        away = me ^ s
        core, chip = lax.rem(away, cores), away // cores
        return core * half + lax.rem(chip, wide) * far + chip // wide

    for n, ref in enumerate((near_ref, other_ref)):
        lines = ref[...].reshape(half * height, ref.shape[2])
        if dense:
            for t in range(tiles_ref.shape[0]):
                flat_ref[t, n * half * height : (n + 1) * half * height, :] = jnp.dot(
                    lines, tiles_ref[t], preferred_element_type=jnp.float32
                )
        else:
            flat_ref[n * half * height : (n + 1) * half * height, :] = lines
    for copy in started:
        copy.wait()

    def project(k, carry):
        acc = None
        for r in range(crossed):
            t = tile_ref[r, k]
            rows = pl.ds(pl.multiple_of(slot_of(slab_ref[r, k]) * height, height), height)
            if dense:
                part = flat_ref[t, rows, :]
            else:
                part = jnp.dot(flat_ref[rows, :], tiles_ref[t], preferred_element_type=jnp.float32)
            acc = part if acc is None else acc + part
        proj_ref[k] = acc
        return carry

    lax.fori_loop(0, blocks, project, 0, unroll=dense)
    for b in range(batches):
        k = block_ref[b]
        for j in range(size):
            i = b * size + j
            residual = images_ref[i].astype(jnp.float32) - wave_ref[i] * proj_ref[k]
            power = residual * residual * noise_ref[...]
            power = sum(power[n * 8 : (n + 1) * 8] for n in range(height // 8))
            part_ref[i * 8 : (i + 1) * 8, :] = sum(power[:, n * LANES : (n + 1) * LANES] for n in range(pixels // LANES))
    total = sum(part_ref[pl.ds(n, count, 8), :] for n in range(8))
    total = jnp.sum(jnp.transpose(total), axis=0, keepdims=True)
    score_ref[...] = total * (1.0 / (height * pixels))


def on_device(volume, tiles, slab_ids, tile_ids, batch_block, images, defocus, inv_sigma2):
    blocks, crossed = slab_ids.shape
    height, length = volume.shape[1:]
    count, _, pixels = images.shape
    kinds = tiles.shape[0]
    devices = lax.axis_size("slab")
    shape = far, wide, cores = grid_of(devices)
    half = devices // 2
    rows = blocks * 2 * height
    slabs, kind_rows, row = slab_ids.T, tile_ids.T, defocus.reshape(1, count)

    def swap(array, offset):
        return lax.ppermute(array, "slab", [(i, i ^ offset) for i in range(devices)])

    vmem = pl.BlockSpec(memory_space=pltpu.VMEM)
    hbm = pl.BlockSpec(memory_space=pltpu.HBM)
    params = pltpu.CompilerParams(vmem_limit_bytes=VMEM_BYTES)
    f32, bf16 = jnp.float32, jnp.bfloat16
    pairs_scratch = [pltpu.SMEM((crossed, blocks), jnp.int32), pltpu.SMEM((crossed, blocks), jnp.int32)]
    block_scratch = pltpu.SMEM(batch_block.shape, jnp.int32)
    noise_scratch = pltpu.VMEM((height, pixels), f32)

    def call(kernel, outs, inputs, operands, scratch, flops, moved, name):
        operands = [
            pltpu.with_memory_space_constraint(x, pltpu.HBM) if spec is hbm else x for x, spec in zip(operands, inputs)
        ]
        return pl.pallas_call(
            kernel,
            out_shape=tuple(jax.ShapeDtypeStruct(s, t) for s, t in outs),
            in_specs=inputs,
            out_specs=(vmem,) * len(outs),
            scratch_shapes=scratch,
            compiler_params=params,
            cost_estimate=pl.CostEstimate(flops=flops, bytes_accessed=moved, transcendentals=0),
            name=name,
        )(*operands)

    column = jnp.concatenate([volume] + [swap(volume, z * wide * cores) for z in range(1, far)], axis=0)

    sums, wave, tiles_near, images_near = call(
        sum_kernel,
        [((rows, pixels), bf16), (images.shape, f32), (tiles.shape, bf16), (images.shape, bf16)],
        [hbm] * 5,
        (batch_block, row, inv_sigma2, tiles, images),
        [
            block_scratch,
            pltpu.VMEM((1, count), f32),
            noise_scratch,
            pltpu.VMEM((2, height, count), f32),
            pltpu.VMEM((2, count, pixels), f32),
            pltpu.VMEM((blocks, 2, height, pixels), f32),
            pltpu.SemaphoreType.DMA((CHUNKS + 4,)),
        ],
        0,
        10 << 20,
        "sums",
    )
    sums, column = lax.optimization_barrier((sums, column))
    near = jnp.concatenate([column] + [swap(column, x * cores) for x in range(1, wide)], axis=0)

    place = (2, height, length)
    send, keep_far, keep_near = call(
        functools.partial(insert_kernel, shape),
        [((half, *place), bf16), (((wide - 1) * far, *place), f32), ((far, *place), f32)],
        [hbm, hbm, vmem, vmem],
        (slabs, kind_rows, sums, tiles_near),
        [
            *pairs_scratch,
            pltpu.VMEM((kinds * rows + 2 * height, length), f32),
            pltpu.SMEM((devices * blocks,), jnp.int32),
            pltpu.SemaphoreType.DMA((2,)),
        ],
        2 * rows * pixels * kinds * length,
        8 << 20,
        "insert",
    )
    send, near = lax.optimization_barrier((send, near))
    other = swap(near, 1)
    mate = swap(send, 1)
    beyond = (keep_far + mate[far:].astype(f32)).astype(bf16)
    other, beyond = lax.optimization_barrier((other, beyond))

    if devices * kinds <= blocks * crossed:
        flat = pltpu.VMEM((kinds, devices * height, pixels), f32)
    else:
        flat = pltpu.VMEM((devices * height, length), bf16)
    (scores,) = call(
        functools.partial(score_kernel, shape),
        [((1, count), f32)],
        [hbm] * 4 + [vmem] * 5,
        (slabs, kind_rows, batch_block, inv_sigma2, wave, near, other, images_near, tiles_near),
        [
            *pairs_scratch,
            block_scratch,
            noise_scratch,
            flat,
            pltpu.VMEM((blocks, height, pixels), f32),
            pltpu.VMEM((count * 8, LANES), f32),
            pltpu.SemaphoreType.DMA((4,)),
        ],
        2 * devices * height * length * kinds * pixels,
        8 << 20,
        "scores",
    )

    mine = keep_near + mate[:far].astype(f32)
    for x in range(1, wide):
        came, scores = lax.optimization_barrier((swap(beyond[(x - 1) * far : x * far], x * cores), scores))
        mine = mine + came.astype(f32)
    total = mine[0]
    for z in range(1, far):
        total = total + swap(mine[z].astype(bf16), z * wide * cores).astype(f32)
    return scores.reshape(count), total[0:1], total[1:2]


def solution(mesh):
    placed = (
        P(("parts", "slab"), None, None),
        P(),
        P(("parts", "slab"), None),
        P(("parts", "slab"), None),
        P(("parts", "slab")),
        P(("parts", "slab"), None, None),
        P(("parts", "slab")),
        P("parts", None),
    )
    return jax.shard_map(
        on_device,
        mesh=mesh,
        in_specs=placed,
        out_specs=(
            P(("parts", "slab")),
            P(("parts", "slab"), None, None),
            P(("parts", "slab"), None, None),
        ),
        check_vma=False,
    )
```

time: 41.8 us -> 38.5 us (0.921)
  Pallas kernels: 15.2 us -> 12.8 us
  other arithmetic: 1.57 us -> 0.27 us
  starting transfers between devices: 11.6 us -> 12.8 us
  local copies, waits for them, and re-layouts: 1.42 us -> 0.68 us
    pallas_call x2 -> x3, Pallas kernels: 15.2 us -> 12.8 us  [call(): pl.pallas_call(kernel, out_shape=tuple((jax.ShapeDtypeStruct(s, t) for s,...]
    add x2 -> x1, other arithmetic: 1.45 us -> 0.04 us  [on_device(): total = total + swap(mine[z].astype(bf16), z * wide * cores).astype(f32)]
    ppermute x10, starting transfers between devices: 11.6 us -> 12.8 us  [swap(): lax.ppermute(array, 'slab', [(i, i ^ offset) for i in range(devices)])]
    unnamed x10 -> x2, local copies, waits for them, and re-layouts: 0.7 us -> 0.01 us
  transfers between devices with their start and end apart: 10 -> 10, of which waited for: 4 -> 6; matrix products, arithmetic and copies ran while one was open for 4% -> 0% of each run, Pallas kernels for 16% -> 33%
where the time goes in v3:
time: 38.5 us; the launch traced here: 38.3 us
  starting transfers between devices  12.8 us (33%)
  Pallas kernels  12.8 us (33%)
  waiting for transfers between devices  11.1 us (29%)
  between operations  0.73 us (2%)
  local copies, waits for them, and re-layouts  0.68 us (2%)
    ppermute x10, starting transfers between devices, swap(): lax.ppermute(array, 'slab', [(i, i ^ offset) for i in range(devices)])  12.8 us
    pallas_call x3, Pallas kernels, call(): pl.pallas_call(kernel, out_shape=tuple((jax.ShapeDtypeStruct(s, t) for s,...  12.8 us
    ppermute x10, waiting for transfers between devices, swap(): lax.ppermute(array, 'slab', [(i, i ^ offset) for i in range(devices)])  11.1 us
  transfers between devices with their start and end apart: 10, of which 6 were waited for; matrix products, arithmetic and copies ran while one was open for 0% of the time, Pallas kernels for 33%

profile of v3, /device:TPU:0, one launch (start us, length us, event | category | flops | bytes accessed | tf_op | source)
XLA Modules:
  0.0 38.3 jit_solution(5301006493478054332)
XLA Ops:
  0.6 3.1 %collective-permute-start = (bf16[1,32,512]{2,1,0:T(8,128)(2,1)}, bf16[1,32,512]{2,1,0:T(8,128)(2,1)S(1)}, u32[]{:S(2)}, u32[]{:S(2)}) collective-permute-start(bf16[1,32,512]{2,1,0:T(8,128)(2,1)} %param.8), channel_id=1, source_target_pairs={{0,4},{1,5},{2,6},{3,7},{4,0},{5,1},{6,2},{7,3},{8,12},{9,13},{10,... | collective-permute-start | bytes 98312 | tf_op jit(solution)/shard_map/ppermute | solution.py:220
  3.7 2.6 %collective-permute-start.1 = (bf16[1,32,512]{2,1,0:T(8,128)(2,1)}, bf16[1,32,512]{2,1,0:T(8,128)(2,1)S(1)}, u32[]{:S(2)}, u32[]{:S(2)}) collective-permute-start(bf16[1,32,512]{2,1,0:T(8,128)(2,1)} %param.8), channel_id=1, source_target_pairs={{0,8},{1,9},{2,10},{3,11},{4,12},{5,13},{6,14},{7,15},{8,0},{9,1},... | collective-permute-start | bytes 98312 | tf_op jit(solution)/shard_map/ppermute | solution.py:220
  6.3 0.0 collective-permute-start.2
  6.3 0.0 copy-start
  6.3 2.8 %sums.1 = (bf16[1024,256]{1,0:T(8,128)(2,1)S(1)}, f32[128,32,256]{2,1,0:T(8,128)S(1)}, bf16[8,512,256]{2,1,0:T(8,128)(2,1)S(1)}, bf16[128,32,256]{2,1,0:T(8,128)(2,1)S(1)}) custom-call(s32[16]{0:T(128)} %block_hbm.3, f32[1,128]{1,0:T(1,128)} %bitcast.22, f32[32,256]{1,0:T(8,128)} %noise_hbm.3, bf16[8,512,256]{2,1,0:T(8,128)(2,1)} %tiles_hbm.1, ...), custom_call_target="tpu_custom_call" | custom-call | bytes 10485760 | tf_op jit(solution)/shard_map/sums/pallas_call | solution.py:234
  9.1 0.0 collective-permute-done
  9.2 0.2 collective-permute-done.1
  9.3 2.9 %collective-permute-done.2 = bf16[1,32,512]{2,1,0:T(8,128)(2,1)S(1)} collective-permute-done((bf16[1,32,512]{2,1,0:T(8,128)(2,1)}, bf16[1,32,512]{2,1,0:T(8,128)(2,1)S(1)}, u32[]{:S(2)}, u32[]{:S(2)}) %collective-permute-start.2) | collective-permute-done | bytes 32800 | tf_op jit(solution)/shard_map/ppermute | solution.py:220
  12.2 0.0 copy-done
  12.3 1.6 %collective-permute-start.3 = (bf16[4,32,512]{2,1,0:T(8,128)(2,1)S(1)}, bf16[4,32,512]{2,1,0:T(8,128)(2,1)S(1)}, u32[]{:S(2)}, u32[]{:S(2)}) collective-permute-start(bf16[4,32,512]{2,1,0:T(8,128)(2,1)S(1)} %pad_maximum_fusion.1), channel_id=1, source_target_pairs={{0,2},{1,3},{2,0},{3,1},{4,6},{5,7},{6,4},{7,5},{8,10},{9,11},{10,... | collective-permute-start | bytes 393224 | tf_op jit(solution)/shard_map/ppermute | solution.py:220
  13.8 5.0 %insert.1 = (bf16[8,2,32,512]{3,2,1,0:T(8,128)(2,1)S(1)}, f32[4,2,32,512]{3,2,1,0:T(8,128)S(1)}, f32[4,2,32,512]{3,2,1,0:T(8,128)S(1)}) custom-call(s32[8,16]{1,0:T(8,128)} %bitcast.18, s32[8,16]{1,0:T(8,128)} %bitcast.20, bf16[1024,256]{1,0:T(8,128)(2,1)S(1)} %get-tuple-element.19.sums_ref, bf16[8,512,256]{2,1,0:T(8,128)(2,1)S(1)} %get-tuple-element.20.tiles_ref), custom_call_target="tpu_custom_call" | custom-call | flops 2147483648 | bytes 8388608 | tf_op jit(solution)/shard_map/insert/pallas_call | solution.py:234
  18.8 0.0 collective-permute-done.3
  18.9 0.1 collective-permute-start.5
  18.9 0.5 %collective-permute-start.4 = (bf16[8,32,512]{2,1,0:T(8,128)(2,1)S(1)}, bf16[8,32,512]{2,1,0:T(8,128)(2,1)S(1)}, u32[]{:S(2)}, u32[]{:S(2)}) collective-permute-start(bf16[8,32,512]{2,1,0:T(8,128)(2,1)S(1)} %pad_maximum_fusion.near_ref), channel_id=1, source_target_pairs={{0,1},{1,0},{2,3},{3,2},{4,5},{5,4},{6,7},{7,6},{8,9},{9,8},{10,11... | collective-permute-start | bytes 786440 | tf_op jit(solution)/shard_map/ppermute | solution.py:220
  19.4 1.4 %collective-permute-done.5 = bf16[8,2,32,512]{3,2,1,0:T(8,128)(2,1)S(1)} collective-permute-done((bf16[8,2,32,512]{3,2,1,0:T(8,128)(2,1)S(1)}, bf16[8,2,32,512]{3,2,1,0:T(8,128)(2,1)S(1)}, u32[]{:S(2)}, u32[]{:S(2)}) %collective-permute-start.5) | collective-permute-done | bytes 524320 | tf_op jit(solution)/shard_map/ppermute | solution.py:220
  20.8 0.1 add_convert_fusion
  20.9 0.3 collective-permute-done.4.other_ref
  21.2 0.5 %collective-permute-start.6 = (bf16[4,2,32,512]{3,2,1,0:T(8,128)(2,1)S(1)}, bf16[4,2,32,512]{3,2,1,0:T(8,128)(2,1)S(1)}, u32[]{:S(2)}, u32[]{:S(2)}) collective-permute-start(bf16[4,2,32,512]{3,2,1,0:T(8,128)(2,1)S(1)} %add_convert_fusion), channel_id=1, source_target_pairs={{0,2},{1,3},{2,0},{3,1},{4,6},{5,7},{6,4},{7,5},{8,10},{9,11},{10,... | collective-permute-start | bytes 786440 | tf_op jit(solution)/shard_map/ppermute | solution.py:220
  21.8 4.9 %scores.1 = f32[1,128]{1,0:T(1,128)} custom-call(s32[8,16]{1,0:T(8,128)} %bitcast.19, s32[8,16]{1,0:T(8,128)} %bitcast.21, s32[16]{0:T(128)} %block_hbm.3, f32[32,256]{1,0:T(8,128)} %noise_hbm.3, f32[128,32,256]{2,1,0:T(8,128)S(1)} %get-tuple-element.27.wave_ref, bf16[8,32,512]{2,1,0:T(8,128)(2,1)S(1)} %pad_maximum_fusion.near_ref, ...), custom_call_target="tpu_custom_call" | custom-call | flops 1073741824 | bytes 8388608 | tf_op jit(solution)/shard_map/scores/pallas_call | solution.py:234
  26.7 2.9 %collective-permute-done.6 = bf16[4,2,32,512]{3,2,1,0:T(8,128)(2,1)S(1)} collective-permute-done((bf16[4,2,32,512]{3,2,1,0:T(8,128)(2,1)S(1)}, bf16[4,2,32,512]{3,2,1,0:T(8,128)(2,1)S(1)}, u32[]{:S(2)}, u32[]{:S(2)}) %collective-permute-start.6) | collective-permute-done | bytes 262176 | tf_op jit(solution)/shard_map/ppermute | solution.py:220
  29.6 0.1 fusion.3
  29.7 0.1 collective-permute-start.7
  29.8 1.3 %collective-permute-start.8 = (bf16[2,32,512]{2,1,0:T(8,128)(2,1)S(1)}, bf16[2,32,512]{2,1,0:T(8,128)(2,1)S(1)}, u32[]{:S(2)}, u32[]{:S(2)}) collective-permute-start(bf16[2,32,512]{2,1,0:T(8,128)(2,1)S(1)} %get-tuple-element.37), channel_id=1, source_target_pairs={{0,8},{1,9},{2,10},{3,11},{4,12},{5,13},{6,14},{7,15},{8,0},{9,1},... | collective-permute-start | bytes 196616 | tf_op jit(solution)/shard_map/ppermute | solution.py:220
  31.1 3.0 %collective-permute-start.9 = (bf16[2,32,512]{2,1,0:T(8,128)(2,1)S(1)}, bf16[2,32,512]{2,1,0:T(8,128)(2,1)S(1)}, u32[]{:S(2)}, u32[]{:S(2)}) collective-permute-start(bf16[2,32,512]{2,1,0:T(8,128)(2,1)S(1)} %get-tuple-element.36), channel_id=1, source_target_pairs={{0,12},{1,13},{2,14},{3,15},{4,8},{5,9},{6,10},{7,11},{8,4},{9,5},... | collective-permute-start | bytes 196616 | tf_op jit(solution)/shard_map/ppermute | solution.py:220
  34.2 0.0 collective-permute-done.7
  34.2 3.4 %collective-permute-done.8 = bf16[2,32,512]{2,1,0:T(8,128)(2,1)S(1)} collective-permute-done((bf16[2,32,512]{2,1,0:T(8,128)(2,1)S(1)}, bf16[2,32,512]{2,1,0:T(8,128)(2,1)S(1)}, u32[]{:S(2)}, u32[]{:S(2)}) %collective-permute-start.8) | collective-permute-done | bytes 65568 | tf_op jit(solution)/shard_map/ppermute | solution.py:220
  37.6 0.0 collective-permute-done.9
  37.6 0.7 %fusion.4 = (f32[1,32,512]{2,1,0:T(8,128)}, f32[1,32,512]{2,1,0:T(8,128)}) fusion(f32[2,32,512]{2,1,0:T(8,128)S(1)} %fusion.2), kind=kLoop, calls=%fused_computation.12 | loop fusion | bytes 262144 | tf_op jit(solution)/shard_map/slice | solution.py:320
  (4 shorter events, 0.1 us)
Async XLA Ops:
  0.6 8.5 %collective-permute-start = (bf16[1,32,512]{2,1,0:T(8,128)(2,1)}, bf16[1,32,512]{2,1,0:T(8,128)(2,1)S(1)}, u32[]{:S(2)}, u32[]{:S(2)}) collective-permute-start(bf16[1,32,512]{2,1,0:T(8,128)(2,1)} %param.8), channel_id=1, source_target_pairs={{0,4},{1,5},{2,6},{3,7},{4,0},{5,1},{6,2},{7,3},{8,12},{9,13},{10,... | collective-permute-start | bytes 98312 | tf_op jit(solution)/shard_map/ppermute | solution.py:220
  3.7 5.6 %collective-permute-start.1 = (bf16[1,32,512]{2,1,0:T(8,128)(2,1)}, bf16[1,32,512]{2,1,0:T(8,128)(2,1)S(1)}, u32[]{:S(2)}, u32[]{:S(2)}) collective-permute-start(bf16[1,32,512]{2,1,0:T(8,128)(2,1)} %param.8), channel_id=1, source_target_pairs={{0,8},{1,9},{2,10},{3,11},{4,12},{5,13},{6,14},{7,15},{8,0},{9,1},... | collective-permute-start | bytes 98312 | tf_op jit(solution)/shard_map/ppermute | solution.py:220
  6.3 5.9 %collective-permute-start.2 = (bf16[1,32,512]{2,1,0:T(8,128)(2,1)}, bf16[1,32,512]{2,1,0:T(8,128)(2,1)S(1)}, u32[]{:S(2)}, u32[]{:S(2)}) collective-permute-start(bf16[1,32,512]{2,1,0:T(8,128)(2,1)} %param.8), channel_id=1, source_target_pairs={{0,12},{1,13},{2,14},{3,15},{4,8},{5,9},{6,10},{7,11},{8,4},{9,5},... | collective-permute-start | bytes 98312 | tf_op jit(solution)/shard_map/ppermute | solution.py:220
  6.3 5.9 %copy-start = (bf16[1,32,512]{2,1,0:T(8,128)(2,1)S(1)}, bf16[1,32,512]{2,1,0:T(8,128)(2,1)}, u32[]{:S(2)}) copy-start(bf16[1,32,512]{2,1,0:T(8,128)(2,1)} %param.8) | copy-start | bytes 98308
  12.3 6.6 %collective-permute-start.3 = (bf16[4,32,512]{2,1,0:T(8,128)(2,1)S(1)}, bf16[4,32,512]{2,1,0:T(8,128)(2,1)S(1)}, u32[]{:S(2)}, u32[]{:S(2)}) collective-permute-start(bf16[4,32,512]{2,1,0:T(8,128)(2,1)S(1)} %pad_maximum_fusion.1), channel_id=1, source_target_pairs={{0,2},{1,3},{2,0},{3,1},{4,6},{5,7},{6,4},{7,5},{8,10},{9,11},{10,... | collective-permute-start | bytes 393224 | tf_op jit(solution)/shard_map/ppermute | solution.py:220
  18.9 2.0 %collective-permute-start.5 = (bf16[8,2,32,512]{3,2,1,0:T(8,128)(2,1)S(1)}, bf16[8,2,32,512]{3,2,1,0:T(8,128)(2,1)S(1)}, u32[]{:S(2)}, u32[]{:S(2)}) collective-permute-start(bf16[8,2,32,512]{3,2,1,0:T(8,128)(2,1)S(1)} %get-tuple-element.25), channel_id=1, source_target_pairs={{0,1},{1,0},{2,3},{3,2},{4,5},{5,4},{6,7},{7,6},{8,9},{9,8},{10,11... | collective-permute-start | bytes 1572872 | tf_op jit(solution)/shard_map/ppermute | solution.py:220
  18.9 2.3 %collective-permute-start.4 = (bf16[8,32,512]{2,1,0:T(8,128)(2,1)S(1)}, bf16[8,32,512]{2,1,0:T(8,128)(2,1)S(1)}, u32[]{:S(2)}, u32[]{:S(2)}) collective-permute-start(bf16[8,32,512]{2,1,0:T(8,128)(2,1)S(1)} %pad_maximum_fusion.near_ref), channel_id=1, source_target_pairs={{0,1},{1,0},{2,3},{3,2},{4,5},{5,4},{6,7},{7,6},{8,9},{9,8},{10,11... | collective-permute-start | bytes 786440 | tf_op jit(solution)/shard_map/ppermute | solution.py:220
  21.2 8.3 %collective-permute-start.6 = (bf16[4,2,32,512]{3,2,1,0:T(8,128)(2,1)S(1)}, bf16[4,2,32,512]{3,2,1,0:T(8,128)(2,1)S(1)}, u32[]{:S(2)}, u32[]{:S(2)}) collective-permute-start(bf16[4,2,32,512]{3,2,1,0:T(8,128)(2,1)S(1)} %add_convert_fusion), channel_id=1, source_target_pairs={{0,2},{1,3},{2,0},{3,1},{4,6},{5,7},{6,4},{7,5},{8,10},{9,11},{10,... | collective-permute-start | bytes 786440 | tf_op jit(solution)/shard_map/ppermute | solution.py:220
  29.7 4.5 %collective-permute-start.7 = (bf16[2,32,512]{2,1,0:T(8,128)(2,1)S(1)}, bf16[2,32,512]{2,1,0:T(8,128)(2,1)S(1)}, u32[]{:S(2)}, u32[]{:S(2)}) collective-permute-start(bf16[2,32,512]{2,1,0:T(8,128)(2,1)S(1)} %get-tuple-element.35), channel_id=1, source_target_pairs={{0,4},{1,5},{2,6},{3,7},{4,0},{5,1},{6,2},{7,3},{8,12},{9,13},{10,... | collective-permute-start | bytes 196616 | tf_op jit(solution)/shard_map/ppermute | solution.py:220
  29.8 7.8 %collective-permute-start.8 = (bf16[2,32,512]{2,1,0:T(8,128)(2,1)S(1)}, bf16[2,32,512]{2,1,0:T(8,128)(2,1)S(1)}, u32[]{:S(2)}, u32[]{:S(2)}) collective-permute-start(bf16[2,32,512]{2,1,0:T(8,128)(2,1)S(1)} %get-tuple-element.37), channel_id=1, source_target_pairs={{0,8},{1,9},{2,10},{3,11},{4,12},{5,13},{6,14},{7,15},{8,0},{9,1},... | collective-permute-start | bytes 196616 | tf_op jit(solution)/shard_map/ppermute | solution.py:220
  31.1 6.5 %collective-permute-start.9 = (bf16[2,32,512]{2,1,0:T(8,128)(2,1)S(1)}, bf16[2,32,512]{2,1,0:T(8,128)(2,1)S(1)}, u32[]{:S(2)}, u32[]{:S(2)}) collective-permute-start(bf16[2,32,512]{2,1,0:T(8,128)(2,1)S(1)} %get-tuple-element.36), channel_id=1, source_target_pairs={{0,12},{1,13},{2,14},{3,15},{4,8},{5,9},{6,10},{7,11},{8,4},{9,5},... | collective-permute-start | bytes 196616 | tf_op jit(solution)/shard_map/ppermute | solution.py:220

commit v4 on v3

--- a/solution.py
+++ b/solution.py
@@ -19,6 +19,10 @@
     while (2 * wide) ** 3 <= chips:
         wide *= 2
     return chips // wide, wide, cores
+
+
+def powers(size):
+    return [1 << n for n in range(size.bit_length() - 1)]
 
 
 def sin_cos(angle):
@@ -90,8 +94,8 @@
             data = data + wave * images_ref[i].astype(jnp.float32)
             weight = weight + wave * wave
         k = block_ref[b]
-        acc_ref[k, 0] = acc_ref[k, 0] + data
-        acc_ref[k, 1] = acc_ref[k, 1] + weight
+        acc_ref[0, k] = acc_ref[0, k] + data
+        acc_ref[1, k] = acc_ref[1, k] + weight
     sums = (acc_ref[...] * noise_ref[...][None, None]).astype(jnp.bfloat16)
     sums_ref[...] = sums.reshape(sums_ref.shape)
     started[-1].wait()
@@ -102,10 +106,29 @@
     far, wide, cores = shape
     started = copies([(slab_hbm, slab_ref), (tile_hbm, tile_ref)], sems)
     crossed, blocks = slab_ref.shape
-    kinds = tiles_ref.shape[0]
-    rows = sums_ref.shape[0]
-    height = rows // (2 * blocks)
+    kinds, length, _ = tiles_ref.shape
+    rows = sums_ref.shape[1]
+    height = rows // blocks
     devices = place_ref.shape[0] // blocks
+    columns = parts_ref.shape[2]
+    per_kind = length // columns
+    pieces = [(kind, n * columns) for kind in range(sums_ref.shape[0]) for n in range(per_kind)]
+    each = devices // kinds
+
+    def multiply(piece, t):
+        kind, start = pieces[piece]
+        at = pl.multiple_of(t * rows, rows)
+        parts_ref[piece % 2, pl.ds(at, rows), :] = lax.dot_general(
+            sums_ref[kind], tiles_ref[t, start : start + columns, :], (((1,), (1,)), ((), ())), preferred_element_type=jnp.float32
+        )
+
+    for n in range(2):
+        parts_ref[n, pl.ds(kinds * rows, height), :] = jnp.zeros((height, columns), jnp.float32)
+    for t in range(kinds // 2):
+        multiply(0, t)
+
+    for copy in started:
+        copy.wait()
 
     def clear(n, carry):
         for m in range(blocks):
@@ -113,39 +136,39 @@
         return carry
 
     lax.fori_loop(0, devices, clear, 0, unroll=devices <= 16)
-    for copy in started:
-        copy.wait()
     for k in range(blocks):
         for r in range(crossed):
-            place_ref[slab_ref[r, k] * blocks + k] = tile_ref[r, k] * rows + k * 2 * height
-    parts_ref[pl.ds(kinds * rows, 2 * height), :] = jnp.zeros((2 * height, parts_ref.shape[1]), jnp.float32)
-    for t in range(kinds):
-        parts_ref[t * rows : (t + 1) * rows, :] = lax.dot_general(
-            sums_ref[...], tiles_ref[t], (((1,), (1,)), ((), ())), preferred_element_type=jnp.float32
-        )
-    me = lax.axis_index("slab")
-
-    def total(x, z, core, kind):
-        s = me ^ ((z * wide + x) * cores + core)
+            place_ref[slab_ref[r, k] * blocks + k] = tile_ref[r, k] * rows + k * height
+    for t in range(kinds // 2, kinds):
+        multiply(0, t)
+
+    low = lax.rem(lax.axis_index("slab"), wide * cores)
+
+    def total(piece, x, z, core):
+        s = z * wide * cores + (low ^ (x * cores + core))
         acc = None
         for k in range(blocks):
-            at = pl.multiple_of(place_ref[s * blocks + k] + kind * height, height)
-            part = parts_ref[pl.ds(at, height), :]
+            at = pl.multiple_of(place_ref[s * blocks + k], height)
+            part = parts_ref[piece % 2, pl.ds(at, height), :]
             acc = part if acc is None else acc + part
         return acc
 
-    def fill(ref, start, core):
-        def step(slot, carry):
-            x, z = start + slot // far, lax.rem(slot, far)
-            for kind in range(2):
-                ref[slot, kind] = total(x, z, core, kind).astype(ref.dtype)
-            return carry
-
-        lax.fori_loop(0, ref.shape[0], step, 0)
-
-    fill(send_ref, 0, 1)
-    fill(far_ref, 1, 0)
-    fill(near_ref, 0, 0)
+    for piece, (kind, start) in enumerate(pieces):
+        done = 0
+        for ref, first, core in ((send_ref, 0, 1), (far_ref, 1, 0), (near_ref, 0, 0)):
+
+            def step(n, carry, ref=ref, first=first, core=core, done=done, piece=piece, kind=kind, start=start):
+                if piece + 1 < len(pieces):
+                    multiply(piece + 1, done + n)
+                for m in range(each):
+                    slot = n * each + m
+                    x, z = first + slot // far, lax.rem(slot, far)
+                    ref[slot, kind, :, start : start + columns] = total(piece, x, z, core).astype(ref.dtype)
+                return carry
+
+            steps = ref.shape[0] // each
+            lax.fori_loop(0, steps, step, 0)
+            done += steps
 
 
 def score_kernel(shape, slab_hbm, tile_hbm, block_hbm, noise_hbm, wave_ref, near_ref, other_ref, images_ref, tiles_ref,
@@ -213,7 +236,7 @@
     devices = lax.axis_size("slab")
     shape = far, wide, cores = grid_of(devices)
     half = devices // 2
-    rows = blocks * 2 * height
+    rows = blocks * height
     slabs, kind_rows, row = slab_ids.T, tile_ids.T, defocus.reshape(1, count)
 
     def swap(array, offset):
@@ -242,11 +265,15 @@
             name=name,
         )(*operands)
 
-    column = jnp.concatenate([volume] + [swap(volume, z * wide * cores) for z in range(1, far)], axis=0)
+    def hop(array, offset):
+        return jnp.concatenate([array, swap(array, offset)], axis=0)
+
+    offsets = [z * wide * cores for z in powers(far)] + [x * cores for x in powers(wide)]
+    gathered = hop(volume, offsets[0])
 
     sums, wave, tiles_near, images_near = call(
         sum_kernel,
-        [((rows, pixels), bf16), (images.shape, f32), (tiles.shape, bf16), (images.shape, bf16)],
+        [((2, rows, pixels), bf16), (images.shape, f32), (tiles.shape, bf16), (images.shape, bf16)],
         [hbm] * 5,
         (batch_block, row, inv_sigma2, tiles, images),
         [
@@ -255,15 +282,15 @@
             noise_scratch,
             pltpu.VMEM((2, height, count), f32),
             pltpu.VMEM((2, count, pixels), f32),
-            pltpu.VMEM((blocks, 2, height, pixels), f32),
+            pltpu.VMEM((2, blocks, height, pixels), f32),
             pltpu.SemaphoreType.DMA((CHUNKS + 4,)),
         ],
         0,
         10 << 20,
         "sums",
     )
-    sums, column = lax.optimization_barrier((sums, column))
-    near = jnp.concatenate([column] + [swap(column, x * cores) for x in range(1, wide)], axis=0)
+    sums, gathered = lax.optimization_barrier((sums, gathered))
+    gathered = hop(gathered, offsets[1])
 
     place = (2, height, length)
     send, keep_far, keep_near = call(
@@ -273,19 +300,21 @@
         (slabs, kind_rows, sums, tiles_near),
         [
             *pairs_scratch,
-            pltpu.VMEM((kinds * rows + 2 * height, length), f32),
+            pltpu.VMEM((2, kinds * rows + height, length // 2), f32),
             pltpu.SMEM((devices * blocks,), jnp.int32),
             pltpu.SemaphoreType.DMA((2,)),
         ],
-        2 * rows * pixels * kinds * length,
+        4 * rows * pixels * kinds * length,
         8 << 20,
         "insert",
     )
-    send, near = lax.optimization_barrier((send, near))
-    other = swap(near, 1)
+    send, gathered = lax.optimization_barrier((send, gathered))
+    for offset in offsets[2:]:
+        gathered = hop(gathered, offset)
+    other = swap(gathered, 1)
     mate = swap(send, 1)
     beyond = (keep_far + mate[far:].astype(f32)).astype(bf16)
-    other, beyond = lax.optimization_barrier((other, beyond))
+    other, _ = lax.optimization_barrier((other, beyond))
 
     if devices * kinds <= blocks * crossed:
         flat = pltpu.VMEM((kinds, devices * height, pixels), f32)
@@ -295,7 +324,7 @@
         functools.partial(score_kernel, shape),
         [((1, count), f32)],
         [hbm] * 4 + [vmem] * 5,
-        (slabs, kind_rows, batch_block, inv_sigma2, wave, near, other, images_near, tiles_near),
+        (slabs, kind_rows, batch_block, inv_sigma2, wave, gathered, other, images_near, tiles_near),
         [
             *pairs_scratch,
             block_scratch,
@@ -314,9 +343,9 @@
     for x in range(1, wide):
         came, scores = lax.optimization_barrier((swap(beyond[(x - 1) * far : x * far], x * cores), scores))
         mine = mine + came.astype(f32)
-    total = mine[0]
-    for z in range(1, far):
-        total = total + swap(mine[z].astype(bf16), z * wide * cores).astype(f32)
+    lines = [[z * wide * cores + low for z in range(far)] for low in range(wide * cores)]
+    came = lax.all_to_all(mine.astype(bf16), "slab", 0, 0, axis_index_groups=lines, tiled=True)
+    total = jnp.sum(came.astype(f32), axis=0)
     return scores.reshape(count), total[0:1], total[1:2]
 
 

time: 38.5 us -> 46.1 us (1.20)
  blocking collectives: 0 us -> 11.4 us
  waiting for transfers between devices: 11.1 us -> 6.63 us
  Pallas kernels: 12.8 us -> 17.1 us
  starting transfers between devices: 12.8 us -> 8.98 us
    all_to_all x0 -> x1, blocking collectives: none -> 11.4 us  [on_device(): lax.all_to_all(mine.astype(bf16), 'slab', 0, 0, axis_index_groups=lines,...]
    ppermute x10 -> x6, waiting for transfers between devices: 11.1 us -> 6.63 us  [swap(): lax.ppermute(array, 'slab', [(i, i ^ offset) for i in range(devices)])]
    pallas_call x3, Pallas kernels: 12.8 us -> 17.1 us  [call(): pl.pallas_call(kernel, out_shape=tuple((jax.ShapeDtypeStruct(s, t) for s,...]
    ppermute x10 -> x6, starting transfers between devices: 12.8 us -> 8.98 us  [swap(): lax.ppermute(array, 'slab', [(i, i ^ offset) for i in range(devices)])]
  transfers between devices with their start and end apart: 10 -> 6, of which waited for: 6 -> 2; matrix products, arithmetic and copies ran while one was open for 0% -> 0% of each run, Pallas kernels for 33% -> 37%
where the time goes in v4:
time: 46.1 us; the launch traced here: 45.8 us
  Pallas kernels  17.1 us (37%)
  blocking collectives  11.4 us (25%)
  starting transfers between devices  8.98 us (19%)
  waiting for transfers between devices  6.63 us (14%)
  between operations  0.74 us (2%)
  local copies, waits for them, and re-layouts  0.68 us (1%)
    pallas_call x3, Pallas kernels, call(): pl.pallas_call(kernel, out_shape=tuple((jax.ShapeDtypeStruct(s, t) for s,...  17.1 us
    all_to_all x1, blocking collectives, on_device(): lax.all_to_all(mine.astype(bf16), 'slab', 0, 0, axis_index_groups=lines,...  11.4 us
    ppermute x6, starting transfers between devices, swap(): lax.ppermute(array, 'slab', [(i, i ^ offset) for i in range(devices)])  8.98 us
    ppermute x6, waiting for transfers between devices, swap(): lax.ppermute(array, 'slab', [(i, i ^ offset) for i in range(devices)])  6.63 us
  transfers between devices with their start and end apart: 6, of which 2 were waited for; matrix products, arithmetic and copies ran while one was open for 0% of the time, Pallas kernels for 37%

profile of v4, /device:TPU:0, one launch (start us, length us, event | category | flops | bytes accessed | tf_op | source)
XLA Modules:
  0.0 45.8 jit_solution(7953285601964192158)
XLA Ops:
  0.6 3.1 %collective-permute-start = (bf16[1,32,512]{2,1,0:T(8,128)(2,1)}, bf16[1,32,512]{2,1,0:T(8,128)(2,1)S(1)}, u32[]{:S(2)}, u32[]{:S(2)}) collective-permute-start(bf16[1,32,512]{2,1,0:T(8,128)(2,1)} %param.8), channel_id=1, source_target_pairs={{0,4},{1,5},{2,6},{3,7},{4,0},{5,1},{6,2},{7,3},{8,12},{9,13},{10,... | collective-permute-start | bytes 98312 | tf_op jit(solution)/shard_map/ppermute | solution.py:243
  3.7 0.0 copy-start
  3.7 2.8 %sums.1 = (bf16[2,512,256]{2,1,0:T(8,128)(2,1)S(1)}, f32[128,32,256]{2,1,0:T(8,128)S(1)}, bf16[8,512,256]{2,1,0:T(8,128)(2,1)S(1)}, bf16[128,32,256]{2,1,0:T(8,128)(2,1)S(1)}) custom-call(s32[16]{0:T(128)} %block_hbm.3, f32[1,128]{1,0:T(1,128)} %bitcast.8, f32[32,256]{1,0:T(8,128)} %noise_hbm.3, bf16[8,512,256]{2,1,0:T(8,128)(2,1)} %tiles_hbm.1, ...), custom_call_target="tpu_custom_call" | custom-call | bytes 10485760 | tf_op jit(solution)/shard_map/sums/pallas_call | solution.py:257
  6.5 0.0 collective-permute-done
  6.6 0.0 copy-done
  6.6 2.7 %collective-permute-start.1 = (bf16[2,32,512]{2,1,0:T(8,128)(2,1)S(1)}, bf16[2,32,512]{2,1,0:T(8,128)(2,1)S(1)}, u32[]{:S(2)}, u32[]{:S(2)}) collective-permute-start(bf16[2,32,512]{2,1,0:T(8,128)(2,1)S(1)} %pad_maximum_fusion.1), channel_id=1, source_target_pairs={{0,8},{1,9},{2,10},{3,11},{4,12},{5,13},{6,14},{7,15},{8,0},{9,1},... | collective-permute-start | bytes 196616 | tf_op jit(solution)/shard_map/ppermute | solution.py:243
  9.2 9.3 %insert.1 = (bf16[8,2,32,512]{3,2,1,0:T(8,128)(2,1)S(1)}, f32[4,2,32,512]{3,2,1,0:T(8,128)S(1)}, f32[4,2,32,512]{3,2,1,0:T(8,128)S(1)}) custom-call(s32[8,16]{1,0:T(8,128)} %bitcast.4, s32[8,16]{1,0:T(8,128)} %bitcast.6, bf16[2,512,256]{2,1,0:T(8,128)(2,1)S(1)} %get-tuple-element.18.sums_ref, bf16[8,512,256]{2,1,0:T(8,128)(2,1)S(1)} %get-tuple-element.19.tiles_ref), custom_call_target="tpu_custom_call" | custom-call | flops 2147483648 | bytes 8388608 | tf_op jit(solution)/shard_map/insert/pallas_call | solution.py:257
  18.6 0.0 collective-permute-done.1
  18.6 0.1 collective-permute-start.2
  18.7 1.5 %collective-permute-start.4 = (bf16[4,32,512]{2,1,0:T(8,128)(2,1)S(1)}, bf16[4,32,512]{2,1,0:T(8,128)(2,1)S(1)}, u32[]{:S(2)}, u32[]{:S(2)}) collective-permute-start(bf16[4,32,512]{2,1,0:T(8,128)(2,1)S(1)} %pad_maximum_fusion), channel_id=1, source_target_pairs={{0,2},{1,3},{2,0},{3,1},{4,6},{5,7},{6,4},{7,5},{8,10},{9,11},{10,... | collective-permute-start | bytes 393224 | tf_op jit(solution)/shard_map/ppermute | solution.py:243
  20.3 4.4 %collective-permute-done.4 = bf16[4,32,512]{2,1,0:T(8,128)(2,1)S(1)} collective-permute-done((bf16[4,32,512]{2,1,0:T(8,128)(2,1)S(1)}, bf16[4,32,512]{2,1,0:T(8,128)(2,1)S(1)}, u32[]{:S(2)}, u32[]{:S(2)}) %collective-permute-start.4) | collective-permute-done | bytes 131104 | tf_op jit(solution)/shard_map/ppermute | solution.py:243
  24.6 0.1 collective-permute-start.5
  24.7 0.0 collective-permute-done.2
  24.7 0.1 add_convert_fusion.1
  24.8 1.5 %collective-permute-start.3 = (bf16[4,2,32,512]{3,2,1,0:T(8,128)(2,1)S(1)}, bf16[4,2,32,512]{3,2,1,0:T(8,128)(2,1)S(1)}, u32[]{:S(2)}, u32[]{:S(2)}) collective-permute-start(bf16[4,2,32,512]{3,2,1,0:T(8,128)(2,1)S(1)} %add_convert_fusion.1), channel_id=1, source_target_pairs={{0,2},{1,3},{2,0},{3,1},{4,6},{5,7},{6,4},{7,5},{8,10},{9,11},{10,... | collective-permute-start | bytes 786440 | tf_op jit(solution)/shard_map/ppermute | solution.py:243
  26.4 0.0 collective-permute-done.5.other_ref
  26.4 4.9 %scores.1 = f32[1,128]{1,0:T(1,128)} custom-call(s32[8,16]{1,0:T(8,128)} %bitcast.5, s32[8,16]{1,0:T(8,128)} %bitcast.7, s32[16]{0:T(128)} %block_hbm.3, f32[32,256]{1,0:T(8,128)} %noise_hbm.3, f32[128,32,256]{2,1,0:T(8,128)S(1)} %get-tuple-element.24.wave_ref, bf16[8,32,512]{2,1,0:T(8,128)(2,1)S(1)} %constant_dynamic-update-slice_fusion.near_ref, ...), custom_call_target="tpu_custom_call" | custom-call | flops 1073741824 | bytes 8388608 | tf_op jit(solution)/shard_map/scores/pallas_call | solution.py:257
  31.3 2.3 %collective-permute-done.3 = bf16[4,2,32,512]{3,2,1,0:T(8,128)(2,1)S(1)} collective-permute-done((bf16[4,2,32,512]{3,2,1,0:T(8,128)(2,1)S(1)}, bf16[4,2,32,512]{3,2,1,0:T(8,128)(2,1)S(1)}, u32[]{:S(2)}, u32[]{:S(2)}) %collective-permute-start.3) | collective-permute-done | bytes 262176 | tf_op jit(solution)/shard_map/ppermute | solution.py:243
  33.6 0.1 add_convert_fusion
  33.7 11.4 %all_to_all.5 = bf16[4,2,32,512]{3,2,1,0:T(8,128)(2,1)S(1)} all-to-all(bf16[4,2,32,512]{3,2,1,0:T(8,128)(2,1)S(1)} %add_convert_fusion), channel_id=1, replica_groups={{0,4,8,12},{1,5,9,13},{2,6,10,14},{3,7,11,15},{16,20,24,28},{17,21,25,2..., dimensions={0} | all-to-all | bytes 524288 | tf_op jit(solution)/shard_map/all_to_all | solution.py:347
  45.1 0.7 %fusion = (f32[1,32,512]{2,1,0:T(8,128)}, f32[1,32,512]{2,1,0:T(8,128)}) fusion(f32[2,32,512]{2,1,0:T(8,128)S(1)} %convert_reduce_fusion), kind=kLoop, calls=%fused_computation.7 | loop fusion | bytes 262144 | tf_op jit(solution)/shard_map/slice | solution.py:349
  (5 shorter events, 0.1 us)
Async XLA Ops:
  0.6 5.9 %collective-permute-start = (bf16[1,32,512]{2,1,0:T(8,128)(2,1)}, bf16[1,32,512]{2,1,0:T(8,128)(2,1)S(1)}, u32[]{:S(2)}, u32[]{:S(2)}) collective-permute-start(bf16[1,32,512]{2,1,0:T(8,128)(2,1)} %param.8), channel_id=1, source_target_pairs={{0,4},{1,5},{2,6},{3,7},{4,0},{5,1},{6,2},{7,3},{8,12},{9,13},{10,... | collective-permute-start | bytes 98312 | tf_op jit(solution)/shard_map/ppermute | solution.py:243
  3.7 2.8 %copy-start = (bf16[1,32,512]{2,1,0:T(8,128)(2,1)S(1)}, bf16[1,32,512]{2,1,0:T(8,128)(2,1)}, u32[]{:S(2)}) copy-start(bf16[1,32,512]{2,1,0:T(8,128)(2,1)} %param.8) | copy-start | bytes 98308
  6.6 12.0 %collective-permute-start.1 = (bf16[2,32,512]{2,1,0:T(8,128)(2,1)S(1)}, bf16[2,32,512]{2,1,0:T(8,128)(2,1)S(1)}, u32[]{:S(2)}, u32[]{:S(2)}) collective-permute-start(bf16[2,32,512]{2,1,0:T(8,128)(2,1)S(1)} %pad_maximum_fusion.1), channel_id=1, source_target_pairs={{0,8},{1,9},{2,10},{3,11},{4,12},{5,13},{6,14},{7,15},{8,0},{9,1},... | collective-permute-start | bytes 196616 | tf_op jit(solution)/shard_map/ppermute | solution.py:243
  18.6 6.1 %collective-permute-start.2 = (bf16[8,2,32,512]{3,2,1,0:T(8,128)(2,1)S(1)}, bf16[8,2,32,512]{3,2,1,0:T(8,128)(2,1)S(1)}, u32[]{:S(2)}, u32[]{:S(2)}) collective-permute-start(bf16[8,2,32,512]{3,2,1,0:T(8,128)(2,1)S(1)} %get-tuple-element.23), channel_id=1, source_target_pairs={{0,1},{1,0},{2,3},{3,2},{4,5},{5,4},{6,7},{7,6},{8,9},{9,8},{10,11... | collective-permute-start | bytes 1572872 | tf_op jit(solution)/shard_map/ppermute | solution.py:243
  18.7 5.9 %collective-permute-start.4 = (bf16[4,32,512]{2,1,0:T(8,128)(2,1)S(1)}, bf16[4,32,512]{2,1,0:T(8,128)(2,1)S(1)}, u32[]{:S(2)}, u32[]{:S(2)}) collective-permute-start(bf16[4,32,512]{2,1,0:T(8,128)(2,1)S(1)} %pad_maximum_fusion), channel_id=1, source_target_pairs={{0,2},{1,3},{2,0},{3,1},{4,6},{5,7},{6,4},{7,5},{8,10},{9,11},{10,... | collective-permute-start | bytes 393224 | tf_op jit(solution)/shard_map/ppermute | solution.py:243
  24.6 1.7 %collective-permute-start.5 = (bf16[8,32,512]{2,1,0:T(8,128)(2,1)S(1)}, bf16[8,32,512]{2,1,0:T(8,128)(2,1)S(1)}, u32[]{:S(2)}, u32[]{:S(2)}) collective-permute-start(bf16[8,32,512]{2,1,0:T(8,128)(2,1)S(1)} %constant_dynamic-update-slice_fusion.near_ref), channel_id=1, source_target_pairs={{0,1},{1,0},{2,3},{3,2},{4,5},{5,4},{6,7},{7,6},{8,9},{9,8},{10,11... | collective-permute-start | bytes 786440 | tf_op jit(solution)/shard_map/ppermute | solution.py:243
  24.8 8.8 %collective-permute-start.3 = (bf16[4,2,32,512]{3,2,1,0:T(8,128)(2,1)S(1)}, bf16[4,2,32,512]{3,2,1,0:T(8,128)(2,1)S(1)}, u32[]{:S(2)}, u32[]{:S(2)}) collective-permute-start(bf16[4,2,32,512]{3,2,1,0:T(8,128)(2,1)S(1)} %add_convert_fusion.1), channel_id=1, source_target_pairs={{0,2},{1,3},{2,0},{3,1},{4,6},{5,7},{6,4},{7,5},{8,10},{9,11},{10,... | collective-permute-start | bytes 786440 | tf_op jit(solution)/shard_map/ppermute | solution.py:243

commit v5 on v4

--- a/solution.py
+++ b/solution.py
@@ -102,28 +102,30 @@
 
 
 def insert_kernel(shape, slab_hbm, tile_hbm, sums_ref, tiles_ref, send_ref, far_ref, near_ref,
-                  slab_ref, tile_ref, parts_ref, place_ref, sems):
+                  slab_ref, tile_ref, first_ref, second_ref, place_ref, sems):
     far, wide, cores = shape
     started = copies([(slab_hbm, slab_ref), (tile_hbm, tile_ref)], sems)
     crossed, blocks = slab_ref.shape
     kinds, length, _ = tiles_ref.shape
-    rows = sums_ref.shape[1]
+    sides, rows, _ = sums_ref.shape
     height = rows // blocks
     devices = place_ref.shape[0] // blocks
-    columns = parts_ref.shape[2]
-    per_kind = length // columns
-    pieces = [(kind, n * columns) for kind in range(sums_ref.shape[0]) for n in range(per_kind)]
+    columns = length // 2
     each = devices // kinds
-
-    def multiply(piece, t):
-        kind, start = pieces[piece]
+    halves = (first_ref, second_ref)
+
+    def multiply(n, t):
         at = pl.multiple_of(t * rows, rows)
-        parts_ref[piece % 2, pl.ds(at, rows), :] = lax.dot_general(
-            sums_ref[kind], tiles_ref[t, start : start + columns, :], (((1,), (1,)), ((), ())), preferred_element_type=jnp.float32
-        )
-
-    for n in range(2):
-        parts_ref[n, pl.ds(kinds * rows, height), :] = jnp.zeros((height, columns), jnp.float32)
+        for side in range(sides):
+            halves[n][side, pl.ds(at, rows), :] = lax.dot_general(
+                sums_ref[side],
+                tiles_ref[t, n * columns : (n + 1) * columns, :],
+                (((1,), (1,)), ((), ())),
+                preferred_element_type=jnp.float32,
+            )
+
+    for ref in halves:
+        ref[:, pl.ds(kinds * rows, height), :] = jnp.zeros((sides, height, columns), jnp.float32)
     for t in range(kinds // 2):
         multiply(0, t)
 
@@ -142,28 +144,30 @@
     for t in range(kinds // 2, kinds):
         multiply(0, t)
 
-    low = lax.rem(lax.axis_index("slab"), wide * cores)
-
-    def total(piece, x, z, core):
-        s = z * wide * cores + (low ^ (x * cores + core))
+    me = lax.axis_index("slab")
+
+    def total(n, side, x, z, core):
+        s = me ^ ((z * wide + x) * cores + core)
         acc = None
         for k in range(blocks):
             at = pl.multiple_of(place_ref[s * blocks + k], height)
-            part = parts_ref[piece % 2, pl.ds(at, height), :]
+            part = halves[n][side, pl.ds(at, height), :]
             acc = part if acc is None else acc + part
         return acc
 
-    for piece, (kind, start) in enumerate(pieces):
+    for n in range(2):
         done = 0
-        for ref, first, core in ((send_ref, 0, 1), (far_ref, 1, 0), (near_ref, 0, 0)):
-
-            def step(n, carry, ref=ref, first=first, core=core, done=done, piece=piece, kind=kind, start=start):
-                if piece + 1 < len(pieces):
-                    multiply(piece + 1, done + n)
+        for ref, start, core in ((send_ref, 0, 1), (far_ref, 1, 0), (near_ref, 0, 0)):
+
+            def step(i, carry, ref=ref, start=start, core=core, done=done, n=n):
                 for m in range(each):
-                    slot = n * each + m
-                    x, z = first + slot // far, lax.rem(slot, far)
-                    ref[slot, kind, :, start : start + columns] = total(piece, x, z, core).astype(ref.dtype)
+                    slot = i * each + m
+                    x, z = start + slot // far, lax.rem(slot, far)
+                    for side in range(sides):
+                        part = total(n, side, x, z, core).astype(ref.dtype)
+                        ref[slot, side, :, n * columns : (n + 1) * columns] = part
+                if n == 0:
+                    multiply(1, done + i)
                 return carry
 
             steps = ref.shape[0] // each
@@ -301,6 +305,7 @@
         [
             *pairs_scratch,
             pltpu.VMEM((2, kinds * rows + height, length // 2), f32),
+            pltpu.VMEM((2, kinds * rows + height, length // 2), f32),
             pltpu.SMEM((devices * blocks,), jnp.int32),
             pltpu.SemaphoreType.DMA((2,)),
         ],
@@ -309,12 +314,12 @@
         "insert",
     )
     send, gathered = lax.optimization_barrier((send, gathered))
-    for offset in offsets[2:]:
-        gathered = hop(gathered, offset)
-    other = swap(gathered, 1)
     mate = swap(send, 1)
     beyond = (keep_far + mate[far:].astype(f32)).astype(bf16)
-    other, _ = lax.optimization_barrier((other, beyond))
+    for offset in offsets[2:]:
+        came, _ = lax.optimization_barrier((swap(gathered, offset), beyond))
+        gathered = jnp.concatenate([gathered, came], axis=0)
+    other = swap(gathered, 1)
 
     if devices * kinds <= blocks * crossed:
         flat = pltpu.VMEM((kinds, devices * height, pixels), f32)
@@ -334,8 +339,8 @@
             pltpu.VMEM((count * 8, LANES), f32),
             pltpu.SemaphoreType.DMA((4,)),
         ],
-        2 * devices * height * length * kinds * pixels,
-        8 << 20,
+        0,
+        0,
         "scores",
     )
 
@@ -343,9 +348,9 @@
     for x in range(1, wide):
         came, scores = lax.optimization_barrier((swap(beyond[(x - 1) * far : x * far], x * cores), scores))
         mine = mine + came.astype(f32)
-    lines = [[z * wide * cores + low for z in range(far)] for low in range(wide * cores)]
-    came = lax.all_to_all(mine.astype(bf16), "slab", 0, 0, axis_index_groups=lines, tiled=True)
-    total = jnp.sum(came.astype(f32), axis=0)
+    total = mine[0]
+    for z in range(far - 1, 0, -1):
+        total = total + swap(mine[z].astype(bf16), z * wide * cores).astype(f32)
     return scores.reshape(count), total[0:1], total[1:2]
 
 

time: 46.1 us -> 39.8 us (0.86)
  blocking collectives: 11.4 us -> 0 us
  starting transfers between devices: 8.98 us -> 13.5 us
  waiting for transfers between devices: 6.63 us -> 10.9 us
  Pallas kernels: 17.1 us -> 13.5 us
    all_to_all x1 -> x0, blocking collectives: 11.4 us -> none  [on_device(): lax.all_to_all(mine.astype(bf16), 'slab', 0, 0, axis_index_groups=lines,...]
    ppermute x6 -> x9, starting transfers between devices: 8.98 us -> 13.5 us  [swap(): lax.ppermute(array, 'slab', [(i, i ^ offset) for i in range(devices)])]
    ppermute x6 -> x9, waiting for transfers between devices: 6.63 us -> 10.9 us  [swap(): lax.ppermute(array, 'slab', [(i, i ^ offset) for i in range(devices)])]
    pallas_call x3, Pallas kernels: 17.1 us -> 13.5 us  [call(): pl.pallas_call(kernel, out_shape=tuple((jax.ShapeDtypeStruct(s, t) for s,...]
  transfers between devices with their start and end apart: 6 -> 9, of which waited for: 2 -> 5; matrix products, arithmetic and copies ran while one was open for 0% -> 0% of each run, Pallas kernels for 37% -> 34%
where the time goes in v5:
time: 39.8 us; the launch traced here: 39.6 us
  starting transfers between devices  13.5 us (34%)
  Pallas kernels  13.5 us (34%)
  waiting for transfers between devices  10.9 us (27%)
  between operations  0.75 us (2%)
  local copies, waits for them, and re-layouts  0.7 us (2%)
    pallas_call x3, Pallas kernels, call(): pl.pallas_call(kernel, out_shape=tuple((jax.ShapeDtypeStruct(s, t) for s,...  13.5 us
    ppermute x9, starting transfers between devices, swap(): lax.ppermute(array, 'slab', [(i, i ^ offset) for i in range(devices)])  13.5 us
    ppermute x9, waiting for transfers between devices, swap(): lax.ppermute(array, 'slab', [(i, i ^ offset) for i in range(devices)])  10.9 us
  transfers between devices with their start and end apart: 9, of which 5 were waited for; matrix products, arithmetic and copies ran while one was open for 0% of the time, Pallas kernels for 34%

profile of v5, /device:TPU:0, one launch (start us, length us, event | category | flops | bytes accessed | tf_op | source)
XLA Modules:
  0.0 39.6 jit_solution(5242019454501451985)
XLA Ops:
  0.6 3.1 %collective-permute-start = (bf16[1,32,512]{2,1,0:T(8,128)(2,1)}, bf16[1,32,512]{2,1,0:T(8,128)(2,1)S(1)}, u32[]{:S(2)}, u32[]{:S(2)}) collective-permute-start(bf16[1,32,512]{2,1,0:T(8,128)(2,1)} %param.8), channel_id=1, source_target_pairs={{0,4},{1,5},{2,6},{3,7},{4,0},{5,1},{6,2},{7,3},{8,12},{9,13},{10,... | collective-permute-start | bytes 98312 | tf_op jit(solution)/shard_map/ppermute | solution.py:247
  3.7 0.0 copy-start
  3.7 2.8 %sums.1 = (bf16[2,512,256]{2,1,0:T(8,128)(2,1)S(1)}, f32[128,32,256]{2,1,0:T(8,128)S(1)}, bf16[8,512,256]{2,1,0:T(8,128)(2,1)S(1)}, bf16[128,32,256]{2,1,0:T(8,128)(2,1)S(1)}) custom-call(s32[16]{0:T(128)} %block_hbm.3, f32[1,128]{1,0:T(1,128)} %bitcast.22, f32[32,256]{1,0:T(8,128)} %noise_hbm.3, bf16[8,512,256]{2,1,0:T(8,128)(2,1)} %tiles_hbm.1, ...), custom_call_target="tpu_custom_call" | custom-call | bytes 10485760 | tf_op jit(solution)/shard_map/sums/pallas_call | solution.py:261
  6.5 0.0 collective-permute-done
  6.6 0.0 copy-done
  6.6 2.7 %collective-permute-start.1 = (bf16[2,32,512]{2,1,0:T(8,128)(2,1)S(1)}, bf16[2,32,512]{2,1,0:T(8,128)(2,1)S(1)}, u32[]{:S(2)}, u32[]{:S(2)}) collective-permute-start(bf16[2,32,512]{2,1,0:T(8,128)(2,1)S(1)} %pad_maximum_fusion.1), channel_id=1, source_target_pairs={{0,8},{1,9},{2,10},{3,11},{4,12},{5,13},{6,14},{7,15},{8,0},{9,1},... | collective-permute-start | bytes 196616 | tf_op jit(solution)/shard_map/ppermute | solution.py:247
  9.2 5.8 %insert.1 = (bf16[8,2,32,512]{3,2,1,0:T(8,128)(2,1)S(1)}, f32[4,2,32,512]{3,2,1,0:T(8,128)S(1)}, f32[4,2,32,512]{3,2,1,0:T(8,128)S(1)}) custom-call(s32[8,16]{1,0:T(8,128)} %bitcast.18, s32[8,16]{1,0:T(8,128)} %bitcast.20, bf16[2,512,256]{2,1,0:T(8,128)(2,1)S(1)} %get-tuple-element.18.sums_ref, bf16[8,512,256]{2,1,0:T(8,128)(2,1)S(1)} %get-tuple-element.19.tiles_ref), custom_call_target="tpu_custom_call" | custom-call | flops 2147483648 | bytes 8388608 | tf_op jit(solution)/shard_map/insert/pallas_call | solution.py:261
  15.0 0.0 collective-permute-done.1
  15.0 0.1 collective-permute-start.2
  15.1 1.6 %collective-permute-start.4 = (bf16[4,32,512]{2,1,0:T(8,128)(2,1)S(1)}, bf16[4,32,512]{2,1,0:T(8,128)(2,1)S(1)}, u32[]{:S(2)}, u32[]{:S(2)}) collective-permute-start(bf16[4,32,512]{2,1,0:T(8,128)(2,1)S(1)} %pad_maximum_fusion), channel_id=1, source_target_pairs={{0,2},{1,3},{2,0},{3,1},{4,6},{5,7},{6,4},{7,5},{8,10},{9,11},{10,... | collective-permute-start | bytes 393224 | tf_op jit(solution)/shard_map/ppermute | solution.py:247
  16.7 0.3 collective-permute-done.2
  17.0 0.1 add_convert_fusion
  17.1 3.9 %collective-permute-done.4 = bf16[4,32,512]{2,1,0:T(8,128)(2,1)S(1)} collective-permute-done((bf16[4,32,512]{2,1,0:T(8,128)(2,1)S(1)}, bf16[4,32,512]{2,1,0:T(8,128)(2,1)S(1)}, u32[]{:S(2)}, u32[]{:S(2)}) %collective-permute-start.4) | collective-permute-done | bytes 131104 | tf_op jit(solution)/shard_map/ppermute | solution.py:247
  21.1 0.1 collective-permute-start.5
  21.1 1.6 %collective-permute-start.3 = (bf16[4,2,32,512]{3,2,1,0:T(8,128)(2,1)S(1)}, bf16[4,2,32,512]{3,2,1,0:T(8,128)(2,1)S(1)}, u32[]{:S(2)}, u32[]{:S(2)}) collective-permute-start(bf16[4,2,32,512]{3,2,1,0:T(8,128)(2,1)S(1)} %add_convert_fusion), channel_id=1, source_target_pairs={{0,2},{1,3},{2,0},{3,1},{4,6},{5,7},{6,4},{7,5},{8,10},{9,11},{10,... | collective-permute-start | bytes 786440 | tf_op jit(solution)/shard_map/ppermute | solution.py:247
  22.7 0.0 collective-permute-done.5.other_ref
  22.7 4.9 %scores.1 = f32[1,128]{1,0:T(1,128)} custom-call(s32[8,16]{1,0:T(8,128)} %bitcast.19, s32[8,16]{1,0:T(8,128)} %bitcast.21, s32[16]{0:T(128)} %block_hbm.3, f32[32,256]{1,0:T(8,128)} %noise_hbm.3, f32[128,32,256]{2,1,0:T(8,128)S(1)} %get-tuple-element.24.wave_ref, bf16[8,32,512]{2,1,0:T(8,128)(2,1)S(1)} %constant_dynamic-update-slice_fusion.near_ref, ...), custom_call_target="tpu_custom_call" | custom-call | tf_op jit(solution)/shard_map/scores/pallas_call | solution.py:261
  27.6 2.2 %collective-permute-done.3 = bf16[4,2,32,512]{3,2,1,0:T(8,128)(2,1)S(1)} collective-permute-done((bf16[4,2,32,512]{3,2,1,0:T(8,128)(2,1)S(1)}, bf16[4,2,32,512]{3,2,1,0:T(8,128)(2,1)S(1)}, u32[]{:S(2)}, u32[]{:S(2)}) %collective-permute-start.3) | collective-permute-done | bytes 262176 | tf_op jit(solution)/shard_map/ppermute | solution.py:247
  29.9 0.1 fusion.3
  30.0 1.1 %collective-permute-start.6 = (bf16[2,32,512]{2,1,0:T(8,128)(2,1)S(1)}, bf16[2,32,512]{2,1,0:T(8,128)(2,1)S(1)}, u32[]{:S(2)}, u32[]{:S(2)}) collective-permute-start(bf16[2,32,512]{2,1,0:T(8,128)(2,1)S(1)} %get-tuple-element.33), channel_id=1, source_target_pairs={{0,12},{1,13},{2,14},{3,15},{4,8},{5,9},{6,10},{7,11},{8,4},{9,5},... | collective-permute-start | bytes 196616 | tf_op jit(solution)/shard_map/ppermute | solution.py:247
  31.1 1.7 %collective-permute-start.7 = (bf16[2,32,512]{2,1,0:T(8,128)(2,1)S(1)}, bf16[2,32,512]{2,1,0:T(8,128)(2,1)S(1)}, u32[]{:S(2)}, u32[]{:S(2)}) collective-permute-start(bf16[2,32,512]{2,1,0:T(8,128)(2,1)S(1)} %get-tuple-element.35), channel_id=1, source_target_pairs={{0,8},{1,9},{2,10},{3,11},{4,12},{5,13},{6,14},{7,15},{8,0},{9,1},... | collective-permute-start | bytes 196616 | tf_op jit(solution)/shard_map/ppermute | solution.py:247
  32.8 1.7 %collective-permute-start.8 = (bf16[2,32,512]{2,1,0:T(8,128)(2,1)S(1)}, bf16[2,32,512]{2,1,0:T(8,128)(2,1)S(1)}, u32[]{:S(2)}, u32[]{:S(2)}) collective-permute-start(bf16[2,32,512]{2,1,0:T(8,128)(2,1)S(1)} %get-tuple-element.34), channel_id=1, source_target_pairs={{0,4},{1,5},{2,6},{3,7},{4,0},{5,1},{6,2},{7,3},{8,12},{9,13},{10,... | collective-permute-start | bytes 196616 | tf_op jit(solution)/shard_map/ppermute | solution.py:247
  34.5 2.4 %collective-permute-done.6 = bf16[2,32,512]{2,1,0:T(8,128)(2,1)S(1)} collective-permute-done((bf16[2,32,512]{2,1,0:T(8,128)(2,1)S(1)}, bf16[2,32,512]{2,1,0:T(8,128)(2,1)S(1)}, u32[]{:S(2)}, u32[]{:S(2)}) %collective-permute-start.6) | collective-permute-done | bytes 65568 | tf_op jit(solution)/shard_map/ppermute | solution.py:247
  36.9 2.0 %collective-permute-done.7 = bf16[2,32,512]{2,1,0:T(8,128)(2,1)S(1)} collective-permute-done((bf16[2,32,512]{2,1,0:T(8,128)(2,1)S(1)}, bf16[2,32,512]{2,1,0:T(8,128)(2,1)S(1)}, u32[]{:S(2)}, u32[]{:S(2)}) %collective-permute-start.7) | collective-permute-done | bytes 65568 | tf_op jit(solution)/shard_map/ppermute | solution.py:247
  38.9 0.0 collective-permute-done.8
  38.9 0.7 %fusion.4 = (f32[1,32,512]{2,1,0:T(8,128)}, f32[1,32,512]{2,1,0:T(8,128)}) fusion(f32[2,32,512]{2,1,0:T(8,128)S(1)} %fusion.2), kind=kLoop, calls=%fused_computation.14 | loop fusion | bytes 262144 | tf_op jit(solution)/shard_map/slice | solution.py:354
  (6 shorter events, 0.1 us)
Async XLA Ops:
  0.6 5.9 %collective-permute-start = (bf16[1,32,512]{2,1,0:T(8,128)(2,1)}, bf16[1,32,512]{2,1,0:T(8,128)(2,1)S(1)}, u32[]{:S(2)}, u32[]{:S(2)}) collective-permute-start(bf16[1,32,512]{2,1,0:T(8,128)(2,1)} %param.8), channel_id=1, source_target_pairs={{0,4},{1,5},{2,6},{3,7},{4,0},{5,1},{6,2},{7,3},{8,12},{9,13},{10,... | collective-permute-start | bytes 98312 | tf_op jit(solution)/shard_map/ppermute | solution.py:247
  3.7 2.8 %copy-start = (bf16[1,32,512]{2,1,0:T(8,128)(2,1)S(1)}, bf16[1,32,512]{2,1,0:T(8,128)(2,1)}, u32[]{:S(2)}) copy-start(bf16[1,32,512]{2,1,0:T(8,128)(2,1)} %param.8) | copy-start | bytes 98308
  6.6 8.4 %collective-permute-start.1 = (bf16[2,32,512]{2,1,0:T(8,128)(2,1)S(1)}, bf16[2,32,512]{2,1,0:T(8,128)(2,1)S(1)}, u32[]{:S(2)}, u32[]{:S(2)}) collective-permute-start(bf16[2,32,512]{2,1,0:T(8,128)(2,1)S(1)} %pad_maximum_fusion.1), channel_id=1, source_target_pairs={{0,8},{1,9},{2,10},{3,11},{4,12},{5,13},{6,14},{7,15},{8,0},{9,1},... | collective-permute-start | bytes 196616 | tf_op jit(solution)/shard_map/ppermute | solution.py:247
  15.0 2.0 %collective-permute-start.2 = (bf16[8,2,32,512]{3,2,1,0:T(8,128)(2,1)S(1)}, bf16[8,2,32,512]{3,2,1,0:T(8,128)(2,1)S(1)}, u32[]{:S(2)}, u32[]{:S(2)}) collective-permute-start(bf16[8,2,32,512]{3,2,1,0:T(8,128)(2,1)S(1)} %get-tuple-element.23), channel_id=1, source_target_pairs={{0,1},{1,0},{2,3},{3,2},{4,5},{5,4},{6,7},{7,6},{8,9},{9,8},{10,11... | collective-permute-start | bytes 1572872 | tf_op jit(solution)/shard_map/ppermute | solution.py:247
  15.1 5.9 %collective-permute-start.4 = (bf16[4,32,512]{2,1,0:T(8,128)(2,1)S(1)}, bf16[4,32,512]{2,1,0:T(8,128)(2,1)S(1)}, u32[]{:S(2)}, u32[]{:S(2)}) collective-permute-start(bf16[4,32,512]{2,1,0:T(8,128)(2,1)S(1)} %pad_maximum_fusion), channel_id=1, source_target_pairs={{0,2},{1,3},{2,0},{3,1},{4,6},{5,7},{6,4},{7,5},{8,10},{9,11},{10,... | collective-permute-start | bytes 393224 | tf_op jit(solution)/shard_map/ppermute | solution.py:247
  21.1 1.6 %collective-permute-start.5 = (bf16[8,32,512]{2,1,0:T(8,128)(2,1)S(1)}, bf16[8,32,512]{2,1,0:T(8,128)(2,1)S(1)}, u32[]{:S(2)}, u32[]{:S(2)}) collective-permute-start(bf16[8,32,512]{2,1,0:T(8,128)(2,1)S(1)} %constant_dynamic-update-slice_fusion.near_ref), channel_id=1, source_target_pairs={{0,1},{1,0},{2,3},{3,2},{4,5},{5,4},{6,7},{7,6},{8,9},{9,8},{10,11... | collective-permute-start | bytes 786440 | tf_op jit(solution)/shard_map/ppermute | solution.py:247
  21.1 8.7 %collective-permute-start.3 = (bf16[4,2,32,512]{3,2,1,0:T(8,128)(2,1)S(1)}, bf16[4,2,32,512]{3,2,1,0:T(8,128)(2,1)S(1)}, u32[]{:S(2)}, u32[]{:S(2)}) collective-permute-start(bf16[4,2,32,512]{3,2,1,0:T(8,128)(2,1)S(1)} %add_convert_fusion), channel_id=1, source_target_pairs={{0,2},{1,3},{2,0},{3,1},{4,6},{5,7},{6,4},{7,5},{8,10},{9,11},{10,... | collective-permute-start | bytes 786440 | tf_op jit(solution)/shard_map/ppermute | solution.py:247
  30.0 6.9 %collective-permute-start.6 = (bf16[2,32,512]{2,1,0:T(8,128)(2,1)S(1)}, bf16[2,32,512]{2,1,0:T(8,128)(2,1)S(1)}, u32[]{:S(2)}, u32[]{:S(2)}) collective-permute-start(bf16[2,32,512]{2,1,0:T(8,128)(2,1)S(1)} %get-tuple-element.33), channel_id=1, source_target_pairs={{0,12},{1,13},{2,14},{3,15},{4,8},{5,9},{6,10},{7,11},{8,4},{9,5},... | collective-permute-start | bytes 196616 | tf_op jit(solution)/shard_map/ppermute | solution.py:247
  31.1 7.8 %collective-permute-start.7 = (bf16[2,32,512]{2,1,0:T(8,128)(2,1)S(1)}, bf16[2,32,512]{2,1,0:T(8,128)(2,1)S(1)}, u32[]{:S(2)}, u32[]{:S(2)}) collective-permute-start(bf16[2,32,512]{2,1,0:T(8,128)(2,1)S(1)} %get-tuple-element.35), channel_id=1, source_target_pairs={{0,8},{1,9},{2,10},{3,11},{4,12},{5,13},{6,14},{7,15},{8,0},{9,1},... | collective-permute-start | bytes 196616 | tf_op jit(solution)/shard_map/ppermute | solution.py:247
  32.8 6.1 %collective-permute-start.8 = (bf16[2,32,512]{2,1,0:T(8,128)(2,1)S(1)}, bf16[2,32,512]{2,1,0:T(8,128)(2,1)S(1)}, u32[]{:S(2)}, u32[]{:S(2)}) collective-permute-start(bf16[2,32,512]{2,1,0:T(8,128)(2,1)S(1)} %get-tuple-element.34), channel_id=1, source_target_pairs={{0,4},{1,5},{2,6},{3,7},{4,0},{5,1},{6,2},{7,3},{8,12},{9,13},{10,... | collective-permute-start | bytes 196616 | tf_op jit(solution)/shard_map/ppermute | solution.py:247

commit v6 on v3

--- a/solution.py
+++ b/solution.py
@@ -19,6 +19,10 @@
     while (2 * wide) ** 3 <= chips:
         wide *= 2
     return chips // wide, wide, cores
+
+
+def powers(size):
+    return [1 << n for n in range(size.bit_length() - 1)]
 
 
 def sin_cos(angle):
@@ -107,22 +111,29 @@
     height = rows // (2 * blocks)
     devices = place_ref.shape[0] // blocks
 
+    def multiply(t):
+        parts_ref[t * rows : (t + 1) * rows, :] = lax.dot_general(
+            sums_ref[...], tiles_ref[t], (((1,), (1,)), ((), ())), preferred_element_type=jnp.float32
+        )
+
+    parts_ref[pl.ds(kinds * rows, 2 * height), :] = jnp.zeros((2 * height, parts_ref.shape[1]), jnp.float32)
+    for t in range(kinds // 2):
+        multiply(t)
+
+    for copy in started:
+        copy.wait()
+
     def clear(n, carry):
         for m in range(blocks):
             place_ref[n * blocks + m] = kinds * rows
         return carry
 
     lax.fori_loop(0, devices, clear, 0, unroll=devices <= 16)
-    for copy in started:
-        copy.wait()
     for k in range(blocks):
         for r in range(crossed):
             place_ref[slab_ref[r, k] * blocks + k] = tile_ref[r, k] * rows + k * 2 * height
-    parts_ref[pl.ds(kinds * rows, 2 * height), :] = jnp.zeros((2 * height, parts_ref.shape[1]), jnp.float32)
-    for t in range(kinds):
-        parts_ref[t * rows : (t + 1) * rows, :] = lax.dot_general(
-            sums_ref[...], tiles_ref[t], (((1,), (1,)), ((), ())), preferred_element_type=jnp.float32
-        )
+    for t in range(kinds // 2, kinds):
+        multiply(t)
     me = lax.axis_index("slab")
 
     def total(x, z, core, kind):
@@ -148,33 +159,32 @@
     fill(near_ref, 0, 0)
 
 
-def score_kernel(shape, slab_hbm, tile_hbm, block_hbm, noise_hbm, wave_ref, near_ref, other_ref, images_ref, tiles_ref,
-                 score_ref, slab_ref, tile_ref, block_ref, noise_ref, flat_ref, proj_ref, part_ref, sems):
+def score_kernel(shape, slab_hbm, tile_hbm, block_hbm, noise_hbm, wave_ref, images_ref, tiles_ref, *refs):
     far, wide, cores = shape
+    columns, refs = refs[: wide * cores], refs[wide * cores :]
+    score_ref, slab_ref, tile_ref, block_ref, noise_ref, flat_ref, proj_ref, part_ref, sems = refs
     started = copies([(slab_hbm, slab_ref), (tile_hbm, tile_ref), (block_hbm, block_ref), (noise_hbm, noise_ref)], sems)
     height, pixels = noise_ref.shape
     crossed, blocks = slab_ref.shape
     batches = block_ref.shape[0]
     count = images_ref.shape[0]
     size = count // batches
-    half = near_ref.shape[0]
     me = lax.axis_index("slab")
-    dense = 2 * half * tiles_ref.shape[0] <= crossed * blocks
+    dense = far * len(columns) * tiles_ref.shape[0] <= crossed * blocks
 
     def slot_of(s):
         away = me ^ s
         core, chip = lax.rem(away, cores), away // cores
-        return core * half + lax.rem(chip, wide) * far + chip // wide
-
-    for n, ref in enumerate((near_ref, other_ref)):
-        lines = ref[...].reshape(half * height, ref.shape[2])
+        return (core * wide + lax.rem(chip, wide)) * far + chip // wide
+
+    for n, ref in enumerate(columns):
+        lines = ref[...].reshape(far * height, ref.shape[2])
+        at = slice(n * far * height, (n + 1) * far * height)
         if dense:
             for t in range(tiles_ref.shape[0]):
-                flat_ref[t, n * half * height : (n + 1) * half * height, :] = jnp.dot(
-                    lines, tiles_ref[t], preferred_element_type=jnp.float32
-                )
+                flat_ref[t, at, :] = jnp.dot(lines, tiles_ref[t], preferred_element_type=jnp.float32)
         else:
-            flat_ref[n * half * height : (n + 1) * half * height, :] = lines
+            flat_ref[at, :] = lines
     for copy in started:
         copy.wait()
 
@@ -242,7 +252,11 @@
             name=name,
         )(*operands)
 
-    column = jnp.concatenate([volume] + [swap(volume, z * wide * cores) for z in range(1, far)], axis=0)
+    def hop(array, offset):
+        return jnp.concatenate([array, swap(array, offset)], axis=0)
+
+    offsets = [z * wide * cores for z in powers(far)]
+    gathered = hop(volume, offsets[0])
 
     sums, wave, tiles_near, images_near = call(
         sum_kernel,
@@ -262,8 +276,9 @@
         10 << 20,
         "sums",
     )
-    sums, column = lax.optimization_barrier((sums, column))
-    near = jnp.concatenate([column] + [swap(column, x * cores) for x in range(1, wide)], axis=0)
+    sums, gathered = lax.optimization_barrier((sums, gathered))
+    for offset in offsets[1:]:
+        gathered = hop(gathered, offset)
 
     place = (2, height, length)
     send, keep_far, keep_near = call(
@@ -281,11 +296,13 @@
         8 << 20,
         "insert",
     )
-    send, near = lax.optimization_barrier((send, near))
-    other = swap(near, 1)
+    send, gathered = lax.optimization_barrier((send, gathered))
     mate = swap(send, 1)
     beyond = (keep_far + mate[far:].astype(f32)).astype(bf16)
-    other, beyond = lax.optimization_barrier((other, beyond))
+    columns = [gathered]
+    for x in range(1, wide):
+        columns.append(lax.optimization_barrier((swap(gathered, x * cores), beyond))[0])
+    columns += [swap(column, 1) for column in columns]
 
     if devices * kinds <= blocks * crossed:
         flat = pltpu.VMEM((kinds, devices * height, pixels), f32)
@@ -294,8 +311,8 @@
     (scores,) = call(
         functools.partial(score_kernel, shape),
         [((1, count), f32)],
-        [hbm] * 4 + [vmem] * 5,
-        (slabs, kind_rows, batch_block, inv_sigma2, wave, near, other, images_near, tiles_near),
+        [hbm] * 4 + [vmem] * (3 + len(columns)),
+        (slabs, kind_rows, batch_block, inv_sigma2, wave, images_near, tiles_near, *columns),
         [
             *pairs_scratch,
             block_scratch,
@@ -305,8 +322,8 @@
             pltpu.VMEM((count * 8, LANES), f32),
             pltpu.SemaphoreType.DMA((4,)),
         ],
-        2 * devices * height * length * kinds * pixels,
-        8 << 20,
+        0,
+        0,
         "scores",
     )
 

time: 38.5 us -> 36.8 us (0.956)
  waiting for transfers between devices: 11.1 us -> 9.39 us
  Pallas kernels: 12.8 us -> 12.2 us
  starting transfers between devices: 12.8 us -> 13.4 us
    ppermute x10, waiting for transfers between devices: 11.1 us -> 9.39 us  [swap(): lax.ppermute(array, 'slab', [(i, i ^ offset) for i in range(devices)])]
    ppermute x10, starting transfers between devices: 12.8 us -> 13.4 us  [swap(): lax.ppermute(array, 'slab', [(i, i ^ offset) for i in range(devices)])]
    pallas_call x3, Pallas kernels: 12.8 us -> 12.2 us  [call(): pl.pallas_call(kernel, out_shape=tuple((jax.ShapeDtypeStruct(s, t) for s,...]
  transfers between devices with their start and end apart: 10 -> 10, of which waited for: 6 -> 4; matrix products, arithmetic and copies ran while one was open for 0% -> 0% of each run, Pallas kernels for 33% -> 33%
where the time goes in v6:
time: 36.8 us; the launch traced here: 36.6 us
  starting transfers between devices  13.4 us (36%)
  Pallas kernels  12.2 us (33%)
  waiting for transfers between devices  9.39 us (26%)
  between operations  0.74 us (2%)
  local copies, waits for them, and re-layouts  0.68 us (2%)
    ppermute x10, starting transfers between devices, swap(): lax.ppermute(array, 'slab', [(i, i ^ offset) for i in range(devices)])  13.4 us
    pallas_call x3, Pallas kernels, call(): pl.pallas_call(kernel, out_shape=tuple((jax.ShapeDtypeStruct(s, t) for s,...  12.2 us
    ppermute x10, waiting for transfers between devices, swap(): lax.ppermute(array, 'slab', [(i, i ^ offset) for i in range(devices)])  9.39 us
  transfers between devices with their start and end apart: 10, of which 4 were waited for; matrix products, arithmetic and copies ran while one was open for 0% of the time, Pallas kernels for 33%

profile of v6, /device:TPU:0, one launch (start us, length us, event | category | flops | bytes accessed | tf_op | source)
XLA Modules:
  0.0 36.6 jit_solution(3280116699035080016)
XLA Ops:
  0.6 3.1 %collective-permute-start = (bf16[1,32,512]{2,1,0:T(8,128)(2,1)}, bf16[1,32,512]{2,1,0:T(8,128)(2,1)S(1)}, u32[]{:S(2)}, u32[]{:S(2)}) collective-permute-start(bf16[1,32,512]{2,1,0:T(8,128)(2,1)} %param.8), channel_id=1, source_target_pairs={{0,4},{1,5},{2,6},{3,7},{4,0},{5,1},{6,2},{7,3},{8,12},{9,13},{10,... | collective-permute-start | bytes 98312 | tf_op jit(solution)/shard_map/ppermute | solution.py:230
  3.7 0.0 copy-start
  3.7 2.8 %sums.1 = (bf16[1024,256]{1,0:T(8,128)(2,1)S(1)}, f32[128,32,256]{2,1,0:T(8,128)S(1)}, bf16[8,512,256]{2,1,0:T(8,128)(2,1)S(1)}, bf16[128,32,256]{2,1,0:T(8,128)(2,1)S(1)}) custom-call(s32[16]{0:T(128)} %block_hbm.3, f32[1,128]{1,0:T(1,128)} %bitcast.22, f32[32,256]{1,0:T(8,128)} %noise_hbm.3, bf16[8,512,256]{2,1,0:T(8,128)(2,1)} %tiles_hbm.1, ...), custom_call_target="tpu_custom_call" | custom-call | bytes 10485760 | tf_op jit(solution)/shard_map/sums/pallas_call | solution.py:244
  6.6 0.0 collective-permute-done
  6.6 0.0 copy-done
  6.6 2.6 %collective-permute-start.1 = (bf16[2,32,512]{2,1,0:T(8,128)(2,1)S(1)}, bf16[2,32,512]{2,1,0:T(8,128)(2,1)S(1)}, u32[]{:S(2)}, u32[]{:S(2)}) collective-permute-start(bf16[2,32,512]{2,1,0:T(8,128)(2,1)S(1)} %pad_maximum_fusion.1), channel_id=1, source_target_pairs={{0,8},{1,9},{2,10},{3,11},{4,12},{5,13},{6,14},{7,15},{8,0},{9,1},... | collective-permute-start | bytes 196616 | tf_op jit(solution)/shard_map/ppermute | solution.py:230
  9.2 4.4 %insert.1 = (bf16[8,2,32,512]{3,2,1,0:T(8,128)(2,1)S(1)}, f32[4,2,32,512]{3,2,1,0:T(8,128)S(1)}, f32[4,2,32,512]{3,2,1,0:T(8,128)S(1)}) custom-call(s32[8,16]{1,0:T(8,128)} %bitcast.18, s32[8,16]{1,0:T(8,128)} %bitcast.20, bf16[1024,256]{1,0:T(8,128)(2,1)S(1)} %get-tuple-element.18.sums_ref, bf16[8,512,256]{2,1,0:T(8,128)(2,1)S(1)} %get-tuple-element.19.tiles_ref), custom_call_target="tpu_custom_call" | custom-call | flops 2147483648 | bytes 8388608 | tf_op jit(solution)/shard_map/insert/pallas_call | solution.py:244
  13.7 0.0 collective-permute-done.1
  13.7 0.1 collective-permute-start.2
  13.8 1.6 %collective-permute-start.4 = (bf16[4,32,512]{2,1,0:T(8,128)(2,1)S(1)}, bf16[4,32,512]{2,1,0:T(8,128)(2,1)S(1)}, u32[]{:S(2)}, u32[]{:S(2)}) collective-permute-start(bf16[4,32,512]{2,1,0:T(8,128)(2,1)S(1)} %pad_maximum_fusion.refs_0_), channel_id=1, source_target_pairs={{0,2},{1,3},{2,0},{3,1},{4,6},{5,7},{6,4},{7,5},{8,10},{9,11},{10,... | collective-permute-start | bytes 393224 | tf_op jit(solution)/shard_map/ppermute | solution.py:230
  15.3 0.3 collective-permute-done.2
  15.7 0.1 add_convert_fusion
  15.8 1.6 %collective-permute-start.3 = (bf16[4,2,32,512]{3,2,1,0:T(8,128)(2,1)S(1)}, bf16[4,2,32,512]{3,2,1,0:T(8,128)(2,1)S(1)}, u32[]{:S(2)}, u32[]{:S(2)}) collective-permute-start(bf16[4,2,32,512]{3,2,1,0:T(8,128)(2,1)S(1)} %add_convert_fusion), channel_id=1, source_target_pairs={{0,2},{1,3},{2,0},{3,1},{4,6},{5,7},{6,4},{7,5},{8,10},{9,11},{10,... | collective-permute-start | bytes 786440 | tf_op jit(solution)/shard_map/ppermute | solution.py:230
  17.3 0.0 collective-permute-start.5
  17.3 2.8 %collective-permute-done.4.refs_1_ = bf16[4,32,512]{2,1,0:T(8,128)(2,1)S(1)} collective-permute-done((bf16[4,32,512]{2,1,0:T(8,128)(2,1)S(1)}, bf16[4,32,512]{2,1,0:T(8,128)(2,1)S(1)}, u32[]{:S(2)}, u32[]{:S(2)}) %collective-permute-start.4) | collective-permute-done | bytes 131104 | tf_op jit(solution)/shard_map/ppermute | solution.py:230
  20.1 0.0 collective-permute-start.6
  20.2 0.0 collective-permute-done.5.refs_2_
  20.2 1.3 %collective-permute-done.6.refs_3_ = bf16[4,32,512]{2,1,0:T(8,128)(2,1)S(1)} collective-permute-done((bf16[4,32,512]{2,1,0:T(8,128)(2,1)S(1)}, bf16[4,32,512]{2,1,0:T(8,128)(2,1)S(1)}, u32[]{:S(2)}, u32[]{:S(2)}) %collective-permute-start.6) | collective-permute-done | bytes 131104 | tf_op jit(solution)/shard_map/ppermute | solution.py:230
  21.5 4.9 %scores.1 = f32[1,128]{1,0:T(1,128)} custom-call(s32[8,16]{1,0:T(8,128)} %bitcast.19, s32[8,16]{1,0:T(8,128)} %bitcast.21, s32[16]{0:T(128)} %block_hbm.3, f32[32,256]{1,0:T(8,128)} %noise_hbm.3, f32[128,32,256]{2,1,0:T(8,128)S(1)} %get-tuple-element.24.wave_ref, bf16[128,32,256]{2,1,0:T(8,128)(2,1)S(1)} %get-tuple-element.25.images_ref, ...), custom_call_target="tpu_custom_call" | custom-call | tf_op jit(solution)/shard_map/scores/pallas_call | solution.py:244
  26.5 0.0 collective-permute-done.3
  26.5 0.1 fusion.3
  26.6 1.3 %collective-permute-start.7 = (bf16[2,32,512]{2,1,0:T(8,128)(2,1)S(1)}, bf16[2,32,512]{2,1,0:T(8,128)(2,1)S(1)}, u32[]{:S(2)}, u32[]{:S(2)}) collective-permute-start(bf16[2,32,512]{2,1,0:T(8,128)(2,1)S(1)} %get-tuple-element.33), channel_id=1, source_target_pairs={{0,4},{1,5},{2,6},{3,7},{4,0},{5,1},{6,2},{7,3},{8,12},{9,13},{10,... | collective-permute-start | bytes 196616 | tf_op jit(solution)/shard_map/ppermute | solution.py:230
  28.0 1.4 %collective-permute-start.8 = (bf16[2,32,512]{2,1,0:T(8,128)(2,1)S(1)}, bf16[2,32,512]{2,1,0:T(8,128)(2,1)S(1)}, u32[]{:S(2)}, u32[]{:S(2)}) collective-permute-start(bf16[2,32,512]{2,1,0:T(8,128)(2,1)S(1)} %get-tuple-element.35), channel_id=1, source_target_pairs={{0,8},{1,9},{2,10},{3,11},{4,12},{5,13},{6,14},{7,15},{8,0},{9,1},... | collective-permute-start | bytes 196616 | tf_op jit(solution)/shard_map/ppermute | solution.py:230
  29.4 1.7 %collective-permute-start.9 = (bf16[2,32,512]{2,1,0:T(8,128)(2,1)S(1)}, bf16[2,32,512]{2,1,0:T(8,128)(2,1)S(1)}, u32[]{:S(2)}, u32[]{:S(2)}) collective-permute-start(bf16[2,32,512]{2,1,0:T(8,128)(2,1)S(1)} %get-tuple-element.34), channel_id=1, source_target_pairs={{0,12},{1,13},{2,14},{3,15},{4,8},{5,9},{6,10},{7,11},{8,4},{9,5},... | collective-permute-start | bytes 196616 | tf_op jit(solution)/shard_map/ppermute | solution.py:230
  31.1 0.0 collective-permute-done.7
  31.1 4.9 %collective-permute-done.8 = bf16[2,32,512]{2,1,0:T(8,128)(2,1)S(1)} collective-permute-done((bf16[2,32,512]{2,1,0:T(8,128)(2,1)S(1)}, bf16[2,32,512]{2,1,0:T(8,128)(2,1)S(1)}, u32[]{:S(2)}, u32[]{:S(2)}) %collective-permute-start.8) | collective-permute-done | bytes 65568 | tf_op jit(solution)/shard_map/ppermute | solution.py:230
  35.9 0.0 collective-permute-done.9
  36.0 0.7 %fusion.4 = (f32[1,32,512]{2,1,0:T(8,128)}, f32[1,32,512]{2,1,0:T(8,128)}) fusion(f32[2,32,512]{2,1,0:T(8,128)S(1)} %fusion.2), kind=kLoop, calls=%fused_computation.12 | loop fusion | bytes 262144 | tf_op jit(solution)/shard_map/slice | solution.py:337
  (4 shorter events, 0.1 us)
Async XLA Ops:
  0.6 5.9 %collective-permute-start = (bf16[1,32,512]{2,1,0:T(8,128)(2,1)}, bf16[1,32,512]{2,1,0:T(8,128)(2,1)S(1)}, u32[]{:S(2)}, u32[]{:S(2)}) collective-permute-start(bf16[1,32,512]{2,1,0:T(8,128)(2,1)} %param.8), channel_id=1, source_target_pairs={{0,4},{1,5},{2,6},{3,7},{4,0},{5,1},{6,2},{7,3},{8,12},{9,13},{10,... | collective-permute-start | bytes 98312 | tf_op jit(solution)/shard_map/ppermute | solution.py:230
  3.7 2.8 %copy-start = (bf16[1,32,512]{2,1,0:T(8,128)(2,1)S(1)}, bf16[1,32,512]{2,1,0:T(8,128)(2,1)}, u32[]{:S(2)}) copy-start(bf16[1,32,512]{2,1,0:T(8,128)(2,1)} %param.8) | copy-start | bytes 98308
  6.6 7.1 %collective-permute-start.1 = (bf16[2,32,512]{2,1,0:T(8,128)(2,1)S(1)}, bf16[2,32,512]{2,1,0:T(8,128)(2,1)S(1)}, u32[]{:S(2)}, u32[]{:S(2)}) collective-permute-start(bf16[2,32,512]{2,1,0:T(8,128)(2,1)S(1)} %pad_maximum_fusion.1), channel_id=1, source_target_pairs={{0,8},{1,9},{2,10},{3,11},{4,12},{5,13},{6,14},{7,15},{8,0},{9,1},... | collective-permute-start | bytes 196616 | tf_op jit(solution)/shard_map/ppermute | solution.py:230
  13.7 2.0 %collective-permute-start.2 = (bf16[8,2,32,512]{3,2,1,0:T(8,128)(2,1)S(1)}, bf16[8,2,32,512]{3,2,1,0:T(8,128)(2,1)S(1)}, u32[]{:S(2)}, u32[]{:S(2)}) collective-permute-start(bf16[8,2,32,512]{3,2,1,0:T(8,128)(2,1)S(1)} %get-tuple-element.23), channel_id=1, source_target_pairs={{0,1},{1,0},{2,3},{3,2},{4,5},{5,4},{6,7},{7,6},{8,9},{9,8},{10,11... | collective-permute-start | bytes 1572872 | tf_op jit(solution)/shard_map/ppermute | solution.py:230
  13.8 6.4 %collective-permute-start.4 = (bf16[4,32,512]{2,1,0:T(8,128)(2,1)S(1)}, bf16[4,32,512]{2,1,0:T(8,128)(2,1)S(1)}, u32[]{:S(2)}, u32[]{:S(2)}) collective-permute-start(bf16[4,32,512]{2,1,0:T(8,128)(2,1)S(1)} %pad_maximum_fusion.refs_0_), channel_id=1, source_target_pairs={{0,2},{1,3},{2,0},{3,1},{4,6},{5,7},{6,4},{7,5},{8,10},{9,11},{10,... | collective-permute-start | bytes 393224 | tf_op jit(solution)/shard_map/ppermute | solution.py:230
  15.8 10.7 %collective-permute-start.3 = (bf16[4,2,32,512]{3,2,1,0:T(8,128)(2,1)S(1)}, bf16[4,2,32,512]{3,2,1,0:T(8,128)(2,1)S(1)}, u32[]{:S(2)}, u32[]{:S(2)}) collective-permute-start(bf16[4,2,32,512]{3,2,1,0:T(8,128)(2,1)S(1)} %add_convert_fusion), channel_id=1, source_target_pairs={{0,2},{1,3},{2,0},{3,1},{4,6},{5,7},{6,4},{7,5},{8,10},{9,11},{10,... | collective-permute-start | bytes 786440 | tf_op jit(solution)/shard_map/ppermute | solution.py:230
  17.3 2.8 %collective-permute-start.5 = (bf16[4,32,512]{2,1,0:T(8,128)(2,1)S(1)}, bf16[4,32,512]{2,1,0:T(8,128)(2,1)S(1)}, u32[]{:S(2)}, u32[]{:S(2)}) collective-permute-start(bf16[4,32,512]{2,1,0:T(8,128)(2,1)S(1)} %pad_maximum_fusion.refs_0_), channel_id=1, source_target_pairs={{0,1},{1,0},{2,3},{3,2},{4,5},{5,4},{6,7},{7,6},{8,9},{9,8},{10,11... | collective-permute-start | bytes 393224 | tf_op jit(solution)/shard_map/ppermute | solution.py:230
  20.1 1.3 %collective-permute-start.6 = (bf16[4,32,512]{2,1,0:T(8,128)(2,1)S(1)}, bf16[4,32,512]{2,1,0:T(8,128)(2,1)S(1)}, u32[]{:S(2)}, u32[]{:S(2)}) collective-permute-start(bf16[4,32,512]{2,1,0:T(8,128)(2,1)S(1)} %collective-permute-done.4.refs_1_), channel_id=1, source_target_pairs={{0,1},{1,0},{2,3},{3,2},{4,5},{5,4},{6,7},{7,6},{8,9},{9,8},{10,11... | collective-permute-start | bytes 393224 | tf_op jit(solution)/shard_map/ppermute | solution.py:230
  26.6 4.5 %collective-permute-start.7 = (bf16[2,32,512]{2,1,0:T(8,128)(2,1)S(1)}, bf16[2,32,512]{2,1,0:T(8,128)(2,1)S(1)}, u32[]{:S(2)}, u32[]{:S(2)}) collective-permute-start(bf16[2,32,512]{2,1,0:T(8,128)(2,1)S(1)} %get-tuple-element.33), channel_id=1, source_target_pairs={{0,4},{1,5},{2,6},{3,7},{4,0},{5,1},{6,2},{7,3},{8,12},{9,13},{10,... | collective-permute-start | bytes 196616 | tf_op jit(solution)/shard_map/ppermute | solution.py:230
  28.0 8.0 %collective-permute-start.8 = (bf16[2,32,512]{2,1,0:T(8,128)(2,1)S(1)}, bf16[2,32,512]{2,1,0:T(8,128)(2,1)S(1)}, u32[]{:S(2)}, u32[]{:S(2)}) collective-permute-start(bf16[2,32,512]{2,1,0:T(8,128)(2,1)S(1)} %get-tuple-element.35), channel_id=1, source_target_pairs={{0,8},{1,9},{2,10},{3,11},{4,12},{5,13},{6,14},{7,15},{8,0},{9,1},... | collective-permute-start | bytes 196616 | tf_op jit(solution)/shard_map/ppermute | solution.py:230
  29.4 6.6 %collective-permute-start.9 = (bf16[2,32,512]{2,1,0:T(8,128)(2,1)S(1)}, bf16[2,32,512]{2,1,0:T(8,128)(2,1)S(1)}, u32[]{:S(2)}, u32[]{:S(2)}) collective-permute-start(bf16[2,32,512]{2,1,0:T(8,128)(2,1)S(1)} %get-tuple-element.34), channel_id=1, source_target_pairs={{0,12},{1,13},{2,14},{3,15},{4,8},{5,9},{6,10},{7,11},{8,4},{9,5},... | collective-permute-start | bytes 196616 | tf_op jit(solution)/shard_map/ppermute | solution.py:230

commit v7 on v6

--- a/solution.py
+++ b/solution.py
@@ -74,7 +74,8 @@
     part = count // CHUNKS
     small = [(defocus_hbm, defocus_ref), (block_hbm, block_ref), (noise_hbm, noise_ref)]
     large = [(images_hbm.at[pl.ds(n * part, part)], images_ref.at[pl.ds(n * part, part)]) for n in range(CHUNKS)]
-    started = copies(small + large + [(tiles_hbm, tiles_ref)], sems)
+    started = copies(small + large, sems)
+    last = pltpu.make_async_copy(tiles_hbm, tiles_ref, sems.at[len(started)])
     height, pixels = noise_ref.shape
     batches = block_ref.shape[0]
     size = count // batches
@@ -85,6 +86,8 @@
     for b in range(batches):
         if b % (batches // CHUNKS) == 0:
             started[len(small) + b // (batches // CHUNKS)].wait()
+        if b == 0:
+            last.start()
         data = jnp.zeros((height, pixels), jnp.float32)
         weight = jnp.zeros((height, pixels), jnp.float32)
         for j in range(size):
@@ -98,7 +101,7 @@
         acc_ref[k, 1] = acc_ref[k, 1] + weight
     sums = (acc_ref[...] * noise_ref[...][None, None]).astype(jnp.bfloat16)
     sums_ref[...] = sums.reshape(sums_ref.shape)
-    started[-1].wait()
+    last.wait()
 
 
 def insert_kernel(shape, slab_hbm, tile_hbm, sums_ref, tiles_ref, send_ref, far_ref, near_ref,
@@ -159,34 +162,28 @@
     fill(near_ref, 0, 0)
 
 
-def score_kernel(shape, slab_hbm, tile_hbm, block_hbm, noise_hbm, wave_ref, images_ref, tiles_ref, *refs):
+def project_kernel(shape, slab_hbm, tile_hbm, tiles_ref, *refs):
     far, wide, cores = shape
     columns, refs = refs[: wide * cores], refs[wide * cores :]
-    score_ref, slab_ref, tile_ref, block_ref, noise_ref, flat_ref, proj_ref, part_ref, sems = refs
-    started = copies([(slab_hbm, slab_ref), (tile_hbm, tile_ref), (block_hbm, block_ref), (noise_hbm, noise_ref)], sems)
-    height, pixels = noise_ref.shape
+    proj_ref, slab_ref, tile_ref, lines_ref, flat_ref, sems = refs
+    started = copies([(slab_hbm, slab_ref), (tile_hbm, tile_ref)], sems)
     crossed, blocks = slab_ref.shape
-    batches = block_ref.shape[0]
-    count = images_ref.shape[0]
-    size = count // batches
+    kinds = tiles_ref.shape[0]
+    _, height, length = columns[0].shape
+    dense = far * len(columns) * kinds <= crossed * blocks
+    for n, ref in enumerate(columns):
+        lines_ref[n * far * height : (n + 1) * far * height, :] = ref[...].reshape(far * height, length)
+    if dense:
+        for t in range(kinds):
+            flat_ref[t] = jnp.dot(lines_ref[...], tiles_ref[t], preferred_element_type=jnp.float32)
+    for copy in started:
+        copy.wait()
     me = lax.axis_index("slab")
-    dense = far * len(columns) * tiles_ref.shape[0] <= crossed * blocks
 
     def slot_of(s):
         away = me ^ s
-        core, chip = lax.rem(away, cores), away // cores
-        return (core * wide + lax.rem(chip, wide)) * far + chip // wide
-
-    for n, ref in enumerate(columns):
-        lines = ref[...].reshape(far * height, ref.shape[2])
-        at = slice(n * far * height, (n + 1) * far * height)
-        if dense:
-            for t in range(tiles_ref.shape[0]):
-                flat_ref[t, at, :] = jnp.dot(lines, tiles_ref[t], preferred_element_type=jnp.float32)
-        else:
-            flat_ref[at, :] = lines
-    for copy in started:
-        copy.wait()
+        core, x, z = away & (cores - 1), (away // cores) & (wide - 1), away // (cores * wide)
+        return (core * wide + x) * far + z
 
     def project(k, carry):
         acc = None
@@ -196,18 +193,29 @@
             if dense:
                 part = flat_ref[t, rows, :]
             else:
-                part = jnp.dot(flat_ref[rows, :], tiles_ref[t], preferred_element_type=jnp.float32)
+                part = jnp.dot(lines_ref[rows, :], tiles_ref[t], preferred_element_type=jnp.float32)
             acc = part if acc is None else acc + part
         proj_ref[k] = acc
         return carry
 
     lax.fori_loop(0, blocks, project, 0, unroll=dense)
+
+
+def score_kernel(block_hbm, noise_hbm, proj_ref, wave_ref, images_ref, score_ref, block_ref, noise_ref, part_ref, sems):
+    started = copies([(block_hbm, block_ref), (noise_hbm, noise_ref)], sems)
+    height, pixels = noise_ref.shape
+    batches = block_ref.shape[0]
+    count = images_ref.shape[0]
+    size = count // batches
+    for copy in started:
+        copy.wait()
+    noise = noise_ref[...]
     for b in range(batches):
-        k = block_ref[b]
+        proj = proj_ref[block_ref[b]]
         for j in range(size):
             i = b * size + j
-            residual = images_ref[i].astype(jnp.float32) - wave_ref[i] * proj_ref[k]
-            power = residual * residual * noise_ref[...]
+            residual = images_ref[i].astype(jnp.float32) - wave_ref[i] * proj
+            power = residual * residual * noise
             power = sum(power[n * 8 : (n + 1) * 8] for n in range(height // 8))
             part_ref[i * 8 : (i + 1) * 8, :] = sum(power[:, n * LANES : (n + 1) * LANES] for n in range(pixels // LANES))
     total = sum(part_ref[pl.ds(n, count, 8), :] for n in range(8))
@@ -303,37 +311,38 @@
     for x in range(1, wide):
         columns.append(lax.optimization_barrier((swap(gathered, x * cores), beyond))[0])
     columns += [swap(column, 1) for column in columns]
-
     if devices * kinds <= blocks * crossed:
         flat = pltpu.VMEM((kinds, devices * height, pixels), f32)
     else:
-        flat = pltpu.VMEM((devices * height, length), bf16)
-    (scores,) = call(
-        functools.partial(score_kernel, shape),
-        [((1, count), f32)],
-        [hbm] * 4 + [vmem] * (3 + len(columns)),
-        (slabs, kind_rows, batch_block, inv_sigma2, wave, images_near, tiles_near, *columns),
-        [
-            *pairs_scratch,
-            block_scratch,
-            noise_scratch,
-            flat,
-            pltpu.VMEM((blocks, height, pixels), f32),
-            pltpu.VMEM((count * 8, LANES), f32),
-            pltpu.SemaphoreType.DMA((4,)),
-        ],
-        0,
-        0,
-        "scores",
+        flat = pltpu.VMEM((8, LANES), f32)
+    (proj,) = call(
+        functools.partial(project_kernel, shape),
+        [((blocks, height, pixels), f32)],
+        [hbm] * 2 + [vmem] * (1 + len(columns)),
+        (slabs, kind_rows, tiles_near, *columns),
+        [*pairs_scratch, pltpu.VMEM((devices * height, length), bf16), flat, pltpu.SemaphoreType.DMA((2,))],
+        2 * devices * height * length * kinds * pixels,
+        8 << 20,
+        "project",
     )
 
     mine = keep_near + mate[:far].astype(f32)
     for x in range(1, wide):
-        came, scores = lax.optimization_barrier((swap(beyond[(x - 1) * far : x * far], x * cores), scores))
-        mine = mine + came.astype(f32)
+        mine = mine + swap(beyond[(x - 1) * far : x * far], x * cores).astype(f32)
+    proj, outgoing = lax.optimization_barrier((proj, mine.astype(bf16)))
+    (scores,) = call(
+        score_kernel,
+        [((1, count), f32)],
+        [hbm] * 2 + [vmem] * 3,
+        (batch_block, inv_sigma2, proj, wave, images_near),
+        [block_scratch, noise_scratch, pltpu.VMEM((count * 8, LANES), f32), pltpu.SemaphoreType.DMA((2,))],
+        1 << 30,
+        8 << 20,
+        "scores",
+    )
     total = mine[0]
     for z in range(1, far):
-        total = total + swap(mine[z].astype(bf16), z * wide * cores).astype(f32)
+        total = total + swap(outgoing[z], z * wide * cores).astype(f32)
     return scores.reshape(count), total[0:1], total[1:2]
 
 

time: 36.8 us -> 35.5 us (0.965)
  waiting for transfers between devices: 9.39 us -> 7.37 us
  Pallas kernels: 12.2 us -> 12.8 us
    ppermute x10, waiting for transfers between devices: 9.39 us -> 7.37 us  [swap(): lax.ppermute(array, 'slab', [(i, i ^ offset) for i in range(devices)])]
    pallas_call x3 -> x4, Pallas kernels: 12.2 us -> 12.8 us  [call(): pl.pallas_call(kernel, out_shape=tuple((jax.ShapeDtypeStruct(s, t) for s,...]
  transfers between devices with their start and end apart: 10 -> 10, of which waited for: 4 -> 5; matrix products, arithmetic and copies ran while one was open for 0% -> 0% of each run, Pallas kernels for 33% -> 36%
where the time goes in v7:
time: 35.5 us; the launch traced here: 35.3 us
  starting transfers between devices  13.4 us (38%)
  Pallas kernels  12.8 us (36%)
  waiting for transfers between devices  7.37 us (21%)
  between operations  0.75 us (2%)
  local copies, waits for them, and re-layouts  0.68 us (2%)
    ppermute x10, starting transfers between devices, swap(): lax.ppermute(array, 'slab', [(i, i ^ offset) for i in range(devices)])  13.4 us
    pallas_call x4, Pallas kernels, call(): pl.pallas_call(kernel, out_shape=tuple((jax.ShapeDtypeStruct(s, t) for s,...  12.8 us
    ppermute x10, waiting for transfers between devices, swap(): lax.ppermute(array, 'slab', [(i, i ^ offset) for i in range(devices)])  7.37 us
  transfers between devices with their start and end apart: 10, of which 5 were waited for; matrix products, arithmetic and copies ran while one was open for 0% of the time, Pallas kernels for 36%

profile of v7, /device:TPU:0, one launch (start us, length us, event | category | flops | bytes accessed | tf_op | source)
XLA Modules:
  0.0 35.3 jit_solution(14403092634545963883)
XLA Ops:
  0.6 3.1 %collective-permute-start = (bf16[1,32,512]{2,1,0:T(8,128)(2,1)}, bf16[1,32,512]{2,1,0:T(8,128)(2,1)S(1)}, u32[]{:S(2)}, u32[]{:S(2)}) collective-permute-start(bf16[1,32,512]{2,1,0:T(8,128)(2,1)} %param.8), channel_id=1, source_target_pairs={{0,4},{1,5},{2,6},{3,7},{4,0},{5,1},{6,2},{7,3},{8,12},{9,13},{10,... | collective-permute-start | bytes 98312 | tf_op jit(solution)/shard_map/ppermute | solution.py:238
  3.7 0.0 copy-start
  3.7 2.9 %sums.1 = (bf16[1024,256]{1,0:T(8,128)(2,1)S(1)}, f32[128,32,256]{2,1,0:T(8,128)S(1)}, bf16[8,512,256]{2,1,0:T(8,128)(2,1)S(1)}, bf16[128,32,256]{2,1,0:T(8,128)(2,1)S(1)}) custom-call(s32[16]{0:T(128)} %block_hbm.3, f32[1,128]{1,0:T(1,128)} %bitcast.18, f32[32,256]{1,0:T(8,128)} %noise_hbm.3, bf16[8,512,256]{2,1,0:T(8,128)(2,1)} %tiles_hbm.1, ...), custom_call_target="tpu_custom_call" | custom-call | bytes 10485760 | tf_op jit(solution)/shard_map/sums/pallas_call | solution.py:252
  6.6 0.0 collective-permute-done
  6.6 0.0 copy-done
  6.6 2.7 %collective-permute-start.1 = (bf16[2,32,512]{2,1,0:T(8,128)(2,1)S(1)}, bf16[2,32,512]{2,1,0:T(8,128)(2,1)S(1)}, u32[]{:S(2)}, u32[]{:S(2)}) collective-permute-start(bf16[2,32,512]{2,1,0:T(8,128)(2,1)S(1)} %pad_maximum_fusion.1), channel_id=1, source_target_pairs={{0,8},{1,9},{2,10},{3,11},{4,12},{5,13},{6,14},{7,15},{8,0},{9,1},... | collective-permute-start | bytes 196616 | tf_op jit(solution)/shard_map/ppermute | solution.py:238
  9.3 4.4 %insert.1 = (bf16[8,2,32,512]{3,2,1,0:T(8,128)(2,1)S(1)}, f32[4,2,32,512]{3,2,1,0:T(8,128)S(1)}, f32[4,2,32,512]{3,2,1,0:T(8,128)S(1)}) custom-call(s32[8,16]{1,0:T(8,128)} %bitcast.20, s32[8,16]{1,0:T(8,128)} %bitcast.22, bf16[1024,256]{1,0:T(8,128)(2,1)S(1)} %get-tuple-element.19.sums_ref, bf16[8,512,256]{2,1,0:T(8,128)(2,1)S(1)} %get-tuple-element.17.tiles_ref), custom_call_target="tpu_custom_call" | custom-call | flops 2147483648 | bytes 8388608 | tf_op jit(solution)/shard_map/insert/pallas_call | solution.py:252
  13.7 0.0 collective-permute-done.1
  13.8 0.1 collective-permute-start.3
  13.8 1.6 %collective-permute-start.2 = (bf16[4,32,512]{2,1,0:T(8,128)(2,1)S(1)}, bf16[4,32,512]{2,1,0:T(8,128)(2,1)S(1)}, u32[]{:S(2)}, u32[]{:S(2)}) collective-permute-start(bf16[4,32,512]{2,1,0:T(8,128)(2,1)S(1)} %pad_maximum_fusion.refs_0_), channel_id=1, source_target_pairs={{0,2},{1,3},{2,0},{3,1},{4,6},{5,7},{6,4},{7,5},{8,10},{9,11},{10,... | collective-permute-start | bytes 393224 | tf_op jit(solution)/shard_map/ppermute | solution.py:238
  15.4 0.3 collective-permute-done.3
  15.7 0.1 add_convert_fusion
  15.8 1.6 %collective-permute-start.6 = (bf16[4,2,32,512]{3,2,1,0:T(8,128)(2,1)S(1)}, bf16[4,2,32,512]{3,2,1,0:T(8,128)(2,1)S(1)}, u32[]{:S(2)}, u32[]{:S(2)}) collective-permute-start(bf16[4,2,32,512]{3,2,1,0:T(8,128)(2,1)S(1)} %add_convert_fusion), channel_id=1, source_target_pairs={{0,2},{1,3},{2,0},{3,1},{4,6},{5,7},{6,4},{7,5},{8,10},{9,11},{10,... | collective-permute-start | bytes 786440 | tf_op jit(solution)/shard_map/ppermute | solution.py:238
  17.4 0.0 collective-permute-start.4
  17.4 2.8 %collective-permute-done.2.refs_1_ = bf16[4,32,512]{2,1,0:T(8,128)(2,1)S(1)} collective-permute-done((bf16[4,32,512]{2,1,0:T(8,128)(2,1)S(1)}, bf16[4,32,512]{2,1,0:T(8,128)(2,1)S(1)}, u32[]{:S(2)}, u32[]{:S(2)}) %collective-permute-start.2) | collective-permute-done | bytes 131104 | tf_op jit(solution)/shard_map/ppermute | solution.py:238
  20.2 0.0 collective-permute-start.5
  20.2 0.0 collective-permute-done.4.refs_2_
  20.2 1.3 %collective-permute-done.5.refs_3_ = bf16[4,32,512]{2,1,0:T(8,128)(2,1)S(1)} collective-permute-done((bf16[4,32,512]{2,1,0:T(8,128)(2,1)S(1)}, bf16[4,32,512]{2,1,0:T(8,128)(2,1)S(1)}, u32[]{:S(2)}, u32[]{:S(2)}) %collective-permute-start.5) | collective-permute-done | bytes 131104 | tf_op jit(solution)/shard_map/ppermute | solution.py:238
  21.5 3.3 %project.1.proj_ref = f32[16,32,256]{2,1,0:T(8,128)S(1)} custom-call(s32[8,16]{1,0:T(8,128)} %bitcast.21, s32[8,16]{1,0:T(8,128)} %bitcast.23, bf16[8,512,256]{2,1,0:T(8,128)(2,1)S(1)} %get-tuple-element.17.tiles_ref, bf16[4,32,512]{2,1,0:T(8,128)(2,1)S(1)} %pad_maximum_fusion.refs_0_, bf16[4,32,512]{2,1,0:T(8,128)(2,1)S(1)} %collective-permute-done.2.refs_1_, ...), custom_call_target="tpu_custom_call" | custom-call | flops 1073741824 | bytes 8388608 | tf_op jit(solution)/shard_map/project/pallas_call | solution.py:252
  24.9 0.5 %collective-permute-done.6 = bf16[4,2,32,512]{3,2,1,0:T(8,128)(2,1)S(1)} collective-permute-done((bf16[4,2,32,512]{3,2,1,0:T(8,128)(2,1)S(1)}, bf16[4,2,32,512]{3,2,1,0:T(8,128)(2,1)S(1)}, u32[]{:S(2)}, u32[]{:S(2)}) %collective-permute-start.6) | collective-permute-done | bytes 262176 | tf_op jit(solution)/shard_map/ppermute | solution.py:238
  25.4 0.1 fusion.3
  25.5 2.1 %collective-permute-start.9 = (bf16[2,32,512]{2,1,0:T(8,128)(2,1)S(1)}, bf16[2,32,512]{2,1,0:T(8,128)(2,1)S(1)}, u32[]{:S(2)}, u32[]{:S(2)}) collective-permute-start(bf16[2,32,512]{2,1,0:T(8,128)(2,1)S(1)} %get-tuple-element.34), channel_id=1, source_target_pairs={{0,12},{1,13},{2,14},{3,15},{4,8},{5,9},{6,10},{7,11},{8,4},{9,5},... | collective-permute-start | bytes 196616 | tf_op jit(solution)/shard_map/ppermute | solution.py:238
  27.7 0.6 %collective-permute-start.8 = (bf16[2,32,512]{2,1,0:T(8,128)(2,1)S(1)}, bf16[2,32,512]{2,1,0:T(8,128)(2,1)S(1)}, u32[]{:S(2)}, u32[]{:S(2)}) collective-permute-start(bf16[2,32,512]{2,1,0:T(8,128)(2,1)S(1)} %get-tuple-element.35), channel_id=1, source_target_pairs={{0,8},{1,9},{2,10},{3,11},{4,12},{5,13},{6,14},{7,15},{8,0},{9,1},... | collective-permute-start | bytes 196616 | tf_op jit(solution)/shard_map/ppermute | solution.py:238
  28.3 1.7 %collective-permute-start.7 = (bf16[2,32,512]{2,1,0:T(8,128)(2,1)S(1)}, bf16[2,32,512]{2,1,0:T(8,128)(2,1)S(1)}, u32[]{:S(2)}, u32[]{:S(2)}) collective-permute-start(bf16[2,32,512]{2,1,0:T(8,128)(2,1)S(1)} %get-tuple-element.33), channel_id=1, source_target_pairs={{0,4},{1,5},{2,6},{3,7},{4,0},{5,1},{6,2},{7,3},{8,12},{9,13},{10,... | collective-permute-start | bytes 196616 | tf_op jit(solution)/shard_map/ppermute | solution.py:238
  30.0 2.2 %scores.1 = f32[1,128]{1,0:T(1,128)} custom-call(s32[16]{0:T(128)} %block_hbm.3, f32[32,256]{1,0:T(8,128)} %noise_hbm.3, f32[16,32,256]{2,1,0:T(8,128)S(1)} %project.1.proj_ref, f32[128,32,256]{2,1,0:T(8,128)S(1)} %get-tuple-element.28.wave_ref, bf16[128,32,256]{2,1,0:T(8,128)(2,1)S(1)} %get-tuple-element.29.images_ref), custom_call_target="tpu_custom_call" | custom-call | flops 1073741824 | bytes 8388608 | tf_op jit(solution)/shard_map/scores/pallas_call | solution.py:252
  32.2 0.0 collective-permute-done.9
  32.2 2.3 %collective-permute-done.8 = bf16[2,32,512]{2,1,0:T(8,128)(2,1)S(1)} collective-permute-done((bf16[2,32,512]{2,1,0:T(8,128)(2,1)S(1)}, bf16[2,32,512]{2,1,0:T(8,128)(2,1)S(1)}, u32[]{:S(2)}, u32[]{:S(2)}) %collective-permute-start.8) | collective-permute-done | bytes 65568 | tf_op jit(solution)/shard_map/ppermute | solution.py:238
  34.6 0.0 collective-permute-done.7
  34.6 0.7 %fusion.4 = (f32[1,32,512]{2,1,0:T(8,128)}, f32[1,32,512]{2,1,0:T(8,128)}) fusion(f32[2,32,512]{2,1,0:T(8,128)S(1)} %fusion.2), kind=kLoop, calls=%fused_computation.12 | loop fusion | bytes 262144 | tf_op jit(solution)/shard_map/slice | solution.py:346
  (4 shorter events, 0.1 us)
Async XLA Ops:
  0.6 6.0 %collective-permute-start = (bf16[1,32,512]{2,1,0:T(8,128)(2,1)}, bf16[1,32,512]{2,1,0:T(8,128)(2,1)S(1)}, u32[]{:S(2)}, u32[]{:S(2)}) collective-permute-start(bf16[1,32,512]{2,1,0:T(8,128)(2,1)} %param.8), channel_id=1, source_target_pairs={{0,4},{1,5},{2,6},{3,7},{4,0},{5,1},{6,2},{7,3},{8,12},{9,13},{10,... | collective-permute-start | bytes 98312 | tf_op jit(solution)/shard_map/ppermute | solution.py:238
  3.7 2.9 %copy-start = (bf16[1,32,512]{2,1,0:T(8,128)(2,1)S(1)}, bf16[1,32,512]{2,1,0:T(8,128)(2,1)}, u32[]{:S(2)}) copy-start(bf16[1,32,512]{2,1,0:T(8,128)(2,1)} %param.8) | copy-start | bytes 98308
  6.6 7.1 %collective-permute-start.1 = (bf16[2,32,512]{2,1,0:T(8,128)(2,1)S(1)}, bf16[2,32,512]{2,1,0:T(8,128)(2,1)S(1)}, u32[]{:S(2)}, u32[]{:S(2)}) collective-permute-start(bf16[2,32,512]{2,1,0:T(8,128)(2,1)S(1)} %pad_maximum_fusion.1), channel_id=1, source_target_pairs={{0,8},{1,9},{2,10},{3,11},{4,12},{5,13},{6,14},{7,15},{8,0},{9,1},... | collective-permute-start | bytes 196616 | tf_op jit(solution)/shard_map/ppermute | solution.py:238
  13.8 2.0 %collective-permute-start.3 = (bf16[8,2,32,512]{3,2,1,0:T(8,128)(2,1)S(1)}, bf16[8,2,32,512]{3,2,1,0:T(8,128)(2,1)S(1)}, u32[]{:S(2)}, u32[]{:S(2)}) collective-permute-start(bf16[8,2,32,512]{3,2,1,0:T(8,128)(2,1)S(1)} %get-tuple-element.24), channel_id=1, source_target_pairs={{0,1},{1,0},{2,3},{3,2},{4,5},{5,4},{6,7},{7,6},{8,9},{9,8},{10,11... | collective-permute-start | bytes 1572872 | tf_op jit(solution)/shard_map/ppermute | solution.py:238
  13.8 6.4 %collective-permute-start.2 = (bf16[4,32,512]{2,1,0:T(8,128)(2,1)S(1)}, bf16[4,32,512]{2,1,0:T(8,128)(2,1)S(1)}, u32[]{:S(2)}, u32[]{:S(2)}) collective-permute-start(bf16[4,32,512]{2,1,0:T(8,128)(2,1)S(1)} %pad_maximum_fusion.refs_0_), channel_id=1, source_target_pairs={{0,2},{1,3},{2,0},{3,1},{4,6},{5,7},{6,4},{7,5},{8,10},{9,11},{10,... | collective-permute-start | bytes 393224 | tf_op jit(solution)/shard_map/ppermute | solution.py:238
  15.8 9.6 %collective-permute-start.6 = (bf16[4,2,32,512]{3,2,1,0:T(8,128)(2,1)S(1)}, bf16[4,2,32,512]{3,2,1,0:T(8,128)(2,1)S(1)}, u32[]{:S(2)}, u32[]{:S(2)}) collective-permute-start(bf16[4,2,32,512]{3,2,1,0:T(8,128)(2,1)S(1)} %add_convert_fusion), channel_id=1, source_target_pairs={{0,2},{1,3},{2,0},{3,1},{4,6},{5,7},{6,4},{7,5},{8,10},{9,11},{10,... | collective-permute-start | bytes 786440 | tf_op jit(solution)/shard_map/ppermute | solution.py:238
  17.4 2.8 %collective-permute-start.4 = (bf16[4,32,512]{2,1,0:T(8,128)(2,1)S(1)}, bf16[4,32,512]{2,1,0:T(8,128)(2,1)S(1)}, u32[]{:S(2)}, u32[]{:S(2)}) collective-permute-start(bf16[4,32,512]{2,1,0:T(8,128)(2,1)S(1)} %pad_maximum_fusion.refs_0_), channel_id=1, source_target_pairs={{0,1},{1,0},{2,3},{3,2},{4,5},{5,4},{6,7},{7,6},{8,9},{9,8},{10,11... | collective-permute-start | bytes 393224 | tf_op jit(solution)/shard_map/ppermute | solution.py:238
  20.2 1.3 %collective-permute-start.5 = (bf16[4,32,512]{2,1,0:T(8,128)(2,1)S(1)}, bf16[4,32,512]{2,1,0:T(8,128)(2,1)S(1)}, u32[]{:S(2)}, u32[]{:S(2)}) collective-permute-start(bf16[4,32,512]{2,1,0:T(8,128)(2,1)S(1)} %collective-permute-done.2.refs_1_), channel_id=1, source_target_pairs={{0,1},{1,0},{2,3},{3,2},{4,5},{5,4},{6,7},{7,6},{8,9},{9,8},{10,11... | collective-permute-start | bytes 393224 | tf_op jit(solution)/shard_map/ppermute | solution.py:238
  25.5 6.7 %collective-permute-start.9 = (bf16[2,32,512]{2,1,0:T(8,128)(2,1)S(1)}, bf16[2,32,512]{2,1,0:T(8,128)(2,1)S(1)}, u32[]{:S(2)}, u32[]{:S(2)}) collective-permute-start(bf16[2,32,512]{2,1,0:T(8,128)(2,1)S(1)} %get-tuple-element.34), channel_id=1, source_target_pairs={{0,12},{1,13},{2,14},{3,15},{4,8},{5,9},{6,10},{7,11},{8,4},{9,5},... | collective-permute-start | bytes 196616 | tf_op jit(solution)/shard_map/ppermute | solution.py:238
  27.7 6.9 %collective-permute-start.8 = (bf16[2,32,512]{2,1,0:T(8,128)(2,1)S(1)}, bf16[2,32,512]{2,1,0:T(8,128)(2,1)S(1)}, u32[]{:S(2)}, u32[]{:S(2)}) collective-permute-start(bf16[2,32,512]{2,1,0:T(8,128)(2,1)S(1)} %get-tuple-element.35), channel_id=1, source_target_pairs={{0,8},{1,9},{2,10},{3,11},{4,12},{5,13},{6,14},{7,15},{8,0},{9,1},... | collective-permute-start | bytes 196616 | tf_op jit(solution)/shard_map/ppermute | solution.py:238
  28.3 6.3 %collective-permute-start.7 = (bf16[2,32,512]{2,1,0:T(8,128)(2,1)S(1)}, bf16[2,32,512]{2,1,0:T(8,128)(2,1)S(1)}, u32[]{:S(2)}, u32[]{:S(2)}) collective-permute-start(bf16[2,32,512]{2,1,0:T(8,128)(2,1)S(1)} %get-tuple-element.33), channel_id=1, source_target_pairs={{0,4},{1,5},{2,6},{3,7},{4,0},{5,1},{6,2},{7,3},{8,12},{9,13},{10,... | collective-permute-start | bytes 196616 | tf_op jit(solution)/shard_map/ppermute | solution.py:238

commit v8 on v7

--- a/solution.py
+++ b/solution.py
@@ -105,14 +105,14 @@
 
 
 def insert_kernel(shape, slab_hbm, tile_hbm, sums_ref, tiles_ref, send_ref, far_ref, near_ref,
-                  slab_ref, tile_ref, parts_ref, place_ref, sems):
+                  slab_ref, tile_ref, parts_ref, place_ref, count_ref, sems):
     far, wide, cores = shape
     started = copies([(slab_hbm, slab_ref), (tile_hbm, tile_ref)], sems)
     crossed, blocks = slab_ref.shape
     kinds = tiles_ref.shape[0]
     rows = sums_ref.shape[0]
     height = rows // (2 * blocks)
-    devices = place_ref.shape[0] // blocks
+    devices = count_ref.shape[0]
 
     def multiply(t):
         parts_ref[t * rows : (t + 1) * rows, :] = lax.dot_general(
@@ -125,34 +125,44 @@
 
     for copy in started:
         copy.wait()
-
-    def clear(n, carry):
-        for m in range(blocks):
-            place_ref[n * blocks + m] = kinds * rows
+    stride = blocks + 1
+
+    def clear(s, carry):
+        count_ref[s] = 0
+        return carry
+
+    def close(s, carry):
+        place_ref[s * stride + count_ref[s]] = kinds * rows
         return carry
 
     lax.fori_loop(0, devices, clear, 0, unroll=devices <= 16)
     for k in range(blocks):
         for r in range(crossed):
-            place_ref[slab_ref[r, k] * blocks + k] = tile_ref[r, k] * rows + k * 2 * height
+            s = slab_ref[r, k]
+            at = count_ref[s]
+            place_ref[s * stride + at] = tile_ref[r, k] * rows + k * 2 * height
+            count_ref[s] = at + 1
+    lax.fori_loop(0, devices, close, 0, unroll=devices <= 16)
     for t in range(kinds // 2, kinds):
         multiply(t)
     me = lax.axis_index("slab")
 
-    def total(x, z, core, kind):
+    def total(x, z, core):
         s = me ^ ((z * wide + x) * cores + core)
-        acc = None
-        for k in range(blocks):
-            at = pl.multiple_of(place_ref[s * blocks + k] + kind * height, height)
-            part = parts_ref[pl.ds(at, height), :]
-            acc = part if acc is None else acc + part
-        return acc
+
+        def rows_of(n):
+            return parts_ref[pl.ds(pl.multiple_of(place_ref[s * stride + n], 2 * height), 2 * height), :]
+
+        def add_two(n, acc):
+            return acc + rows_of(2 * n) + rows_of(2 * n + 1)
+
+        zero = jnp.zeros((2 * height, parts_ref.shape[1]), jnp.float32)
+        return lax.fori_loop(0, (count_ref[s] + 1) >> 1, add_two, zero)
 
     def fill(ref, start, core):
         def step(slot, carry):
             x, z = start + slot // far, lax.rem(slot, far)
-            for kind in range(2):
-                ref[slot, kind] = total(x, z, core, kind).astype(ref.dtype)
+            ref[slot] = total(x, z, core).astype(ref.dtype).reshape(2, height, parts_ref.shape[1])
             return carry
 
         lax.fori_loop(0, ref.shape[0], step, 0)
@@ -172,7 +182,10 @@
     _, height, length = columns[0].shape
     dense = far * len(columns) * kinds <= crossed * blocks
     for n, ref in enumerate(columns):
-        lines_ref[n * far * height : (n + 1) * far * height, :] = ref[...].reshape(far * height, length)
+        core, x = n // wide, n % wide
+        for z in range(far):
+            away = (z * wide + x) * cores + core
+            lines_ref[away * height : (away + 1) * height, :] = ref[z]
     if dense:
         for t in range(kinds):
             flat_ref[t] = jnp.dot(lines_ref[...], tiles_ref[t], preferred_element_type=jnp.float32)
@@ -180,16 +193,11 @@
         copy.wait()
     me = lax.axis_index("slab")
 
-    def slot_of(s):
-        away = me ^ s
-        core, x, z = away & (cores - 1), (away // cores) & (wide - 1), away // (cores * wide)
-        return (core * wide + x) * far + z
-
     def project(k, carry):
         acc = None
         for r in range(crossed):
             t = tile_ref[r, k]
-            rows = pl.ds(pl.multiple_of(slot_of(slab_ref[r, k]) * height, height), height)
+            rows = pl.ds(pl.multiple_of((me ^ slab_ref[r, k]) * height, height), height)
             if dense:
                 part = flat_ref[t, rows, :]
             else:
@@ -297,7 +305,8 @@
         [
             *pairs_scratch,
             pltpu.VMEM((kinds * rows + 2 * height, length), f32),
-            pltpu.SMEM((devices * blocks,), jnp.int32),
+            pltpu.SMEM((devices * (blocks + 1),), jnp.int32),
+            pltpu.SMEM((devices,), jnp.int32),
             pltpu.SemaphoreType.DMA((2,)),
         ],
         2 * rows * pixels * kinds * length,

time: 35.5 us -> 35.8 us (level)
  waiting for transfers between devices: 7.37 us -> 8.38 us
  Pallas kernels: 12.8 us -> 12.1 us
    ppermute x10, waiting for transfers between devices: 7.37 us -> 8.38 us  [swap(): lax.ppermute(array, 'slab', [(i, i ^ offset) for i in range(devices)])]
    pallas_call x4, Pallas kernels: 12.8 us -> 12.1 us  [call(): pl.pallas_call(kernel, out_shape=tuple((jax.ShapeDtypeStruct(s, t) for s,...]
  transfers between devices with their start and end apart: 10 -> 10, of which waited for: 5 -> 5; matrix products, arithmetic and copies ran while one was open for 0% -> 0% of each run, Pallas kernels for 36% -> 34%
where the time goes in v8:
time: 35.8 us; the launch traced here: 35.6 us
  starting transfers between devices  13.4 us (37%)
  Pallas kernels  12.1 us (34%)
  waiting for transfers between devices  8.38 us (23%)
  between operations  0.75 us (2%)
  local copies, waits for them, and re-layouts  0.68 us (2%)
    ppermute x10, starting transfers between devices, swap(): lax.ppermute(array, 'slab', [(i, i ^ offset) for i in range(devices)])  13.4 us
    pallas_call x4, Pallas kernels, call(): pl.pallas_call(kernel, out_shape=tuple((jax.ShapeDtypeStruct(s, t) for s,...  12.1 us
    ppermute x10, waiting for transfers between devices, swap(): lax.ppermute(array, 'slab', [(i, i ^ offset) for i in range(devices)])  8.38 us
  transfers between devices with their start and end apart: 10, of which 5 were waited for; matrix products, arithmetic and copies ran while one was open for 0% of the time, Pallas kernels for 34%

profile of v8, /device:TPU:0, one launch (start us, length us, event | category | flops | bytes accessed | tf_op | source)
XLA Modules:
  0.0 35.6 jit_solution(1398581159978462896)
XLA Ops:
  0.6 3.1 %collective-permute-start = (bf16[1,32,512]{2,1,0:T(8,128)(2,1)}, bf16[1,32,512]{2,1,0:T(8,128)(2,1)S(1)}, u32[]{:S(2)}, u32[]{:S(2)}) collective-permute-start(bf16[1,32,512]{2,1,0:T(8,128)(2,1)} %param.8), channel_id=1, source_target_pairs={{0,4},{1,5},{2,6},{3,7},{4,0},{5,1},{6,2},{7,3},{8,12},{9,13},{10,... | collective-permute-start | bytes 98312 | tf_op jit(solution)/shard_map/ppermute | solution.py:246
  3.7 0.0 copy-start
  3.7 2.9 %sums.1 = (bf16[1024,256]{1,0:T(8,128)(2,1)S(1)}, f32[128,32,256]{2,1,0:T(8,128)S(1)}, bf16[8,512,256]{2,1,0:T(8,128)(2,1)S(1)}, bf16[128,32,256]{2,1,0:T(8,128)(2,1)S(1)}) custom-call(s32[16]{0:T(128)} %block_hbm.3, f32[1,128]{1,0:T(1,128)} %bitcast.18, f32[32,256]{1,0:T(8,128)} %noise_hbm.3, bf16[8,512,256]{2,1,0:T(8,128)(2,1)} %tiles_hbm.1, ...), custom_call_target="tpu_custom_call" | custom-call | bytes 10485760 | tf_op jit(solution)/shard_map/sums/pallas_call | solution.py:260
  6.6 0.0 collective-permute-done
  6.6 0.0 copy-done
  6.6 2.7 %collective-permute-start.1 = (bf16[2,32,512]{2,1,0:T(8,128)(2,1)S(1)}, bf16[2,32,512]{2,1,0:T(8,128)(2,1)S(1)}, u32[]{:S(2)}, u32[]{:S(2)}) collective-permute-start(bf16[2,32,512]{2,1,0:T(8,128)(2,1)S(1)} %pad_maximum_fusion.1), channel_id=1, source_target_pairs={{0,8},{1,9},{2,10},{3,11},{4,12},{5,13},{6,14},{7,15},{8,0},{9,1},... | collective-permute-start | bytes 196616 | tf_op jit(solution)/shard_map/ppermute | solution.py:246
  9.3 4.7 %insert.1 = (bf16[8,2,32,512]{3,2,1,0:T(8,128)(2,1)S(1)}, f32[4,2,32,512]{3,2,1,0:T(8,128)S(1)}, f32[4,2,32,512]{3,2,1,0:T(8,128)S(1)}) custom-call(s32[8,16]{1,0:T(8,128)} %bitcast.20, s32[8,16]{1,0:T(8,128)} %bitcast.22, bf16[1024,256]{1,0:T(8,128)(2,1)S(1)} %get-tuple-element.19.sums_ref, bf16[8,512,256]{2,1,0:T(8,128)(2,1)S(1)} %get-tuple-element.17.tiles_ref), custom_call_target="tpu_custom_call" | custom-call | flops 2147483648 | bytes 8388608 | tf_op jit(solution)/shard_map/insert/pallas_call | solution.py:260
  14.0 0.0 collective-permute-done.1
  14.1 0.1 collective-permute-start.3
  14.1 1.6 %collective-permute-start.2 = (bf16[4,32,512]{2,1,0:T(8,128)(2,1)S(1)}, bf16[4,32,512]{2,1,0:T(8,128)(2,1)S(1)}, u32[]{:S(2)}, u32[]{:S(2)}) collective-permute-start(bf16[4,32,512]{2,1,0:T(8,128)(2,1)S(1)} %pad_maximum_fusion.refs_0_), channel_id=1, source_target_pairs={{0,2},{1,3},{2,0},{3,1},{4,6},{5,7},{6,4},{7,5},{8,10},{9,11},{10,... | collective-permute-start | bytes 393224 | tf_op jit(solution)/shard_map/ppermute | solution.py:246
  15.7 0.3 collective-permute-done.3
  16.0 0.1 add_convert_fusion
  16.1 1.6 %collective-permute-start.6 = (bf16[4,2,32,512]{3,2,1,0:T(8,128)(2,1)S(1)}, bf16[4,2,32,512]{3,2,1,0:T(8,128)(2,1)S(1)}, u32[]{:S(2)}, u32[]{:S(2)}) collective-permute-start(bf16[4,2,32,512]{3,2,1,0:T(8,128)(2,1)S(1)} %add_convert_fusion), channel_id=1, source_target_pairs={{0,2},{1,3},{2,0},{3,1},{4,6},{5,7},{6,4},{7,5},{8,10},{9,11},{10,... | collective-permute-start | bytes 786440 | tf_op jit(solution)/shard_map/ppermute | solution.py:246
  17.7 0.0 collective-permute-start.4
  17.7 2.8 %collective-permute-done.2.refs_1_ = bf16[4,32,512]{2,1,0:T(8,128)(2,1)S(1)} collective-permute-done((bf16[4,32,512]{2,1,0:T(8,128)(2,1)S(1)}, bf16[4,32,512]{2,1,0:T(8,128)(2,1)S(1)}, u32[]{:S(2)}, u32[]{:S(2)}) %collective-permute-start.2) | collective-permute-done | bytes 131104 | tf_op jit(solution)/shard_map/ppermute | solution.py:246
  20.5 0.0 collective-permute-start.5
  20.5 0.0 collective-permute-done.4.refs_2_
  20.5 1.3 %collective-permute-done.5.refs_3_ = bf16[4,32,512]{2,1,0:T(8,128)(2,1)S(1)} collective-permute-done((bf16[4,32,512]{2,1,0:T(8,128)(2,1)S(1)}, bf16[4,32,512]{2,1,0:T(8,128)(2,1)S(1)}, u32[]{:S(2)}, u32[]{:S(2)}) %collective-permute-start.5) | collective-permute-done | bytes 131104 | tf_op jit(solution)/shard_map/ppermute | solution.py:246
  21.9 2.3 %project.1.proj_ref = f32[16,32,256]{2,1,0:T(8,128)S(1)} custom-call(s32[8,16]{1,0:T(8,128)} %bitcast.21, s32[8,16]{1,0:T(8,128)} %bitcast.23, bf16[8,512,256]{2,1,0:T(8,128)(2,1)S(1)} %get-tuple-element.17.tiles_ref, bf16[4,32,512]{2,1,0:T(8,128)(2,1)S(1)} %pad_maximum_fusion.refs_0_, bf16[4,32,512]{2,1,0:T(8,128)(2,1)S(1)} %collective-permute-done.2.refs_1_, ...), custom_call_target="tpu_custom_call" | custom-call | flops 1073741824 | bytes 8388608 | tf_op jit(solution)/shard_map/project/pallas_call | solution.py:260
  24.1 1.6 %collective-permute-done.6 = bf16[4,2,32,512]{3,2,1,0:T(8,128)(2,1)S(1)} collective-permute-done((bf16[4,2,32,512]{3,2,1,0:T(8,128)(2,1)S(1)}, bf16[4,2,32,512]{3,2,1,0:T(8,128)(2,1)S(1)}, u32[]{:S(2)}, u32[]{:S(2)}) %collective-permute-start.6) | collective-permute-done | bytes 262176 | tf_op jit(solution)/shard_map/ppermute | solution.py:246
  25.7 0.1 fusion.3
  25.8 1.8 %collective-permute-start.9 = (bf16[2,32,512]{2,1,0:T(8,128)(2,1)S(1)}, bf16[2,32,512]{2,1,0:T(8,128)(2,1)S(1)}, u32[]{:S(2)}, u32[]{:S(2)}) collective-permute-start(bf16[2,32,512]{2,1,0:T(8,128)(2,1)S(1)} %get-tuple-element.34), channel_id=1, source_target_pairs={{0,12},{1,13},{2,14},{3,15},{4,8},{5,9},{6,10},{7,11},{8,4},{9,5},... | collective-permute-start | bytes 196616 | tf_op jit(solution)/shard_map/ppermute | solution.py:246
  27.7 0.9 %collective-permute-start.8 = (bf16[2,32,512]{2,1,0:T(8,128)(2,1)S(1)}, bf16[2,32,512]{2,1,0:T(8,128)(2,1)S(1)}, u32[]{:S(2)}, u32[]{:S(2)}) collective-permute-start(bf16[2,32,512]{2,1,0:T(8,128)(2,1)S(1)} %get-tuple-element.35), channel_id=1, source_target_pairs={{0,8},{1,9},{2,10},{3,11},{4,12},{5,13},{6,14},{7,15},{8,0},{9,1},... | collective-permute-start | bytes 196616 | tf_op jit(solution)/shard_map/ppermute | solution.py:246
  28.6 1.7 %collective-permute-start.7 = (bf16[2,32,512]{2,1,0:T(8,128)(2,1)S(1)}, bf16[2,32,512]{2,1,0:T(8,128)(2,1)S(1)}, u32[]{:S(2)}, u32[]{:S(2)}) collective-permute-start(bf16[2,32,512]{2,1,0:T(8,128)(2,1)S(1)} %get-tuple-element.33), channel_id=1, source_target_pairs={{0,4},{1,5},{2,6},{3,7},{4,0},{5,1},{6,2},{7,3},{8,12},{9,13},{10,... | collective-permute-start | bytes 196616 | tf_op jit(solution)/shard_map/ppermute | solution.py:246
  30.3 2.2 %scores.1 = f32[1,128]{1,0:T(1,128)} custom-call(s32[16]{0:T(128)} %block_hbm.3, f32[32,256]{1,0:T(8,128)} %noise_hbm.3, f32[16,32,256]{2,1,0:T(8,128)S(1)} %project.1.proj_ref, f32[128,32,256]{2,1,0:T(8,128)S(1)} %get-tuple-element.28.wave_ref, bf16[128,32,256]{2,1,0:T(8,128)(2,1)S(1)} %get-tuple-element.29.images_ref), custom_call_target="tpu_custom_call" | custom-call | flops 1073741824 | bytes 8388608 | tf_op jit(solution)/shard_map/scores/pallas_call | solution.py:260
  32.5 0.0 collective-permute-done.9
  32.5 2.3 %collective-permute-done.8 = bf16[2,32,512]{2,1,0:T(8,128)(2,1)S(1)} collective-permute-done((bf16[2,32,512]{2,1,0:T(8,128)(2,1)S(1)}, bf16[2,32,512]{2,1,0:T(8,128)(2,1)S(1)}, u32[]{:S(2)}, u32[]{:S(2)}) %collective-permute-start.8) | collective-permute-done | bytes 65568 | tf_op jit(solution)/shard_map/ppermute | solution.py:246
  34.9 0.0 collective-permute-done.7
  34.9 0.7 %fusion.4 = (f32[1,32,512]{2,1,0:T(8,128)}, f32[1,32,512]{2,1,0:T(8,128)}) fusion(f32[2,32,512]{2,1,0:T(8,128)S(1)} %fusion.2), kind=kLoop, calls=%fused_computation.12 | loop fusion | bytes 262144 | tf_op jit(solution)/shard_map/slice | solution.py:355
  (4 shorter events, 0.1 us)
Async XLA Ops:
  0.6 6.0 %collective-permute-start = (bf16[1,32,512]{2,1,0:T(8,128)(2,1)}, bf16[1,32,512]{2,1,0:T(8,128)(2,1)S(1)}, u32[]{:S(2)}, u32[]{:S(2)}) collective-permute-start(bf16[1,32,512]{2,1,0:T(8,128)(2,1)} %param.8), channel_id=1, source_target_pairs={{0,4},{1,5},{2,6},{3,7},{4,0},{5,1},{6,2},{7,3},{8,12},{9,13},{10,... | collective-permute-start | bytes 98312 | tf_op jit(solution)/shard_map/ppermute | solution.py:246
  3.7 2.9 %copy-start = (bf16[1,32,512]{2,1,0:T(8,128)(2,1)S(1)}, bf16[1,32,512]{2,1,0:T(8,128)(2,1)}, u32[]{:S(2)}) copy-start(bf16[1,32,512]{2,1,0:T(8,128)(2,1)} %param.8) | copy-start | bytes 98308
  6.6 7.4 %collective-permute-start.1 = (bf16[2,32,512]{2,1,0:T(8,128)(2,1)S(1)}, bf16[2,32,512]{2,1,0:T(8,128)(2,1)S(1)}, u32[]{:S(2)}, u32[]{:S(2)}) collective-permute-start(bf16[2,32,512]{2,1,0:T(8,128)(2,1)S(1)} %pad_maximum_fusion.1), channel_id=1, source_target_pairs={{0,8},{1,9},{2,10},{3,11},{4,12},{5,13},{6,14},{7,15},{8,0},{9,1},... | collective-permute-start | bytes 196616 | tf_op jit(solution)/shard_map/ppermute | solution.py:246
  14.1 2.0 %collective-permute-start.3 = (bf16[8,2,32,512]{3,2,1,0:T(8,128)(2,1)S(1)}, bf16[8,2,32,512]{3,2,1,0:T(8,128)(2,1)S(1)}, u32[]{:S(2)}, u32[]{:S(2)}) collective-permute-start(bf16[8,2,32,512]{3,2,1,0:T(8,128)(2,1)S(1)} %get-tuple-element.24), channel_id=1, source_target_pairs={{0,1},{1,0},{2,3},{3,2},{4,5},{5,4},{6,7},{7,6},{8,9},{9,8},{10,11... | collective-permute-start | bytes 1572872 | tf_op jit(solution)/shard_map/ppermute | solution.py:246
  14.1 6.4 %collective-permute-start.2 = (bf16[4,32,512]{2,1,0:T(8,128)(2,1)S(1)}, bf16[4,32,512]{2,1,0:T(8,128)(2,1)S(1)}, u32[]{:S(2)}, u32[]{:S(2)}) collective-permute-start(bf16[4,32,512]{2,1,0:T(8,128)(2,1)S(1)} %pad_maximum_fusion.refs_0_), channel_id=1, source_target_pairs={{0,2},{1,3},{2,0},{3,1},{4,6},{5,7},{6,4},{7,5},{8,10},{9,11},{10,... | collective-permute-start | bytes 393224 | tf_op jit(solution)/shard_map/ppermute | solution.py:246
  16.1 9.6 %collective-permute-start.6 = (bf16[4,2,32,512]{3,2,1,0:T(8,128)(2,1)S(1)}, bf16[4,2,32,512]{3,2,1,0:T(8,128)(2,1)S(1)}, u32[]{:S(2)}, u32[]{:S(2)}) collective-permute-start(bf16[4,2,32,512]{3,2,1,0:T(8,128)(2,1)S(1)} %add_convert_fusion), channel_id=1, source_target_pairs={{0,2},{1,3},{2,0},{3,1},{4,6},{5,7},{6,4},{7,5},{8,10},{9,11},{10,... | collective-permute-start | bytes 786440 | tf_op jit(solution)/shard_map/ppermute | solution.py:246
  17.7 2.8 %collective-permute-start.4 = (bf16[4,32,512]{2,1,0:T(8,128)(2,1)S(1)}, bf16[4,32,512]{2,1,0:T(8,128)(2,1)S(1)}, u32[]{:S(2)}, u32[]{:S(2)}) collective-permute-start(bf16[4,32,512]{2,1,0:T(8,128)(2,1)S(1)} %pad_maximum_fusion.refs_0_), channel_id=1, source_target_pairs={{0,1},{1,0},{2,3},{3,2},{4,5},{5,4},{6,7},{7,6},{8,9},{9,8},{10,11... | collective-permute-start | bytes 393224 | tf_op jit(solution)/shard_map/ppermute | solution.py:246
  20.5 1.3 %collective-permute-start.5 = (bf16[4,32,512]{2,1,0:T(8,128)(2,1)S(1)}, bf16[4,32,512]{2,1,0:T(8,128)(2,1)S(1)}, u32[]{:S(2)}, u32[]{:S(2)}) collective-permute-start(bf16[4,32,512]{2,1,0:T(8,128)(2,1)S(1)} %collective-permute-done.2.refs_1_), channel_id=1, source_target_pairs={{0,1},{1,0},{2,3},{3,2},{4,5},{5,4},{6,7},{7,6},{8,9},{9,8},{10,11... | collective-permute-start | bytes 393224 | tf_op jit(solution)/shard_map/ppermute | solution.py:246
  25.8 6.7 %collective-permute-start.9 = (bf16[2,32,512]{2,1,0:T(8,128)(2,1)S(1)}, bf16[2,32,512]{2,1,0:T(8,128)(2,1)S(1)}, u32[]{:S(2)}, u32[]{:S(2)}) collective-permute-start(bf16[2,32,512]{2,1,0:T(8,128)(2,1)S(1)} %get-tuple-element.34), channel_id=1, source_target_pairs={{0,12},{1,13},{2,14},{3,15},{4,8},{5,9},{6,10},{7,11},{8,4},{9,5},... | collective-permute-start | bytes 196616 | tf_op jit(solution)/shard_map/ppermute | solution.py:246
  27.7 7.2 %collective-permute-start.8 = (bf16[2,32,512]{2,1,0:T(8,128)(2,1)S(1)}, bf16[2,32,512]{2,1,0:T(8,128)(2,1)S(1)}, u32[]{:S(2)}, u32[]{:S(2)}) collective-permute-start(bf16[2,32,512]{2,1,0:T(8,128)(2,1)S(1)} %get-tuple-element.35), channel_id=1, source_target_pairs={{0,8},{1,9},{2,10},{3,11},{4,12},{5,13},{6,14},{7,15},{8,0},{9,1},... | collective-permute-start | bytes 196616 | tf_op jit(solution)/shard_map/ppermute | solution.py:246
  28.6 6.3 %collective-permute-start.7 = (bf16[2,32,512]{2,1,0:T(8,128)(2,1)S(1)}, bf16[2,32,512]{2,1,0:T(8,128)(2,1)S(1)}, u32[]{:S(2)}, u32[]{:S(2)}) collective-permute-start(bf16[2,32,512]{2,1,0:T(8,128)(2,1)S(1)} %get-tuple-element.33), channel_id=1, source_target_pairs={{0,4},{1,5},{2,6},{3,7},{4,0},{5,1},{6,2},{7,3},{8,12},{9,13},{10,... | collective-permute-start | bytes 196616 | tf_op jit(solution)/shard_map/ppermute | solution.py:246

commit v9 on v8

--- a/solution.py
+++ b/solution.py
@@ -67,12 +67,30 @@
     return started
 
 
-def sum_kernel(block_hbm, defocus_hbm, noise_hbm, tiles_hbm, images_hbm,
-               sums_ref, wave_ref, tiles_ref, images_ref,
-               block_ref, defocus_ref, noise_ref, line_ref, pixel_ref, acc_ref, sems):
+def row_tables(shape, kinds, height, slab, tile, place_ref, route_ref):
+    far, wide, cores = shape
+    devices, blocks = place_ref.shape
+    rows, half = blocks * 2 * height, devices // 2
+    me = lax.axis_index("slab")
+    slot = lax.broadcasted_iota(jnp.int32, (devices, blocks), 0)
+    block = lax.broadcasted_iota(jnp.int32, (devices, blocks), 1)
+    within = slot & (half - 1)
+    core = jnp.where(slot < half, cores - 1, 0)
+    named = me ^ (((within & (far - 1)) * wide + within // far) * cores + core)
+    place = jnp.full((devices, blocks), kinds * rows, jnp.int32)
+    for r in range(slab.shape[0]):
+        row = tile[r : r + 1, :] * rows + block * (2 * height)
+        place = jnp.where(slab[r : r + 1, :] == named, row, place)
+    place_ref[...] = place
+    route_ref[...] = (tile * devices + (me ^ slab)) * height
+
+
+def sum_kernel(shape, kinds, slab_hbm, tile_hbm, block_hbm, defocus_hbm, noise_hbm, tiles_hbm, images_hbm,
+               sums_ref, wave_ref, tiles_ref, images_ref, place_ref, route_ref,
+               slab_ref, tile_ref, block_ref, defocus_ref, noise_ref, line_ref, pixel_ref, acc_ref, sems):
     count = images_ref.shape[0]
     part = count // CHUNKS
-    small = [(defocus_hbm, defocus_ref), (block_hbm, block_ref), (noise_hbm, noise_ref)]
+    small = [(defocus_hbm, defocus_ref), (block_hbm, block_ref), (noise_hbm, noise_ref), (slab_hbm, slab_ref), (tile_hbm, tile_ref)]
     large = [(images_hbm.at[pl.ds(n * part, part)], images_ref.at[pl.ds(n * part, part)]) for n in range(CHUNKS)]
     started = copies(small + large, sems)
     last = pltpu.make_async_copy(tiles_hbm, tiles_ref, sems.at[len(started)])
@@ -83,6 +101,7 @@
     for copy in started[: len(small)]:
         copy.wait()
     tables(defocus_ref, height, pixels, line_ref, pixel_ref)
+    row_tables(shape, kinds, height, slab_ref[...], tile_ref[...], place_ref, route_ref)
     for b in range(batches):
         if b % (batches // CHUNKS) == 0:
             started[len(small) + b // (batches // CHUNKS)].wait()
@@ -104,82 +123,48 @@
     last.wait()
 
 
-def insert_kernel(shape, slab_hbm, tile_hbm, sums_ref, tiles_ref, send_ref, far_ref, near_ref,
-                  slab_ref, tile_ref, parts_ref, place_ref, count_ref, sems):
+def insert_kernel(shape, place_vmem, sums_ref, tiles_ref, send_ref, far_ref, near_ref, parts_ref, place_ref, sems):
     far, wide, cores = shape
-    started = copies([(slab_hbm, slab_ref), (tile_hbm, tile_ref)], sems)
-    crossed, blocks = slab_ref.shape
+    (started,) = copies([(place_vmem, place_ref)], sems)
+    devices, blocks = place_ref.shape
     kinds = tiles_ref.shape[0]
     rows = sums_ref.shape[0]
+    length = parts_ref.shape[1]
     height = rows // (2 * blocks)
-    devices = count_ref.shape[0]
-
-    def multiply(t):
+    half = devices // 2
+    parts_ref[pl.ds(kinds * rows, 2 * height), :] = jnp.zeros((2 * height, length), jnp.float32)
+    for t in range(kinds):
         parts_ref[t * rows : (t + 1) * rows, :] = lax.dot_general(
             sums_ref[...], tiles_ref[t], (((1,), (1,)), ((), ())), preferred_element_type=jnp.float32
         )
-
-    parts_ref[pl.ds(kinds * rows, 2 * height), :] = jnp.zeros((2 * height, parts_ref.shape[1]), jnp.float32)
-    for t in range(kinds // 2):
-        multiply(t)
-
-    for copy in started:
-        copy.wait()
-    stride = blocks + 1
-
-    def clear(s, carry):
-        count_ref[s] = 0
-        return carry
-
-    def close(s, carry):
-        place_ref[s * stride + count_ref[s]] = kinds * rows
-        return carry
-
-    lax.fori_loop(0, devices, clear, 0, unroll=devices <= 16)
-    for k in range(blocks):
-        for r in range(crossed):
-            s = slab_ref[r, k]
-            at = count_ref[s]
-            place_ref[s * stride + at] = tile_ref[r, k] * rows + k * 2 * height
-            count_ref[s] = at + 1
-    lax.fori_loop(0, devices, close, 0, unroll=devices <= 16)
-    for t in range(kinds // 2, kinds):
-        multiply(t)
-    me = lax.axis_index("slab")
-
-    def total(x, z, core):
-        s = me ^ ((z * wide + x) * cores + core)
-
-        def rows_of(n):
-            return parts_ref[pl.ds(pl.multiple_of(place_ref[s * stride + n], 2 * height), 2 * height), :]
-
-        def add_two(n, acc):
-            return acc + rows_of(2 * n) + rows_of(2 * n + 1)
-
-        zero = jnp.zeros((2 * height, parts_ref.shape[1]), jnp.float32)
-        return lax.fori_loop(0, (count_ref[s] + 1) >> 1, add_two, zero)
-
-    def fill(ref, start, core):
+    started.wait()
+
+    def fill(ref, start):
         def step(slot, carry):
-            x, z = start + slot // far, lax.rem(slot, far)
-            ref[slot] = total(x, z, core).astype(ref.dtype).reshape(2, height, parts_ref.shape[1])
+            acc = None
+            for k in range(blocks):
+                at = pl.multiple_of(place_ref[start + slot, k], 2 * height)
+                part = parts_ref[pl.ds(at, 2 * height), :]
+                acc = part if acc is None else acc + part
+            ref[slot] = acc.astype(ref.dtype).reshape(2, height, length)
             return carry
 
         lax.fori_loop(0, ref.shape[0], step, 0)
 
-    fill(send_ref, 0, 1)
-    fill(far_ref, 1, 0)
-    fill(near_ref, 0, 0)
-
-
-def project_kernel(shape, slab_hbm, tile_hbm, tiles_ref, *refs):
+    fill(send_ref, 0)
+    fill(far_ref, half + far)
+    fill(near_ref, half)
+
+
+def project_kernel(shape, route_vmem, tiles_ref, *refs):
     far, wide, cores = shape
     columns, refs = refs[: wide * cores], refs[wide * cores :]
-    proj_ref, slab_ref, tile_ref, lines_ref, flat_ref, sems = refs
-    started = copies([(slab_hbm, slab_ref), (tile_hbm, tile_ref)], sems)
-    crossed, blocks = slab_ref.shape
+    proj_ref, route_ref, lines_ref, flat_ref, sems = refs
+    (started,) = copies([(route_vmem, route_ref)], sems)
+    crossed, blocks = route_ref.shape
     kinds = tiles_ref.shape[0]
-    _, height, length = columns[0].shape
+    height = columns[0].shape[1]
+    rows = lines_ref.shape[0]
     dense = far * len(columns) * kinds <= crossed * blocks
     for n, ref in enumerate(columns):
         core, x = n // wide, n % wide
@@ -188,20 +173,18 @@
             lines_ref[away * height : (away + 1) * height, :] = ref[z]
     if dense:
         for t in range(kinds):
-            flat_ref[t] = jnp.dot(lines_ref[...], tiles_ref[t], preferred_element_type=jnp.float32)
-    for copy in started:
-        copy.wait()
-    me = lax.axis_index("slab")
+            flat_ref[t * rows : (t + 1) * rows, :] = jnp.dot(lines_ref[...], tiles_ref[t], preferred_element_type=jnp.float32)
+    started.wait()
 
     def project(k, carry):
         acc = None
         for r in range(crossed):
-            t = tile_ref[r, k]
-            rows = pl.ds(pl.multiple_of((me ^ slab_ref[r, k]) * height, height), height)
+            at = route_ref[r, k]
             if dense:
-                part = flat_ref[t, rows, :]
+                part = flat_ref[pl.ds(pl.multiple_of(at, height), height), :]
             else:
-                part = jnp.dot(lines_ref[rows, :], tiles_ref[t], preferred_element_type=jnp.float32)
+                t, at = at // rows, pl.multiple_of(lax.rem(at, rows), height)
+                part = jnp.dot(lines_ref[pl.ds(at, height), :], tiles_ref[t], preferred_element_type=jnp.float32)
             acc = part if acc is None else acc + part
         proj_ref[k] = acc
         return carry
@@ -249,7 +232,7 @@
     hbm = pl.BlockSpec(memory_space=pltpu.HBM)
     params = pltpu.CompilerParams(vmem_limit_bytes=VMEM_BYTES)
     f32, bf16 = jnp.float32, jnp.bfloat16
-    pairs_scratch = [pltpu.SMEM((crossed, blocks), jnp.int32), pltpu.SMEM((crossed, blocks), jnp.int32)]
+    i32 = jnp.int32
     block_scratch = pltpu.SMEM(batch_block.shape, jnp.int32)
     noise_scratch = pltpu.VMEM((height, pixels), f32)
 
@@ -274,19 +257,28 @@
     offsets = [z * wide * cores for z in powers(far)]
     gathered = hop(volume, offsets[0])
 
-    sums, wave, tiles_near, images_near = call(
-        sum_kernel,
-        [((rows, pixels), bf16), (images.shape, f32), (tiles.shape, bf16), (images.shape, bf16)],
-        [hbm] * 5,
-        (batch_block, row, inv_sigma2, tiles, images),
+    sums, wave, tiles_near, images_near, place_rows, route_rows = call(
+        functools.partial(sum_kernel, shape, kinds),
         [
+            ((rows, pixels), bf16),
+            (images.shape, f32),
+            (tiles.shape, bf16),
+            (images.shape, bf16),
+            ((devices, blocks), i32),
+            ((crossed, blocks), i32),
+        ],
+        [hbm] * 7,
+        (slabs, kind_rows, batch_block, row, inv_sigma2, tiles, images),
+        [
+            pltpu.VMEM((crossed, blocks), i32),
+            pltpu.VMEM((crossed, blocks), i32),
             block_scratch,
             pltpu.VMEM((1, count), f32),
             noise_scratch,
             pltpu.VMEM((2, height, count), f32),
             pltpu.VMEM((2, count, pixels), f32),
             pltpu.VMEM((blocks, 2, height, pixels), f32),
-            pltpu.SemaphoreType.DMA((CHUNKS + 4,)),
+            pltpu.SemaphoreType.DMA((CHUNKS + 6,)),
         ],
         0,
         10 << 20,
@@ -300,14 +292,12 @@
     send, keep_far, keep_near = call(
         functools.partial(insert_kernel, shape),
         [((half, *place), bf16), (((wide - 1) * far, *place), f32), ((far, *place), f32)],
-        [hbm, hbm, vmem, vmem],
-        (slabs, kind_rows, sums, tiles_near),
+        [vmem] * 3,
+        (place_rows, sums, tiles_near),
         [
-            *pairs_scratch,
             pltpu.VMEM((kinds * rows + 2 * height, length), f32),
-            pltpu.SMEM((devices * (blocks + 1),), jnp.int32),
-            pltpu.SMEM((devices,), jnp.int32),
-            pltpu.SemaphoreType.DMA((2,)),
+            pltpu.SMEM((devices, blocks), i32),
+            pltpu.SemaphoreType.DMA((1,)),
         ],
         2 * rows * pixels * kinds * length,
         8 << 20,
@@ -321,15 +311,15 @@
         columns.append(lax.optimization_barrier((swap(gathered, x * cores), beyond))[0])
     columns += [swap(column, 1) for column in columns]
     if devices * kinds <= blocks * crossed:
-        flat = pltpu.VMEM((kinds, devices * height, pixels), f32)
+        flat = pltpu.VMEM((kinds * devices * height, pixels), f32)
     else:
         flat = pltpu.VMEM((8, LANES), f32)
     (proj,) = call(
         functools.partial(project_kernel, shape),
         [((blocks, height, pixels), f32)],
-        [hbm] * 2 + [vmem] * (1 + len(columns)),
-        (slabs, kind_rows, tiles_near, *columns),
-        [*pairs_scratch, pltpu.VMEM((devices * height, length), bf16), flat, pltpu.SemaphoreType.DMA((2,))],
+        [vmem] * (2 + len(columns)),
+        (route_rows, tiles_near, *columns),
+        [pltpu.SMEM((crossed, blocks), i32), pltpu.VMEM((devices * height, length), bf16), flat, pltpu.SemaphoreType.DMA((1,))],
         2 * devices * height * length * kinds * pixels,
         8 << 20,
         "project",

time: 35.8 us -> 35.2 us (0.983)
  Pallas kernels: 12.1 us -> 10.7 us
  waiting for transfers between devices: 8.38 us -> 9.14 us
    pallas_call x4, Pallas kernels: 12.1 us -> 10.7 us  [call(): pl.pallas_call(kernel, out_shape=tuple((jax.ShapeDtypeStruct(s, t) for s,...]
    ppermute x10, waiting for transfers between devices: 8.38 us -> 9.14 us  [swap(): lax.ppermute(array, 'slab', [(i, i ^ offset) for i in range(devices)])]
  transfers between devices with their start and end apart: 10 -> 10, of which waited for: 5 -> 5; matrix products, arithmetic and copies ran while one was open for 0% -> 0% of each run, Pallas kernels for 34% -> 31%
where the time goes in v9:
time: 35.2 us; the launch traced here: 35 us
  starting transfers between devices  13.4 us (38%)
  Pallas kernels  10.7 us (30%)
  waiting for transfers between devices  9.14 us (26%)
  between operations  0.75 us (2%)
  local copies, waits for them, and re-layouts  0.68 us (2%)
    ppermute x10, starting transfers between devices, swap(): lax.ppermute(array, 'slab', [(i, i ^ offset) for i in range(devices)])  13.4 us
    pallas_call x4, Pallas kernels, call(): pl.pallas_call(kernel, out_shape=tuple((jax.ShapeDtypeStruct(s, t) for s,...  10.7 us
    ppermute x10, waiting for transfers between devices, swap(): lax.ppermute(array, 'slab', [(i, i ^ offset) for i in range(devices)])  9.14 us
  transfers between devices with their start and end apart: 10, of which 5 were waited for; matrix products, arithmetic and copies ran while one was open for 0% of the time, Pallas kernels for 31%

profile of v9, /device:TPU:0, one launch (start us, length us, event | category | flops | bytes accessed | tf_op | source)
XLA Modules:
  0.0 35.0 jit_solution(2411311544766217800)
XLA Ops:
  0.6 3.1 %collective-permute-start = (bf16[1,32,512]{2,1,0:T(8,128)(2,1)}, bf16[1,32,512]{2,1,0:T(8,128)(2,1)S(1)}, u32[]{:S(2)}, u32[]{:S(2)}) collective-permute-start(bf16[1,32,512]{2,1,0:T(8,128)(2,1)} %param.8), channel_id=1, source_target_pairs={{0,4},{1,5},{2,6},{3,7},{4,0},{5,1},{6,2},{7,3},{8,12},{9,13},{10,... | collective-permute-start | bytes 98312 | tf_op jit(solution)/shard_map/ppermute | solution.py:229
  3.7 0.0 copy-start
  3.7 2.9 %sums.1 = (bf16[1024,256]{1,0:T(8,128)(2,1)S(1)}, f32[128,32,256]{2,1,0:T(8,128)S(1)}, bf16[8,512,256]{2,1,0:T(8,128)(2,1)S(1)}, bf16[128,32,256]{2,1,0:T(8,128)...) custom-call(s32[8,16]{1,0:T(8,128)} %bitcast.18, s32[8,16]{1,0:T(8,128)} %bitcast.19, s32[16]{0:T(128)} %block_hbm.3, ...), custom_call_target="tpu_custom_call" | custom-call | bytes 10485760 | tf_op jit(solution)/shard_map/sums/pallas_call | solution.py:243
  6.6 0.0 collective-permute-done
  6.7 0.0 copy-done
  6.7 2.7 %collective-permute-start.1 = (bf16[2,32,512]{2,1,0:T(8,128)(2,1)S(1)}, bf16[2,32,512]{2,1,0:T(8,128)(2,1)S(1)}, u32[]{:S(2)}, u32[]{:S(2)}) collective-permute-start(bf16[2,32,512]{2,1,0:T(8,128)(2,1)S(1)} %pad_maximum_fusion.1), channel_id=1, source_target_pairs={{0,8},{1,9},{2,10},{3,11},{4,12},{5,13},{6,14},{7,15},{8,0},{9,1},... | collective-permute-start | bytes 196616 | tf_op jit(solution)/shard_map/ppermute | solution.py:229
  9.3 4.1 %insert.1 = (bf16[8,2,32,512]{3,2,1,0:T(8,128)(2,1)S(1)}, f32[4,2,32,512]{3,2,1,0:T(8,128)S(1)}, f32[4,2,32,512]{3,2,1,0:T(8,128)S(1)}) custom-call(s32[16,16]{1,0:T(8,128)S(1)} %get-tuple-element.21.place_vmem, bf16[1024,256]{1,0:T(8,128)(2,1)S(1)} %get-tuple-element.23.sums_ref, bf16[8,512,256]{2,1,0:T(8,128)(2,1)S(1)} %get-tuple-element.20.tiles_ref), custom_call_target="tpu_custom_call" | custom-call | flops 2147483648 | bytes 8388608 | tf_op jit(solution)/shard_map/insert/pallas_call | solution.py:243
  13.4 0.0 collective-permute-done.1
  13.5 0.1 collective-permute-start.3
  13.5 1.6 %collective-permute-start.2 = (bf16[4,32,512]{2,1,0:T(8,128)(2,1)S(1)}, bf16[4,32,512]{2,1,0:T(8,128)(2,1)S(1)}, u32[]{:S(2)}, u32[]{:S(2)}) collective-permute-start(bf16[4,32,512]{2,1,0:T(8,128)(2,1)S(1)} %pad_maximum_fusion.refs_0_), channel_id=1, source_target_pairs={{0,2},{1,3},{2,0},{3,1},{4,6},{5,7},{6,4},{7,5},{8,10},{9,11},{10,... | collective-permute-start | bytes 393224 | tf_op jit(solution)/shard_map/ppermute | solution.py:229
  15.1 0.3 collective-permute-done.3
  15.4 0.1 add_convert_fusion
  15.5 1.6 %collective-permute-start.6 = (bf16[4,2,32,512]{3,2,1,0:T(8,128)(2,1)S(1)}, bf16[4,2,32,512]{3,2,1,0:T(8,128)(2,1)S(1)}, u32[]{:S(2)}, u32[]{:S(2)}) collective-permute-start(bf16[4,2,32,512]{3,2,1,0:T(8,128)(2,1)S(1)} %add_convert_fusion), channel_id=1, source_target_pairs={{0,2},{1,3},{2,0},{3,1},{4,6},{5,7},{6,4},{7,5},{8,10},{9,11},{10,... | collective-permute-start | bytes 786440 | tf_op jit(solution)/shard_map/ppermute | solution.py:229
  17.1 0.0 collective-permute-start.4
  17.1 2.8 %collective-permute-done.2.refs_1_ = bf16[4,32,512]{2,1,0:T(8,128)(2,1)S(1)} collective-permute-done((bf16[4,32,512]{2,1,0:T(8,128)(2,1)S(1)}, bf16[4,32,512]{2,1,0:T(8,128)(2,1)S(1)}, u32[]{:S(2)}, u32[]{:S(2)}) %collective-permute-start.2) | collective-permute-done | bytes 131104 | tf_op jit(solution)/shard_map/ppermute | solution.py:229
  19.9 0.0 collective-permute-start.5
  19.9 0.0 collective-permute-done.4.refs_2_
  19.9 1.3 %collective-permute-done.5.refs_3_ = bf16[4,32,512]{2,1,0:T(8,128)(2,1)S(1)} collective-permute-done((bf16[4,32,512]{2,1,0:T(8,128)(2,1)S(1)}, bf16[4,32,512]{2,1,0:T(8,128)(2,1)S(1)}, u32[]{:S(2)}, u32[]{:S(2)}) %collective-permute-start.5) | collective-permute-done | bytes 131104 | tf_op jit(solution)/shard_map/ppermute | solution.py:229
  21.3 1.5 %project.1.proj_ref = f32[16,32,256]{2,1,0:T(8,128)S(1)} custom-call(s32[8,16]{1,0:T(8,128)S(1)} %get-tuple-element.19.route_vmem, bf16[8,512,256]{2,1,0:T(8,128)(2,1)S(1)} %get-tuple-element.20.tiles_ref, bf16[4,32,512]{2,1,0:T(8,128)(2,1)S(1)} %pad_maximum_fusion.refs_0_, bf16[4,32,512]{2,1,0:T(8,128)(2,1)S(1)} %collective-permute-done.2.refs_1_, ...), custom_call_target="tpu_custom_call" | custom-call | flops 1073741824 | bytes 8388608 | tf_op jit(solution)/shard_map/project/pallas_call | solution.py:243
  22.7 2.3 %collective-permute-done.6 = bf16[4,2,32,512]{3,2,1,0:T(8,128)(2,1)S(1)} collective-permute-done((bf16[4,2,32,512]{3,2,1,0:T(8,128)(2,1)S(1)}, bf16[4,2,32,512]{3,2,1,0:T(8,128)(2,1)S(1)}, u32[]{:S(2)}, u32[]{:S(2)}) %collective-permute-start.6) | collective-permute-done | bytes 262176 | tf_op jit(solution)/shard_map/ppermute | solution.py:229
  25.1 0.1 fusion.3
  25.2 2.4 %collective-permute-start.9 = (bf16[2,32,512]{2,1,0:T(8,128)(2,1)S(1)}, bf16[2,32,512]{2,1,0:T(8,128)(2,1)S(1)}, u32[]{:S(2)}, u32[]{:S(2)}) collective-permute-start(bf16[2,32,512]{2,1,0:T(8,128)(2,1)S(1)} %get-tuple-element.38), channel_id=1, source_target_pairs={{0,12},{1,13},{2,14},{3,15},{4,8},{5,9},{6,10},{7,11},{8,4},{9,5},... | collective-permute-start | bytes 196616 | tf_op jit(solution)/shard_map/ppermute | solution.py:229
  27.7 0.3 collective-permute-start.8
  27.9 1.7 %collective-permute-start.7 = (bf16[2,32,512]{2,1,0:T(8,128)(2,1)S(1)}, bf16[2,32,512]{2,1,0:T(8,128)(2,1)S(1)}, u32[]{:S(2)}, u32[]{:S(2)}) collective-permute-start(bf16[2,32,512]{2,1,0:T(8,128)(2,1)S(1)} %get-tuple-element.37), channel_id=1, source_target_pairs={{0,4},{1,5},{2,6},{3,7},{4,0},{5,1},{6,2},{7,3},{8,12},{9,13},{10,... | collective-permute-start | bytes 196616 | tf_op jit(solution)/shard_map/ppermute | solution.py:229
  29.7 2.3 %scores.1 = f32[1,128]{1,0:T(1,128)} custom-call(s32[16]{0:T(128)} %block_hbm.3, f32[32,256]{1,0:T(8,128)} %noise_hbm.3, f32[16,32,256]{2,1,0:T(8,128)S(1)} %project.1.proj_ref, f32[128,32,256]{2,1,0:T(8,128)S(1)} %get-tuple-element.32.wave_ref, bf16[128,32,256]{2,1,0:T(8,128)(2,1)S(1)} %get-tuple-element.33.images_ref), custom_call_target="tpu_custom_call" | custom-call | flops 1073741824 | bytes 8388608 | tf_op jit(solution)/shard_map/scores/pallas_call | solution.py:243
  32.0 0.0 collective-permute-done.9
  32.0 2.3 %collective-permute-done.8 = bf16[2,32,512]{2,1,0:T(8,128)(2,1)S(1)} collective-permute-done((bf16[2,32,512]{2,1,0:T(8,128)(2,1)S(1)}, bf16[2,32,512]{2,1,0:T(8,128)(2,1)S(1)}, u32[]{:S(2)}, u32[]{:S(2)}) %collective-permute-start.8) | collective-permute-done | bytes 65568 | tf_op jit(solution)/shard_map/ppermute | solution.py:229
  34.3 0.0 collective-permute-done.7
  34.3 0.7 %fusion.4 = (f32[1,32,512]{2,1,0:T(8,128)}, f32[1,32,512]{2,1,0:T(8,128)}) fusion(f32[2,32,512]{2,1,0:T(8,128)S(1)} %fusion.2), kind=kLoop, calls=%fused_computation.12 | loop fusion | bytes 262144 | tf_op jit(solution)/shard_map/slice | solution.py:345
  (4 shorter events, 0.1 us)
Async XLA Ops:
  0.6 6.0 %collective-permute-start = (bf16[1,32,512]{2,1,0:T(8,128)(2,1)}, bf16[1,32,512]{2,1,0:T(8,128)(2,1)S(1)}, u32[]{:S(2)}, u32[]{:S(2)}) collective-permute-start(bf16[1,32,512]{2,1,0:T(8,128)(2,1)} %param.8), channel_id=1, source_target_pairs={{0,4},{1,5},{2,6},{3,7},{4,0},{5,1},{6,2},{7,3},{8,12},{9,13},{10,... | collective-permute-start | bytes 98312 | tf_op jit(solution)/shard_map/ppermute | solution.py:229
  3.7 2.9 %copy-start = (bf16[1,32,512]{2,1,0:T(8,128)(2,1)S(1)}, bf16[1,32,512]{2,1,0:T(8,128)(2,1)}, u32[]{:S(2)}) copy-start(bf16[1,32,512]{2,1,0:T(8,128)(2,1)} %param.8) | copy-start | bytes 98308
  6.7 6.8 %collective-permute-start.1 = (bf16[2,32,512]{2,1,0:T(8,128)(2,1)S(1)}, bf16[2,32,512]{2,1,0:T(8,128)(2,1)S(1)}, u32[]{:S(2)}, u32[]{:S(2)}) collective-permute-start(bf16[2,32,512]{2,1,0:T(8,128)(2,1)S(1)} %pad_maximum_fusion.1), channel_id=1, source_target_pairs={{0,8},{1,9},{2,10},{3,11},{4,12},{5,13},{6,14},{7,15},{8,0},{9,1},... | collective-permute-start | bytes 196616 | tf_op jit(solution)/shard_map/ppermute | solution.py:229
  13.5 2.0 %collective-permute-start.3 = (bf16[8,2,32,512]{3,2,1,0:T(8,128)(2,1)S(1)}, bf16[8,2,32,512]{3,2,1,0:T(8,128)(2,1)S(1)}, u32[]{:S(2)}, u32[]{:S(2)}) collective-permute-start(bf16[8,2,32,512]{3,2,1,0:T(8,128)(2,1)S(1)} %get-tuple-element.28), channel_id=1, source_target_pairs={{0,1},{1,0},{2,3},{3,2},{4,5},{5,4},{6,7},{7,6},{8,9},{9,8},{10,11... | collective-permute-start | bytes 1572872 | tf_op jit(solution)/shard_map/ppermute | solution.py:229
  13.5 6.4 %collective-permute-start.2 = (bf16[4,32,512]{2,1,0:T(8,128)(2,1)S(1)}, bf16[4,32,512]{2,1,0:T(8,128)(2,1)S(1)}, u32[]{:S(2)}, u32[]{:S(2)}) collective-permute-start(bf16[4,32,512]{2,1,0:T(8,128)(2,1)S(1)} %pad_maximum_fusion.refs_0_), channel_id=1, source_target_pairs={{0,2},{1,3},{2,0},{3,1},{4,6},{5,7},{6,4},{7,5},{8,10},{9,11},{10,... | collective-permute-start | bytes 393224 | tf_op jit(solution)/shard_map/ppermute | solution.py:229
  15.5 9.5 %collective-permute-start.6 = (bf16[4,2,32,512]{3,2,1,0:T(8,128)(2,1)S(1)}, bf16[4,2,32,512]{3,2,1,0:T(8,128)(2,1)S(1)}, u32[]{:S(2)}, u32[]{:S(2)}) collective-permute-start(bf16[4,2,32,512]{3,2,1,0:T(8,128)(2,1)S(1)} %add_convert_fusion), channel_id=1, source_target_pairs={{0,2},{1,3},{2,0},{3,1},{4,6},{5,7},{6,4},{7,5},{8,10},{9,11},{10,... | collective-permute-start | bytes 786440 | tf_op jit(solution)/shard_map/ppermute | solution.py:229
  17.1 2.8 %collective-permute-start.4 = (bf16[4,32,512]{2,1,0:T(8,128)(2,1)S(1)}, bf16[4,32,512]{2,1,0:T(8,128)(2,1)S(1)}, u32[]{:S(2)}, u32[]{:S(2)}) collective-permute-start(bf16[4,32,512]{2,1,0:T(8,128)(2,1)S(1)} %pad_maximum_fusion.refs_0_), channel_id=1, source_target_pairs={{0,1},{1,0},{2,3},{3,2},{4,5},{5,4},{6,7},{7,6},{8,9},{9,8},{10,11... | collective-permute-start | bytes 393224 | tf_op jit(solution)/shard_map/ppermute | solution.py:229
  19.9 1.3 %collective-permute-start.5 = (bf16[4,32,512]{2,1,0:T(8,128)(2,1)S(1)}, bf16[4,32,512]{2,1,0:T(8,128)(2,1)S(1)}, u32[]{:S(2)}, u32[]{:S(2)}) collective-permute-start(bf16[4,32,512]{2,1,0:T(8,128)(2,1)S(1)} %collective-permute-done.2.refs_1_), channel_id=1, source_target_pairs={{0,1},{1,0},{2,3},{3,2},{4,5},{5,4},{6,7},{7,6},{8,9},{9,8},{10,11... | collective-permute-start | bytes 393224 | tf_op jit(solution)/shard_map/ppermute | solution.py:229
  25.2 6.7 %collective-permute-start.9 = (bf16[2,32,512]{2,1,0:T(8,128)(2,1)S(1)}, bf16[2,32,512]{2,1,0:T(8,128)(2,1)S(1)}, u32[]{:S(2)}, u32[]{:S(2)}) collective-permute-start(bf16[2,32,512]{2,1,0:T(8,128)(2,1)S(1)} %get-tuple-element.38), channel_id=1, source_target_pairs={{0,12},{1,13},{2,14},{3,15},{4,8},{5,9},{6,10},{7,11},{8,4},{9,5},... | collective-permute-start | bytes 196616 | tf_op jit(solution)/shard_map/ppermute | solution.py:229
  27.7 6.6 %collective-permute-start.8 = (bf16[2,32,512]{2,1,0:T(8,128)(2,1)S(1)}, bf16[2,32,512]{2,1,0:T(8,128)(2,1)S(1)}, u32[]{:S(2)}, u32[]{:S(2)}) collective-permute-start(bf16[2,32,512]{2,1,0:T(8,128)(2,1)S(1)} %get-tuple-element.39), channel_id=1, source_target_pairs={{0,8},{1,9},{2,10},{3,11},{4,12},{5,13},{6,14},{7,15},{8,0},{9,1},... | collective-permute-start | bytes 196616 | tf_op jit(solution)/shard_map/ppermute | solution.py:229
  27.9 6.3 %collective-permute-start.7 = (bf16[2,32,512]{2,1,0:T(8,128)(2,1)S(1)}, bf16[2,32,512]{2,1,0:T(8,128)(2,1)S(1)}, u32[]{:S(2)}, u32[]{:S(2)}) collective-permute-start(bf16[2,32,512]{2,1,0:T(8,128)(2,1)S(1)} %get-tuple-element.37), channel_id=1, source_target_pairs={{0,4},{1,5},{2,6},{3,7},{4,0},{5,1},{6,2},{7,3},{8,12},{9,13},{10,... | collective-permute-start | bytes 196616 | tf_op jit(solution)/shard_map/ppermute | solution.py:229

commit v10 on v9

--- a/solution.py
+++ b/solution.py
@@ -9,7 +9,7 @@
 
 LANES = 128
 CHUNKS = 4
-VMEM_BYTES = 32 * 1024 * 1024
+VMEM_BYTES = 24 * 1024 * 1024
 
 
 def grid_of(devices):
@@ -123,37 +123,44 @@
     last.wait()
 
 
-def insert_kernel(shape, place_vmem, sums_ref, tiles_ref, send_ref, far_ref, near_ref, parts_ref, place_ref, sems):
-    far, wide, cores = shape
+def fill(ref, start, place_ref, parts_ref, mate_ref=None, offset=0):
+    sides, height, length = ref.shape[1:]
+
+    def step(slot, carry):
+        acc = None
+        for k in range(place_ref.shape[1]):
+            at = pl.multiple_of(place_ref[start + slot, k], sides * height)
+            part = parts_ref[pl.ds(at, sides * height), :]
+            acc = part if acc is None else acc + part
+        acc = acc.reshape(sides, height, length)
+        if mate_ref is not None:
+            acc = acc + mate_ref[offset + slot].astype(jnp.float32)
+        ref[slot] = acc.astype(ref.dtype)
+        return carry
+
+    lax.fori_loop(0, ref.shape[0], step, 0)
+
+
+def insert_kernel(place_vmem, sums_ref, tiles_ref, send_ref, parts_ref, place_ref, sems):
     (started,) = copies([(place_vmem, place_ref)], sems)
-    devices, blocks = place_ref.shape
     kinds = tiles_ref.shape[0]
     rows = sums_ref.shape[0]
-    length = parts_ref.shape[1]
-    height = rows // (2 * blocks)
-    half = devices // 2
-    parts_ref[pl.ds(kinds * rows, 2 * height), :] = jnp.zeros((2 * height, length), jnp.float32)
+    zeros = parts_ref.shape[0] - kinds * rows
+    parts_ref[kinds * rows :, :] = jnp.zeros((zeros, parts_ref.shape[1]), jnp.float32)
     for t in range(kinds):
         parts_ref[t * rows : (t + 1) * rows, :] = lax.dot_general(
             sums_ref[...], tiles_ref[t], (((1,), (1,)), ((), ())), preferred_element_type=jnp.float32
         )
     started.wait()
-
-    def fill(ref, start):
-        def step(slot, carry):
-            acc = None
-            for k in range(blocks):
-                at = pl.multiple_of(place_ref[start + slot, k], 2 * height)
-                part = parts_ref[pl.ds(at, 2 * height), :]
-                acc = part if acc is None else acc + part
-            ref[slot] = acc.astype(ref.dtype).reshape(2, height, length)
-            return carry
-
-        lax.fori_loop(0, ref.shape[0], step, 0)
-
-    fill(send_ref, 0)
-    fill(far_ref, half + far)
-    fill(near_ref, half)
+    fill(send_ref, 0, place_ref, parts_ref)
+
+
+def keep_kernel(place_vmem, parts_ref, mate_ref, far_ref, near_ref, place_ref, sems):
+    (started,) = copies([(place_vmem, place_ref)], sems)
+    half, far = place_ref.shape[0] // 2, near_ref.shape[0]
+    started.wait()
+    fill(far_ref, half + far, place_ref, parts_ref, mate_ref, far)
+    fill(near_ref, half, place_ref, parts_ref, mate_ref, 0)
 
 
 def project_kernel(shape, route_vmem, tiles_ref, *refs):
@@ -284,32 +291,38 @@
         10 << 20,
         "sums",
     )
-    sums, gathered = lax.optimization_barrier((sums, gathered))
-    for offset in offsets[1:]:
-        gathered = hop(gathered, offset)
 
     place = (2, height, length)
-    send, keep_far, keep_near = call(
-        functools.partial(insert_kernel, shape),
-        [((half, *place), bf16), (((wide - 1) * far, *place), f32), ((far, *place), f32)],
+    send, parts = call(
+        insert_kernel,
+        [((half, *place), bf16), ((kinds * rows + 2 * height, length), f32)],
         [vmem] * 3,
         (place_rows, sums, tiles_near),
-        [
-            pltpu.VMEM((kinds * rows + 2 * height, length), f32),
-            pltpu.SMEM((devices, blocks), i32),
-            pltpu.SemaphoreType.DMA((1,)),
-        ],
+        [pltpu.SMEM((devices, blocks), i32), pltpu.SemaphoreType.DMA((1,))],
         2 * rows * pixels * kinds * length,
         8 << 20,
         "insert",
     )
     send, gathered = lax.optimization_barrier((send, gathered))
-    mate = swap(send, 1)
-    beyond = (keep_far + mate[far:].astype(f32)).astype(bf16)
-    columns = [gathered]
+    for offset in offsets[1:]:
+        gathered = hop(gathered, offset)
+    beyond, mine = call(
+        keep_kernel,
+        [(((wide - 1) * far, *place), bf16), ((far, *place), f32)],
+        [vmem] * 3,
+        (place_rows, parts, swap(send, 1)),
+        [pltpu.SMEM((devices, blocks), i32), pltpu.SemaphoreType.DMA((1,))],
+        0,
+        0,
+        "keep",
+    )
+    held, _ = lax.optimization_barrier((gathered, beyond))
+    columns = [gathered] + [swap(held, x * cores) for x in range(1, wide)]
+    columns += [swap(column, 1) for column in columns]
     for x in range(1, wide):
-        columns.append(lax.optimization_barrier((swap(gathered, x * cores), beyond))[0])
-    columns += [swap(column, 1) for column in columns]
+        mine = mine + swap(beyond[(x - 1) * far : x * far], x * cores).astype(f32)
+    outgoing = mine.astype(bf16)
+    _, *columns = lax.optimization_barrier((outgoing, *columns))
     if devices * kinds <= blocks * crossed:
         flat = pltpu.VMEM((kinds * devices * height, pixels), f32)
     else:
@@ -320,23 +333,19 @@
         [vmem] * (2 + len(columns)),
         (route_rows, tiles_near, *columns),
         [pltpu.SMEM((crossed, blocks), i32), pltpu.VMEM((devices * height, length), bf16), flat, pltpu.SemaphoreType.DMA((1,))],
-        2 * devices * height * length * kinds * pixels,
-        8 << 20,
+        0,
+        0,
         "project",
     )
 
-    mine = keep_near + mate[:far].astype(f32)
-    for x in range(1, wide):
-        mine = mine + swap(beyond[(x - 1) * far : x * far], x * cores).astype(f32)
-    proj, outgoing = lax.optimization_barrier((proj, mine.astype(bf16)))
     (scores,) = call(
         score_kernel,
         [((1, count), f32)],
         [hbm] * 2 + [vmem] * 3,
         (batch_block, inv_sigma2, proj, wave, images_near),
         [block_scratch, noise_scratch, pltpu.VMEM((count * 8, LANES), f32), pltpu.SemaphoreType.DMA((2,))],
-        1 << 30,
-        8 << 20,
+        0,
+        0,
         "scores",
     )
     total = mine[0]

time: 35.2 us -> 35.3 us (level)
  Pallas kernels: 10.7 us -> 11.4 us
  waiting for transfers between devices: 9.14 us -> 8.61 us
    pallas_call x4 -> x5, Pallas kernels: 10.7 us -> 11.4 us  [call(): pl.pallas_call(kernel, out_shape=tuple((jax.ShapeDtypeStruct(s, t) for s,...]
    ppermute x10, waiting for transfers between devices: 9.14 us -> 8.61 us  [swap(): lax.ppermute(array, 'slab', [(i, i ^ offset) for i in range(devices)])]
  transfers between devices with their start and end apart: 10 -> 10, of which waited for: 5 -> 3; matrix products, arithmetic and copies ran while one was open for 0% -> 0% of each run, Pallas kernels for 31% -> 33%
where the time goes in v10:
time: 35.3 us; the launch traced here: 35 us
  starting transfers between devices  13.4 us (38%)
  Pallas kernels  11.4 us (32%)
  waiting for transfers between devices  8.61 us (24%)
  between operations  0.76 us (2%)
  local copies, waits for them, and re-layouts  0.69 us (2%)
    ppermute x10, starting transfers between devices, swap(): lax.ppermute(array, 'slab', [(i, i ^ offset) for i in range(devices)])  13.4 us
    pallas_call x5, Pallas kernels, call(): pl.pallas_call(kernel, out_shape=tuple((jax.ShapeDtypeStruct(s, t) for s,...  11.4 us
    ppermute x10, waiting for transfers between devices, swap(): lax.ppermute(array, 'slab', [(i, i ^ offset) for i in range(devices)])  8.61 us
  transfers between devices with their start and end apart: 10, of which 3 were waited for; matrix products, arithmetic and copies ran while one was open for 0% of the time, Pallas kernels for 33%

profile of v10, /device:TPU:0, one launch (start us, length us, event | category | flops | bytes accessed | tf_op | source)
XLA Modules:
  0.0 35.0 jit_solution(728050505563377056)
XLA Ops:
  0.6 3.1 %collective-permute-start = (bf16[1,32,512]{2,1,0:T(8,128)(2,1)}, bf16[1,32,512]{2,1,0:T(8,128)(2,1)S(1)}, u32[]{:S(2)}, u32[]{:S(2)}) collective-permute-start(bf16[1,32,512]{2,1,0:T(8,128)(2,1)} %param.8), channel_id=1, source_target_pairs={{0,4},{1,5},{2,6},{3,7},{4,0},{5,1},{6,2},{7,3},{8,12},{9,13},{10,... | collective-permute-start | bytes 98312 | tf_op jit(solution)/shard_map/ppermute | solution.py:236
  3.7 2.9 %sums.1 = (bf16[1024,256]{1,0:T(8,128)(2,1)S(1)}, f32[128,32,256]{2,1,0:T(8,128)S(1)}, bf16[8,512,256]{2,1,0:T(8,128)(2,1)S(1)}, bf16[128,32,256]{2,1,0:T(8,128)...) custom-call(s32[8,16]{1,0:T(8,128)} %bitcast.18, s32[8,16]{1,0:T(8,128)} %bitcast.19, s32[16]{0:T(128)} %block_hbm.3, ...), custom_call_target="tpu_custom_call" | custom-call | bytes 10485760 | tf_op jit(solution)/shard_map/sums/pallas_call | solution.py:250
  6.6 0.0 copy-start
  6.6 3.2 %insert.1 = (bf16[8,2,32,512]{3,2,1,0:T(8,128)(2,1)S(1)}, f32[8256,512]{1,0:T(8,128)S(1)}) custom-call(s32[16,16]{1,0:T(8,128)S(1)} %get-tuple-element.22.place_vmem, bf16[1024,256]{1,0:T(8,128)(2,1)S(1)} %get-tuple-element.23.sums_ref, bf16[8,512,256]{2,1,0:T(8,128)(2,1)S(1)} %get-tuple-element.21.tiles_ref), custom_call_target="tpu_custom_call" | custom-call | flops 2147483648 | bytes 8388608 | tf_op jit(solution)/shard_map/insert/pallas_call | solution.py:250
  9.9 0.0 collective-permute-done
  9.9 0.0 copy-done
  9.9 0.1 collective-permute-start.1
  10.0 2.7 %collective-permute-start.3 = (bf16[2,32,512]{2,1,0:T(8,128)(2,1)S(1)}, bf16[2,32,512]{2,1,0:T(8,128)(2,1)S(1)}, u32[]{:S(2)}, u32[]{:S(2)}) collective-permute-start(bf16[2,32,512]{2,1,0:T(8,128)(2,1)S(1)} %pad_maximum_fusion), channel_id=1, source_target_pairs={{0,8},{1,9},{2,10},{3,11},{4,12},{5,13},{6,14},{7,15},{8,0},{9,1},... | collective-permute-start | bytes 196616 | tf_op jit(solution)/shard_map/ppermute | solution.py:236
  12.7 0.0 collective-permute-done.1.mate_ref
  12.7 1.5 %keep.1 = (bf16[4,2,32,512]{3,2,1,0:T(8,128)(2,1)S(1)}, f32[4,2,32,512]{3,2,1,0:T(8,128)S(1)}) custom-call(s32[16,16]{1,0:T(8,128)S(1)} %get-tuple-element.22.place_vmem, f32[8256,512]{1,0:T(8,128)S(1)} %get-tuple-element.24.parts_ref, bf16[8,2,32,512]{3,2,1,0:T(8,128)(2,1)S(1)} %collective-permute-done.1.mate_ref), custom_call_target="tpu_custom_call" | custom-call | tf_op jit(solution)/shard_map/keep/pallas_call | solution.py:250
  14.2 1.6 %collective-permute-start.2 = (bf16[4,2,32,512]{3,2,1,0:T(8,128)(2,1)S(1)}, bf16[4,2,32,512]{3,2,1,0:T(8,128)(2,1)S(1)}, u32[]{:S(2)}, u32[]{:S(2)}) collective-permute-start(bf16[4,2,32,512]{3,2,1,0:T(8,128)(2,1)S(1)} %get-tuple-element.28), channel_id=1, source_target_pairs={{0,2},{1,3},{2,0},{3,1},{4,6},{5,7},{6,4},{7,5},{8,10},{9,11},{10,... | collective-permute-start | bytes 786440 | tf_op jit(solution)/shard_map/ppermute | solution.py:236
  15.8 0.9 %collective-permute-done.3 = bf16[2,32,512]{2,1,0:T(8,128)(2,1)S(1)} collective-permute-done((bf16[2,32,512]{2,1,0:T(8,128)(2,1)S(1)}, bf16[2,32,512]{2,1,0:T(8,128)(2,1)S(1)}, u32[]{:S(2)}, u32[]{:S(2)}) %collective-permute-start.3) | collective-permute-done | bytes 65568 | tf_op jit(solution)/shard_map/ppermute | solution.py:236
  16.6 1.6 %collective-permute-start.4 = (bf16[4,32,512]{2,1,0:T(8,128)(2,1)S(1)}, bf16[4,32,512]{2,1,0:T(8,128)(2,1)S(1)}, u32[]{:S(2)}, u32[]{:S(2)}) collective-permute-start(bf16[4,32,512]{2,1,0:T(8,128)(2,1)S(1)} %constant_dynamic-update-slice_fusion.refs_0_), channel_id=1, source_target_pairs={{0,2},{1,3},{2,0},{3,1},{4,6},{5,7},{6,4},{7,5},{8,10},{9,11},{10,... | collective-permute-start | bytes 393224 | tf_op jit(solution)/shard_map/ppermute | solution.py:236
  18.2 0.0 collective-permute-start.5
  18.2 7.3 %collective-permute-done.4.refs_1_ = bf16[4,32,512]{2,1,0:T(8,128)(2,1)S(1)} collective-permute-done((bf16[4,32,512]{2,1,0:T(8,128)(2,1)S(1)}, bf16[4,32,512]{2,1,0:T(8,128)(2,1)S(1)}, u32[]{:S(2)}, u32[]{:S(2)}) %collective-permute-start.4) | collective-permute-done | bytes 131104 | tf_op jit(solution)/shard_map/ppermute | solution.py:236
  25.5 0.0 collective-permute-start.6
  25.5 0.0 collective-permute-done.2
  25.5 0.1 fusion.3
  25.6 0.5 %collective-permute-start.7 = (bf16[2,32,512]{2,1,0:T(8,128)(2,1)S(1)}, bf16[2,32,512]{2,1,0:T(8,128)(2,1)S(1)}, u32[]{:S(2)}, u32[]{:S(2)}) collective-permute-start(bf16[2,32,512]{2,1,0:T(8,128)(2,1)S(1)} %get-tuple-element.39), channel_id=1, source_target_pairs={{0,4},{1,5},{2,6},{3,7},{4,0},{5,1},{6,2},{7,3},{8,12},{9,13},{10,... | collective-permute-start | bytes 196616 | tf_op jit(solution)/shard_map/ppermute | solution.py:236
  26.1 1.8 %collective-permute-start.8 = (bf16[2,32,512]{2,1,0:T(8,128)(2,1)S(1)}, bf16[2,32,512]{2,1,0:T(8,128)(2,1)S(1)}, u32[]{:S(2)}, u32[]{:S(2)}) collective-permute-start(bf16[2,32,512]{2,1,0:T(8,128)(2,1)S(1)} %get-tuple-element.41), channel_id=1, source_target_pairs={{0,8},{1,9},{2,10},{3,11},{4,12},{5,13},{6,14},{7,15},{8,0},{9,1},... | collective-permute-start | bytes 196616 | tf_op jit(solution)/shard_map/ppermute | solution.py:236
  27.9 2.1 %collective-permute-start.9 = (bf16[2,32,512]{2,1,0:T(8,128)(2,1)S(1)}, bf16[2,32,512]{2,1,0:T(8,128)(2,1)S(1)}, u32[]{:S(2)}, u32[]{:S(2)}) collective-permute-start(bf16[2,32,512]{2,1,0:T(8,128)(2,1)S(1)} %get-tuple-element.40), channel_id=1, source_target_pairs={{0,12},{1,13},{2,14},{3,15},{4,8},{5,9},{6,10},{7,11},{8,4},{9,5},... | collective-permute-start | bytes 196616 | tf_op jit(solution)/shard_map/ppermute | solution.py:236
  30.1 0.0 collective-permute-done.5.refs_2_
  30.1 0.0 collective-permute-done.6.refs_3_
  30.1 1.5 %project.1.proj_ref = f32[16,32,256]{2,1,0:T(8,128)S(1)} custom-call(s32[8,16]{1,0:T(8,128)S(1)} %get-tuple-element.20.route_vmem, bf16[8,512,256]{2,1,0:T(8,128)(2,1)S(1)} %get-tuple-element.21.tiles_ref, bf16[4,32,512]{2,1,0:T(8,128)(2,1)S(1)} %constant_dynamic-update-slice_fusion.refs_0_, bf16[4,32,512]{2,1,0:T(8,128)(2,1)S(1)} %collective-permute-done.4.refs_1_, ...), custom_call_target="tpu_custom_call" | custom-call | tf_op jit(solution)/shard_map/project/pallas_call | solution.py:250
  31.5 2.3 %scores.1 = f32[1,128]{1,0:T(1,128)} custom-call(s32[16]{0:T(128)} %block_hbm.3, f32[32,256]{1,0:T(8,128)} %noise_hbm.3, f32[16,32,256]{2,1,0:T(8,128)S(1)} %project.1.proj_ref, f32[128,32,256]{2,1,0:T(8,128)S(1)} %get-tuple-element.35.wave_ref, bf16[128,32,256]{2,1,0:T(8,128)(2,1)S(1)} %get-tuple-element.36.images_ref), custom_call_target="tpu_custom_call" | custom-call | tf_op jit(solution)/shard_map/scores/pallas_call | solution.py:250
  33.8 0.0 collective-permute-done.7
  33.8 0.0 collective-permute-done.8
  33.9 0.5 %collective-permute-done.9 = bf16[2,32,512]{2,1,0:T(8,128)(2,1)S(1)} collective-permute-done((bf16[2,32,512]{2,1,0:T(8,128)(2,1)S(1)}, bf16[2,32,512]{2,1,0:T(8,128)(2,1)S(1)}, u32[]{:S(2)}, u32[]{:S(2)}) %collective-permute-start.9) | collective-permute-done | bytes 65568 | tf_op jit(solution)/shard_map/ppermute | solution.py:236
  34.4 0.7 %fusion.4 = (f32[1,32,512]{2,1,0:T(8,128)}, f32[1,32,512]{2,1,0:T(8,128)}) fusion(f32[2,32,512]{2,1,0:T(8,128)S(1)} %fusion.2), kind=kLoop, calls=%fused_computation.12 | loop fusion | bytes 262144 | tf_op jit(solution)/shard_map/slice | solution.py:354
  (5 shorter events, 0.1 us)
Async XLA Ops:
  0.6 9.3 %collective-permute-start = (bf16[1,32,512]{2,1,0:T(8,128)(2,1)}, bf16[1,32,512]{2,1,0:T(8,128)(2,1)S(1)}, u32[]{:S(2)}, u32[]{:S(2)}) collective-permute-start(bf16[1,32,512]{2,1,0:T(8,128)(2,1)} %param.8), channel_id=1, source_target_pairs={{0,4},{1,5},{2,6},{3,7},{4,0},{5,1},{6,2},{7,3},{8,12},{9,13},{10,... | collective-permute-start | bytes 98312 | tf_op jit(solution)/shard_map/ppermute | solution.py:236
  6.6 3.3 %copy-start = (bf16[1,32,512]{2,1,0:T(8,128)(2,1)S(1)}, bf16[1,32,512]{2,1,0:T(8,128)(2,1)}, u32[]{:S(2)}) copy-start(bf16[1,32,512]{2,1,0:T(8,128)(2,1)} %param.8) | copy-start | bytes 98308
  9.9 2.7 %collective-permute-start.1 = (bf16[8,2,32,512]{3,2,1,0:T(8,128)(2,1)S(1)}, bf16[8,2,32,512]{3,2,1,0:T(8,128)(2,1)S(1)}, u32[]{:S(2)}, u32[]{:S(2)}) collective-permute-start(bf16[8,2,32,512]{3,2,1,0:T(8,128)(2,1)S(1)} %get-tuple-element.26), channel_id=1, source_target_pairs={{0,1},{1,0},{2,3},{3,2},{4,5},{5,4},{6,7},{7,6},{8,9},{9,8},{10,11... | collective-permute-start | bytes 1572872 | tf_op jit(solution)/shard_map/ppermute | solution.py:236
  10.0 6.6 %collective-permute-start.3 = (bf16[2,32,512]{2,1,0:T(8,128)(2,1)S(1)}, bf16[2,32,512]{2,1,0:T(8,128)(2,1)S(1)}, u32[]{:S(2)}, u32[]{:S(2)}) collective-permute-start(bf16[2,32,512]{2,1,0:T(8,128)(2,1)S(1)} %pad_maximum_fusion), channel_id=1, source_target_pairs={{0,8},{1,9},{2,10},{3,11},{4,12},{5,13},{6,14},{7,15},{8,0},{9,1},... | collective-permute-start | bytes 196616 | tf_op jit(solution)/shard_map/ppermute | solution.py:236
  14.2 11.3 %collective-permute-start.2 = (bf16[4,2,32,512]{3,2,1,0:T(8,128)(2,1)S(1)}, bf16[4,2,32,512]{3,2,1,0:T(8,128)(2,1)S(1)}, u32[]{:S(2)}, u32[]{:S(2)}) collective-permute-start(bf16[4,2,32,512]{3,2,1,0:T(8,128)(2,1)S(1)} %get-tuple-element.28), channel_id=1, source_target_pairs={{0,2},{1,3},{2,0},{3,1},{4,6},{5,7},{6,4},{7,5},{8,10},{9,11},{10,... | collective-permute-start | bytes 786440 | tf_op jit(solution)/shard_map/ppermute | solution.py:236
  16.6 8.8 %collective-permute-start.4 = (bf16[4,32,512]{2,1,0:T(8,128)(2,1)S(1)}, bf16[4,32,512]{2,1,0:T(8,128)(2,1)S(1)}, u32[]{:S(2)}, u32[]{:S(2)}) collective-permute-start(bf16[4,32,512]{2,1,0:T(8,128)(2,1)S(1)} %constant_dynamic-update-slice_fusion.refs_0_), channel_id=1, source_target_pairs={{0,2},{1,3},{2,0},{3,1},{4,6},{5,7},{6,4},{7,5},{8,10},{9,11},{10,... | collective-permute-start | bytes 393224 | tf_op jit(solution)/shard_map/ppermute | solution.py:236
  18.2 11.9 %collective-permute-start.5 = (bf16[4,32,512]{2,1,0:T(8,128)(2,1)S(1)}, bf16[4,32,512]{2,1,0:T(8,128)(2,1)S(1)}, u32[]{:S(2)}, u32[]{:S(2)}) collective-permute-start(bf16[4,32,512]{2,1,0:T(8,128)(2,1)S(1)} %constant_dynamic-update-slice_fusion.refs_0_), channel_id=1, source_target_pairs={{0,1},{1,0},{2,3},{3,2},{4,5},{5,4},{6,7},{7,6},{8,9},{9,8},{10,11... | collective-permute-start | bytes 393224 | tf_op jit(solution)/shard_map/ppermute | solution.py:236
  25.5 4.6 %collective-permute-start.6 = (bf16[4,32,512]{2,1,0:T(8,128)(2,1)S(1)}, bf16[4,32,512]{2,1,0:T(8,128)(2,1)S(1)}, u32[]{:S(2)}, u32[]{:S(2)}) collective-permute-start(bf16[4,32,512]{2,1,0:T(8,128)(2,1)S(1)} %collective-permute-done.4.refs_1_), channel_id=1, source_target_pairs={{0,1},{1,0},{2,3},{3,2},{4,5},{5,4},{6,7},{7,6},{8,9},{9,8},{10,11... | collective-permute-start | bytes 393224 | tf_op jit(solution)/shard_map/ppermute | solution.py:236
  25.6 8.2 %collective-permute-start.7 = (bf16[2,32,512]{2,1,0:T(8,128)(2,1)S(1)}, bf16[2,32,512]{2,1,0:T(8,128)(2,1)S(1)}, u32[]{:S(2)}, u32[]{:S(2)}) collective-permute-start(bf16[2,32,512]{2,1,0:T(8,128)(2,1)S(1)} %get-tuple-element.39), channel_id=1, source_target_pairs={{0,4},{1,5},{2,6},{3,7},{4,0},{5,1},{6,2},{7,3},{8,12},{9,13},{10,... | collective-permute-start | bytes 196616 | tf_op jit(solution)/shard_map/ppermute | solution.py:236
  26.1 7.7 %collective-permute-start.8 = (bf16[2,32,512]{2,1,0:T(8,128)(2,1)S(1)}, bf16[2,32,512]{2,1,0:T(8,128)(2,1)S(1)}, u32[]{:S(2)}, u32[]{:S(2)}) collective-permute-start(bf16[2,32,512]{2,1,0:T(8,128)(2,1)S(1)} %get-tuple-element.41), channel_id=1, source_target_pairs={{0,8},{1,9},{2,10},{3,11},{4,12},{5,13},{6,14},{7,15},{8,0},{9,1},... | collective-permute-start | bytes 196616 | tf_op jit(solution)/shard_map/ppermute | solution.py:236
  27.9 6.4 %collective-permute-start.9 = (bf16[2,32,512]{2,1,0:T(8,128)(2,1)S(1)}, bf16[2,32,512]{2,1,0:T(8,128)(2,1)S(1)}, u32[]{:S(2)}, u32[]{:S(2)}) collective-permute-start(bf16[2,32,512]{2,1,0:T(8,128)(2,1)S(1)} %get-tuple-element.40), channel_id=1, source_target_pairs={{0,12},{1,13},{2,14},{3,15},{4,8},{5,9},{6,10},{7,11},{8,4},{9,5},... | collective-permute-start | bytes 196616 | tf_op jit(solution)/shard_map/ppermute | solution.py:236

commit v11 on v10

--- a/solution.py
+++ b/solution.py
@@ -163,21 +163,18 @@
     fill(near_ref, half, place_ref, parts_ref, mate_ref, 0)
 
 
-def project_kernel(shape, route_vmem, tiles_ref, *refs):
-    far, wide, cores = shape
-    columns, refs = refs[: wide * cores], refs[wide * cores :]
+def project_kernel(places, route_vmem, tiles_ref, *refs):
+    columns, refs = refs[: len(places)], refs[len(places) :]
     proj_ref, route_ref, lines_ref, flat_ref, sems = refs
     (started,) = copies([(route_vmem, route_ref)], sems)
     crossed, blocks = route_ref.shape
     kinds = tiles_ref.shape[0]
     height = columns[0].shape[1]
     rows = lines_ref.shape[0]
-    dense = far * len(columns) * kinds <= crossed * blocks
-    for n, ref in enumerate(columns):
-        core, x = n // wide, n % wide
-        for z in range(far):
-            away = (z * wide + x) * cores + core
-            lines_ref[away * height : (away + 1) * height, :] = ref[z]
+    dense = rows // height * kinds <= crossed * blocks
+    for ref, aways in zip(columns, places):
+        for n, away in enumerate(aways):
+            lines_ref[away * height : (away + 1) * height, :] = ref[n]
     if dense:
         for t in range(kinds):
             flat_ref[t * rows : (t + 1) * rows, :] = jnp.dot(lines_ref[...], tiles_ref[t], preferred_element_type=jnp.float32)
@@ -261,7 +258,11 @@
     def hop(array, offset):
         return jnp.concatenate([array, swap(array, offset)], axis=0)
 
-    offsets = [z * wide * cores for z in powers(far)]
+    along_z = [z * wide * cores for z in reversed(powers(far))]
+    offsets = along_z[:1] + [x * cores for x in powers(wide)] + along_z[1:]
+    away = [0]
+    for offset in offsets[:-1]:
+        away += [a ^ offset for a in away]
     gathered = hop(volume, offsets[0])
 
     sums, wave, tiles_near, images_near, place_rows, route_rows = call(
@@ -304,7 +305,7 @@
         "insert",
     )
     send, gathered = lax.optimization_barrier((send, gathered))
-    for offset in offsets[1:]:
+    for offset in offsets[1:-1]:
         gathered = hop(gathered, offset)
     beyond, mine = call(
         keep_kernel,
@@ -317,8 +318,9 @@
         "keep",
     )
     held, _ = lax.optimization_barrier((gathered, beyond))
-    columns = [gathered] + [swap(held, x * cores) for x in range(1, wide)]
+    columns = [gathered, swap(held, offsets[-1])]
     columns += [swap(column, 1) for column in columns]
+    places = [[a ^ last for a in away] for last in (0, offsets[-1], 1, offsets[-1] ^ 1)]
     for x in range(1, wide):
         mine = mine + swap(beyond[(x - 1) * far : x * far], x * cores).astype(f32)
     outgoing = mine.astype(bf16)
@@ -328,7 +330,7 @@
     else:
         flat = pltpu.VMEM((8, LANES), f32)
     (proj,) = call(
-        functools.partial(project_kernel, shape),
+        functools.partial(project_kernel, places),
         [((blocks, height, pixels), f32)],
         [vmem] * (2 + len(columns)),
         (route_rows, tiles_near, *columns),

time: 35.3 us -> 32.8 us (0.929)
  waiting for transfers between devices: 8.61 us -> 5.85 us
  Pallas kernels: 11.4 us -> 11.8 us
    ppermute x10, waiting for transfers between devices: 8.61 us -> 5.85 us  [swap(): lax.ppermute(array, 'slab', [(i, i ^ offset) for i in range(devices)])]
  transfers between devices with their start and end apart: 10 -> 10, of which waited for: 3 -> 4; matrix products, arithmetic and copies ran while one was open for 0% -> 0% of each run, Pallas kernels for 33% -> 36%
where the time goes in v11:
time: 32.8 us; the launch traced here: 32.6 us
  starting transfers between devices  13.4 us (41%)
  Pallas kernels  11.8 us (36%)
  waiting for transfers between devices  5.85 us (18%)
  between operations  0.76 us (2%)
  local copies, waits for them, and re-layouts  0.69 us (2%)
    ppermute x10, starting transfers between devices, swap(): lax.ppermute(array, 'slab', [(i, i ^ offset) for i in range(devices)])  13.4 us
    pallas_call x5, Pallas kernels, call(): pl.pallas_call(kernel, out_shape=tuple((jax.ShapeDtypeStruct(s, t) for s,...  11.8 us
    ppermute x10, waiting for transfers between devices, swap(): lax.ppermute(array, 'slab', [(i, i ^ offset) for i in range(devices)])  5.85 us
    slice x1, local copies, waits for them, and re-layouts, on_device(): return (scores.reshape(count), total[0:1], total[1:2])  0.66 us
  transfers between devices with their start and end apart: 10, of which 4 were waited for; matrix products, arithmetic and copies ran while one was open for 0% of the time, Pallas kernels for 36%

profile of v11, /device:TPU:0, one launch (start us, length us, event | category | flops | bytes accessed | tf_op | source)
XLA Modules:
  0.0 32.6 jit_solution(4599782103955412167)
XLA Ops:
  0.6 4.1 %collective-permute-start = (bf16[1,32,512]{2,1,0:T(8,128)(2,1)}, bf16[1,32,512]{2,1,0:T(8,128)(2,1)S(1)}, u32[]{:S(2)}, u32[]{:S(2)}) collective-permute-start(bf16[1,32,512]{2,1,0:T(8,128)(2,1)} %param.8), channel_id=1, source_target_pairs={{0,8},{1,9},{2,10},{3,11},{4,12},{5,13},{6,14},{7,15},{8,0},{9,1},... | collective-permute-start | bytes 98312 | tf_op jit(solution)/shard_map/ppermute | solution.py:233
  4.7 2.9 %sums.1 = (bf16[1024,256]{1,0:T(8,128)(2,1)S(1)}, f32[128,32,256]{2,1,0:T(8,128)S(1)}, bf16[8,512,256]{2,1,0:T(8,128)(2,1)S(1)}, bf16[128,32,256]{2,1,0:T(8,128)...) custom-call(s32[8,16]{1,0:T(8,128)} %bitcast.18, s32[8,16]{1,0:T(8,128)} %bitcast.19, s32[16]{0:T(128)} %block_hbm.3, ...), custom_call_target="tpu_custom_call" | custom-call | bytes 10485760 | tf_op jit(solution)/shard_map/sums/pallas_call | solution.py:247
  7.6 0.0 copy-start
  7.7 3.2 %insert.1 = (bf16[8,2,32,512]{3,2,1,0:T(8,128)(2,1)S(1)}, f32[8256,512]{1,0:T(8,128)S(1)}) custom-call(s32[16,16]{1,0:T(8,128)S(1)} %get-tuple-element.22.place_vmem, bf16[1024,256]{1,0:T(8,128)(2,1)S(1)} %get-tuple-element.23.sums_ref, bf16[8,512,256]{2,1,0:T(8,128)(2,1)S(1)} %get-tuple-element.21.tiles_ref), custom_call_target="tpu_custom_call" | custom-call | flops 2147483648 | bytes 8388608 | tf_op jit(solution)/shard_map/insert/pallas_call | solution.py:247
  10.9 0.0 collective-permute-done
  10.9 0.0 copy-done
  10.9 0.1 collective-permute-start.1
  11.0 1.6 %collective-permute-start.3 = (bf16[2,32,512]{2,1,0:T(8,128)(2,1)S(1)}, bf16[2,32,512]{2,1,0:T(8,128)(2,1)S(1)}, u32[]{:S(2)}, u32[]{:S(2)}) collective-permute-start(bf16[2,32,512]{2,1,0:T(8,128)(2,1)S(1)} %pad_maximum_fusion), channel_id=1, source_target_pairs={{0,2},{1,3},{2,0},{3,1},{4,6},{5,7},{6,4},{7,5},{8,10},{9,11},{10,... | collective-permute-start | bytes 196616 | tf_op jit(solution)/shard_map/ppermute | solution.py:233
  12.6 0.3 %collective-permute-done.1.mate_ref = bf16[8,2,32,512]{3,2,1,0:T(8,128)(2,1)S(1)} collective-permute-done((bf16[8,2,32,512]{3,2,1,0:T(8,128)(2,1)S(1)}, bf16[8,2,32,512]{3,2,1,0:T(8,128)(2,1)S(1)}, u32[]{:S(2)}, u32[]{:S(2)}) %collective-permute-start.1) | collective-permute-done | bytes 524320 | tf_op jit(solution)/shard_map/ppermute | solution.py:233
  12.9 1.5 %keep.1 = (bf16[4,2,32,512]{3,2,1,0:T(8,128)(2,1)S(1)}, f32[4,2,32,512]{3,2,1,0:T(8,128)S(1)}) custom-call(s32[16,16]{1,0:T(8,128)S(1)} %get-tuple-element.22.place_vmem, f32[8256,512]{1,0:T(8,128)S(1)} %get-tuple-element.24.parts_ref, bf16[8,2,32,512]{3,2,1,0:T(8,128)(2,1)S(1)} %collective-permute-done.1.mate_ref), custom_call_target="tpu_custom_call" | custom-call | tf_op jit(solution)/shard_map/keep/pallas_call | solution.py:247
  14.5 1.6 %collective-permute-start.2 = (bf16[4,2,32,512]{3,2,1,0:T(8,128)(2,1)S(1)}, bf16[4,2,32,512]{3,2,1,0:T(8,128)(2,1)S(1)}, u32[]{:S(2)}, u32[]{:S(2)}) collective-permute-start(bf16[4,2,32,512]{3,2,1,0:T(8,128)(2,1)S(1)} %get-tuple-element.28), channel_id=1, source_target_pairs={{0,2},{1,3},{2,0},{3,1},{4,6},{5,7},{6,4},{7,5},{8,10},{9,11},{10,... | collective-permute-start | bytes 786440 | tf_op jit(solution)/shard_map/ppermute | solution.py:233
  16.0 0.0 collective-permute-done.3
  16.1 1.6 %collective-permute-start.4 = (bf16[4,32,512]{2,1,0:T(8,128)(2,1)S(1)}, bf16[4,32,512]{2,1,0:T(8,128)(2,1)S(1)}, u32[]{:S(2)}, u32[]{:S(2)}) collective-permute-start(bf16[4,32,512]{2,1,0:T(8,128)(2,1)S(1)} %constant_dynamic-update-slice_fusion.refs_0_), channel_id=1, source_target_pairs={{0,4},{1,5},{2,6},{3,7},{4,0},{5,1},{6,2},{7,3},{8,12},{9,13},{10,... | collective-permute-start | bytes 393224 | tf_op jit(solution)/shard_map/ppermute | solution.py:233
  17.7 0.0 collective-permute-start.5
  17.7 3.7 %collective-permute-done.4.refs_1_ = bf16[4,32,512]{2,1,0:T(8,128)(2,1)S(1)} collective-permute-done((bf16[4,32,512]{2,1,0:T(8,128)(2,1)S(1)}, bf16[4,32,512]{2,1,0:T(8,128)(2,1)S(1)}, u32[]{:S(2)}, u32[]{:S(2)}) %collective-permute-start.4) | collective-permute-done | bytes 131104 | tf_op jit(solution)/shard_map/ppermute | solution.py:233
  21.4 0.0 collective-permute-start.6
  21.4 1.5 %collective-permute-done.2 = bf16[4,2,32,512]{3,2,1,0:T(8,128)(2,1)S(1)} collective-permute-done((bf16[4,2,32,512]{3,2,1,0:T(8,128)(2,1)S(1)}, bf16[4,2,32,512]{3,2,1,0:T(8,128)(2,1)S(1)}, u32[]{:S(2)}, u32[]{:S(2)}) %collective-permute-start.2) | collective-permute-done | bytes 262176 | tf_op jit(solution)/shard_map/ppermute | solution.py:233
  22.9 0.1 fusion.3
  23.0 1.6 %collective-permute-start.7 = (bf16[2,32,512]{2,1,0:T(8,128)(2,1)S(1)}, bf16[2,32,512]{2,1,0:T(8,128)(2,1)S(1)}, u32[]{:S(2)}, u32[]{:S(2)}) collective-permute-start(bf16[2,32,512]{2,1,0:T(8,128)(2,1)S(1)} %get-tuple-element.39), channel_id=1, source_target_pairs={{0,4},{1,5},{2,6},{3,7},{4,0},{5,1},{6,2},{7,3},{8,12},{9,13},{10,... | collective-permute-start | bytes 196616 | tf_op jit(solution)/shard_map/ppermute | solution.py:233
  24.7 0.3 %collective-permute-start.8 = (bf16[2,32,512]{2,1,0:T(8,128)(2,1)S(1)}, bf16[2,32,512]{2,1,0:T(8,128)(2,1)S(1)}, u32[]{:S(2)}, u32[]{:S(2)}) collective-permute-start(bf16[2,32,512]{2,1,0:T(8,128)(2,1)S(1)} %get-tuple-element.41), channel_id=1, source_target_pairs={{0,8},{1,9},{2,10},{3,11},{4,12},{5,13},{6,14},{7,15},{8,0},{9,1},... | collective-permute-start | bytes 196616 | tf_op jit(solution)/shard_map/ppermute | solution.py:233
  25.0 2.5 %collective-permute-start.9 = (bf16[2,32,512]{2,1,0:T(8,128)(2,1)S(1)}, bf16[2,32,512]{2,1,0:T(8,128)(2,1)S(1)}, u32[]{:S(2)}, u32[]{:S(2)}) collective-permute-start(bf16[2,32,512]{2,1,0:T(8,128)(2,1)S(1)} %get-tuple-element.40), channel_id=1, source_target_pairs={{0,12},{1,13},{2,14},{3,15},{4,8},{5,9},{6,10},{7,11},{8,4},{9,5},... | collective-permute-start | bytes 196616 | tf_op jit(solution)/shard_map/ppermute | solution.py:233
  27.5 0.0 collective-permute-done.5.refs_2_
  27.5 0.0 collective-permute-done.6.refs_3_
  27.5 1.8 %project.1.proj_ref = f32[16,32,256]{2,1,0:T(8,128)S(1)} custom-call(s32[8,16]{1,0:T(8,128)S(1)} %get-tuple-element.20.route_vmem, bf16[8,512,256]{2,1,0:T(8,128)(2,1)S(1)} %get-tuple-element.21.tiles_ref, bf16[4,32,512]{2,1,0:T(8,128)(2,1)S(1)} %constant_dynamic-update-slice_fusion.refs_0_, bf16[4,32,512]{2,1,0:T(8,128)(2,1)S(1)} %collective-permute-done.4.refs_1_, ...), custom_call_target="tpu_custom_call" | custom-call | tf_op jit(solution)/shard_map/project/pallas_call | solution.py:247
  29.3 2.3 %scores.1 = f32[1,128]{1,0:T(1,128)} custom-call(s32[16]{0:T(128)} %block_hbm.3, f32[32,256]{1,0:T(8,128)} %noise_hbm.3, f32[16,32,256]{2,1,0:T(8,128)S(1)} %project.1.proj_ref, f32[128,32,256]{2,1,0:T(8,128)S(1)} %get-tuple-element.35.wave_ref, bf16[128,32,256]{2,1,0:T(8,128)(2,1)S(1)} %get-tuple-element.36.images_ref), custom_call_target="tpu_custom_call" | custom-call | tf_op jit(solution)/shard_map/scores/pallas_call | solution.py:247
  31.6 0.0 collective-permute-done.7
  31.6 0.3 collective-permute-done.8
  31.9 0.0 collective-permute-done.9
  31.9 0.7 %fusion.4 = (f32[1,32,512]{2,1,0:T(8,128)}, f32[1,32,512]{2,1,0:T(8,128)}) fusion(f32[2,32,512]{2,1,0:T(8,128)S(1)} %fusion.2), kind=kLoop, calls=%fused_computation.12 | loop fusion | bytes 262144 | tf_op jit(solution)/shard_map/slice | solution.py:356
  (5 shorter events, 0.1 us)
Async XLA Ops:
  0.6 10.3 %collective-permute-start = (bf16[1,32,512]{2,1,0:T(8,128)(2,1)}, bf16[1,32,512]{2,1,0:T(8,128)(2,1)S(1)}, u32[]{:S(2)}, u32[]{:S(2)}) collective-permute-start(bf16[1,32,512]{2,1,0:T(8,128)(2,1)} %param.8), channel_id=1, source_target_pairs={{0,8},{1,9},{2,10},{3,11},{4,12},{5,13},{6,14},{7,15},{8,0},{9,1},... | collective-permute-start | bytes 98312 | tf_op jit(solution)/shard_map/ppermute | solution.py:233
  7.6 3.3 %copy-start = (bf16[1,32,512]{2,1,0:T(8,128)(2,1)S(1)}, bf16[1,32,512]{2,1,0:T(8,128)(2,1)}, u32[]{:S(2)}) copy-start(bf16[1,32,512]{2,1,0:T(8,128)(2,1)} %param.8) | copy-start | bytes 98308
  10.9 2.0 %collective-permute-start.1 = (bf16[8,2,32,512]{3,2,1,0:T(8,128)(2,1)S(1)}, bf16[8,2,32,512]{3,2,1,0:T(8,128)(2,1)S(1)}, u32[]{:S(2)}, u32[]{:S(2)}) collective-permute-start(bf16[8,2,32,512]{3,2,1,0:T(8,128)(2,1)S(1)} %get-tuple-element.26), channel_id=1, source_target_pairs={{0,1},{1,0},{2,3},{3,2},{4,5},{5,4},{6,7},{7,6},{8,9},{9,8},{10,11... | collective-permute-start | bytes 1572872 | tf_op jit(solution)/shard_map/ppermute | solution.py:233
  11.0 5.0 %collective-permute-start.3 = (bf16[2,32,512]{2,1,0:T(8,128)(2,1)S(1)}, bf16[2,32,512]{2,1,0:T(8,128)(2,1)S(1)}, u32[]{:S(2)}, u32[]{:S(2)}) collective-permute-start(bf16[2,32,512]{2,1,0:T(8,128)(2,1)S(1)} %pad_maximum_fusion), channel_id=1, source_target_pairs={{0,2},{1,3},{2,0},{3,1},{4,6},{5,7},{6,4},{7,5},{8,10},{9,11},{10,... | collective-permute-start | bytes 196616 | tf_op jit(solution)/shard_map/ppermute | solution.py:233
  14.5 8.4 %collective-permute-start.2 = (bf16[4,2,32,512]{3,2,1,0:T(8,128)(2,1)S(1)}, bf16[4,2,32,512]{3,2,1,0:T(8,128)(2,1)S(1)}, u32[]{:S(2)}, u32[]{:S(2)}) collective-permute-start(bf16[4,2,32,512]{3,2,1,0:T(8,128)(2,1)S(1)} %get-tuple-element.28), channel_id=1, source_target_pairs={{0,2},{1,3},{2,0},{3,1},{4,6},{5,7},{6,4},{7,5},{8,10},{9,11},{10,... | collective-permute-start | bytes 786440 | tf_op jit(solution)/shard_map/ppermute | solution.py:233
  16.1 5.3 %collective-permute-start.4 = (bf16[4,32,512]{2,1,0:T(8,128)(2,1)S(1)}, bf16[4,32,512]{2,1,0:T(8,128)(2,1)S(1)}, u32[]{:S(2)}, u32[]{:S(2)}) collective-permute-start(bf16[4,32,512]{2,1,0:T(8,128)(2,1)S(1)} %constant_dynamic-update-slice_fusion.refs_0_), channel_id=1, source_target_pairs={{0,4},{1,5},{2,6},{3,7},{4,0},{5,1},{6,2},{7,3},{8,12},{9,13},{10,... | collective-permute-start | bytes 393224 | tf_op jit(solution)/shard_map/ppermute | solution.py:233
  17.7 9.8 %collective-permute-start.5 = (bf16[4,32,512]{2,1,0:T(8,128)(2,1)S(1)}, bf16[4,32,512]{2,1,0:T(8,128)(2,1)S(1)}, u32[]{:S(2)}, u32[]{:S(2)}) collective-permute-start(bf16[4,32,512]{2,1,0:T(8,128)(2,1)S(1)} %constant_dynamic-update-slice_fusion.refs_0_), channel_id=1, source_target_pairs={{0,1},{1,0},{2,3},{3,2},{4,5},{5,4},{6,7},{7,6},{8,9},{9,8},{10,11... | collective-permute-start | bytes 393224 | tf_op jit(solution)/shard_map/ppermute | solution.py:233
  21.4 6.1 %collective-permute-start.6 = (bf16[4,32,512]{2,1,0:T(8,128)(2,1)S(1)}, bf16[4,32,512]{2,1,0:T(8,128)(2,1)S(1)}, u32[]{:S(2)}, u32[]{:S(2)}) collective-permute-start(bf16[4,32,512]{2,1,0:T(8,128)(2,1)S(1)} %collective-permute-done.4.refs_1_), channel_id=1, source_target_pairs={{0,1},{1,0},{2,3},{3,2},{4,5},{5,4},{6,7},{7,6},{8,9},{9,8},{10,11... | collective-permute-start | bytes 393224 | tf_op jit(solution)/shard_map/ppermute | solution.py:233
  23.0 8.5 %collective-permute-start.7 = (bf16[2,32,512]{2,1,0:T(8,128)(2,1)S(1)}, bf16[2,32,512]{2,1,0:T(8,128)(2,1)S(1)}, u32[]{:S(2)}, u32[]{:S(2)}) collective-permute-start(bf16[2,32,512]{2,1,0:T(8,128)(2,1)S(1)} %get-tuple-element.39), channel_id=1, source_target_pairs={{0,4},{1,5},{2,6},{3,7},{4,0},{5,1},{6,2},{7,3},{8,12},{9,13},{10,... | collective-permute-start | bytes 196616 | tf_op jit(solution)/shard_map/ppermute | solution.py:233
  24.7 7.2 %collective-permute-start.8 = (bf16[2,32,512]{2,1,0:T(8,128)(2,1)S(1)}, bf16[2,32,512]{2,1,0:T(8,128)(2,1)S(1)}, u32[]{:S(2)}, u32[]{:S(2)}) collective-permute-start(bf16[2,32,512]{2,1,0:T(8,128)(2,1)S(1)} %get-tuple-element.41), channel_id=1, source_target_pairs={{0,8},{1,9},{2,10},{3,11},{4,12},{5,13},{6,14},{7,15},{8,0},{9,1},... | collective-permute-start | bytes 196616 | tf_op jit(solution)/shard_map/ppermute | solution.py:233
  25.0 6.9 %collective-permute-start.9 = (bf16[2,32,512]{2,1,0:T(8,128)(2,1)S(1)}, bf16[2,32,512]{2,1,0:T(8,128)(2,1)S(1)}, u32[]{:S(2)}, u32[]{:S(2)}) collective-permute-start(bf16[2,32,512]{2,1,0:T(8,128)(2,1)S(1)} %get-tuple-element.40), channel_id=1, source_target_pairs={{0,12},{1,13},{2,14},{3,15},{4,8},{5,9},{6,10},{7,11},{8,4},{9,5},... | collective-permute-start | bytes 196616 | tf_op jit(solution)/shard_map/ppermute | solution.py:233

commit v12 on v11

--- a/solution.py
+++ b/solution.py
@@ -155,12 +155,22 @@
     fill(send_ref, 0, place_ref, parts_ref)
 
 
-def keep_kernel(place_vmem, parts_ref, mate_ref, far_ref, near_ref, place_ref, sems):
+def far_kernel(place_vmem, parts_ref, mate_ref, main_ref, own_ref, place_ref, sems):
     (started,) = copies([(place_vmem, place_ref)], sems)
-    half, far = place_ref.shape[0] // 2, near_ref.shape[0]
+    half, far = place_ref.shape[0] // 2, main_ref.shape[1] + 1
     started.wait()
-    fill(far_ref, half + far, place_ref, parts_ref, mate_ref, far)
-    fill(near_ref, half, place_ref, parts_ref, mate_ref, 0)
+    for n in range(main_ref.shape[0]):
+        slot = (n + 1) * far
+        fill(main_ref.at[n], half + slot + 1, place_ref, parts_ref, mate_ref, slot + 1)
+    for n in range(main_ref.shape[0]):
+        slot = (n + 1) * far
+        fill(own_ref.at[pl.ds(n, 1)], half + slot, place_ref, parts_ref, mate_ref, slot)
+
+
+def near_kernel(place_vmem, parts_ref, mate_ref, near_ref, place_ref, sems):
+    (started,) = copies([(place_vmem, place_ref)], sems)
+    started.wait()
+    fill(near_ref, place_ref.shape[0] // 2, place_ref, parts_ref, mate_ref)
 
 
 def project_kernel(places, route_vmem, tiles_ref, *refs):
@@ -307,22 +317,31 @@
     send, gathered = lax.optimization_barrier((send, gathered))
     for offset in offsets[1:-1]:
         gathered = hop(gathered, offset)
-    beyond, mine = call(
-        keep_kernel,
-        [(((wide - 1) * far, *place), bf16), ((far, *place), f32)],
+    mate = swap(send, 1)
+    place_scratch = [pltpu.SMEM((devices, blocks), i32), pltpu.SemaphoreType.DMA((1,))]
+    main, own = call(
+        far_kernel,
+        [((wide - 1, far - 1, *place), bf16), ((wide - 1, *place), bf16)],
         [vmem] * 3,
-        (place_rows, parts, swap(send, 1)),
-        [pltpu.SMEM((devices, blocks), i32), pltpu.SemaphoreType.DMA((1,))],
-        0,
-        0,
-        "keep",
-    )
-    held, _ = lax.optimization_barrier((gathered, beyond))
+        (place_rows, parts, mate),
+        place_scratch,
+        0,
+        0,
+        "far",
+    )
+    (near,) = call(
+        near_kernel, [((far, *place), f32)], [vmem] * 3, (place_rows, parts, mate), place_scratch, 0, 0, "near"
+    )
+    held, _ = lax.optimization_barrier((gathered, main))
     columns = [gathered, swap(held, offsets[-1])]
     columns += [swap(column, 1) for column in columns]
     places = [[a ^ last for a in away] for last in (0, offsets[-1], 1, offsets[-1] ^ 1)]
+    mine = near[1:]
     for x in range(1, wide):
-        mine = mine + swap(beyond[(x - 1) * far : x * far], x * cores).astype(f32)
+        mine = mine + swap(main[x - 1], x * cores).astype(f32)
+    total = near[0]
+    for x in range(1, wide):
+        total = total + swap(own[x - 1], x * cores).astype(f32)
     outgoing = mine.astype(bf16)
     _, *columns = lax.optimization_barrier((outgoing, *columns))
     if devices * kinds <= blocks * crossed:
@@ -350,9 +369,11 @@
         0,
         "scores",
     )
-    total = mine[0]
     for z in range(1, far):
-        total = total + swap(outgoing[z], z * wide * cores).astype(f32)
+        came = swap(outgoing[z - 1], z * wide * cores)
+        if z == far - 1:
+            came, scores = lax.optimization_barrier((came, scores))
+        total = total + came.astype(f32)
     return scores.reshape(count), total[0:1], total[1:2]
 
 

time: 32.8 us -> 31.8 us (0.970)
  waiting for transfers between devices: 5.85 us -> 2.86 us
  starting transfers between devices: 13.4 us -> 14.7 us
  Pallas kernels: 11.8 us -> 12.4 us
    ppermute x10 -> x11, waiting for transfers between devices: 5.85 us -> 2.86 us  [swap(): lax.ppermute(array, 'slab', [(i, i ^ offset) for i in range(devices)])]
    ppermute x10 -> x11, starting transfers between devices: 13.4 us -> 14.7 us  [swap(): lax.ppermute(array, 'slab', [(i, i ^ offset) for i in range(devices)])]
    pallas_call x5 -> x6, Pallas kernels: 11.8 us -> 12.4 us  [call(): pl.pallas_call(kernel, out_shape=tuple((jax.ShapeDtypeStruct(s, t) for s,...]
  transfers between devices with their start and end apart: 10 -> 11, of which waited for: 4 -> 4; matrix products, arithmetic and copies ran while one was open for 0% -> 0% of each run, Pallas kernels for 36% -> 39%
where the time goes in v12:
time: 31.8 us; the launch traced here: 31.6 us
  starting transfers between devices  14.7 us (46%)
  Pallas kernels  12.4 us (39%)
  waiting for transfers between devices  2.86 us (9%)
  between operations  0.76 us (2%)
  local copies, waits for them, and re-layouts  0.69 us (2%)
    ppermute x11, starting transfers between devices, swap(): lax.ppermute(array, 'slab', [(i, i ^ offset) for i in range(devices)])  14.7 us
    pallas_call x6, Pallas kernels, call(): pl.pallas_call(kernel, out_shape=tuple((jax.ShapeDtypeStruct(s, t) for s,...  12.4 us
    ppermute x11, waiting for transfers between devices, swap(): lax.ppermute(array, 'slab', [(i, i ^ offset) for i in range(devices)])  2.86 us
    slice x1, local copies, waits for them, and re-layouts, on_device(): return (scores.reshape(count), total[0:1], total[1:2])  0.66 us
  transfers between devices with their start and end apart: 11, of which 4 were waited for; matrix products, arithmetic and copies ran while one was open for 0% of the time, Pallas kernels for 39%

profile of v12, /device:TPU:0, one launch (start us, length us, event | category | flops | bytes accessed | tf_op | source)
XLA Modules:
  0.0 31.6 jit_solution(4321022124604236048)
XLA Ops:
  0.6 4.1 %collective-permute-start = (bf16[1,32,512]{2,1,0:T(8,128)(2,1)}, bf16[1,32,512]{2,1,0:T(8,128)(2,1)S(1)}, u32[]{:S(2)}, u32[]{:S(2)}) collective-permute-start(bf16[1,32,512]{2,1,0:T(8,128)(2,1)} %param.8), channel_id=1, source_target_pairs={{0,8},{1,9},{2,10},{3,11},{4,12},{5,13},{6,14},{7,15},{8,0},{9,1},... | collective-permute-start | bytes 98312 | tf_op jit(solution)/shard_map/ppermute | solution.py:243
  4.7 2.9 %sums.1 = (bf16[1024,256]{1,0:T(8,128)(2,1)S(1)}, f32[128,32,256]{2,1,0:T(8,128)S(1)}, bf16[8,512,256]{2,1,0:T(8,128)(2,1)S(1)}, bf16[128,32,256]{2,1,0:T(8,128)...) custom-call(s32[8,16]{1,0:T(8,128)} %bitcast.24, s32[8,16]{1,0:T(8,128)} %bitcast.25, s32[16]{0:T(128)} %block_hbm.3, ...), custom_call_target="tpu_custom_call" | custom-call | bytes 10485760 | tf_op jit(solution)/shard_map/sums/pallas_call | solution.py:257
  7.6 0.0 copy-start
  7.7 3.2 %insert.1 = (bf16[8,2,32,512]{3,2,1,0:T(8,128)(2,1)S(1)}, f32[8256,512]{1,0:T(8,128)S(1)}) custom-call(s32[16,16]{1,0:T(8,128)S(1)} %get-tuple-element.22.place_vmem, bf16[1024,256]{1,0:T(8,128)(2,1)S(1)} %get-tuple-element.23.sums_ref, bf16[8,512,256]{2,1,0:T(8,128)(2,1)S(1)} %get-tuple-element.24.tiles_ref), custom_call_target="tpu_custom_call" | custom-call | flops 2147483648 | bytes 8388608 | tf_op jit(solution)/shard_map/insert/pallas_call | solution.py:257
  10.9 0.0 collective-permute-done
  10.9 0.0 copy-done
  10.9 0.1 collective-permute-start.1
  11.0 1.6 %collective-permute-start.4 = (bf16[2,32,512]{2,1,0:T(8,128)(2,1)S(1)}, bf16[2,32,512]{2,1,0:T(8,128)(2,1)S(1)}, u32[]{:S(2)}, u32[]{:S(2)}) collective-permute-start(bf16[2,32,512]{2,1,0:T(8,128)(2,1)S(1)} %pad_maximum_fusion), channel_id=1, source_target_pairs={{0,2},{1,3},{2,0},{3,1},{4,6},{5,7},{6,4},{7,5},{8,10},{9,11},{10,... | collective-permute-start | bytes 196616 | tf_op jit(solution)/shard_map/ppermute | solution.py:243
  12.6 0.3 %collective-permute-done.1.mate_ref = bf16[8,2,32,512]{3,2,1,0:T(8,128)(2,1)S(1)} collective-permute-done((bf16[8,2,32,512]{3,2,1,0:T(8,128)(2,1)S(1)}, bf16[8,2,32,512]{3,2,1,0:T(8,128)(2,1)S(1)}, u32[]{:S(2)}, u32[]{:S(2)}) %collective-permute-start.1) | collective-permute-done | bytes 524320 | tf_op jit(solution)/shard_map/ppermute | solution.py:243
  12.9 1.1 %far.1 = (bf16[1,3,2,32,512]{4,3,2,1,0:T(8,128)(2,1)S(1)}, bf16[1,2,32,512]{3,2,1,0:T(8,128)(2,1)S(1)}) custom-call(s32[16,16]{1,0:T(8,128)S(1)} %get-tuple-element.22.place_vmem, f32[8256,512]{1,0:T(8,128)S(1)} %get-tuple-element.25.parts_ref, bf16[8,2,32,512]{3,2,1,0:T(8,128)(2,1)S(1)} %collective-permute-done.1.mate_ref), custom_call_target="tpu_custom_call" | custom-call | tf_op jit(solution)/shard_map/far/pallas_call | solution.py:257
  14.0 1.6 %collective-permute-start.2 = (bf16[3,2,32,512]{3,2,1,0:T(8,128)(2,1)S(1)}, bf16[3,2,32,512]{3,2,1,0:T(8,128)(2,1)S(1)}, u32[]{:S(2)}, u32[]{:S(2)}) collective-permute-start(bf16[3,2,32,512]{3,2,1,0:T(8,128)(2,1)S(1)} %bitcast.22), channel_id=1, source_target_pairs={{0,2},{1,3},{2,0},{3,1},{4,6},{5,7},{6,4},{7,5},{8,10},{9,11},{10,... | collective-permute-start | bytes 589832 | tf_op jit(solution)/shard_map/ppermute | solution.py:243
  15.6 0.0 collective-permute-done.4
  15.6 1.6 %collective-permute-start.5 = (bf16[4,32,512]{2,1,0:T(8,128)(2,1)S(1)}, bf16[4,32,512]{2,1,0:T(8,128)(2,1)S(1)}, u32[]{:S(2)}, u32[]{:S(2)}) collective-permute-start(bf16[4,32,512]{2,1,0:T(8,128)(2,1)S(1)} %constant_dynamic-update-slice_fusion.refs_0_), channel_id=1, source_target_pairs={{0,4},{1,5},{2,6},{3,7},{4,0},{5,1},{6,2},{7,3},{8,12},{9,13},{10,... | collective-permute-start | bytes 393224 | tf_op jit(solution)/shard_map/ppermute | solution.py:243
  17.2 0.0 collective-permute-start.6
  17.3 1.4 %collective-permute-start.8 = (bf16[2,32,512]{2,1,0:T(8,128)(2,1)S(1)}, bf16[2,32,512]{2,1,0:T(8,128)(2,1)S(1)}, u32[]{:S(2)}, u32[]{:S(2)}) collective-permute-start(bf16[2,32,512]{2,1,0:T(8,128)(2,1)S(1)} %bitcast.23), channel_id=1, source_target_pairs={{0,2},{1,3},{2,0},{3,1},{4,6},{5,7},{6,4},{7,5},{8,10},{9,11},{10,... | collective-permute-start | bytes 196616 | tf_op jit(solution)/shard_map/ppermute | solution.py:243
  18.6 1.1 %near.1 = f32[4,2,32,512]{3,2,1,0:T(8,128)S(1)} custom-call(s32[16,16]{1,0:T(8,128)S(1)} %get-tuple-element.22.place_vmem, f32[8256,512]{1,0:T(8,128)S(1)} %get-tuple-element.25.parts_ref, bf16[8,2,32,512]{3,2,1,0:T(8,128)(2,1)S(1)} %collective-permute-done.1.mate_ref), custom_call_target="tpu_custom_call" | custom-call | tf_op jit(solution)/shard_map/near/pallas_call | solution.py:257
  19.7 1.2 %collective-permute-done.5.refs_1_ = bf16[4,32,512]{2,1,0:T(8,128)(2,1)S(1)} collective-permute-done((bf16[4,32,512]{2,1,0:T(8,128)(2,1)S(1)}, bf16[4,32,512]{2,1,0:T(8,128)(2,1)S(1)}, u32[]{:S(2)}, u32[]{:S(2)}) %collective-permute-start.5) | collective-permute-done | bytes 131104 | tf_op jit(solution)/shard_map/ppermute | solution.py:243
  20.9 0.0 collective-permute-start.7
  20.9 0.7 %collective-permute-done.2 = bf16[3,2,32,512]{3,2,1,0:T(8,128)(2,1)S(1)} collective-permute-done((bf16[3,2,32,512]{3,2,1,0:T(8,128)(2,1)S(1)}, bf16[3,2,32,512]{3,2,1,0:T(8,128)(2,1)S(1)}, u32[]{:S(2)}, u32[]{:S(2)}) %collective-permute-start.2) | collective-permute-done | bytes 196640 | tf_op jit(solution)/shard_map/ppermute | solution.py:243
  21.7 1.5 %collective-permute-start.3 = (bf16[2,32,512]{2,1,0:T(8,128)(2,1)S(1)}, bf16[2,32,512]{2,1,0:T(8,128)(2,1)S(1)}, u32[]{:S(2)}, u32[]{:S(2)}) collective-permute-start(bf16[2,32,512]{2,1,0:T(8,128)(2,1)S(1)} %get-tuple-element.43), channel_id=1, source_target_pairs={{0,12},{1,13},{2,14},{3,15},{4,8},{5,9},{6,10},{7,11},{8,4},{9,5},... | collective-permute-start | bytes 196616 | tf_op jit(solution)/shard_map/ppermute | solution.py:243
  23.2 1.7 %collective-permute-start.10 = (bf16[2,32,512]{2,1,0:T(8,128)(2,1)S(1)}, bf16[2,32,512]{2,1,0:T(8,128)(2,1)S(1)}, u32[]{:S(2)}, u32[]{:S(2)}) collective-permute-start(bf16[2,32,512]{2,1,0:T(8,128)(2,1)S(1)} %get-tuple-element.42), channel_id=1, source_target_pairs={{0,8},{1,9},{2,10},{3,11},{4,12},{5,13},{6,14},{7,15},{8,0},{9,1},... | collective-permute-start | bytes 196616 | tf_op jit(solution)/shard_map/ppermute | solution.py:243
  24.9 0.0 collective-permute-done.6.refs_2_
  24.9 1.3 %collective-permute-start.9 = (bf16[2,32,512]{2,1,0:T(8,128)(2,1)S(1)}, bf16[2,32,512]{2,1,0:T(8,128)(2,1)S(1)}, u32[]{:S(2)}, u32[]{:S(2)}) collective-permute-start(bf16[2,32,512]{2,1,0:T(8,128)(2,1)S(1)} %get-tuple-element.41), channel_id=1, source_target_pairs={{0,4},{1,5},{2,6},{3,7},{4,0},{5,1},{6,2},{7,3},{8,12},{9,13},{10,... | collective-permute-start | bytes 196616 | tf_op jit(solution)/shard_map/ppermute | solution.py:243
  26.2 0.0 collective-permute-done.7.refs_3_
  26.2 1.8 %project.1.proj_ref = f32[16,32,256]{2,1,0:T(8,128)S(1)} custom-call(s32[8,16]{1,0:T(8,128)S(1)} %get-tuple-element.29.route_vmem, bf16[8,512,256]{2,1,0:T(8,128)(2,1)S(1)} %get-tuple-element.24.tiles_ref, bf16[4,32,512]{2,1,0:T(8,128)(2,1)S(1)} %constant_dynamic-update-slice_fusion.refs_0_, bf16[4,32,512]{2,1,0:T(8,128)(2,1)S(1)} %collective-permute-done.5.refs_1_, ...), custom_call_target="tpu_custom_call" | custom-call | tf_op jit(solution)/shard_map/project/pallas_call | solution.py:257
  28.0 2.3 %scores.1 = f32[1,128]{1,0:T(1,128)} custom-call(s32[16]{0:T(128)} %block_hbm.3, f32[32,256]{1,0:T(8,128)} %noise_hbm.3, f32[16,32,256]{2,1,0:T(8,128)S(1)} %project.1.proj_ref, f32[128,32,256]{2,1,0:T(8,128)S(1)} %get-tuple-element.36.wave_ref, bf16[128,32,256]{2,1,0:T(8,128)(2,1)S(1)} %get-tuple-element.37.images_ref), custom_call_target="tpu_custom_call" | custom-call | tf_op jit(solution)/shard_map/scores/pallas_call | solution.py:257
  30.3 0.0 collective-permute-done.3
  30.3 0.0 collective-permute-done.8
  30.3 0.6 %collective-permute-done.10 = bf16[2,32,512]{2,1,0:T(8,128)(2,1)S(1)} collective-permute-done((bf16[2,32,512]{2,1,0:T(8,128)(2,1)S(1)}, bf16[2,32,512]{2,1,0:T(8,128)(2,1)S(1)}, u32[]{:S(2)}, u32[]{:S(2)}) %collective-permute-start.10) | collective-permute-done | bytes 65568 | tf_op jit(solution)/shard_map/ppermute | solution.py:243
  30.9 0.0 collective-permute-done.9
  30.9 0.7 %fusion.5 = (f32[1,32,512]{2,1,0:T(8,128)}, f32[1,32,512]{2,1,0:T(8,128)}) fusion(f32[2,32,512]{2,1,0:T(8,128)S(1)} %fusion.4), kind=kLoop, calls=%fused_computation.13 | loop fusion | bytes 262144 | tf_op jit(solution)/shard_map/slice | solution.py:377
  (6 shorter events, 0.1 us)
Async XLA Ops:
  0.6 10.3 %collective-permute-start = (bf16[1,32,512]{2,1,0:T(8,128)(2,1)}, bf16[1,32,512]{2,1,0:T(8,128)(2,1)S(1)}, u32[]{:S(2)}, u32[]{:S(2)}) collective-permute-start(bf16[1,32,512]{2,1,0:T(8,128)(2,1)} %param.8), channel_id=1, source_target_pairs={{0,8},{1,9},{2,10},{3,11},{4,12},{5,13},{6,14},{7,15},{8,0},{9,1},... | collective-permute-start | bytes 98312 | tf_op jit(solution)/shard_map/ppermute | solution.py:243
  7.6 3.3 %copy-start = (bf16[1,32,512]{2,1,0:T(8,128)(2,1)S(1)}, bf16[1,32,512]{2,1,0:T(8,128)(2,1)}, u32[]{:S(2)}) copy-start(bf16[1,32,512]{2,1,0:T(8,128)(2,1)} %param.8) | copy-start | bytes 98308
  10.9 2.0 %collective-permute-start.1 = (bf16[8,2,32,512]{3,2,1,0:T(8,128)(2,1)S(1)}, bf16[8,2,32,512]{3,2,1,0:T(8,128)(2,1)S(1)}, u32[]{:S(2)}, u32[]{:S(2)}) collective-permute-start(bf16[8,2,32,512]{3,2,1,0:T(8,128)(2,1)S(1)} %get-tuple-element.27), channel_id=1, source_target_pairs={{0,1},{1,0},{2,3},{3,2},{4,5},{5,4},{6,7},{7,6},{8,9},{9,8},{10,11... | collective-permute-start | bytes 1572872 | tf_op jit(solution)/shard_map/ppermute | solution.py:243
  11.0 4.6 %collective-permute-start.4 = (bf16[2,32,512]{2,1,0:T(8,128)(2,1)S(1)}, bf16[2,32,512]{2,1,0:T(8,128)(2,1)S(1)}, u32[]{:S(2)}, u32[]{:S(2)}) collective-permute-start(bf16[2,32,512]{2,1,0:T(8,128)(2,1)S(1)} %pad_maximum_fusion), channel_id=1, source_target_pairs={{0,2},{1,3},{2,0},{3,1},{4,6},{5,7},{6,4},{7,5},{8,10},{9,11},{10,... | collective-permute-start | bytes 196616 | tf_op jit(solution)/shard_map/ppermute | solution.py:243
  14.0 7.6 %collective-permute-start.2 = (bf16[3,2,32,512]{3,2,1,0:T(8,128)(2,1)S(1)}, bf16[3,2,32,512]{3,2,1,0:T(8,128)(2,1)S(1)}, u32[]{:S(2)}, u32[]{:S(2)}) collective-permute-start(bf16[3,2,32,512]{3,2,1,0:T(8,128)(2,1)S(1)} %bitcast.22), channel_id=1, source_target_pairs={{0,2},{1,3},{2,0},{3,1},{4,6},{5,7},{6,4},{7,5},{8,10},{9,11},{10,... | collective-permute-start | bytes 589832 | tf_op jit(solution)/shard_map/ppermute | solution.py:243
  15.6 5.3 %collective-permute-start.5 = (bf16[4,32,512]{2,1,0:T(8,128)(2,1)S(1)}, bf16[4,32,512]{2,1,0:T(8,128)(2,1)S(1)}, u32[]{:S(2)}, u32[]{:S(2)}) collective-permute-start(bf16[4,32,512]{2,1,0:T(8,128)(2,1)S(1)} %constant_dynamic-update-slice_fusion.refs_0_), channel_id=1, source_target_pairs={{0,4},{1,5},{2,6},{3,7},{4,0},{5,1},{6,2},{7,3},{8,12},{9,13},{10,... | collective-permute-start | bytes 393224 | tf_op jit(solution)/shard_map/ppermute | solution.py:243
  17.2 7.7 %collective-permute-start.6 = (bf16[4,32,512]{2,1,0:T(8,128)(2,1)S(1)}, bf16[4,32,512]{2,1,0:T(8,128)(2,1)S(1)}, u32[]{:S(2)}, u32[]{:S(2)}) collective-permute-start(bf16[4,32,512]{2,1,0:T(8,128)(2,1)S(1)} %constant_dynamic-update-slice_fusion.refs_0_), channel_id=1, source_target_pairs={{0,1},{1,0},{2,3},{3,2},{4,5},{5,4},{6,7},{7,6},{8,9},{9,8},{10,11... | collective-permute-start | bytes 393224 | tf_op jit(solution)/shard_map/ppermute | solution.py:243
  17.3 13.0 %collective-permute-start.8 = (bf16[2,32,512]{2,1,0:T(8,128)(2,1)S(1)}, bf16[2,32,512]{2,1,0:T(8,128)(2,1)S(1)}, u32[]{:S(2)}, u32[]{:S(2)}) collective-permute-start(bf16[2,32,512]{2,1,0:T(8,128)(2,1)S(1)} %bitcast.23), channel_id=1, source_target_pairs={{0,2},{1,3},{2,0},{3,1},{4,6},{5,7},{6,4},{7,5},{8,10},{9,11},{10,... | collective-permute-start | bytes 196616 | tf_op jit(solution)/shard_map/ppermute | solution.py:243
  20.9 5.3 %collective-permute-start.7 = (bf16[4,32,512]{2,1,0:T(8,128)(2,1)S(1)}, bf16[4,32,512]{2,1,0:T(8,128)(2,1)S(1)}, u32[]{:S(2)}, u32[]{:S(2)}) collective-permute-start(bf16[4,32,512]{2,1,0:T(8,128)(2,1)S(1)} %collective-permute-done.5.refs_1_), channel_id=1, source_target_pairs={{0,1},{1,0},{2,3},{3,2},{4,5},{5,4},{6,7},{7,6},{8,9},{9,8},{10,11... | collective-permute-start | bytes 393224 | tf_op jit(solution)/shard_map/ppermute | solution.py:243
  21.7 8.5 %collective-permute-start.3 = (bf16[2,32,512]{2,1,0:T(8,128)(2,1)S(1)}, bf16[2,32,512]{2,1,0:T(8,128)(2,1)S(1)}, u32[]{:S(2)}, u32[]{:S(2)}) collective-permute-start(bf16[2,32,512]{2,1,0:T(8,128)(2,1)S(1)} %get-tuple-element.43), channel_id=1, source_target_pairs={{0,12},{1,13},{2,14},{3,15},{4,8},{5,9},{6,10},{7,11},{8,4},{9,5},... | collective-permute-start | bytes 196616 | tf_op jit(solution)/shard_map/ppermute | solution.py:243
  23.2 7.7 %collective-permute-start.10 = (bf16[2,32,512]{2,1,0:T(8,128)(2,1)S(1)}, bf16[2,32,512]{2,1,0:T(8,128)(2,1)S(1)}, u32[]{:S(2)}, u32[]{:S(2)}) collective-permute-start(bf16[2,32,512]{2,1,0:T(8,128)(2,1)S(1)} %get-tuple-element.42), channel_id=1, source_target_pairs={{0,8},{1,9},{2,10},{3,11},{4,12},{5,13},{6,14},{7,15},{8,0},{9,1},... | collective-permute-start | bytes 196616 | tf_op jit(solution)/shard_map/ppermute | solution.py:243
  24.9 6.0 %collective-permute-start.9 = (bf16[2,32,512]{2,1,0:T(8,128)(2,1)S(1)}, bf16[2,32,512]{2,1,0:T(8,128)(2,1)S(1)}, u32[]{:S(2)}, u32[]{:S(2)}) collective-permute-start(bf16[2,32,512]{2,1,0:T(8,128)(2,1)S(1)} %get-tuple-element.41), channel_id=1, source_target_pairs={{0,4},{1,5},{2,6},{3,7},{4,0},{5,1},{6,2},{7,3},{8,12},{9,13},{10,... | collective-permute-start | bytes 196616 | tf_op jit(solution)/shard_map/ppermute | solution.py:243

commit v13 on v12

--- a/solution.py
+++ b/solution.py
@@ -67,7 +67,7 @@
     return started
 
 
-def row_tables(shape, kinds, height, slab, tile, place_ref, route_ref):
+def row_tables(shape, kinds, height, slab, tile, owner, place_ref, route_ref):
     far, wide, cores = shape
     devices, blocks = place_ref.shape
     rows, half = blocks * 2 * height, devices // 2
@@ -82,15 +82,20 @@
         row = tile[r : r + 1, :] * rows + block * (2 * height)
         place = jnp.where(slab[r : r + 1, :] == named, row, place)
     place_ref[...] = place
-    route_ref[...] = (tile * devices + (me ^ slab)) * height
-
-
-def sum_kernel(shape, kinds, slab_hbm, tile_hbm, block_hbm, defocus_hbm, noise_hbm, tiles_hbm, images_hbm,
-               sums_ref, wave_ref, tiles_ref, images_ref, place_ref, route_ref,
-               slab_ref, tile_ref, block_ref, defocus_ref, noise_ref, line_ref, pixel_ref, acc_ref, sems):
+    row = (tile * devices + (me ^ slab)) * height
+    route = jnp.zeros(route_ref.shape, jnp.int32)
+    for k in range(blocks):
+        route = jnp.where(owner == k, row[:, k : k + 1], route)
+    route_ref[...] = route
+
+
+def sum_kernel(shape, kinds, slab_hbm, tile_hbm, block_hbm, owner_hbm, defocus_hbm, noise_hbm, tiles_hbm, images_hbm,
+               sums_ref, wave_ref, tiles_ref, images_ref, noise_ref, place_ref, route_ref,
+               slab_ref, tile_ref, block_ref, owner_ref, defocus_ref, line_ref, pixel_ref, acc_ref, sems):
     count = images_ref.shape[0]
     part = count // CHUNKS
-    small = [(defocus_hbm, defocus_ref), (block_hbm, block_ref), (noise_hbm, noise_ref), (slab_hbm, slab_ref), (tile_hbm, tile_ref)]
+    small = [(defocus_hbm, defocus_ref), (block_hbm, block_ref), (noise_hbm, noise_ref)]
+    small += [(slab_hbm, slab_ref), (tile_hbm, tile_ref), (owner_hbm, owner_ref)]
     large = [(images_hbm.at[pl.ds(n * part, part)], images_ref.at[pl.ds(n * part, part)]) for n in range(CHUNKS)]
     started = copies(small + large, sems)
     last = pltpu.make_async_copy(tiles_hbm, tiles_ref, sems.at[len(started)])
@@ -101,7 +106,7 @@
     for copy in started[: len(small)]:
         copy.wait()
     tables(defocus_ref, height, pixels, line_ref, pixel_ref)
-    row_tables(shape, kinds, height, slab_ref[...], tile_ref[...], place_ref, route_ref)
+    row_tables(shape, kinds, height, slab_ref[...], tile_ref[...], owner_ref[...], place_ref, route_ref)
     for b in range(batches):
         if b % (batches // CHUNKS) == 0:
             started[len(small) + b // (batches // CHUNKS)].wait()
@@ -123,7 +128,7 @@
     last.wait()
 
 
-def fill(ref, start, place_ref, parts_ref, mate_ref=None, offset=0):
+def fill(ref, start, place_ref, parts_ref, mate_ref=None):
     sides, height, length = ref.shape[1:]
 
     def step(slot, carry):
@@ -134,14 +139,14 @@
             acc = part if acc is None else acc + part
         acc = acc.reshape(sides, height, length)
         if mate_ref is not None:
-            acc = acc + mate_ref[offset + slot].astype(jnp.float32)
+            acc = acc + mate_ref[slot].astype(jnp.float32)
         ref[slot] = acc.astype(ref.dtype)
         return carry
 
     lax.fori_loop(0, ref.shape[0], step, 0)
 
 
-def insert_kernel(place_vmem, sums_ref, tiles_ref, send_ref, parts_ref, place_ref, sems):
+def insert_kernel(place_vmem, sums_ref, tiles_ref, send_ref, far_ref, parts_ref, place_ref, sems):
     (started,) = copies([(place_vmem, place_ref)], sems)
     kinds = tiles_ref.shape[0]
     rows = sums_ref.shape[0]
@@ -153,18 +158,8 @@
         )
     started.wait()
     fill(send_ref, 0, place_ref, parts_ref)
-
-
-def far_kernel(place_vmem, parts_ref, mate_ref, main_ref, own_ref, place_ref, sems):
-    (started,) = copies([(place_vmem, place_ref)], sems)
-    half, far = place_ref.shape[0] // 2, main_ref.shape[1] + 1
-    started.wait()
-    for n in range(main_ref.shape[0]):
-        slot = (n + 1) * far
-        fill(main_ref.at[n], half + slot + 1, place_ref, parts_ref, mate_ref, slot + 1)
-    for n in range(main_ref.shape[0]):
-        slot = (n + 1) * far
-        fill(own_ref.at[pl.ds(n, 1)], half + slot, place_ref, parts_ref, mate_ref, slot)
+    devices = place_ref.shape[0]
+    fill(far_ref, devices - far_ref.shape[0], place_ref, parts_ref)
 
 
 def near_kernel(place_vmem, parts_ref, mate_ref, near_ref, place_ref, sems):
@@ -177,11 +172,11 @@
     columns, refs = refs[: len(places)], refs[len(places) :]
     proj_ref, route_ref, lines_ref, flat_ref, sems = refs
     (started,) = copies([(route_vmem, route_ref)], sems)
-    crossed, blocks = route_ref.shape
+    crossed, batches = route_ref.shape
     kinds = tiles_ref.shape[0]
     height = columns[0].shape[1]
     rows = lines_ref.shape[0]
-    dense = rows // height * kinds <= crossed * blocks
+    dense = rows // height * kinds <= crossed * batches
     for ref, aways in zip(columns, places):
         for n, away in enumerate(aways):
             lines_ref[away * height : (away + 1) * height, :] = ref[n]
@@ -190,33 +185,29 @@
             flat_ref[t * rows : (t + 1) * rows, :] = jnp.dot(lines_ref[...], tiles_ref[t], preferred_element_type=jnp.float32)
     started.wait()
 
-    def project(k, carry):
+    def project(b, carry):
         acc = None
         for r in range(crossed):
-            at = route_ref[r, k]
+            at = route_ref[r, b]
             if dense:
                 part = flat_ref[pl.ds(pl.multiple_of(at, height), height), :]
             else:
                 t, at = at // rows, pl.multiple_of(lax.rem(at, rows), height)
                 part = jnp.dot(lines_ref[pl.ds(at, height), :], tiles_ref[t], preferred_element_type=jnp.float32)
             acc = part if acc is None else acc + part
-        proj_ref[k] = acc
+        proj_ref[b] = acc
         return carry
 
-    lax.fori_loop(0, blocks, project, 0, unroll=dense)
-
-
-def score_kernel(block_hbm, noise_hbm, proj_ref, wave_ref, images_ref, score_ref, block_ref, noise_ref, part_ref, sems):
-    started = copies([(block_hbm, block_ref), (noise_hbm, noise_ref)], sems)
+    lax.fori_loop(0, batches, project, 0, unroll=dense)
+
+
+def score_kernel(noise_ref, proj_ref, wave_ref, images_ref, score_ref, part_ref):
     height, pixels = noise_ref.shape
-    batches = block_ref.shape[0]
     count = images_ref.shape[0]
-    size = count // batches
-    for copy in started:
-        copy.wait()
+    size = count // proj_ref.shape[0]
     noise = noise_ref[...]
-    for b in range(batches):
-        proj = proj_ref[block_ref[b]]
+    for b in range(count // size):
+        proj = proj_ref[b]
         for j in range(size):
             i = b * size + j
             residual = images_ref[i].astype(jnp.float32) - wave_ref[i] * proj
@@ -247,8 +238,6 @@
     params = pltpu.CompilerParams(vmem_limit_bytes=VMEM_BYTES)
     f32, bf16 = jnp.float32, jnp.bfloat16
     i32 = jnp.int32
-    block_scratch = pltpu.SMEM(batch_block.shape, jnp.int32)
-    noise_scratch = pltpu.VMEM((height, pixels), f32)
 
     def call(kernel, outs, inputs, operands, scratch, flops, moved, name):
         operands = [
@@ -275,28 +264,30 @@
         away += [a ^ offset for a in away]
     gathered = hop(volume, offsets[0])
 
-    sums, wave, tiles_near, images_near, place_rows, route_rows = call(
+    batches = batch_block.shape[0]
+    sums, wave, tiles_near, images_near, noise_near, place_rows, route_rows = call(
         functools.partial(sum_kernel, shape, kinds),
         [
             ((rows, pixels), bf16),
             (images.shape, f32),
             (tiles.shape, bf16),
             (images.shape, bf16),
+            (inv_sigma2.shape, f32),
             ((devices, blocks), i32),
-            ((crossed, blocks), i32),
+            ((crossed, batches), i32),
         ],
-        [hbm] * 7,
-        (slabs, kind_rows, batch_block, row, inv_sigma2, tiles, images),
+        [hbm] * 8,
+        (slabs, kind_rows, batch_block, batch_block.reshape(1, batches), row, inv_sigma2, tiles, images),
         [
             pltpu.VMEM((crossed, blocks), i32),
             pltpu.VMEM((crossed, blocks), i32),
-            block_scratch,
+            pltpu.SMEM((batches,), i32),
+            pltpu.VMEM((1, batches), i32),
             pltpu.VMEM((1, count), f32),
-            noise_scratch,
             pltpu.VMEM((2, height, count), f32),
             pltpu.VMEM((2, count, pixels), f32),
             pltpu.VMEM((blocks, 2, height, pixels), f32),
-            pltpu.SemaphoreType.DMA((CHUNKS + 6,)),
+            pltpu.SemaphoreType.DMA((CHUNKS + 7,)),
         ],
         0,
         10 << 20,
@@ -304,56 +295,49 @@
     )
 
     place = (2, height, length)
-    send, parts = call(
+    place_scratch = [pltpu.SMEM((devices, blocks), i32), pltpu.SemaphoreType.DMA((1,))]
+    send, keep, parts = call(
         insert_kernel,
-        [((half, *place), bf16), ((kinds * rows + 2 * height, length), f32)],
+        [((half, *place), bf16), ((half - far, *place), f32), ((kinds * rows + 2 * height, length), f32)],
         [vmem] * 3,
         (place_rows, sums, tiles_near),
-        [pltpu.SMEM((devices, blocks), i32), pltpu.SemaphoreType.DMA((1,))],
+        place_scratch,
         2 * rows * pixels * kinds * length,
         8 << 20,
         "insert",
     )
     send, gathered = lax.optimization_barrier((send, gathered))
-    for offset in offsets[1:-1]:
-        gathered = hop(gathered, offset)
     mate = swap(send, 1)
-    place_scratch = [pltpu.SMEM((devices, blocks), i32), pltpu.SemaphoreType.DMA((1,))]
-    main, own = call(
-        far_kernel,
-        [((wide - 1, far - 1, *place), bf16), ((wide - 1, *place), bf16)],
-        [vmem] * 3,
-        (place_rows, parts, mate),
-        place_scratch,
-        0,
-        0,
-        "far",
-    )
+    def along_x(start, stop):
+        return (keep[start:stop] + mate[far + start : far + stop].astype(f32)).astype(bf16)
+
+    main = [along_x(x * far + 1, (x + 1) * far) for x in range(wide - 1)]
+    later = [along_x(x * far, x * far + 1) for x in range(wide - 1)]
     (near,) = call(
         near_kernel, [((far, *place), f32)], [vmem] * 3, (place_rows, parts, mate), place_scratch, 0, 0, "near"
     )
-    held, _ = lax.optimization_barrier((gathered, main))
-    columns = [gathered, swap(held, offsets[-1])]
+    for offset in offsets[1:-1]:
+        came, _ = lax.optimization_barrier((swap(gathered, offset), main[0]))
+        gathered = jnp.concatenate([gathered, came], axis=0)
+    columns = [gathered, swap(gathered, offsets[-1])]
     columns += [swap(column, 1) for column in columns]
     places = [[a ^ last for a in away] for last in (0, offsets[-1], 1, offsets[-1] ^ 1)]
-    mine = near[1:]
+    mine, total = near[1:], near[0]
     for x in range(1, wide):
         mine = mine + swap(main[x - 1], x * cores).astype(f32)
-    total = near[0]
-    for x in range(1, wide):
-        total = total + swap(own[x - 1], x * cores).astype(f32)
+        total = total + swap(later[x - 1], x * cores)[0].astype(f32)
     outgoing = mine.astype(bf16)
     _, *columns = lax.optimization_barrier((outgoing, *columns))
-    if devices * kinds <= blocks * crossed:
+    if devices * kinds <= batches * crossed:
         flat = pltpu.VMEM((kinds * devices * height, pixels), f32)
     else:
         flat = pltpu.VMEM((8, LANES), f32)
     (proj,) = call(
         functools.partial(project_kernel, places),
-        [((blocks, height, pixels), f32)],
+        [((batches, height, pixels), f32)],
         [vmem] * (2 + len(columns)),
         (route_rows, tiles_near, *columns),
-        [pltpu.SMEM((crossed, blocks), i32), pltpu.VMEM((devices * height, length), bf16), flat, pltpu.SemaphoreType.DMA((1,))],
+        [pltpu.SMEM((crossed, batches), i32), pltpu.VMEM((devices * height, length), bf16), flat, pltpu.SemaphoreType.DMA((1,))],
         0,
         0,
         "project",
@@ -362,14 +346,14 @@
     (scores,) = call(
         score_kernel,
         [((1, count), f32)],
-        [hbm] * 2 + [vmem] * 3,
-        (batch_block, inv_sigma2, proj, wave, images_near),
-        [block_scratch, noise_scratch, pltpu.VMEM((count * 8, LANES), f32), pltpu.SemaphoreType.DMA((2,))],
+        [vmem] * 4,
+        (noise_near, proj, wave, images_near),
+        [pltpu.VMEM((count * 8, LANES), f32)],
         0,
         0,
         "scores",
     )
-    for z in range(1, far):
+    for z in range(far - 1, 0, -1):
         came = swap(outgoing[z - 1], z * wide * cores)
         if z == far - 1:
             came, scores = lax.optimization_barrier((came, scores))

time: 31.8 us -> 31.8 us (level)
  Pallas kernels: 12.4 us -> 11 us
  waiting for transfers between devices: 2.86 us -> 4.2 us
    pallas_call x6 -> x5, Pallas kernels: 12.4 us -> 11 us  [call(): pl.pallas_call(kernel, out_shape=tuple((jax.ShapeDtypeStruct(s, t) for s,...]
    ppermute x11, waiting for transfers between devices: 2.86 us -> 4.2 us  [swap(): lax.ppermute(array, 'slab', [(i, i ^ offset) for i in range(devices)])]
  transfers between devices with their start and end apart: 11 -> 11, of which waited for: 4 -> 4; matrix products, arithmetic and copies ran while one was open for 0% -> 0% of each run, Pallas kernels for 39% -> 35%
where the time goes in v13:
time: 31.8 us; the launch traced here: 31.7 us
  starting transfers between devices  14.9 us (47%)
  Pallas kernels  11 us (35%)
  waiting for transfers between devices  4.2 us (13%)
  between operations  0.74 us (2%)
  local copies, waits for them, and re-layouts  0.69 us (2%)
    ppermute x11, starting transfers between devices, swap(): lax.ppermute(array, 'slab', [(i, i ^ offset) for i in range(devices)])  14.9 us
    pallas_call x5, Pallas kernels, call(): pl.pallas_call(kernel, out_shape=tuple((jax.ShapeDtypeStruct(s, t) for s,...  11 us
    ppermute x11, waiting for transfers between devices, swap(): lax.ppermute(array, 'slab', [(i, i ^ offset) for i in range(devices)])  4.2 us
    slice x1, local copies, waits for them, and re-layouts, on_device(): return (scores.reshape(count), total[0:1], total[1:2])  0.66 us
  transfers between devices with their start and end apart: 11, of which 4 were waited for; matrix products, arithmetic and copies ran while one was open for 0% of the time, Pallas kernels for 35%

profile of v13, /device:TPU:0, one launch (start us, length us, event | category | flops | bytes accessed | tf_op | source)
XLA Modules:
  0.0 31.7 jit_solution(1101394910313656019)
XLA Ops:
  0.6 4.1 %collective-permute-start = (bf16[1,32,512]{2,1,0:T(8,128)(2,1)}, bf16[1,32,512]{2,1,0:T(8,128)(2,1)S(1)}, u32[]{:S(2)}, u32[]{:S(2)}) collective-permute-start(bf16[1,32,512]{2,1,0:T(8,128)(2,1)} %param.8), channel_id=1, source_target_pairs={{0,8},{1,9},{2,10},{3,11},{4,12},{5,13},{6,14},{7,15},{8,0},{9,1},... | collective-permute-start | bytes 98312 | tf_op jit(solution)/shard_map/ppermute | solution.py:234
  4.7 2.9 %sums.1 = (bf16[1024,256]{1,0:T(8,128)(2,1)S(1)}, f32[128,32,256]{2,1,0:T(8,128)S(1)}, bf16[8,512,256]{2,1,0:T(8,128)(2,1)S(1)}, bf16[128,32,256]{2,1,0:T(8,128)...) custom-call(s32[8,16]{1,0:T(8,128)} %bitcast.19, s32[8,16]{1,0:T(8,128)} %bitcast.20, ...), custom_call_target="tpu_custom_call" | custom-call | bytes 10485760 | tf_op jit(solution)/shard_map/sums/pallas_call | solution.py:246
  7.7 0.0 copy-start
  7.7 3.7 %insert.1 = (bf16[8,2,32,512]{3,2,1,0:T(8,128)(2,1)S(1)}, f32[4,2,32,512]{3,2,1,0:T(8,128)S(1)}, f32[8256,512]{1,0:T(8,128)S(1)}) custom-call(s32[16,16]{1,0:T(8,128)S(1)} %get-tuple-element.22.place_vmem, bf16[1024,256]{1,0:T(8,128)(2,1)S(1)} %get-tuple-element.23.sums_ref, bf16[8,512,256]{2,1,0:T(8,128)(2,1)S(1)} %get-tuple-element.24.tiles_ref), custom_call_target="tpu_custom_call" | custom-call | flops 2147483648 | bytes 8388608 | tf_op jit(solution)/shard_map/insert/pallas_call | solution.py:246
  11.4 0.0 collective-permute-done
  11.4 0.0 copy-done
  11.4 0.1 collective-permute-start.1
  11.5 1.6 %collective-permute-start.4 = (bf16[2,32,512]{2,1,0:T(8,128)(2,1)S(1)}, bf16[2,32,512]{2,1,0:T(8,128)(2,1)S(1)}, u32[]{:S(2)}, u32[]{:S(2)}) collective-permute-start(bf16[2,32,512]{2,1,0:T(8,128)(2,1)S(1)} %pad_maximum_fusion), channel_id=1, source_target_pairs={{0,2},{1,3},{2,0},{3,1},{4,6},{5,7},{6,4},{7,5},{8,10},{9,11},{10,... | collective-permute-start | bytes 196616 | tf_op jit(solution)/shard_map/ppermute | solution.py:234
  13.0 0.3 %collective-permute-done.1.mate_ref = bf16[8,2,32,512]{3,2,1,0:T(8,128)(2,1)S(1)} collective-permute-done((bf16[8,2,32,512]{3,2,1,0:T(8,128)(2,1)S(1)}, bf16[8,2,32,512]{3,2,1,0:T(8,128)(2,1)S(1)}, u32[]{:S(2)}, u32[]{:S(2)}) %collective-permute-start.1) | collective-permute-done | bytes 524320 | tf_op jit(solution)/shard_map/ppermute | solution.py:234
  13.4 0.1 add_convert_fusion
  13.4 1.6 %collective-permute-start.2 = (bf16[3,2,32,512]{3,2,1,0:T(8,128)(2,1)S(1)}, bf16[3,2,32,512]{3,2,1,0:T(8,128)(2,1)S(1)}, u32[]{:S(2)}, u32[]{:S(2)}) collective-permute-start(bf16[3,2,32,512]{3,2,1,0:T(8,128)(2,1)S(1)} %add_convert_fusion), channel_id=1, source_target_pairs={{0,2},{1,3},{2,0},{3,1},{4,6},{5,7},{6,4},{7,5},{8,10},{9,11},{10,... | collective-permute-start | bytes 589832 | tf_op jit(solution)/shard_map/ppermute | solution.py:234
  15.0 1.0 %collective-permute-done.4 = bf16[2,32,512]{2,1,0:T(8,128)(2,1)S(1)} collective-permute-done((bf16[2,32,512]{2,1,0:T(8,128)(2,1)S(1)}, bf16[2,32,512]{2,1,0:T(8,128)(2,1)S(1)}, u32[]{:S(2)}, u32[]{:S(2)}) %collective-permute-start.4) | collective-permute-done | bytes 65568 | tf_op jit(solution)/shard_map/ppermute | solution.py:234
  16.0 1.6 %collective-permute-start.5 = (bf16[4,32,512]{2,1,0:T(8,128)(2,1)S(1)}, bf16[4,32,512]{2,1,0:T(8,128)(2,1)S(1)}, u32[]{:S(2)}, u32[]{:S(2)}) collective-permute-start(bf16[4,32,512]{2,1,0:T(8,128)(2,1)S(1)} %constant_dynamic-update-slice_fusion.refs_0_), channel_id=1, source_target_pairs={{0,4},{1,5},{2,6},{3,7},{4,0},{5,1},{6,2},{7,3},{8,12},{9,13},{10,... | collective-permute-start | bytes 393224 | tf_op jit(solution)/shard_map/ppermute | solution.py:234
  17.6 0.0 collective-permute-start.6
  17.6 1.6 %collective-permute-start.8 = (bf16[1,2,32,512]{3,2,1,0:T(8,128)(2,1)S(1)}, bf16[1,2,32,512]{3,2,1,0:T(8,128)(2,1)S(1)}, u32[]{:S(2)}, u32[]{:S(2)}) collective-permute-start(bf16[1,2,32,512]{3,2,1,0:T(8,128)(2,1)S(1)} %add_convert_fusion.1), channel_id=1, source_target_pairs={{0,2},{1,3},{2,0},{3,1},{4,6},{5,7},{6,4},{7,5},{8,10},{9,11},{10,... | collective-permute-start | bytes 196616 | tf_op jit(solution)/shard_map/ppermute | solution.py:234
  19.1 1.1 %near.1 = f32[4,2,32,512]{3,2,1,0:T(8,128)S(1)} custom-call(s32[16,16]{1,0:T(8,128)S(1)} %get-tuple-element.22.place_vmem, f32[8256,512]{1,0:T(8,128)S(1)} %get-tuple-element.25.parts_ref, bf16[8,2,32,512]{3,2,1,0:T(8,128)(2,1)S(1)} %collective-permute-done.1.mate_ref), custom_call_target="tpu_custom_call" | custom-call | tf_op jit(solution)/shard_map/near/pallas_call | solution.py:246
  20.3 0.8 %collective-permute-done.5.refs_1_ = bf16[4,32,512]{2,1,0:T(8,128)(2,1)S(1)} collective-permute-done((bf16[4,32,512]{2,1,0:T(8,128)(2,1)S(1)}, bf16[4,32,512]{2,1,0:T(8,128)(2,1)S(1)}, u32[]{:S(2)}, u32[]{:S(2)}) %collective-permute-start.5) | collective-permute-done | bytes 131104 | tf_op jit(solution)/shard_map/ppermute | solution.py:234
  21.1 0.0 collective-permute-start.7
  21.1 0.0 collective-permute-done.2
  21.1 0.1 fusion
  21.1 1.5 %collective-permute-start.3 = (bf16[2,32,512]{2,1,0:T(8,128)(2,1)S(1)}, bf16[2,32,512]{2,1,0:T(8,128)(2,1)S(1)}, u32[]{:S(2)}, u32[]{:S(2)}) collective-permute-start(bf16[2,32,512]{2,1,0:T(8,128)(2,1)S(1)} %get-tuple-element.43), channel_id=1, source_target_pairs={{0,12},{1,13},{2,14},{3,15},{4,8},{5,9},{6,10},{7,11},{8,4},{9,5},... | collective-permute-start | bytes 196616 | tf_op jit(solution)/shard_map/ppermute | solution.py:234
  22.6 0.3 collective-permute-start.10
  22.9 0.0 collective-permute-done.6.refs_2_
  22.9 2.7 %collective-permute-start.9 = (bf16[2,32,512]{2,1,0:T(8,128)(2,1)S(1)}, bf16[2,32,512]{2,1,0:T(8,128)(2,1)S(1)}, u32[]{:S(2)}, u32[]{:S(2)}) collective-permute-start(bf16[2,32,512]{2,1,0:T(8,128)(2,1)S(1)} %get-tuple-element.41), channel_id=1, source_target_pairs={{0,8},{1,9},{2,10},{3,11},{4,12},{5,13},{6,14},{7,15},{8,0},{9,1},... | collective-permute-start | bytes 196616 | tf_op jit(solution)/shard_map/ppermute | solution.py:234
  25.6 0.0 collective-permute-done.7.refs_3_
  25.6 1.8 %project.1.proj_ref = f32[16,32,256]{2,1,0:T(8,128)S(1)} custom-call(s32[8,16]{1,0:T(8,128)S(1)} %get-tuple-element.30.route_vmem, bf16[8,512,256]{2,1,0:T(8,128)(2,1)S(1)} %get-tuple-element.24.tiles_ref, bf16[4,32,512]{2,1,0:T(8,128)(2,1)S(1)} %constant_dynamic-update-slice_fusion.refs_0_, bf16[4,32,512]{2,1,0:T(8,128)(2,1)S(1)} %collective-permute-done.5.refs_1_, ...), custom_call_target="tpu_custom_call" | custom-call | tf_op jit(solution)/shard_map/project/pallas_call | solution.py:246
  27.4 1.5 %scores.1 = f32[1,128]{1,0:T(1,128)} custom-call(f32[32,256]{1,0:T(8,128)S(1)} %get-tuple-element.29.noise_ref, f32[16,32,256]{2,1,0:T(8,128)S(1)} %project.1.proj_ref, f32[128,32,256]{2,1,0:T(8,128)S(1)} %get-tuple-element.37.wave_ref, bf16[128,32,256]{2,1,0:T(8,128)(2,1)S(1)} %get-tuple-element.38.images_ref), custom_call_target="tpu_custom_call" | custom-call | tf_op jit(solution)/shard_map/scores/pallas_call | solution.py:246
  28.9 0.0 collective-permute-done.3
  28.9 0.0 collective-permute-done.8
  28.9 0.0 collective-permute-done.10
  28.9 2.1 %collective-permute-done.9 = bf16[2,32,512]{2,1,0:T(8,128)(2,1)S(1)} collective-permute-done((bf16[2,32,512]{2,1,0:T(8,128)(2,1)S(1)}, bf16[2,32,512]{2,1,0:T(8,128)(2,1)S(1)}, u32[]{:S(2)}, u32[]{:S(2)}) %collective-permute-start.9) | collective-permute-done | bytes 65568 | tf_op jit(solution)/shard_map/ppermute | solution.py:234
  31.0 0.7 %fusion.5 = (f32[1,32,512]{2,1,0:T(8,128)}, f32[1,32,512]{2,1,0:T(8,128)}) fusion(f32[2,32,512]{2,1,0:T(8,128)S(1)} %fusion.4), kind=kLoop, calls=%fused_computation.15 | loop fusion | bytes 262144 | tf_op jit(solution)/shard_map/slice | solution.py:361
  (6 shorter events, 0.1 us)
Async XLA Ops:
  0.6 10.7 %collective-permute-start = (bf16[1,32,512]{2,1,0:T(8,128)(2,1)}, bf16[1,32,512]{2,1,0:T(8,128)(2,1)S(1)}, u32[]{:S(2)}, u32[]{:S(2)}) collective-permute-start(bf16[1,32,512]{2,1,0:T(8,128)(2,1)} %param.8), channel_id=1, source_target_pairs={{0,8},{1,9},{2,10},{3,11},{4,12},{5,13},{6,14},{7,15},{8,0},{9,1},... | collective-permute-start | bytes 98312 | tf_op jit(solution)/shard_map/ppermute | solution.py:234
  7.7 3.7 %copy-start = (bf16[1,32,512]{2,1,0:T(8,128)(2,1)S(1)}, bf16[1,32,512]{2,1,0:T(8,128)(2,1)}, u32[]{:S(2)}) copy-start(bf16[1,32,512]{2,1,0:T(8,128)(2,1)} %param.8) | copy-start | bytes 98308
  11.4 2.0 %collective-permute-start.1 = (bf16[8,2,32,512]{3,2,1,0:T(8,128)(2,1)S(1)}, bf16[8,2,32,512]{3,2,1,0:T(8,128)(2,1)S(1)}, u32[]{:S(2)}, u32[]{:S(2)}) collective-permute-start(bf16[8,2,32,512]{3,2,1,0:T(8,128)(2,1)S(1)} %get-tuple-element.27), channel_id=1, source_target_pairs={{0,1},{1,0},{2,3},{3,2},{4,5},{5,4},{6,7},{7,6},{8,9},{9,8},{10,11... | collective-permute-start | bytes 1572872 | tf_op jit(solution)/shard_map/ppermute | solution.py:234
  11.5 4.5 %collective-permute-start.4 = (bf16[2,32,512]{2,1,0:T(8,128)(2,1)S(1)}, bf16[2,32,512]{2,1,0:T(8,128)(2,1)S(1)}, u32[]{:S(2)}, u32[]{:S(2)}) collective-permute-start(bf16[2,32,512]{2,1,0:T(8,128)(2,1)S(1)} %pad_maximum_fusion), channel_id=1, source_target_pairs={{0,2},{1,3},{2,0},{3,1},{4,6},{5,7},{6,4},{7,5},{8,10},{9,11},{10,... | collective-permute-start | bytes 196616 | tf_op jit(solution)/shard_map/ppermute | solution.py:234
  13.4 7.6 %collective-permute-start.2 = (bf16[3,2,32,512]{3,2,1,0:T(8,128)(2,1)S(1)}, bf16[3,2,32,512]{3,2,1,0:T(8,128)(2,1)S(1)}, u32[]{:S(2)}, u32[]{:S(2)}) collective-permute-start(bf16[3,2,32,512]{3,2,1,0:T(8,128)(2,1)S(1)} %add_convert_fusion), channel_id=1, source_target_pairs={{0,2},{1,3},{2,0},{3,1},{4,6},{5,7},{6,4},{7,5},{8,10},{9,11},{10,... | collective-permute-start | bytes 589832 | tf_op jit(solution)/shard_map/ppermute | solution.py:234
  16.0 5.1 %collective-permute-start.5 = (bf16[4,32,512]{2,1,0:T(8,128)(2,1)S(1)}, bf16[4,32,512]{2,1,0:T(8,128)(2,1)S(1)}, u32[]{:S(2)}, u32[]{:S(2)}) collective-permute-start(bf16[4,32,512]{2,1,0:T(8,128)(2,1)S(1)} %constant_dynamic-update-slice_fusion.refs_0_), channel_id=1, source_target_pairs={{0,4},{1,5},{2,6},{3,7},{4,0},{5,1},{6,2},{7,3},{8,12},{9,13},{10,... | collective-permute-start | bytes 393224 | tf_op jit(solution)/shard_map/ppermute | solution.py:234
  17.6 5.4 %collective-permute-start.6 = (bf16[4,32,512]{2,1,0:T(8,128)(2,1)S(1)}, bf16[4,32,512]{2,1,0:T(8,128)(2,1)S(1)}, u32[]{:S(2)}, u32[]{:S(2)}) collective-permute-start(bf16[4,32,512]{2,1,0:T(8,128)(2,1)S(1)} %constant_dynamic-update-slice_fusion.refs_0_), channel_id=1, source_target_pairs={{0,1},{1,0},{2,3},{3,2},{4,5},{5,4},{6,7},{7,6},{8,9},{9,8},{10,11... | collective-permute-start | bytes 393224 | tf_op jit(solution)/shard_map/ppermute | solution.py:234
  17.6 11.3 %collective-permute-start.8 = (bf16[1,2,32,512]{3,2,1,0:T(8,128)(2,1)S(1)}, bf16[1,2,32,512]{3,2,1,0:T(8,128)(2,1)S(1)}, u32[]{:S(2)}, u32[]{:S(2)}) collective-permute-start(bf16[1,2,32,512]{3,2,1,0:T(8,128)(2,1)S(1)} %add_convert_fusion.1), channel_id=1, source_target_pairs={{0,2},{1,3},{2,0},{3,1},{4,6},{5,7},{6,4},{7,5},{8,10},{9,11},{10,... | collective-permute-start | bytes 196616 | tf_op jit(solution)/shard_map/ppermute | solution.py:234
  21.1 4.5 %collective-permute-start.7 = (bf16[4,32,512]{2,1,0:T(8,128)(2,1)S(1)}, bf16[4,32,512]{2,1,0:T(8,128)(2,1)S(1)}, u32[]{:S(2)}, u32[]{:S(2)}) collective-permute-start(bf16[4,32,512]{2,1,0:T(8,128)(2,1)S(1)} %collective-permute-done.5.refs_1_), channel_id=1, source_target_pairs={{0,1},{1,0},{2,3},{3,2},{4,5},{5,4},{6,7},{7,6},{8,9},{9,8},{10,11... | collective-permute-start | bytes 393224 | tf_op jit(solution)/shard_map/ppermute | solution.py:234
  21.1 7.7 %collective-permute-start.3 = (bf16[2,32,512]{2,1,0:T(8,128)(2,1)S(1)}, bf16[2,32,512]{2,1,0:T(8,128)(2,1)S(1)}, u32[]{:S(2)}, u32[]{:S(2)}) collective-permute-start(bf16[2,32,512]{2,1,0:T(8,128)(2,1)S(1)} %get-tuple-element.43), channel_id=1, source_target_pairs={{0,12},{1,13},{2,14},{3,15},{4,8},{5,9},{6,10},{7,11},{8,4},{9,5},... | collective-permute-start | bytes 196616 | tf_op jit(solution)/shard_map/ppermute | solution.py:234
  22.6 6.2 %collective-permute-start.10 = (bf16[2,32,512]{2,1,0:T(8,128)(2,1)S(1)}, bf16[2,32,512]{2,1,0:T(8,128)(2,1)S(1)}, u32[]{:S(2)}, u32[]{:S(2)}) collective-permute-start(bf16[2,32,512]{2,1,0:T(8,128)(2,1)S(1)} %get-tuple-element.42), channel_id=1, source_target_pairs={{0,4},{1,5},{2,6},{3,7},{4,0},{5,1},{6,2},{7,3},{8,12},{9,13},{10,... | collective-permute-start | bytes 196616 | tf_op jit(solution)/shard_map/ppermute | solution.py:234
  22.9 8.0 %collective-permute-start.9 = (bf16[2,32,512]{2,1,0:T(8,128)(2,1)S(1)}, bf16[2,32,512]{2,1,0:T(8,128)(2,1)S(1)}, u32[]{:S(2)}, u32[]{:S(2)}) collective-permute-start(bf16[2,32,512]{2,1,0:T(8,128)(2,1)S(1)} %get-tuple-element.41), channel_id=1, source_target_pairs={{0,8},{1,9},{2,10},{3,11},{4,12},{5,13},{6,14},{7,15},{8,0},{9,1},... | collective-permute-start | bytes 196616 | tf_op jit(solution)/shard_map/ppermute | solution.py:234

commit v14 on v13

--- a/solution.py
+++ b/solution.py
@@ -322,12 +322,13 @@
     columns = [gathered, swap(gathered, offsets[-1])]
     columns += [swap(column, 1) for column in columns]
     places = [[a ^ last for a in away] for last in (0, offsets[-1], 1, offsets[-1] ^ 1)]
-    mine, total = near[1:], near[0]
+    total, outgoing = near[0], [near[z] for z in range(1, far)]
     for x in range(1, wide):
-        mine = mine + swap(main[x - 1], x * cores).astype(f32)
+        came = swap(main[x - 1], x * cores)
+        outgoing = [mine + came[z].astype(f32) for z, mine in enumerate(outgoing)]
         total = total + swap(later[x - 1], x * cores)[0].astype(f32)
-    outgoing = mine.astype(bf16)
-    _, *columns = lax.optimization_barrier((outgoing, *columns))
+    outgoing = [mine.astype(bf16) for mine in outgoing]
+    _, *columns = lax.optimization_barrier((outgoing[0], *columns))
     if devices * kinds <= batches * crossed:
         flat = pltpu.VMEM((kinds * devices * height, pixels), f32)
     else:
@@ -353,7 +354,7 @@
         0,
         "scores",
     )
-    for z in range(far - 1, 0, -1):
+    for z in range(1, far):
         came = swap(outgoing[z - 1], z * wide * cores)
         if z == far - 1:
             came, scores = lax.optimization_barrier((came, scores))

time: 31.8 us -> 31.8 us (level)
  no operation moved by 1% of the time
where the time goes in v14:
time: 31.8 us; the launch traced here: 31.6 us
  starting transfers between devices  14.9 us (47%)
  Pallas kernels  11 us (35%)
  waiting for transfers between devices  4.2 us (13%)
  between operations  0.73 us (2%)
  local copies, waits for them, and re-layouts  0.68 us (2%)
    ppermute x11, starting transfers between devices, swap(): lax.ppermute(array, 'slab', [(i, i ^ offset) for i in range(devices)])  14.9 us
    pallas_call x5, Pallas kernels, call(): pl.pallas_call(kernel, out_shape=tuple((jax.ShapeDtypeStruct(s, t) for s,...  11 us
    ppermute x11, waiting for transfers between devices, swap(): lax.ppermute(array, 'slab', [(i, i ^ offset) for i in range(devices)])  4.2 us
    slice x1, local copies, waits for them, and re-layouts, on_device(): return (scores.reshape(count), total[0:1], total[1:2])  0.66 us
  transfers between devices with their start and end apart: 11, of which 4 were waited for; matrix products, arithmetic and copies ran while one was open for 0% of the time, Pallas kernels for 35%

profile of v14, /device:TPU:0, one launch (start us, length us, event | category | flops | bytes accessed | tf_op | source)
XLA Modules:
  0.0 31.6 jit_solution(15933440424859866734)
XLA Ops:
  0.6 4.1 %collective-permute-start = (bf16[1,32,512]{2,1,0:T(8,128)(2,1)}, bf16[1,32,512]{2,1,0:T(8,128)(2,1)S(1)}, u32[]{:S(2)}, u32[]{:S(2)}) collective-permute-start(bf16[1,32,512]{2,1,0:T(8,128)(2,1)} %param.8), channel_id=1, source_target_pairs={{0,8},{1,9},{2,10},{3,11},{4,12},{5,13},{6,14},{7,15},{8,0},{9,1},... | collective-permute-start | bytes 98312 | tf_op jit(solution)/shard_map/ppermute | solution.py:234
  4.7 2.9 %sums.1 = (bf16[1024,256]{1,0:T(8,128)(2,1)S(1)}, f32[128,32,256]{2,1,0:T(8,128)S(1)}, bf16[8,512,256]{2,1,0:T(8,128)(2,1)S(1)}, bf16[128,32,256]{2,1,0:T(8,128)...) custom-call(s32[8,16]{1,0:T(8,128)} %bitcast.19, s32[8,16]{1,0:T(8,128)} %bitcast.20, ...), custom_call_target="tpu_custom_call" | custom-call | bytes 10485760 | tf_op jit(solution)/shard_map/sums/pallas_call | solution.py:246
  7.7 0.0 copy-start
  7.7 3.7 %insert.1 = (bf16[8,2,32,512]{3,2,1,0:T(8,128)(2,1)S(1)}, f32[4,2,32,512]{3,2,1,0:T(8,128)S(1)}, f32[8256,512]{1,0:T(8,128)S(1)}) custom-call(s32[16,16]{1,0:T(8,128)S(1)} %get-tuple-element.22.place_vmem, bf16[1024,256]{1,0:T(8,128)(2,1)S(1)} %get-tuple-element.23.sums_ref, bf16[8,512,256]{2,1,0:T(8,128)(2,1)S(1)} %get-tuple-element.24.tiles_ref), custom_call_target="tpu_custom_call" | custom-call | flops 2147483648 | bytes 8388608 | tf_op jit(solution)/shard_map/insert/pallas_call | solution.py:246
  11.4 0.0 collective-permute-done
  11.4 0.0 copy-done
  11.4 0.1 collective-permute-start.1
  11.5 1.6 %collective-permute-start.4 = (bf16[2,32,512]{2,1,0:T(8,128)(2,1)S(1)}, bf16[2,32,512]{2,1,0:T(8,128)(2,1)S(1)}, u32[]{:S(2)}, u32[]{:S(2)}) collective-permute-start(bf16[2,32,512]{2,1,0:T(8,128)(2,1)S(1)} %pad_maximum_fusion), channel_id=1, source_target_pairs={{0,2},{1,3},{2,0},{3,1},{4,6},{5,7},{6,4},{7,5},{8,10},{9,11},{10,... | collective-permute-start | bytes 196616 | tf_op jit(solution)/shard_map/ppermute | solution.py:234
  13.0 0.3 %collective-permute-done.1.mate_ref = bf16[8,2,32,512]{3,2,1,0:T(8,128)(2,1)S(1)} collective-permute-done((bf16[8,2,32,512]{3,2,1,0:T(8,128)(2,1)S(1)}, bf16[8,2,32,512]{3,2,1,0:T(8,128)(2,1)S(1)}, u32[]{:S(2)}, u32[]{:S(2)}) %collective-permute-start.1) | collective-permute-done | bytes 524320 | tf_op jit(solution)/shard_map/ppermute | solution.py:234
  13.4 0.1 add_convert_fusion
  13.4 1.6 %collective-permute-start.2 = (bf16[3,2,32,512]{3,2,1,0:T(8,128)(2,1)S(1)}, bf16[3,2,32,512]{3,2,1,0:T(8,128)(2,1)S(1)}, u32[]{:S(2)}, u32[]{:S(2)}) collective-permute-start(bf16[3,2,32,512]{3,2,1,0:T(8,128)(2,1)S(1)} %add_convert_fusion), channel_id=1, source_target_pairs={{0,2},{1,3},{2,0},{3,1},{4,6},{5,7},{6,4},{7,5},{8,10},{9,11},{10,... | collective-permute-start | bytes 589832 | tf_op jit(solution)/shard_map/ppermute | solution.py:234
  15.0 1.0 %collective-permute-done.4 = bf16[2,32,512]{2,1,0:T(8,128)(2,1)S(1)} collective-permute-done((bf16[2,32,512]{2,1,0:T(8,128)(2,1)S(1)}, bf16[2,32,512]{2,1,0:T(8,128)(2,1)S(1)}, u32[]{:S(2)}, u32[]{:S(2)}) %collective-permute-start.4) | collective-permute-done | bytes 65568 | tf_op jit(solution)/shard_map/ppermute | solution.py:234
  16.0 1.6 %collective-permute-start.5 = (bf16[4,32,512]{2,1,0:T(8,128)(2,1)S(1)}, bf16[4,32,512]{2,1,0:T(8,128)(2,1)S(1)}, u32[]{:S(2)}, u32[]{:S(2)}) collective-permute-start(bf16[4,32,512]{2,1,0:T(8,128)(2,1)S(1)} %constant_dynamic-update-slice_fusion.refs_0_), channel_id=1, source_target_pairs={{0,4},{1,5},{2,6},{3,7},{4,0},{5,1},{6,2},{7,3},{8,12},{9,13},{10,... | collective-permute-start | bytes 393224 | tf_op jit(solution)/shard_map/ppermute | solution.py:234
  17.6 0.0 collective-permute-start.6
  17.6 1.6 %collective-permute-start.8 = (bf16[1,2,32,512]{3,2,1,0:T(8,128)(2,1)S(1)}, bf16[1,2,32,512]{3,2,1,0:T(8,128)(2,1)S(1)}, u32[]{:S(2)}, u32[]{:S(2)}) collective-permute-start(bf16[1,2,32,512]{3,2,1,0:T(8,128)(2,1)S(1)} %add_convert_fusion.1), channel_id=1, source_target_pairs={{0,2},{1,3},{2,0},{3,1},{4,6},{5,7},{6,4},{7,5},{8,10},{9,11},{10,... | collective-permute-start | bytes 196616 | tf_op jit(solution)/shard_map/ppermute | solution.py:234
  19.1 1.1 %near.1 = f32[4,2,32,512]{3,2,1,0:T(8,128)S(1)} custom-call(s32[16,16]{1,0:T(8,128)S(1)} %get-tuple-element.22.place_vmem, f32[8256,512]{1,0:T(8,128)S(1)} %get-tuple-element.25.parts_ref, bf16[8,2,32,512]{3,2,1,0:T(8,128)(2,1)S(1)} %collective-permute-done.1.mate_ref), custom_call_target="tpu_custom_call" | custom-call | tf_op jit(solution)/shard_map/near/pallas_call | solution.py:246
  20.3 0.8 %collective-permute-done.5.refs_1_ = bf16[4,32,512]{2,1,0:T(8,128)(2,1)S(1)} collective-permute-done((bf16[4,32,512]{2,1,0:T(8,128)(2,1)S(1)}, bf16[4,32,512]{2,1,0:T(8,128)(2,1)S(1)}, u32[]{:S(2)}, u32[]{:S(2)}) %collective-permute-start.5) | collective-permute-done | bytes 131104 | tf_op jit(solution)/shard_map/ppermute | solution.py:234
  21.1 0.0 collective-permute-start.7
  21.1 0.0 collective-permute-done.2
  21.1 0.1 fusion.9
  21.1 1.5 %collective-permute-start.3 = (bf16[2,32,512]{2,1,0:T(8,128)(2,1)S(1)}, bf16[2,32,512]{2,1,0:T(8,128)(2,1)S(1)}, u32[]{:S(2)}, u32[]{:S(2)}) collective-permute-start(bf16[2,32,512]{2,1,0:T(8,128)(2,1)S(1)} %get-tuple-element.43), channel_id=1, source_target_pairs={{0,12},{1,13},{2,14},{3,15},{4,8},{5,9},{6,10},{7,11},{8,4},{9,5},... | collective-permute-start | bytes 196616 | tf_op jit(solution)/shard_map/ppermute | solution.py:234
  22.6 1.7 %collective-permute-start.10 = (bf16[2,32,512]{2,1,0:T(8,128)(2,1)S(1)}, bf16[2,32,512]{2,1,0:T(8,128)(2,1)S(1)}, u32[]{:S(2)}, u32[]{:S(2)}) collective-permute-start(bf16[2,32,512]{2,1,0:T(8,128)(2,1)S(1)} %get-tuple-element.41), channel_id=1, source_target_pairs={{0,8},{1,9},{2,10},{3,11},{4,12},{5,13},{6,14},{7,15},{8,0},{9,1},... | collective-permute-start | bytes 196616 | tf_op jit(solution)/shard_map/ppermute | solution.py:234
  24.3 0.0 collective-permute-done.6.refs_2_
  24.3 1.3 %collective-permute-start.9 = (bf16[2,32,512]{2,1,0:T(8,128)(2,1)S(1)}, bf16[2,32,512]{2,1,0:T(8,128)(2,1)S(1)}, u32[]{:S(2)}, u32[]{:S(2)}) collective-permute-start(bf16[2,32,512]{2,1,0:T(8,128)(2,1)S(1)} %get-tuple-element.42), channel_id=1, source_target_pairs={{0,4},{1,5},{2,6},{3,7},{4,0},{5,1},{6,2},{7,3},{8,12},{9,13},{10,... | collective-permute-start | bytes 196616 | tf_op jit(solution)/shard_map/ppermute | solution.py:234
  25.6 0.0 collective-permute-done.7.refs_3_
  25.6 1.8 %project.1.proj_ref = f32[16,32,256]{2,1,0:T(8,128)S(1)} custom-call(s32[8,16]{1,0:T(8,128)S(1)} %get-tuple-element.30.route_vmem, bf16[8,512,256]{2,1,0:T(8,128)(2,1)S(1)} %get-tuple-element.24.tiles_ref, bf16[4,32,512]{2,1,0:T(8,128)(2,1)S(1)} %constant_dynamic-update-slice_fusion.refs_0_, bf16[4,32,512]{2,1,0:T(8,128)(2,1)S(1)} %collective-permute-done.5.refs_1_, ...), custom_call_target="tpu_custom_call" | custom-call | tf_op jit(solution)/shard_map/project/pallas_call | solution.py:246
  27.4 1.5 %scores.1 = f32[1,128]{1,0:T(1,128)} custom-call(f32[32,256]{1,0:T(8,128)S(1)} %get-tuple-element.29.noise_ref, f32[16,32,256]{2,1,0:T(8,128)S(1)} %project.1.proj_ref, f32[128,32,256]{2,1,0:T(8,128)S(1)} %get-tuple-element.37.wave_ref, bf16[128,32,256]{2,1,0:T(8,128)(2,1)S(1)} %get-tuple-element.38.images_ref), custom_call_target="tpu_custom_call" | custom-call | tf_op jit(solution)/shard_map/scores/pallas_call | solution.py:246
  28.8 0.0 collective-permute-done.3
  28.8 0.0 collective-permute-done.8
  28.8 2.1 %collective-permute-done.10 = bf16[2,32,512]{2,1,0:T(8,128)(2,1)S(1)} collective-permute-done((bf16[2,32,512]{2,1,0:T(8,128)(2,1)S(1)}, bf16[2,32,512]{2,1,0:T(8,128)(2,1)S(1)}, u32[]{:S(2)}, u32[]{:S(2)}) %collective-permute-start.10) | collective-permute-done | bytes 65568 | tf_op jit(solution)/shard_map/ppermute | solution.py:234
  30.9 0.0 collective-permute-done.9
  31.0 0.7 %fusion.10 = (f32[1,32,512]{2,1,0:T(8,128)}, f32[1,32,512]{2,1,0:T(8,128)}) fusion(f32[2,32,512]{2,1,0:T(8,128)S(1)} %fusion.4), kind=kLoop, calls=%fused_computation.19 | loop fusion | bytes 262144 | tf_op jit(solution)/shard_map/slice | solution.py:362
  (5 shorter events, 0.1 us)
Async XLA Ops:
  0.6 10.7 %collective-permute-start = (bf16[1,32,512]{2,1,0:T(8,128)(2,1)}, bf16[1,32,512]{2,1,0:T(8,128)(2,1)S(1)}, u32[]{:S(2)}, u32[]{:S(2)}) collective-permute-start(bf16[1,32,512]{2,1,0:T(8,128)(2,1)} %param.8), channel_id=1, source_target_pairs={{0,8},{1,9},{2,10},{3,11},{4,12},{5,13},{6,14},{7,15},{8,0},{9,1},... | collective-permute-start | bytes 98312 | tf_op jit(solution)/shard_map/ppermute | solution.py:234
  7.7 3.7 %copy-start = (bf16[1,32,512]{2,1,0:T(8,128)(2,1)S(1)}, bf16[1,32,512]{2,1,0:T(8,128)(2,1)}, u32[]{:S(2)}) copy-start(bf16[1,32,512]{2,1,0:T(8,128)(2,1)} %param.8) | copy-start | bytes 98308
  11.4 2.0 %collective-permute-start.1 = (bf16[8,2,32,512]{3,2,1,0:T(8,128)(2,1)S(1)}, bf16[8,2,32,512]{3,2,1,0:T(8,128)(2,1)S(1)}, u32[]{:S(2)}, u32[]{:S(2)}) collective-permute-start(bf16[8,2,32,512]{3,2,1,0:T(8,128)(2,1)S(1)} %get-tuple-element.27), channel_id=1, source_target_pairs={{0,1},{1,0},{2,3},{3,2},{4,5},{5,4},{6,7},{7,6},{8,9},{9,8},{10,11... | collective-permute-start | bytes 1572872 | tf_op jit(solution)/shard_map/ppermute | solution.py:234
  11.5 4.5 %collective-permute-start.4 = (bf16[2,32,512]{2,1,0:T(8,128)(2,1)S(1)}, bf16[2,32,512]{2,1,0:T(8,128)(2,1)S(1)}, u32[]{:S(2)}, u32[]{:S(2)}) collective-permute-start(bf16[2,32,512]{2,1,0:T(8,128)(2,1)S(1)} %pad_maximum_fusion), channel_id=1, source_target_pairs={{0,2},{1,3},{2,0},{3,1},{4,6},{5,7},{6,4},{7,5},{8,10},{9,11},{10,... | collective-permute-start | bytes 196616 | tf_op jit(solution)/shard_map/ppermute | solution.py:234
  13.4 7.6 %collective-permute-start.2 = (bf16[3,2,32,512]{3,2,1,0:T(8,128)(2,1)S(1)}, bf16[3,2,32,512]{3,2,1,0:T(8,128)(2,1)S(1)}, u32[]{:S(2)}, u32[]{:S(2)}) collective-permute-start(bf16[3,2,32,512]{3,2,1,0:T(8,128)(2,1)S(1)} %add_convert_fusion), channel_id=1, source_target_pairs={{0,2},{1,3},{2,0},{3,1},{4,6},{5,7},{6,4},{7,5},{8,10},{9,11},{10,... | collective-permute-start | bytes 589832 | tf_op jit(solution)/shard_map/ppermute | solution.py:234
  16.0 5.1 %collective-permute-start.5 = (bf16[4,32,512]{2,1,0:T(8,128)(2,1)S(1)}, bf16[4,32,512]{2,1,0:T(8,128)(2,1)S(1)}, u32[]{:S(2)}, u32[]{:S(2)}) collective-permute-start(bf16[4,32,512]{2,1,0:T(8,128)(2,1)S(1)} %constant_dynamic-update-slice_fusion.refs_0_), channel_id=1, source_target_pairs={{0,4},{1,5},{2,6},{3,7},{4,0},{5,1},{6,2},{7,3},{8,12},{9,13},{10,... | collective-permute-start | bytes 393224 | tf_op jit(solution)/shard_map/ppermute | solution.py:234
  17.6 6.7 %collective-permute-start.6 = (bf16[4,32,512]{2,1,0:T(8,128)(2,1)S(1)}, bf16[4,32,512]{2,1,0:T(8,128)(2,1)S(1)}, u32[]{:S(2)}, u32[]{:S(2)}) collective-permute-start(bf16[4,32,512]{2,1,0:T(8,128)(2,1)S(1)} %constant_dynamic-update-slice_fusion.refs_0_), channel_id=1, source_target_pairs={{0,1},{1,0},{2,3},{3,2},{4,5},{5,4},{6,7},{7,6},{8,9},{9,8},{10,11... | collective-permute-start | bytes 393224 | tf_op jit(solution)/shard_map/ppermute | solution.py:234
  17.6 11.3 %collective-permute-start.8 = (bf16[1,2,32,512]{3,2,1,0:T(8,128)(2,1)S(1)}, bf16[1,2,32,512]{3,2,1,0:T(8,128)(2,1)S(1)}, u32[]{:S(2)}, u32[]{:S(2)}) collective-permute-start(bf16[1,2,32,512]{3,2,1,0:T(8,128)(2,1)S(1)} %add_convert_fusion.1), channel_id=1, source_target_pairs={{0,2},{1,3},{2,0},{3,1},{4,6},{5,7},{6,4},{7,5},{8,10},{9,11},{10,... | collective-permute-start | bytes 196616 | tf_op jit(solution)/shard_map/ppermute | solution.py:234
  21.1 4.5 %collective-permute-start.7 = (bf16[4,32,512]{2,1,0:T(8,128)(2,1)S(1)}, bf16[4,32,512]{2,1,0:T(8,128)(2,1)S(1)}, u32[]{:S(2)}, u32[]{:S(2)}) collective-permute-start(bf16[4,32,512]{2,1,0:T(8,128)(2,1)S(1)} %collective-permute-done.5.refs_1_), channel_id=1, source_target_pairs={{0,1},{1,0},{2,3},{3,2},{4,5},{5,4},{6,7},{7,6},{8,9},{9,8},{10,11... | collective-permute-start | bytes 393224 | tf_op jit(solution)/shard_map/ppermute | solution.py:234
  21.1 7.7 %collective-permute-start.3 = (bf16[2,32,512]{2,1,0:T(8,128)(2,1)S(1)}, bf16[2,32,512]{2,1,0:T(8,128)(2,1)S(1)}, u32[]{:S(2)}, u32[]{:S(2)}) collective-permute-start(bf16[2,32,512]{2,1,0:T(8,128)(2,1)S(1)} %get-tuple-element.43), channel_id=1, source_target_pairs={{0,12},{1,13},{2,14},{3,15},{4,8},{5,9},{6,10},{7,11},{8,4},{9,5},... | collective-permute-start | bytes 196616 | tf_op jit(solution)/shard_map/ppermute | solution.py:234
  22.6 8.3 %collective-permute-start.10 = (bf16[2,32,512]{2,1,0:T(8,128)(2,1)S(1)}, bf16[2,32,512]{2,1,0:T(8,128)(2,1)S(1)}, u32[]{:S(2)}, u32[]{:S(2)}) collective-permute-start(bf16[2,32,512]{2,1,0:T(8,128)(2,1)S(1)} %get-tuple-element.41), channel_id=1, source_target_pairs={{0,8},{1,9},{2,10},{3,11},{4,12},{5,13},{6,14},{7,15},{8,0},{9,1},... | collective-permute-start | bytes 196616 | tf_op jit(solution)/shard_map/ppermute | solution.py:234
  24.3 6.6 %collective-permute-start.9 = (bf16[2,32,512]{2,1,0:T(8,128)(2,1)S(1)}, bf16[2,32,512]{2,1,0:T(8,128)(2,1)S(1)}, u32[]{:S(2)}, u32[]{:S(2)}) collective-permute-start(bf16[2,32,512]{2,1,0:T(8,128)(2,1)S(1)} %get-tuple-element.42), channel_id=1, source_target_pairs={{0,4},{1,5},{2,6},{3,7},{4,0},{5,1},{6,2},{7,3},{8,12},{9,13},{10,... | collective-permute-start | bytes 196616 | tf_op jit(solution)/shard_map/ppermute | solution.py:234

commit v15 on v14

--- a/solution.py
+++ b/solution.py
@@ -311,24 +311,32 @@
     def along_x(start, stop):
         return (keep[start:stop] + mate[far + start : far + stop].astype(f32)).astype(bf16)
 
-    main = [along_x(x * far + 1, (x + 1) * far) for x in range(wide - 1)]
-    later = [along_x(x * far, x * far + 1) for x in range(wide - 1)]
+    cut = max(1, far // 2)
+    main = [along_x(x * far + cut, (x + 1) * far) for x in range(wide - 1)]
+    later = [along_x(x * far, x * far + cut) for x in range(wide - 1)]
     (near,) = call(
         near_kernel, [((far, *place), f32)], [vmem] * 3, (place_rows, parts, mate), place_scratch, 0, 0, "near"
     )
     for offset in offsets[1:-1]:
-        came, _ = lax.optimization_barrier((swap(gathered, offset), main[0]))
+        came, _ = lax.optimization_barrier((swap(gathered, offset), near))
         gathered = jnp.concatenate([gathered, came], axis=0)
+    mine = [near[z] for z in range(far)]
+    for x in range(1, wide):
+        came = swap(main[x - 1], x * cores)
+        for z in range(cut, far):
+            mine[z] = mine[z] + came[z - cut].astype(f32)
+    outgoing = {z: mine[z].astype(bf16) for z in range(cut, far)}
+    for x in range(1, wide):
+        came, _ = lax.optimization_barrier((swap(later[x - 1], x * cores), outgoing[far - 1]))
+        for z in range(cut):
+            mine[z] = mine[z] + came[z].astype(f32)
+    outgoing.update({z: mine[z].astype(bf16) for z in range(1, cut)})
+    total = mine[0]
+
     columns = [gathered, swap(gathered, offsets[-1])]
     columns += [swap(column, 1) for column in columns]
+    _, *columns = lax.optimization_barrier((outgoing[1], *columns))
     places = [[a ^ last for a in away] for last in (0, offsets[-1], 1, offsets[-1] ^ 1)]
-    total, outgoing = near[0], [near[z] for z in range(1, far)]
-    for x in range(1, wide):
-        came = swap(main[x - 1], x * cores)
-        outgoing = [mine + came[z].astype(f32) for z, mine in enumerate(outgoing)]
-        total = total + swap(later[x - 1], x * cores)[0].astype(f32)
-    outgoing = [mine.astype(bf16) for mine in outgoing]
-    _, *columns = lax.optimization_barrier((outgoing[0], *columns))
     if devices * kinds <= batches * crossed:
         flat = pltpu.VMEM((kinds * devices * height, pixels), f32)
     else:
@@ -355,8 +363,8 @@
         "scores",
     )
     for z in range(1, far):
-        came = swap(outgoing[z - 1], z * wide * cores)
-        if z == far - 1:
+        came = swap(outgoing[z], z * wide * cores)
+        if z >= cut:
             came, scores = lax.optimization_barrier((came, scores))
         total = total + came.astype(f32)
     return scores.reshape(count), total[0:1], total[1:2]

time: 31.8 us -> 30.9 us (0.972)
  starting transfers between devices: 14.9 us -> 12.4 us
  waiting for transfers between devices: 4.2 us -> 5.74 us
    ppermute x11, starting transfers between devices: 14.9 us -> 12.4 us  [swap(): lax.ppermute(array, 'slab', [(i, i ^ offset) for i in range(devices)])]
    ppermute x11, waiting for transfers between devices: 4.2 us -> 5.74 us  [swap(): lax.ppermute(array, 'slab', [(i, i ^ offset) for i in range(devices)])]
  transfers between devices with their start and end apart: 11 -> 11, of which waited for: 4 -> 5; matrix products, arithmetic and copies ran while one was open for 0% -> 0% of each run, Pallas kernels for 35% -> 36%
where the time goes in v15:
time: 30.9 us; the launch traced here: 30.8 us
  starting transfers between devices  12.4 us (40%)
  Pallas kernels  11 us (36%)
  waiting for transfers between devices  5.74 us (19%)
  between operations  0.75 us (2%)
  local copies, waits for them, and re-layouts  0.68 us (2%)
    ppermute x11, starting transfers between devices, swap(): lax.ppermute(array, 'slab', [(i, i ^ offset) for i in range(devices)])  12.4 us
    pallas_call x5, Pallas kernels, call(): pl.pallas_call(kernel, out_shape=tuple((jax.ShapeDtypeStruct(s, t) for s,...  11 us
    ppermute x11, waiting for transfers between devices, swap(): lax.ppermute(array, 'slab', [(i, i ^ offset) for i in range(devices)])  5.74 us
    slice x1, local copies, waits for them, and re-layouts, on_device(): return (scores.reshape(count), total[0:1], total[1:2])  0.66 us
  transfers between devices with their start and end apart: 11, of which 5 were waited for; matrix products, arithmetic and copies ran while one was open for 0% of the time, Pallas kernels for 36%

profile of v15, /device:TPU:0, one launch (start us, length us, event | category | flops | bytes accessed | tf_op | source)
XLA Modules:
  0.0 30.8 jit_solution(907959759365880084)
XLA Ops:
  0.6 4.1 %collective-permute-start = (bf16[1,32,512]{2,1,0:T(8,128)(2,1)}, bf16[1,32,512]{2,1,0:T(8,128)(2,1)S(1)}, u32[]{:S(2)}, u32[]{:S(2)}) collective-permute-start(bf16[1,32,512]{2,1,0:T(8,128)(2,1)} %param.8), channel_id=1, source_target_pairs={{0,8},{1,9},{2,10},{3,11},{4,12},{5,13},{6,14},{7,15},{8,0},{9,1},... | collective-permute-start | bytes 98312 | tf_op jit(solution)/shard_map/ppermute | solution.py:234
  4.7 2.9 %sums.1 = (bf16[1024,256]{1,0:T(8,128)(2,1)S(1)}, f32[128,32,256]{2,1,0:T(8,128)S(1)}, bf16[8,512,256]{2,1,0:T(8,128)(2,1)S(1)}, bf16[128,32,256]{2,1,0:T(8,128)...) custom-call(s32[8,16]{1,0:T(8,128)} %bitcast.19, s32[8,16]{1,0:T(8,128)} %bitcast.20, ...), custom_call_target="tpu_custom_call" | custom-call | bytes 10485760 | tf_op jit(solution)/shard_map/sums/pallas_call | solution.py:246
  7.7 0.0 copy-start
  7.7 3.7 %insert.1 = (bf16[8,2,32,512]{3,2,1,0:T(8,128)(2,1)S(1)}, f32[4,2,32,512]{3,2,1,0:T(8,128)S(1)}, f32[8256,512]{1,0:T(8,128)S(1)}) custom-call(s32[16,16]{1,0:T(8,128)S(1)} %get-tuple-element.25.place_vmem, bf16[1024,256]{1,0:T(8,128)(2,1)S(1)} %get-tuple-element.26.sums_ref, bf16[8,512,256]{2,1,0:T(8,128)(2,1)S(1)} %get-tuple-element.27.tiles_ref), custom_call_target="tpu_custom_call" | custom-call | flops 2147483648 | bytes 8388608 | tf_op jit(solution)/shard_map/insert/pallas_call | solution.py:246
  11.4 0.0 collective-permute-done
  11.4 0.0 copy-done
  11.4 0.1 collective-permute-start.1
  11.5 1.6 %collective-permute-start.6 = (bf16[2,32,512]{2,1,0:T(8,128)(2,1)S(1)}, bf16[2,32,512]{2,1,0:T(8,128)(2,1)S(1)}, u32[]{:S(2)}, u32[]{:S(2)}) collective-permute-start(bf16[2,32,512]{2,1,0:T(8,128)(2,1)S(1)} %pad_maximum_fusion), channel_id=1, source_target_pairs={{0,2},{1,3},{2,0},{3,1},{4,6},{5,7},{6,4},{7,5},{8,10},{9,11},{10,... | collective-permute-start | bytes 196616 | tf_op jit(solution)/shard_map/ppermute | solution.py:234
  13.0 0.3 %collective-permute-done.1.mate_ref = bf16[8,2,32,512]{3,2,1,0:T(8,128)(2,1)S(1)} collective-permute-done((bf16[8,2,32,512]{3,2,1,0:T(8,128)(2,1)S(1)}, bf16[8,2,32,512]{3,2,1,0:T(8,128)(2,1)S(1)}, u32[]{:S(2)}, u32[]{:S(2)}) %collective-permute-start.1) | collective-permute-done | bytes 524320 | tf_op jit(solution)/shard_map/ppermute | solution.py:234
  13.4 0.1 add_convert_fusion
  13.5 1.6 %collective-permute-start.2 = (bf16[2,2,32,512]{3,2,1,0:T(8,128)(2,1)S(1)}, bf16[2,2,32,512]{3,2,1,0:T(8,128)(2,1)S(1)}, u32[]{:S(2)}, u32[]{:S(2)}) collective-permute-start(bf16[2,2,32,512]{3,2,1,0:T(8,128)(2,1)S(1)} %get-tuple-element.48), channel_id=1, source_target_pairs={{0,2},{1,3},{2,0},{3,1},{4,6},{5,7},{6,4},{7,5},{8,10},{9,11},{10,... | collective-permute-start | bytes 393224 | tf_op jit(solution)/shard_map/ppermute | solution.py:234
  15.0 1.1 %near.1 = f32[4,2,32,512]{3,2,1,0:T(8,128)S(1)} custom-call(s32[16,16]{1,0:T(8,128)S(1)} %get-tuple-element.25.place_vmem, f32[8256,512]{1,0:T(8,128)S(1)} %get-tuple-element.28.parts_ref, bf16[8,2,32,512]{3,2,1,0:T(8,128)(2,1)S(1)} %collective-permute-done.1.mate_ref), custom_call_target="tpu_custom_call" | custom-call | tf_op jit(solution)/shard_map/near/pallas_call | solution.py:246
  16.1 0.0 collective-permute-done.6
  16.2 1.6 %collective-permute-start.7 = (bf16[4,32,512]{2,1,0:T(8,128)(2,1)S(1)}, bf16[4,32,512]{2,1,0:T(8,128)(2,1)S(1)}, u32[]{:S(2)}, u32[]{:S(2)}) collective-permute-start(bf16[4,32,512]{2,1,0:T(8,128)(2,1)S(1)} %constant_dynamic-update-slice_fusion.refs_0_), channel_id=1, source_target_pairs={{0,4},{1,5},{2,6},{3,7},{4,0},{5,1},{6,2},{7,3},{8,12},{9,13},{10,... | collective-permute-start | bytes 393224 | tf_op jit(solution)/shard_map/ppermute | solution.py:234
  17.8 0.0 collective-permute-start.8
  17.8 1.2 %collective-permute-start.5 = (bf16[2,2,32,512]{3,2,1,0:T(8,128)(2,1)S(1)}, bf16[2,2,32,512]{3,2,1,0:T(8,128)(2,1)S(1)}, u32[]{:S(2)}, u32[]{:S(2)}) collective-permute-start(bf16[2,2,32,512]{3,2,1,0:T(8,128)(2,1)S(1)} %get-tuple-element.47), channel_id=1, source_target_pairs={{0,2},{1,3},{2,0},{3,1},{4,6},{5,7},{6,4},{7,5},{8,10},{9,11},{10,... | collective-permute-start | bytes 393224 | tf_op jit(solution)/shard_map/ppermute | solution.py:234
  19.1 0.0 collective-permute-done.2
  19.1 1.4 %collective-permute-start.3 = (bf16[2,32,512]{2,1,0:T(8,128)(2,1)S(1)}, bf16[2,32,512]{2,1,0:T(8,128)(2,1)S(1)}, u32[]{:S(2)}, u32[]{:S(2)}) collective-permute-start(bf16[2,32,512]{2,1,0:T(8,128)(2,1)S(1)} %get-tuple-element.50), channel_id=1, source_target_pairs={{0,12},{1,13},{2,14},{3,15},{4,8},{5,9},{6,10},{7,11},{8,4},{9,5},... | collective-permute-start | bytes 196616 | tf_op jit(solution)/shard_map/ppermute | solution.py:234
  20.5 3.2 %collective-permute-done.5 = bf16[2,2,32,512]{3,2,1,0:T(8,128)(2,1)S(1)} collective-permute-done((bf16[2,2,32,512]{3,2,1,0:T(8,128)(2,1)S(1)}, bf16[2,2,32,512]{3,2,1,0:T(8,128)(2,1)S(1)}, u32[]{:S(2)}, u32[]{:S(2)}) %collective-permute-start.5) | collective-permute-done | bytes 131104 | tf_op jit(solution)/shard_map/ppermute | solution.py:234
  23.7 0.3 %collective-permute-start.4 = (bf16[2,32,512]{2,1,0:T(8,128)(2,1)S(1)}, bf16[2,32,512]{2,1,0:T(8,128)(2,1)S(1)}, u32[]{:S(2)}, u32[]{:S(2)}) collective-permute-start(bf16[2,32,512]{2,1,0:T(8,128)(2,1)S(1)} %get-tuple-element.49), channel_id=1, source_target_pairs={{0,8},{1,9},{2,10},{3,11},{4,12},{5,13},{6,14},{7,15},{8,0},{9,1},... | collective-permute-start | bytes 196616 | tf_op jit(solution)/shard_map/ppermute | solution.py:234
  24.1 0.0 collective-permute-done.7.refs_1_
  24.1 0.0 collective-permute-start.9
  24.1 0.5 %collective-permute-start.10 = (bf16[2,32,512]{2,1,0:T(8,128)(2,1)S(1)}, bf16[2,32,512]{2,1,0:T(8,128)(2,1)S(1)}, u32[]{:S(2)}, u32[]{:S(2)}) collective-permute-start(bf16[2,32,512]{2,1,0:T(8,128)(2,1)S(1)} %fusion.9), channel_id=1, source_target_pairs={{0,4},{1,5},{2,6},{3,7},{4,0},{5,1},{6,2},{7,3},{8,12},{9,13},{10,... | collective-permute-start | bytes 196616 | tf_op jit(solution)/shard_map/ppermute | solution.py:234
  24.6 0.0 collective-permute-done.8.refs_2_
  24.6 0.8 %collective-permute-done.9.refs_3_ = bf16[4,32,512]{2,1,0:T(8,128)(2,1)S(1)} collective-permute-done((bf16[4,32,512]{2,1,0:T(8,128)(2,1)S(1)}, bf16[4,32,512]{2,1,0:T(8,128)(2,1)S(1)}, u32[]{:S(2)}, u32[]{:S(2)}) %collective-permute-start.9) | collective-permute-done | bytes 131104 | tf_op jit(solution)/shard_map/ppermute | solution.py:234
  25.4 1.8 %project.1.proj_ref = f32[16,32,256]{2,1,0:T(8,128)S(1)} custom-call(s32[8,16]{1,0:T(8,128)S(1)} %get-tuple-element.33.route_vmem, bf16[8,512,256]{2,1,0:T(8,128)(2,1)S(1)} %get-tuple-element.27.tiles_ref, bf16[4,32,512]{2,1,0:T(8,128)(2,1)S(1)} %constant_dynamic-update-slice_fusion.refs_0_, bf16[4,32,512]{2,1,0:T(8,128)(2,1)S(1)} %collective-permute-done.7.refs_1_, ...), custom_call_target="tpu_custom_call" | custom-call | tf_op jit(solution)/shard_map/project/pallas_call | solution.py:246
  27.2 1.5 %scores.1 = f32[1,128]{1,0:T(1,128)} custom-call(f32[32,256]{1,0:T(8,128)S(1)} %get-tuple-element.32.noise_ref, f32[16,32,256]{2,1,0:T(8,128)S(1)} %project.1.proj_ref, f32[128,32,256]{2,1,0:T(8,128)S(1)} %get-tuple-element.41.wave_ref, bf16[128,32,256]{2,1,0:T(8,128)(2,1)S(1)} %get-tuple-element.42.images_ref), custom_call_target="tpu_custom_call" | custom-call | tf_op jit(solution)/shard_map/scores/pallas_call | solution.py:246
  28.7 1.1 %collective-permute-done.4 = bf16[2,32,512]{2,1,0:T(8,128)(2,1)S(1)} collective-permute-done((bf16[2,32,512]{2,1,0:T(8,128)(2,1)S(1)}, bf16[2,32,512]{2,1,0:T(8,128)(2,1)S(1)}, u32[]{:S(2)}, u32[]{:S(2)}) %collective-permute-start.4) | collective-permute-done | bytes 65568 | tf_op jit(solution)/shard_map/ppermute | solution.py:234
  29.8 0.0 collective-permute-done.3
  29.8 0.3 collective-permute-done.10
  30.1 0.7 %fusion.10 = (f32[1,32,512]{2,1,0:T(8,128)}, f32[1,32,512]{2,1,0:T(8,128)}) fusion(f32[2,32,512]{2,1,0:T(8,128)S(1)} %fusion.3), kind=kLoop, calls=%fused_computation.19 | loop fusion | bytes 262144 | tf_op jit(solution)/shard_map/slice | solution.py:370
  (6 shorter events, 0.1 us)
Async XLA Ops:
  0.6 10.7 %collective-permute-start = (bf16[1,32,512]{2,1,0:T(8,128)(2,1)}, bf16[1,32,512]{2,1,0:T(8,128)(2,1)S(1)}, u32[]{:S(2)}, u32[]{:S(2)}) collective-permute-start(bf16[1,32,512]{2,1,0:T(8,128)(2,1)} %param.8), channel_id=1, source_target_pairs={{0,8},{1,9},{2,10},{3,11},{4,12},{5,13},{6,14},{7,15},{8,0},{9,1},... | collective-permute-start | bytes 98312 | tf_op jit(solution)/shard_map/ppermute | solution.py:234
  7.7 3.7 %copy-start = (bf16[1,32,512]{2,1,0:T(8,128)(2,1)S(1)}, bf16[1,32,512]{2,1,0:T(8,128)(2,1)}, u32[]{:S(2)}) copy-start(bf16[1,32,512]{2,1,0:T(8,128)(2,1)} %param.8) | copy-start | bytes 98308
  11.4 2.0 %collective-permute-start.1 = (bf16[8,2,32,512]{3,2,1,0:T(8,128)(2,1)S(1)}, bf16[8,2,32,512]{3,2,1,0:T(8,128)(2,1)S(1)}, u32[]{:S(2)}, u32[]{:S(2)}) collective-permute-start(bf16[8,2,32,512]{3,2,1,0:T(8,128)(2,1)S(1)} %get-tuple-element.30), channel_id=1, source_target_pairs={{0,1},{1,0},{2,3},{3,2},{4,5},{5,4},{6,7},{7,6},{8,9},{9,8},{10,11... | collective-permute-start | bytes 1572872 | tf_op jit(solution)/shard_map/ppermute | solution.py:234
  11.5 4.7 %collective-permute-start.6 = (bf16[2,32,512]{2,1,0:T(8,128)(2,1)S(1)}, bf16[2,32,512]{2,1,0:T(8,128)(2,1)S(1)}, u32[]{:S(2)}, u32[]{:S(2)}) collective-permute-start(bf16[2,32,512]{2,1,0:T(8,128)(2,1)S(1)} %pad_maximum_fusion), channel_id=1, source_target_pairs={{0,2},{1,3},{2,0},{3,1},{4,6},{5,7},{6,4},{7,5},{8,10},{9,11},{10,... | collective-permute-start | bytes 196616 | tf_op jit(solution)/shard_map/ppermute | solution.py:234
  13.5 5.6 %collective-permute-start.2 = (bf16[2,2,32,512]{3,2,1,0:T(8,128)(2,1)S(1)}, bf16[2,2,32,512]{3,2,1,0:T(8,128)(2,1)S(1)}, u32[]{:S(2)}, u32[]{:S(2)}) collective-permute-start(bf16[2,2,32,512]{3,2,1,0:T(8,128)(2,1)S(1)} %get-tuple-element.48), channel_id=1, source_target_pairs={{0,2},{1,3},{2,0},{3,1},{4,6},{5,7},{6,4},{7,5},{8,10},{9,11},{10,... | collective-permute-start | bytes 393224 | tf_op jit(solution)/shard_map/ppermute | solution.py:234
  16.2 7.9 %collective-permute-start.7 = (bf16[4,32,512]{2,1,0:T(8,128)(2,1)S(1)}, bf16[4,32,512]{2,1,0:T(8,128)(2,1)S(1)}, u32[]{:S(2)}, u32[]{:S(2)}) collective-permute-start(bf16[4,32,512]{2,1,0:T(8,128)(2,1)S(1)} %constant_dynamic-update-slice_fusion.refs_0_), channel_id=1, source_target_pairs={{0,4},{1,5},{2,6},{3,7},{4,0},{5,1},{6,2},{7,3},{8,12},{9,13},{10,... | collective-permute-start | bytes 393224 | tf_op jit(solution)/shard_map/ppermute | solution.py:234
  17.8 6.8 %collective-permute-start.8 = (bf16[4,32,512]{2,1,0:T(8,128)(2,1)S(1)}, bf16[4,32,512]{2,1,0:T(8,128)(2,1)S(1)}, u32[]{:S(2)}, u32[]{:S(2)}) collective-permute-start(bf16[4,32,512]{2,1,0:T(8,128)(2,1)S(1)} %constant_dynamic-update-slice_fusion.refs_0_), channel_id=1, source_target_pairs={{0,1},{1,0},{2,3},{3,2},{4,5},{5,4},{6,7},{7,6},{8,9},{9,8},{10,11... | collective-permute-start | bytes 393224 | tf_op jit(solution)/shard_map/ppermute | solution.py:234
  17.8 5.9 %collective-permute-start.5 = (bf16[2,2,32,512]{3,2,1,0:T(8,128)(2,1)S(1)}, bf16[2,2,32,512]{3,2,1,0:T(8,128)(2,1)S(1)}, u32[]{:S(2)}, u32[]{:S(2)}) collective-permute-start(bf16[2,2,32,512]{3,2,1,0:T(8,128)(2,1)S(1)} %get-tuple-element.47), channel_id=1, source_target_pairs={{0,2},{1,3},{2,0},{3,1},{4,6},{5,7},{6,4},{7,5},{8,10},{9,11},{10,... | collective-permute-start | bytes 393224 | tf_op jit(solution)/shard_map/ppermute | solution.py:234
  19.1 10.7 %collective-permute-start.3 = (bf16[2,32,512]{2,1,0:T(8,128)(2,1)S(1)}, bf16[2,32,512]{2,1,0:T(8,128)(2,1)S(1)}, u32[]{:S(2)}, u32[]{:S(2)}) collective-permute-start(bf16[2,32,512]{2,1,0:T(8,128)(2,1)S(1)} %get-tuple-element.50), channel_id=1, source_target_pairs={{0,12},{1,13},{2,14},{3,15},{4,8},{5,9},{6,10},{7,11},{8,4},{9,5},... | collective-permute-start | bytes 196616 | tf_op jit(solution)/shard_map/ppermute | solution.py:234
  23.7 6.0 %collective-permute-start.4 = (bf16[2,32,512]{2,1,0:T(8,128)(2,1)S(1)}, bf16[2,32,512]{2,1,0:T(8,128)(2,1)S(1)}, u32[]{:S(2)}, u32[]{:S(2)}) collective-permute-start(bf16[2,32,512]{2,1,0:T(8,128)(2,1)S(1)} %get-tuple-element.49), channel_id=1, source_target_pairs={{0,8},{1,9},{2,10},{3,11},{4,12},{5,13},{6,14},{7,15},{8,0},{9,1},... | collective-permute-start | bytes 196616 | tf_op jit(solution)/shard_map/ppermute | solution.py:234
  24.1 1.3 %collective-permute-start.9 = (bf16[4,32,512]{2,1,0:T(8,128)(2,1)S(1)}, bf16[4,32,512]{2,1,0:T(8,128)(2,1)S(1)}, u32[]{:S(2)}, u32[]{:S(2)}) collective-permute-start(bf16[4,32,512]{2,1,0:T(8,128)(2,1)S(1)} %collective-permute-done.7.refs_1_), channel_id=1, source_target_pairs={{0,1},{1,0},{2,3},{3,2},{4,5},{5,4},{6,7},{7,6},{8,9},{9,8},{10,11... | collective-permute-start | bytes 393224 | tf_op jit(solution)/shard_map/ppermute | solution.py:234
  24.1 5.9 %collective-permute-start.10 = (bf16[2,32,512]{2,1,0:T(8,128)(2,1)S(1)}, bf16[2,32,512]{2,1,0:T(8,128)(2,1)S(1)}, u32[]{:S(2)}, u32[]{:S(2)}) collective-permute-start(bf16[2,32,512]{2,1,0:T(8,128)(2,1)S(1)} %fusion.9), channel_id=1, source_target_pairs={{0,4},{1,5},{2,6},{3,7},{4,0},{5,1},{6,2},{7,3},{8,12},{9,13},{10,... | collective-permute-start | bytes 196616 | tf_op jit(solution)/shard_map/ppermute | solution.py:234

commit v16 on v15

--- a/solution.py
+++ b/solution.py
@@ -333,7 +333,8 @@
     outgoing.update({z: mine[z].astype(bf16) for z in range(1, cut)})
     total = mine[0]
 
-    columns = [gathered, swap(gathered, offsets[-1])]
+    held, _ = lax.optimization_barrier((gathered, later[0]))
+    columns = [gathered, swap(held, offsets[-1])]
     columns += [swap(column, 1) for column in columns]
     _, *columns = lax.optimization_barrier((outgoing[1], *columns))
     places = [[a ^ last for a in away] for last in (0, offsets[-1], 1, offsets[-1] ^ 1)]

time: 30.9 us -> 29.9 us (0.968)
  waiting for transfers between devices: 5.74 us -> 2.78 us
  starting transfers between devices: 12.4 us -> 14.3 us
    ppermute x11, waiting for transfers between devices: 5.74 us -> 2.78 us  [swap(): lax.ppermute(array, 'slab', [(i, i ^ offset) for i in range(devices)])]
    ppermute x11, starting transfers between devices: 12.4 us -> 14.3 us  [swap(): lax.ppermute(array, 'slab', [(i, i ^ offset) for i in range(devices)])]
  transfers between devices with their start and end apart: 11 -> 11, of which waited for: 5 -> 4; matrix products, arithmetic and copies ran while one was open for 0% -> 0% of each run, Pallas kernels for 36% -> 37%
where the time goes in v16:
time: 29.9 us; the launch traced here: 29.7 us
  starting transfers between devices  14.3 us (48%)
  Pallas kernels  11 us (37%)
  waiting for transfers between devices  2.78 us (9%)
  between operations  0.75 us (3%)
  local copies, waits for them, and re-layouts  0.68 us (2%)
    ppermute x11, starting transfers between devices, swap(): lax.ppermute(array, 'slab', [(i, i ^ offset) for i in range(devices)])  14.3 us
    pallas_call x5, Pallas kernels, call(): pl.pallas_call(kernel, out_shape=tuple((jax.ShapeDtypeStruct(s, t) for s,...  11 us
    ppermute x11, waiting for transfers between devices, swap(): lax.ppermute(array, 'slab', [(i, i ^ offset) for i in range(devices)])  2.78 us
    slice x1, local copies, waits for them, and re-layouts, on_device(): return (scores.reshape(count), total[0:1], total[1:2])  0.66 us
  transfers between devices with their start and end apart: 11, of which 4 were waited for; matrix products, arithmetic and copies ran while one was open for 0% of the time, Pallas kernels for 37%

profile of v16, /device:TPU:0, one launch (start us, length us, event | category | flops | bytes accessed | tf_op | source)
XLA Modules:
  0.0 29.7 jit_solution(17331515600896820857)
XLA Ops:
  0.6 4.1 %collective-permute-start = (bf16[1,32,512]{2,1,0:T(8,128)(2,1)}, bf16[1,32,512]{2,1,0:T(8,128)(2,1)S(1)}, u32[]{:S(2)}, u32[]{:S(2)}) collective-permute-start(bf16[1,32,512]{2,1,0:T(8,128)(2,1)} %param.8), channel_id=1, source_target_pairs={{0,8},{1,9},{2,10},{3,11},{4,12},{5,13},{6,14},{7,15},{8,0},{9,1},... | collective-permute-start | bytes 98312 | tf_op jit(solution)/shard_map/ppermute | solution.py:234
  4.7 2.9 %sums.1 = (bf16[1024,256]{1,0:T(8,128)(2,1)S(1)}, f32[128,32,256]{2,1,0:T(8,128)S(1)}, bf16[8,512,256]{2,1,0:T(8,128)(2,1)S(1)}, bf16[128,32,256]{2,1,0:T(8,128)...) custom-call(s32[8,16]{1,0:T(8,128)} %bitcast.19, s32[8,16]{1,0:T(8,128)} %bitcast.20, ...), custom_call_target="tpu_custom_call" | custom-call | bytes 10485760 | tf_op jit(solution)/shard_map/sums/pallas_call | solution.py:246
  7.7 0.0 copy-start
  7.7 3.7 %insert.1 = (bf16[8,2,32,512]{3,2,1,0:T(8,128)(2,1)S(1)}, f32[4,2,32,512]{3,2,1,0:T(8,128)S(1)}, f32[8256,512]{1,0:T(8,128)S(1)}) custom-call(s32[16,16]{1,0:T(8,128)S(1)} %get-tuple-element.26.place_vmem, bf16[1024,256]{1,0:T(8,128)(2,1)S(1)} %get-tuple-element.27.sums_ref, bf16[8,512,256]{2,1,0:T(8,128)(2,1)S(1)} %get-tuple-element.28.tiles_ref), custom_call_target="tpu_custom_call" | custom-call | flops 2147483648 | bytes 8388608 | tf_op jit(solution)/shard_map/insert/pallas_call | solution.py:246
  11.4 0.0 collective-permute-done
  11.4 0.0 copy-done
  11.4 0.1 collective-permute-start.1
  11.5 1.6 %collective-permute-start.6 = (bf16[2,32,512]{2,1,0:T(8,128)(2,1)S(1)}, bf16[2,32,512]{2,1,0:T(8,128)(2,1)S(1)}, u32[]{:S(2)}, u32[]{:S(2)}) collective-permute-start(bf16[2,32,512]{2,1,0:T(8,128)(2,1)S(1)} %pad_maximum_fusion), channel_id=1, source_target_pairs={{0,2},{1,3},{2,0},{3,1},{4,6},{5,7},{6,4},{7,5},{8,10},{9,11},{10,... | collective-permute-start | bytes 196616 | tf_op jit(solution)/shard_map/ppermute | solution.py:234
  13.0 0.3 %collective-permute-done.1.mate_ref = bf16[8,2,32,512]{3,2,1,0:T(8,128)(2,1)S(1)} collective-permute-done((bf16[8,2,32,512]{3,2,1,0:T(8,128)(2,1)S(1)}, bf16[8,2,32,512]{3,2,1,0:T(8,128)(2,1)S(1)}, u32[]{:S(2)}, u32[]{:S(2)}) %collective-permute-start.1) | collective-permute-done | bytes 524320 | tf_op jit(solution)/shard_map/ppermute | solution.py:234
  13.4 0.1 add_convert_fusion
  13.5 1.6 %collective-permute-start.2 = (bf16[2,2,32,512]{3,2,1,0:T(8,128)(2,1)S(1)}, bf16[2,2,32,512]{3,2,1,0:T(8,128)(2,1)S(1)}, u32[]{:S(2)}, u32[]{:S(2)}) collective-permute-start(bf16[2,2,32,512]{3,2,1,0:T(8,128)(2,1)S(1)} %get-tuple-element.50), channel_id=1, source_target_pairs={{0,2},{1,3},{2,0},{3,1},{4,6},{5,7},{6,4},{7,5},{8,10},{9,11},{10,... | collective-permute-start | bytes 393224 | tf_op jit(solution)/shard_map/ppermute | solution.py:234
  15.0 1.1 %near.1 = f32[4,2,32,512]{3,2,1,0:T(8,128)S(1)} custom-call(s32[16,16]{1,0:T(8,128)S(1)} %get-tuple-element.26.place_vmem, f32[8256,512]{1,0:T(8,128)S(1)} %get-tuple-element.29.parts_ref, bf16[8,2,32,512]{3,2,1,0:T(8,128)(2,1)S(1)} %collective-permute-done.1.mate_ref), custom_call_target="tpu_custom_call" | custom-call | tf_op jit(solution)/shard_map/near/pallas_call | solution.py:246
  16.1 0.0 collective-permute-done.6
  16.2 0.1 collective-permute-start.8
  16.3 1.3 %collective-permute-start.5 = (bf16[2,2,32,512]{3,2,1,0:T(8,128)(2,1)S(1)}, bf16[2,2,32,512]{3,2,1,0:T(8,128)(2,1)S(1)}, u32[]{:S(2)}, u32[]{:S(2)}) collective-permute-start(bf16[2,2,32,512]{3,2,1,0:T(8,128)(2,1)S(1)} %get-tuple-element.49), channel_id=1, source_target_pairs={{0,2},{1,3},{2,0},{3,1},{4,6},{5,7},{6,4},{7,5},{8,10},{9,11},{10,... | collective-permute-start | bytes 393224 | tf_op jit(solution)/shard_map/ppermute | solution.py:234
  17.6 1.6 %collective-permute-start.7 = (bf16[4,32,512]{2,1,0:T(8,128)(2,1)S(1)}, bf16[4,32,512]{2,1,0:T(8,128)(2,1)S(1)}, u32[]{:S(2)}, u32[]{:S(2)}) collective-permute-start(bf16[4,32,512]{2,1,0:T(8,128)(2,1)S(1)} %constant_dynamic-update-slice_fusion.refs_0_), channel_id=1, source_target_pairs={{0,4},{1,5},{2,6},{3,7},{4,0},{5,1},{6,2},{7,3},{8,12},{9,13},{10,... | collective-permute-start | bytes 393224 | tf_op jit(solution)/shard_map/ppermute | solution.py:234
  19.1 0.0 collective-permute-done.2
  19.2 1.3 %collective-permute-start.3 = (bf16[2,32,512]{2,1,0:T(8,128)(2,1)S(1)}, bf16[2,32,512]{2,1,0:T(8,128)(2,1)S(1)}, u32[]{:S(2)}, u32[]{:S(2)}) collective-permute-start(bf16[2,32,512]{2,1,0:T(8,128)(2,1)S(1)} %get-tuple-element.52), channel_id=1, source_target_pairs={{0,12},{1,13},{2,14},{3,15},{4,8},{5,9},{6,10},{7,11},{8,4},{9,5},... | collective-permute-start | bytes 196616 | tf_op jit(solution)/shard_map/ppermute | solution.py:234
  20.5 1.7 %collective-permute-done.5 = bf16[2,2,32,512]{3,2,1,0:T(8,128)(2,1)S(1)} collective-permute-done((bf16[2,2,32,512]{3,2,1,0:T(8,128)(2,1)S(1)}, bf16[2,2,32,512]{3,2,1,0:T(8,128)(2,1)S(1)}, u32[]{:S(2)}, u32[]{:S(2)}) %collective-permute-start.5) | collective-permute-done | bytes 131104 | tf_op jit(solution)/shard_map/ppermute | solution.py:234
  22.2 0.3 %collective-permute-start.4 = (bf16[2,32,512]{2,1,0:T(8,128)(2,1)S(1)}, bf16[2,32,512]{2,1,0:T(8,128)(2,1)S(1)}, u32[]{:S(2)}, u32[]{:S(2)}) collective-permute-start(bf16[2,32,512]{2,1,0:T(8,128)(2,1)S(1)} %get-tuple-element.51), channel_id=1, source_target_pairs={{0,8},{1,9},{2,10},{3,11},{4,12},{5,13},{6,14},{7,15},{8,0},{9,1},... | collective-permute-start | bytes 196616 | tf_op jit(solution)/shard_map/ppermute | solution.py:234
  22.5 0.6 %collective-permute-done.7.refs_1_ = bf16[4,32,512]{2,1,0:T(8,128)(2,1)S(1)} collective-permute-done((bf16[4,32,512]{2,1,0:T(8,128)(2,1)S(1)}, bf16[4,32,512]{2,1,0:T(8,128)(2,1)S(1)}, u32[]{:S(2)}, u32[]{:S(2)}) %collective-permute-start.7) | collective-permute-done | bytes 131104 | tf_op jit(solution)/shard_map/ppermute | solution.py:234
  23.1 0.0 collective-permute-start.9
  23.1 2.4 %collective-permute-start.10 = (bf16[2,32,512]{2,1,0:T(8,128)(2,1)S(1)}, bf16[2,32,512]{2,1,0:T(8,128)(2,1)S(1)}, u32[]{:S(2)}, u32[]{:S(2)}) collective-permute-start(bf16[2,32,512]{2,1,0:T(8,128)(2,1)S(1)} %fusion.9), channel_id=1, source_target_pairs={{0,4},{1,5},{2,6},{3,7},{4,0},{5,1},{6,2},{7,3},{8,12},{9,13},{10,... | collective-permute-start | bytes 196616 | tf_op jit(solution)/shard_map/ppermute | solution.py:234
  25.6 0.0 collective-permute-done.8.refs_2_
  25.6 0.0 collective-permute-done.9.refs_3_
  25.6 1.8 %project.1.proj_ref = f32[16,32,256]{2,1,0:T(8,128)S(1)} custom-call(s32[8,16]{1,0:T(8,128)S(1)} %get-tuple-element.34.route_vmem, bf16[8,512,256]{2,1,0:T(8,128)(2,1)S(1)} %get-tuple-element.28.tiles_ref, bf16[4,32,512]{2,1,0:T(8,128)(2,1)S(1)} %constant_dynamic-update-slice_fusion.refs_0_, bf16[4,32,512]{2,1,0:T(8,128)(2,1)S(1)} %collective-permute-done.7.refs_1_, ...), custom_call_target="tpu_custom_call" | custom-call | tf_op jit(solution)/shard_map/project/pallas_call | solution.py:246
  27.4 1.5 %scores.1 = f32[1,128]{1,0:T(1,128)} custom-call(f32[32,256]{1,0:T(8,128)S(1)} %get-tuple-element.33.noise_ref, f32[16,32,256]{2,1,0:T(8,128)S(1)} %project.1.proj_ref, f32[128,32,256]{2,1,0:T(8,128)S(1)} %get-tuple-element.43.wave_ref, bf16[128,32,256]{2,1,0:T(8,128)(2,1)S(1)} %get-tuple-element.44.images_ref), custom_call_target="tpu_custom_call" | custom-call | tf_op jit(solution)/shard_map/scores/pallas_call | solution.py:246
  28.8 0.0 collective-permute-done.4
  28.8 0.0 collective-permute-done.3
  28.8 0.2 collective-permute-done.10
  29.1 0.7 %fusion.10 = (f32[1,32,512]{2,1,0:T(8,128)}, f32[1,32,512]{2,1,0:T(8,128)}) fusion(f32[2,32,512]{2,1,0:T(8,128)S(1)} %fusion.3), kind=kLoop, calls=%fused_computation.19 | loop fusion | bytes 262144 | tf_op jit(solution)/shard_map/slice | solution.py:371
  (6 shorter events, 0.1 us)
Async XLA Ops:
  0.6 10.7 %collective-permute-start = (bf16[1,32,512]{2,1,0:T(8,128)(2,1)}, bf16[1,32,512]{2,1,0:T(8,128)(2,1)S(1)}, u32[]{:S(2)}, u32[]{:S(2)}) collective-permute-start(bf16[1,32,512]{2,1,0:T(8,128)(2,1)} %param.8), channel_id=1, source_target_pairs={{0,8},{1,9},{2,10},{3,11},{4,12},{5,13},{6,14},{7,15},{8,0},{9,1},... | collective-permute-start | bytes 98312 | tf_op jit(solution)/shard_map/ppermute | solution.py:234
  7.7 3.7 %copy-start = (bf16[1,32,512]{2,1,0:T(8,128)(2,1)S(1)}, bf16[1,32,512]{2,1,0:T(8,128)(2,1)}, u32[]{:S(2)}) copy-start(bf16[1,32,512]{2,1,0:T(8,128)(2,1)} %param.8) | copy-start | bytes 98308
  11.4 2.0 %collective-permute-start.1 = (bf16[8,2,32,512]{3,2,1,0:T(8,128)(2,1)S(1)}, bf16[8,2,32,512]{3,2,1,0:T(8,128)(2,1)S(1)}, u32[]{:S(2)}, u32[]{:S(2)}) collective-permute-start(bf16[8,2,32,512]{3,2,1,0:T(8,128)(2,1)S(1)} %get-tuple-element.31), channel_id=1, source_target_pairs={{0,1},{1,0},{2,3},{3,2},{4,5},{5,4},{6,7},{7,6},{8,9},{9,8},{10,11... | collective-permute-start | bytes 1572872 | tf_op jit(solution)/shard_map/ppermute | solution.py:234
  11.5 4.7 %collective-permute-start.6 = (bf16[2,32,512]{2,1,0:T(8,128)(2,1)S(1)}, bf16[2,32,512]{2,1,0:T(8,128)(2,1)S(1)}, u32[]{:S(2)}, u32[]{:S(2)}) collective-permute-start(bf16[2,32,512]{2,1,0:T(8,128)(2,1)S(1)} %pad_maximum_fusion), channel_id=1, source_target_pairs={{0,2},{1,3},{2,0},{3,1},{4,6},{5,7},{6,4},{7,5},{8,10},{9,11},{10,... | collective-permute-start | bytes 196616 | tf_op jit(solution)/shard_map/ppermute | solution.py:234
  13.5 5.7 %collective-permute-start.2 = (bf16[2,2,32,512]{3,2,1,0:T(8,128)(2,1)S(1)}, bf16[2,2,32,512]{3,2,1,0:T(8,128)(2,1)S(1)}, u32[]{:S(2)}, u32[]{:S(2)}) collective-permute-start(bf16[2,2,32,512]{3,2,1,0:T(8,128)(2,1)S(1)} %get-tuple-element.50), channel_id=1, source_target_pairs={{0,2},{1,3},{2,0},{3,1},{4,6},{5,7},{6,4},{7,5},{8,10},{9,11},{10,... | collective-permute-start | bytes 393224 | tf_op jit(solution)/shard_map/ppermute | solution.py:234
  16.2 9.4 %collective-permute-start.8 = (bf16[4,32,512]{2,1,0:T(8,128)(2,1)S(1)}, bf16[4,32,512]{2,1,0:T(8,128)(2,1)S(1)}, u32[]{:S(2)}, u32[]{:S(2)}) collective-permute-start(bf16[4,32,512]{2,1,0:T(8,128)(2,1)S(1)} %constant_dynamic-update-slice_fusion.refs_0_), channel_id=1, source_target_pairs={{0,1},{1,0},{2,3},{3,2},{4,5},{5,4},{6,7},{7,6},{8,9},{9,8},{10,11... | collective-permute-start | bytes 393224 | tf_op jit(solution)/shard_map/ppermute | solution.py:234
  16.3 5.9 %collective-permute-start.5 = (bf16[2,2,32,512]{3,2,1,0:T(8,128)(2,1)S(1)}, bf16[2,2,32,512]{3,2,1,0:T(8,128)(2,1)S(1)}, u32[]{:S(2)}, u32[]{:S(2)}) collective-permute-start(bf16[2,2,32,512]{3,2,1,0:T(8,128)(2,1)S(1)} %get-tuple-element.49), channel_id=1, source_target_pairs={{0,2},{1,3},{2,0},{3,1},{4,6},{5,7},{6,4},{7,5},{8,10},{9,11},{10,... | collective-permute-start | bytes 393224 | tf_op jit(solution)/shard_map/ppermute | solution.py:234
  17.6 5.6 %collective-permute-start.7 = (bf16[4,32,512]{2,1,0:T(8,128)(2,1)S(1)}, bf16[4,32,512]{2,1,0:T(8,128)(2,1)S(1)}, u32[]{:S(2)}, u32[]{:S(2)}) collective-permute-start(bf16[4,32,512]{2,1,0:T(8,128)(2,1)S(1)} %constant_dynamic-update-slice_fusion.refs_0_), channel_id=1, source_target_pairs={{0,4},{1,5},{2,6},{3,7},{4,0},{5,1},{6,2},{7,3},{8,12},{9,13},{10,... | collective-permute-start | bytes 393224 | tf_op jit(solution)/shard_map/ppermute | solution.py:234
  19.2 9.7 %collective-permute-start.3 = (bf16[2,32,512]{2,1,0:T(8,128)(2,1)S(1)}, bf16[2,32,512]{2,1,0:T(8,128)(2,1)S(1)}, u32[]{:S(2)}, u32[]{:S(2)}) collective-permute-start(bf16[2,32,512]{2,1,0:T(8,128)(2,1)S(1)} %get-tuple-element.52), channel_id=1, source_target_pairs={{0,12},{1,13},{2,14},{3,15},{4,8},{5,9},{6,10},{7,11},{8,4},{9,5},... | collective-permute-start | bytes 196616 | tf_op jit(solution)/shard_map/ppermute | solution.py:234
  22.2 6.7 %collective-permute-start.4 = (bf16[2,32,512]{2,1,0:T(8,128)(2,1)S(1)}, bf16[2,32,512]{2,1,0:T(8,128)(2,1)S(1)}, u32[]{:S(2)}, u32[]{:S(2)}) collective-permute-start(bf16[2,32,512]{2,1,0:T(8,128)(2,1)S(1)} %get-tuple-element.51), channel_id=1, source_target_pairs={{0,8},{1,9},{2,10},{3,11},{4,12},{5,13},{6,14},{7,15},{8,0},{9,1},... | collective-permute-start | bytes 196616 | tf_op jit(solution)/shard_map/ppermute | solution.py:234
  23.1 2.5 %collective-permute-start.9 = (bf16[4,32,512]{2,1,0:T(8,128)(2,1)S(1)}, bf16[4,32,512]{2,1,0:T(8,128)(2,1)S(1)}, u32[]{:S(2)}, u32[]{:S(2)}) collective-permute-start(bf16[4,32,512]{2,1,0:T(8,128)(2,1)S(1)} %collective-permute-done.7.refs_1_), channel_id=1, source_target_pairs={{0,1},{1,0},{2,3},{3,2},{4,5},{5,4},{6,7},{7,6},{8,9},{9,8},{10,11... | collective-permute-start | bytes 393224 | tf_op jit(solution)/shard_map/ppermute | solution.py:234
  23.1 5.9 %collective-permute-start.10 = (bf16[2,32,512]{2,1,0:T(8,128)(2,1)S(1)}, bf16[2,32,512]{2,1,0:T(8,128)(2,1)S(1)}, u32[]{:S(2)}, u32[]{:S(2)}) collective-permute-start(bf16[2,32,512]{2,1,0:T(8,128)(2,1)S(1)} %fusion.9), channel_id=1, source_target_pairs={{0,4},{1,5},{2,6},{3,7},{4,0},{5,1},{6,2},{7,3},{8,12},{9,13},{10,... | collective-permute-start | bytes 196616 | tf_op jit(solution)/shard_map/ppermute | solution.py:234

commit v17 on v16

--- a/solution.py
+++ b/solution.py
@@ -67,7 +67,7 @@
     return started
 
 
-def row_tables(shape, kinds, height, slab, tile, owner, place_ref, route_ref):
+def row_tables(shape, kinds, height, bit, slab, tile, owner, place_ref, *route_refs):
     far, wide, cores = shape
     devices, blocks = place_ref.shape
     rows, half = blocks * 2 * height, devices // 2
@@ -82,15 +82,18 @@
         row = tile[r : r + 1, :] * rows + block * (2 * height)
         place = jnp.where(slab[r : r + 1, :] == named, row, place)
     place_ref[...] = place
-    row = (tile * devices + (me ^ slab)) * height
-    route = jnp.zeros(route_ref.shape, jnp.int32)
-    for k in range(blocks):
-        route = jnp.where(owner == k, row[:, k : k + 1], route)
-    route_ref[...] = route
-
-
-def sum_kernel(shape, kinds, slab_hbm, tile_hbm, block_hbm, owner_hbm, defocus_hbm, noise_hbm, tiles_hbm, images_hbm,
-               sums_ref, wave_ref, tiles_ref, images_ref, noise_ref, place_ref, route_ref,
+    away = me ^ slab
+    row = (tile * half + (away & (bit - 1)) + away // (2 * bit) * bit) * height
+    for side, route_ref in enumerate(route_refs):
+        named = jnp.where((away // bit) & 1 == side, row, kinds * half * height)
+        route = jnp.zeros(route_ref.shape, jnp.int32)
+        for k in range(blocks):
+            route = jnp.where(owner == k, named[:, k : k + 1], route)
+        route_ref[...] = route
+
+
+def sum_kernel(shape, kinds, bit, slab_hbm, tile_hbm, block_hbm, owner_hbm, defocus_hbm, noise_hbm, tiles_hbm, images_hbm,
+               sums_ref, wave_ref, tiles_ref, images_ref, noise_ref, place_ref, first_ref, second_ref,
                slab_ref, tile_ref, block_ref, owner_ref, defocus_ref, line_ref, pixel_ref, acc_ref, sems):
     count = images_ref.shape[0]
     part = count // CHUNKS
@@ -106,7 +109,7 @@
     for copy in started[: len(small)]:
         copy.wait()
     tables(defocus_ref, height, pixels, line_ref, pixel_ref)
-    row_tables(shape, kinds, height, slab_ref[...], tile_ref[...], owner_ref[...], place_ref, route_ref)
+    row_tables(shape, kinds, height, bit, slab_ref[...], tile_ref[...], owner_ref[...], place_ref, first_ref, second_ref)
     for b in range(batches):
         if b % (batches // CHUNKS) == 0:
             started[len(small) + b // (batches // CHUNKS)].wait()
@@ -170,30 +173,32 @@
 
 def project_kernel(places, route_vmem, tiles_ref, *refs):
     columns, refs = refs[: len(places)], refs[len(places) :]
-    proj_ref, route_ref, lines_ref, flat_ref, sems = refs
+    *base, proj_ref, route_ref, lines_ref, flat_ref, sems = refs
     (started,) = copies([(route_vmem, route_ref)], sems)
     crossed, batches = route_ref.shape
     kinds = tiles_ref.shape[0]
     height = columns[0].shape[1]
     rows = lines_ref.shape[0]
-    dense = rows // height * kinds <= crossed * batches
-    for ref, aways in zip(columns, places):
-        for n, away in enumerate(aways):
-            lines_ref[away * height : (away + 1) * height, :] = ref[n]
+    dense = flat_ref.shape[0] > kinds * rows
+    for ref, slots in zip(columns, places):
+        for n, slot in enumerate(slots):
+            lines_ref[slot * height : (slot + 1) * height, :] = ref[n]
     if dense:
         for t in range(kinds):
             flat_ref[t * rows : (t + 1) * rows, :] = jnp.dot(lines_ref[...], tiles_ref[t], preferred_element_type=jnp.float32)
+        flat_ref[kinds * rows :, :] = jnp.zeros((height, flat_ref.shape[1]), jnp.float32)
     started.wait()
 
     def project(b, carry):
-        acc = None
+        acc = base[0][b] if base else None
         for r in range(crossed):
             at = route_ref[r, b]
             if dense:
                 part = flat_ref[pl.ds(pl.multiple_of(at, height), height), :]
             else:
-                t, at = at // rows, pl.multiple_of(lax.rem(at, rows), height)
-                part = jnp.dot(lines_ref[pl.ds(at, height), :], tiles_ref[t], preferred_element_type=jnp.float32)
+                t, from_row = jnp.minimum(at // rows, kinds - 1), pl.multiple_of(lax.rem(at, rows), height)
+                part = jnp.dot(lines_ref[pl.ds(from_row, height), :], tiles_ref[t], preferred_element_type=jnp.float32)
+                part = part * jnp.where(at < kinds * rows, 1.0, 0.0)
             acc = part if acc is None else acc + part
         proj_ref[b] = acc
         return carry
@@ -265,8 +270,8 @@
     gathered = hop(volume, offsets[0])
 
     batches = batch_block.shape[0]
-    sums, wave, tiles_near, images_near, noise_near, place_rows, route_rows = call(
-        functools.partial(sum_kernel, shape, kinds),
+    sums, wave, tiles_near, images_near, noise_near, place_rows, *route_rows = call(
+        functools.partial(sum_kernel, shape, kinds, offsets[-1]),
         [
             ((rows, pixels), bf16),
             (images.shape, f32),
@@ -274,6 +279,7 @@
             (images.shape, bf16),
             (inv_sigma2.shape, f32),
             ((devices, blocks), i32),
+            ((crossed, batches), i32),
             ((crossed, batches), i32),
         ],
         [hbm] * 8,
@@ -320,6 +326,30 @@
     for offset in offsets[1:-1]:
         came, _ = lax.optimization_barrier((swap(gathered, offset), near))
         gathered = jnp.concatenate([gathered, came], axis=0)
+    bit = offsets[-1]
+    places = [[(a & (bit - 1)) + a // (2 * bit) * bit for a in [b ^ core for b in away]] for core in (0, 1)]
+    flat_rows = kinds * half * height + height if devices * kinds <= batches * crossed else 8
+    flat_columns = pixels if flat_rows > 8 else LANES
+
+    def project(route, columns, *base):
+        (proj,) = call(
+            functools.partial(project_kernel, places),
+            [((batches, height, pixels), f32)],
+            [vmem] * (4 + len(base)),
+            (route, tiles_near, *columns, *base),
+            [
+                pltpu.SMEM((crossed, batches), i32),
+                pltpu.VMEM((half * height, length), bf16),
+                pltpu.VMEM((flat_rows, flat_columns), f32),
+                pltpu.SemaphoreType.DMA((1,)),
+            ],
+            0,
+            0,
+            "project",
+        )
+        return proj
+
+    proj = project(route_rows[0], (gathered, swap(gathered, 1)))
     mine = [near[z] for z in range(far)]
     for x in range(1, wide):
         came = swap(main[x - 1], x * cores)
@@ -327,32 +357,16 @@
             mine[z] = mine[z] + came[z - cut].astype(f32)
     outgoing = {z: mine[z].astype(bf16) for z in range(cut, far)}
     for x in range(1, wide):
-        came, _ = lax.optimization_barrier((swap(later[x - 1], x * cores), outgoing[far - 1]))
+        came, _, _ = lax.optimization_barrier((swap(later[x - 1], x * cores), outgoing[far - 1], proj))
         for z in range(cut):
             mine[z] = mine[z] + came[z].astype(f32)
     outgoing.update({z: mine[z].astype(bf16) for z in range(1, cut)})
     total = mine[0]
 
     held, _ = lax.optimization_barrier((gathered, later[0]))
-    columns = [gathered, swap(held, offsets[-1])]
-    columns += [swap(column, 1) for column in columns]
-    _, *columns = lax.optimization_barrier((outgoing[1], *columns))
-    places = [[a ^ last for a in away] for last in (0, offsets[-1], 1, offsets[-1] ^ 1)]
-    if devices * kinds <= batches * crossed:
-        flat = pltpu.VMEM((kinds * devices * height, pixels), f32)
-    else:
-        flat = pltpu.VMEM((8, LANES), f32)
-    (proj,) = call(
-        functools.partial(project_kernel, places),
-        [((batches, height, pixels), f32)],
-        [vmem] * (2 + len(columns)),
-        (route_rows, tiles_near, *columns),
-        [pltpu.SMEM((crossed, batches), i32), pltpu.VMEM((devices * height, length), bf16), flat, pltpu.SemaphoreType.DMA((1,))],
-        0,
-        0,
-        "project",
-    )
-
+    column = swap(held, bit)
+    _, column, mirror = lax.optimization_barrier((outgoing[1], column, swap(column, 1)))
+    proj = project(route_rows[1], (column, mirror), proj)
     (scores,) = call(
         score_kernel,
         [((1, count), f32)],

time: 29.9 us -> 29.9 us (level)
  waiting for transfers between devices: 2.78 us -> 2.02 us
  starting transfers between devices: 14.3 us -> 15 us
    ppermute x11, waiting for transfers between devices: 2.78 us -> 2.02 us  [swap(): lax.ppermute(array, 'slab', [(i, i ^ offset) for i in range(devices)])]
    ppermute x11, starting transfers between devices: 14.3 us -> 15 us  [swap(): lax.ppermute(array, 'slab', [(i, i ^ offset) for i in range(devices)])]
    pallas_call x5 -> x6, Pallas kernels: 11 us -> 11.1 us  [call(): pl.pallas_call(kernel, out_shape=tuple((jax.ShapeDtypeStruct(s, t) for s,...]
  transfers between devices with their start and end apart: 11 -> 11, of which waited for: 4 -> 3; matrix products, arithmetic and copies ran while one was open for 0% -> 0% of each run, Pallas kernels for 37% -> 37%
where the time goes in v17:
time: 29.9 us; the launch traced here: 29.7 us
  starting transfers between devices  15 us (50%)
  Pallas kernels  11.1 us (37%)
  waiting for transfers between devices  2.02 us (7%)
  between operations  0.76 us (3%)
  local copies, waits for them, and re-layouts  0.68 us (2%)
    ppermute x11, starting transfers between devices, swap(): lax.ppermute(array, 'slab', [(i, i ^ offset) for i in range(devices)])  15 us
    pallas_call x6, Pallas kernels, call(): pl.pallas_call(kernel, out_shape=tuple((jax.ShapeDtypeStruct(s, t) for s,...  11.1 us
    ppermute x11, waiting for transfers between devices, swap(): lax.ppermute(array, 'slab', [(i, i ^ offset) for i in range(devices)])  2.02 us
    slice x1, local copies, waits for them, and re-layouts, on_device(): return (scores.reshape(count), total[0:1], total[1:2])  0.66 us
  transfers between devices with their start and end apart: 11, of which 3 were waited for; matrix products, arithmetic and copies ran while one was open for 0% of the time, Pallas kernels for 37%

profile of v17, /device:TPU:0, one launch (start us, length us, event | category | flops | bytes accessed | tf_op | source)
XLA Modules:
  0.0 29.7 jit_solution(5298843209383399680)
XLA Ops:
  0.6 4.1 %collective-permute-start = (bf16[1,32,512]{2,1,0:T(8,128)(2,1)}, bf16[1,32,512]{2,1,0:T(8,128)(2,1)S(1)}, u32[]{:S(2)}, u32[]{:S(2)}) collective-permute-start(bf16[1,32,512]{2,1,0:T(8,128)(2,1)} %param.8), channel_id=1, source_target_pairs={{0,8},{1,9},{2,10},{3,11},{4,12},{5,13},{6,14},{7,15},{8,0},{9,1},... | collective-permute-start | bytes 98312 | tf_op jit(solution)/shard_map/ppermute | solution.py:239
  4.7 2.9 %sums.1 = (bf16[1024,256]{1,0:T(8,128)(2,1)S(1)}, f32[128,32,256]{2,1,0:T(8,128)S(1)}, bf16[8,512,256]{2,1,0:T(8,128)(2,1)S(1)}, bf16[128,32,256]{2,1,0:T(8,128)...) custom-call(s32[8,16]{1,0:T(8,128)} %bitcast.19, ...), custom_call_target="tpu_custom_call" | custom-call | bytes 10485760 | tf_op jit(solution)/shard_map/sums/pallas_call | solution.py:251
  7.7 0.0 copy-start
  7.7 3.7 %insert.1 = (bf16[8,2,32,512]{3,2,1,0:T(8,128)(2,1)S(1)}, f32[4,2,32,512]{3,2,1,0:T(8,128)S(1)}, f32[8256,512]{1,0:T(8,128)S(1)}) custom-call(s32[16,16]{1,0:T(8,128)S(1)} %get-tuple-element.25.place_vmem, bf16[1024,256]{1,0:T(8,128)(2,1)S(1)} %get-tuple-element.26.sums_ref, bf16[8,512,256]{2,1,0:T(8,128)(2,1)S(1)} %get-tuple-element.27.tiles_ref), custom_call_target="tpu_custom_call" | custom-call | flops 2147483648 | bytes 8388608 | tf_op jit(solution)/shard_map/insert/pallas_call | solution.py:251
  11.4 0.0 collective-permute-done
  11.4 0.0 copy-done
  11.4 0.1 collective-permute-start.1
  11.5 1.6 %collective-permute-start.6 = (bf16[2,32,512]{2,1,0:T(8,128)(2,1)S(1)}, bf16[2,32,512]{2,1,0:T(8,128)(2,1)S(1)}, u32[]{:S(2)}, u32[]{:S(2)}) collective-permute-start(bf16[2,32,512]{2,1,0:T(8,128)(2,1)S(1)} %pad_maximum_fusion), channel_id=1, source_target_pairs={{0,2},{1,3},{2,0},{3,1},{4,6},{5,7},{6,4},{7,5},{8,10},{9,11},{10,... | collective-permute-start | bytes 196616 | tf_op jit(solution)/shard_map/ppermute | solution.py:239
  13.0 0.3 %collective-permute-done.1.mate_ref = bf16[8,2,32,512]{3,2,1,0:T(8,128)(2,1)S(1)} collective-permute-done((bf16[8,2,32,512]{3,2,1,0:T(8,128)(2,1)S(1)}, bf16[8,2,32,512]{3,2,1,0:T(8,128)(2,1)S(1)}, u32[]{:S(2)}, u32[]{:S(2)}) %collective-permute-start.1) | collective-permute-done | bytes 524320 | tf_op jit(solution)/shard_map/ppermute | solution.py:239
  13.4 0.1 add_convert_fusion
  13.5 1.6 %collective-permute-start.2 = (bf16[2,2,32,512]{3,2,1,0:T(8,128)(2,1)S(1)}, bf16[2,2,32,512]{3,2,1,0:T(8,128)(2,1)S(1)}, u32[]{:S(2)}, u32[]{:S(2)}) collective-permute-start(bf16[2,2,32,512]{3,2,1,0:T(8,128)(2,1)S(1)} %get-tuple-element.48), channel_id=1, source_target_pairs={{0,2},{1,3},{2,0},{3,1},{4,6},{5,7},{6,4},{7,5},{8,10},{9,11},{10,... | collective-permute-start | bytes 393224 | tf_op jit(solution)/shard_map/ppermute | solution.py:239
  15.0 1.1 %near.1 = f32[4,2,32,512]{3,2,1,0:T(8,128)S(1)} custom-call(s32[16,16]{1,0:T(8,128)S(1)} %get-tuple-element.25.place_vmem, f32[8256,512]{1,0:T(8,128)S(1)} %get-tuple-element.28.parts_ref, bf16[8,2,32,512]{3,2,1,0:T(8,128)(2,1)S(1)} %collective-permute-done.1.mate_ref), custom_call_target="tpu_custom_call" | custom-call | tf_op jit(solution)/shard_map/near/pallas_call | solution.py:251
  16.1 0.0 collective-permute-done.6
  16.2 0.1 collective-permute-start.7
  16.2 1.3 %collective-permute-start.5 = (bf16[2,2,32,512]{3,2,1,0:T(8,128)(2,1)S(1)}, bf16[2,2,32,512]{3,2,1,0:T(8,128)(2,1)S(1)}, u32[]{:S(2)}, u32[]{:S(2)}) collective-permute-start(bf16[2,2,32,512]{3,2,1,0:T(8,128)(2,1)S(1)} %get-tuple-element.47), channel_id=1, source_target_pairs={{0,2},{1,3},{2,0},{3,1},{4,6},{5,7},{6,4},{7,5},{8,10},{9,11},{10,... | collective-permute-start | bytes 393224 | tf_op jit(solution)/shard_map/ppermute | solution.py:239
  17.6 1.6 %collective-permute-start.8 = (bf16[4,32,512]{2,1,0:T(8,128)(2,1)S(1)}, bf16[4,32,512]{2,1,0:T(8,128)(2,1)S(1)}, u32[]{:S(2)}, u32[]{:S(2)}) collective-permute-start(bf16[4,32,512]{2,1,0:T(8,128)(2,1)S(1)} %constant_dynamic-update-slice_fusion.refs_0_), channel_id=1, source_target_pairs={{0,4},{1,5},{2,6},{3,7},{4,0},{5,1},{6,2},{7,3},{8,12},{9,13},{10,... | collective-permute-start | bytes 393224 | tf_op jit(solution)/shard_map/ppermute | solution.py:239
  19.1 0.0 collective-permute-done.2
  19.2 1.3 %collective-permute-start.3 = (bf16[2,32,512]{2,1,0:T(8,128)(2,1)S(1)}, bf16[2,32,512]{2,1,0:T(8,128)(2,1)S(1)}, u32[]{:S(2)}, u32[]{:S(2)}) collective-permute-start(bf16[2,32,512]{2,1,0:T(8,128)(2,1)S(1)} %get-tuple-element.50), channel_id=1, source_target_pairs={{0,12},{1,13},{2,14},{3,15},{4,8},{5,9},{6,10},{7,11},{8,4},{9,5},... | collective-permute-start | bytes 196616 | tf_op jit(solution)/shard_map/ppermute | solution.py:239
  20.5 0.0 collective-permute-done.7.refs_1_
  20.5 0.9 %project.2.refs_2_ = f32[16,32,256]{2,1,0:T(8,128)S(1)} custom-call(s32[8,16]{1,0:T(8,128)S(1)} %get-tuple-element.34.route_vmem, bf16[8,512,256]{2,1,0:T(8,128)(2,1)S(1)} %get-tuple-element.27.tiles_ref, bf16[4,32,512]{2,1,0:T(8,128)(2,1)S(1)} %constant_dynamic-update-slice_fusion.refs_0_, bf16[4,32,512]{2,1,0:T(8,128)(2,1)S(1)} %collective-permute-done.7.refs_1_), custom_call_target="tpu_custom_call" | custom-call | tf_op jit(solution)/shard_map/project/pallas_call | solution.py:251
  21.4 0.7 %collective-permute-done.5 = bf16[2,2,32,512]{3,2,1,0:T(8,128)(2,1)S(1)} collective-permute-done((bf16[2,2,32,512]{3,2,1,0:T(8,128)(2,1)S(1)}, bf16[2,2,32,512]{3,2,1,0:T(8,128)(2,1)S(1)}, u32[]{:S(2)}, u32[]{:S(2)}) %collective-permute-start.5) | collective-permute-done | bytes 131104 | tf_op jit(solution)/shard_map/ppermute | solution.py:239
  22.2 1.0 %collective-permute-start.4 = (bf16[2,32,512]{2,1,0:T(8,128)(2,1)S(1)}, bf16[2,32,512]{2,1,0:T(8,128)(2,1)S(1)}, u32[]{:S(2)}, u32[]{:S(2)}) collective-permute-start(bf16[2,32,512]{2,1,0:T(8,128)(2,1)S(1)} %get-tuple-element.49), channel_id=1, source_target_pairs={{0,8},{1,9},{2,10},{3,11},{4,12},{5,13},{6,14},{7,15},{8,0},{9,1},... | collective-permute-start | bytes 196616 | tf_op jit(solution)/shard_map/ppermute | solution.py:239
  23.2 0.0 collective-permute-done.8.refs_0_
  23.2 0.0 collective-permute-start.9
  23.2 2.3 %collective-permute-start.10 = (bf16[2,32,512]{2,1,0:T(8,128)(2,1)S(1)}, bf16[2,32,512]{2,1,0:T(8,128)(2,1)S(1)}, u32[]{:S(2)}, u32[]{:S(2)}) collective-permute-start(bf16[2,32,512]{2,1,0:T(8,128)(2,1)S(1)} %fusion.9), channel_id=1, source_target_pairs={{0,4},{1,5},{2,6},{3,7},{4,0},{5,1},{6,2},{7,3},{8,12},{9,13},{10,... | collective-permute-start | bytes 196616 | tf_op jit(solution)/shard_map/ppermute | solution.py:239
  25.6 0.0 collective-permute-done.9.refs_1_
  25.6 1.0 %project.3.proj_ref = f32[16,32,256]{2,1,0:T(8,128)S(1)} custom-call(s32[8,16]{1,0:T(8,128)S(1)} %get-tuple-element.33.route_vmem, bf16[8,512,256]{2,1,0:T(8,128)(2,1)S(1)} %get-tuple-element.27.tiles_ref, bf16[4,32,512]{2,1,0:T(8,128)(2,1)S(1)} %collective-permute-done.8.refs_0_, bf16[4,32,512]{2,1,0:T(8,128)(2,1)S(1)} %collective-permute-done.9.refs_1_, ...), custom_call_target="tpu_custom_call" | custom-call | tf_op jit(solution)/shard_map/project/pallas_call | solution.py:251
  26.6 1.5 %scores.1 = f32[1,128]{1,0:T(1,128)} custom-call(f32[32,256]{1,0:T(8,128)S(1)} %get-tuple-element.32.noise_ref, f32[16,32,256]{2,1,0:T(8,128)S(1)} %project.3.proj_ref, f32[128,32,256]{2,1,0:T(8,128)S(1)} %get-tuple-element.41.wave_ref, bf16[128,32,256]{2,1,0:T(8,128)(2,1)S(1)} %get-tuple-element.42.images_ref), custom_call_target="tpu_custom_call" | custom-call | tf_op jit(solution)/shard_map/scores/pallas_call | solution.py:251
  28.1 0.0 collective-permute-done.4
  28.1 0.0 collective-permute-done.3
  28.1 0.9 %collective-permute-done.10 = bf16[2,32,512]{2,1,0:T(8,128)(2,1)S(1)} collective-permute-done((bf16[2,32,512]{2,1,0:T(8,128)(2,1)S(1)}, bf16[2,32,512]{2,1,0:T(8,128)(2,1)S(1)}, u32[]{:S(2)}, u32[]{:S(2)}) %collective-permute-start.10) | collective-permute-done | bytes 65568 | tf_op jit(solution)/shard_map/ppermute | solution.py:239
  29.1 0.7 %fusion.10 = (f32[1,32,512]{2,1,0:T(8,128)}, f32[1,32,512]{2,1,0:T(8,128)}) fusion(f32[2,32,512]{2,1,0:T(8,128)S(1)} %fusion.3), kind=kLoop, calls=%fused_computation.19 | loop fusion | bytes 262144 | tf_op jit(solution)/shard_map/slice | solution.py:385
  (6 shorter events, 0.1 us)
Async XLA Ops:
  0.6 10.7 %collective-permute-start = (bf16[1,32,512]{2,1,0:T(8,128)(2,1)}, bf16[1,32,512]{2,1,0:T(8,128)(2,1)S(1)}, u32[]{:S(2)}, u32[]{:S(2)}) collective-permute-start(bf16[1,32,512]{2,1,0:T(8,128)(2,1)} %param.8), channel_id=1, source_target_pairs={{0,8},{1,9},{2,10},{3,11},{4,12},{5,13},{6,14},{7,15},{8,0},{9,1},... | collective-permute-start | bytes 98312 | tf_op jit(solution)/shard_map/ppermute | solution.py:239
  7.7 3.7 %copy-start = (bf16[1,32,512]{2,1,0:T(8,128)(2,1)S(1)}, bf16[1,32,512]{2,1,0:T(8,128)(2,1)}, u32[]{:S(2)}) copy-start(bf16[1,32,512]{2,1,0:T(8,128)(2,1)} %param.8) | copy-start | bytes 98308
  11.4 2.0 %collective-permute-start.1 = (bf16[8,2,32,512]{3,2,1,0:T(8,128)(2,1)S(1)}, bf16[8,2,32,512]{3,2,1,0:T(8,128)(2,1)S(1)}, u32[]{:S(2)}, u32[]{:S(2)}) collective-permute-start(bf16[8,2,32,512]{3,2,1,0:T(8,128)(2,1)S(1)} %get-tuple-element.30), channel_id=1, source_target_pairs={{0,1},{1,0},{2,3},{3,2},{4,5},{5,4},{6,7},{7,6},{8,9},{9,8},{10,11... | collective-permute-start | bytes 1572872 | tf_op jit(solution)/shard_map/ppermute | solution.py:239
  11.5 4.7 %collective-permute-start.6 = (bf16[2,32,512]{2,1,0:T(8,128)(2,1)S(1)}, bf16[2,32,512]{2,1,0:T(8,128)(2,1)S(1)}, u32[]{:S(2)}, u32[]{:S(2)}) collective-permute-start(bf16[2,32,512]{2,1,0:T(8,128)(2,1)S(1)} %pad_maximum_fusion), channel_id=1, source_target_pairs={{0,2},{1,3},{2,0},{3,1},{4,6},{5,7},{6,4},{7,5},{8,10},{9,11},{10,... | collective-permute-start | bytes 196616 | tf_op jit(solution)/shard_map/ppermute | solution.py:239
  13.5 5.7 %collective-permute-start.2 = (bf16[2,2,32,512]{3,2,1,0:T(8,128)(2,1)S(1)}, bf16[2,2,32,512]{3,2,1,0:T(8,128)(2,1)S(1)}, u32[]{:S(2)}, u32[]{:S(2)}) collective-permute-start(bf16[2,2,32,512]{3,2,1,0:T(8,128)(2,1)S(1)} %get-tuple-element.48), channel_id=1, source_target_pairs={{0,2},{1,3},{2,0},{3,1},{4,6},{5,7},{6,4},{7,5},{8,10},{9,11},{10,... | collective-permute-start | bytes 393224 | tf_op jit(solution)/shard_map/ppermute | solution.py:239
  16.2 4.3 %collective-permute-start.7 = (bf16[4,32,512]{2,1,0:T(8,128)(2,1)S(1)}, bf16[4,32,512]{2,1,0:T(8,128)(2,1)S(1)}, u32[]{:S(2)}, u32[]{:S(2)}) collective-permute-start(bf16[4,32,512]{2,1,0:T(8,128)(2,1)S(1)} %constant_dynamic-update-slice_fusion.refs_0_), channel_id=1, source_target_pairs={{0,1},{1,0},{2,3},{3,2},{4,5},{5,4},{6,7},{7,6},{8,9},{9,8},{10,11... | collective-permute-start | bytes 393224 | tf_op jit(solution)/shard_map/ppermute | solution.py:239
  16.2 5.9 %collective-permute-start.5 = (bf16[2,2,32,512]{3,2,1,0:T(8,128)(2,1)S(1)}, bf16[2,2,32,512]{3,2,1,0:T(8,128)(2,1)S(1)}, u32[]{:S(2)}, u32[]{:S(2)}) collective-permute-start(bf16[2,2,32,512]{3,2,1,0:T(8,128)(2,1)S(1)} %get-tuple-element.47), channel_id=1, source_target_pairs={{0,2},{1,3},{2,0},{3,1},{4,6},{5,7},{6,4},{7,5},{8,10},{9,11},{10,... | collective-permute-start | bytes 393224 | tf_op jit(solution)/shard_map/ppermute | solution.py:239
  17.6 5.7 %collective-permute-start.8 = (bf16[4,32,512]{2,1,0:T(8,128)(2,1)S(1)}, bf16[4,32,512]{2,1,0:T(8,128)(2,1)S(1)}, u32[]{:S(2)}, u32[]{:S(2)}) collective-permute-start(bf16[4,32,512]{2,1,0:T(8,128)(2,1)S(1)} %constant_dynamic-update-slice_fusion.refs_0_), channel_id=1, source_target_pairs={{0,4},{1,5},{2,6},{3,7},{4,0},{5,1},{6,2},{7,3},{8,12},{9,13},{10,... | collective-permute-start | bytes 393224 | tf_op jit(solution)/shard_map/ppermute | solution.py:239
  19.2 8.9 %collective-permute-start.3 = (bf16[2,32,512]{2,1,0:T(8,128)(2,1)S(1)}, bf16[2,32,512]{2,1,0:T(8,128)(2,1)S(1)}, u32[]{:S(2)}, u32[]{:S(2)}) collective-permute-start(bf16[2,32,512]{2,1,0:T(8,128)(2,1)S(1)} %get-tuple-element.50), channel_id=1, source_target_pairs={{0,12},{1,13},{2,14},{3,15},{4,8},{5,9},{6,10},{7,11},{8,4},{9,5},... | collective-permute-start | bytes 196616 | tf_op jit(solution)/shard_map/ppermute | solution.py:239
  22.2 5.9 %collective-permute-start.4 = (bf16[2,32,512]{2,1,0:T(8,128)(2,1)S(1)}, bf16[2,32,512]{2,1,0:T(8,128)(2,1)S(1)}, u32[]{:S(2)}, u32[]{:S(2)}) collective-permute-start(bf16[2,32,512]{2,1,0:T(8,128)(2,1)S(1)} %get-tuple-element.49), channel_id=1, source_target_pairs={{0,8},{1,9},{2,10},{3,11},{4,12},{5,13},{6,14},{7,15},{8,0},{9,1},... | collective-permute-start | bytes 196616 | tf_op jit(solution)/shard_map/ppermute | solution.py:239
  23.2 2.4 %collective-permute-start.9 = (bf16[4,32,512]{2,1,0:T(8,128)(2,1)S(1)}, bf16[4,32,512]{2,1,0:T(8,128)(2,1)S(1)}, u32[]{:S(2)}, u32[]{:S(2)}) collective-permute-start(bf16[4,32,512]{2,1,0:T(8,128)(2,1)S(1)} %collective-permute-done.8.refs_0_), channel_id=1, source_target_pairs={{0,1},{1,0},{2,3},{3,2},{4,5},{5,4},{6,7},{7,6},{8,9},{9,8},{10,11... | collective-permute-start | bytes 393224 | tf_op jit(solution)/shard_map/ppermute | solution.py:239
  23.2 5.8 %collective-permute-start.10 = (bf16[2,32,512]{2,1,0:T(8,128)(2,1)S(1)}, bf16[2,32,512]{2,1,0:T(8,128)(2,1)S(1)}, u32[]{:S(2)}, u32[]{:S(2)}) collective-permute-start(bf16[2,32,512]{2,1,0:T(8,128)(2,1)S(1)} %fusion.9), channel_id=1, source_target_pairs={{0,4},{1,5},{2,6},{3,7},{4,0},{5,1},{6,2},{7,3},{8,12},{9,13},{10,... | collective-permute-start | bytes 196616 | tf_op jit(solution)/shard_map/ppermute | solution.py:239

commit v18 on v17

--- a/solution.py
+++ b/solution.py
@@ -92,8 +92,8 @@
         route_ref[...] = route
 
 
-def sum_kernel(shape, kinds, bit, slab_hbm, tile_hbm, block_hbm, owner_hbm, defocus_hbm, noise_hbm, tiles_hbm, images_hbm,
-               sums_ref, wave_ref, tiles_ref, images_ref, noise_ref, place_ref, first_ref, second_ref,
+def sum_kernel(shape, kinds, bit, slab_hbm, tile_hbm, block_hbm, owner_hbm, defocus_hbm, noise_hbm, images_hbm,
+               sums_ref, wave_ref, images_ref, noise_ref, place_ref, first_ref, second_ref,
                slab_ref, tile_ref, block_ref, owner_ref, defocus_ref, line_ref, pixel_ref, acc_ref, sems):
     count = images_ref.shape[0]
     part = count // CHUNKS
@@ -101,20 +101,18 @@
     small += [(slab_hbm, slab_ref), (tile_hbm, tile_ref), (owner_hbm, owner_ref)]
     large = [(images_hbm.at[pl.ds(n * part, part)], images_ref.at[pl.ds(n * part, part)]) for n in range(CHUNKS)]
     started = copies(small + large, sems)
-    last = pltpu.make_async_copy(tiles_hbm, tiles_ref, sems.at[len(started)])
     height, pixels = noise_ref.shape
     batches = block_ref.shape[0]
     size = count // batches
     acc_ref[...] = jnp.zeros_like(acc_ref)
-    for copy in started[: len(small)]:
+    started[0].wait()
+    tables(defocus_ref, height, pixels, line_ref, pixel_ref)
+    for copy in started[1 : len(small)]:
         copy.wait()
-    tables(defocus_ref, height, pixels, line_ref, pixel_ref)
     row_tables(shape, kinds, height, bit, slab_ref[...], tile_ref[...], owner_ref[...], place_ref, first_ref, second_ref)
     for b in range(batches):
         if b % (batches // CHUNKS) == 0:
             started[len(small) + b // (batches // CHUNKS)].wait()
-        if b == 0:
-            last.start()
         data = jnp.zeros((height, pixels), jnp.float32)
         weight = jnp.zeros((height, pixels), jnp.float32)
         for j in range(size):
@@ -128,7 +126,6 @@
         acc_ref[k, 1] = acc_ref[k, 1] + weight
     sums = (acc_ref[...] * noise_ref[...][None, None]).astype(jnp.bfloat16)
     sums_ref[...] = sums.reshape(sums_ref.shape)
-    last.wait()
 
 
 def fill(ref, start, place_ref, parts_ref, mate_ref=None):
@@ -270,20 +267,19 @@
     gathered = hop(volume, offsets[0])
 
     batches = batch_block.shape[0]
-    sums, wave, tiles_near, images_near, noise_near, place_rows, *route_rows = call(
+    sums, wave, images_near, noise_near, place_rows, *route_rows = call(
         functools.partial(sum_kernel, shape, kinds, offsets[-1]),
         [
             ((rows, pixels), bf16),
             (images.shape, f32),
-            (tiles.shape, bf16),
             (images.shape, bf16),
             (inv_sigma2.shape, f32),
             ((devices, blocks), i32),
             ((crossed, batches), i32),
             ((crossed, batches), i32),
         ],
-        [hbm] * 8,
-        (slabs, kind_rows, batch_block, batch_block.reshape(1, batches), row, inv_sigma2, tiles, images),
+        [hbm] * 7,
+        (slabs, kind_rows, batch_block, batch_block.reshape(1, batches), row, inv_sigma2, images),
         [
             pltpu.VMEM((crossed, blocks), i32),
             pltpu.VMEM((crossed, blocks), i32),
@@ -293,7 +289,7 @@
             pltpu.VMEM((2, height, count), f32),
             pltpu.VMEM((2, count, pixels), f32),
             pltpu.VMEM((blocks, 2, height, pixels), f32),
-            pltpu.SemaphoreType.DMA((CHUNKS + 7,)),
+            pltpu.SemaphoreType.DMA((CHUNKS + 6,)),
         ],
         0,
         10 << 20,
@@ -306,7 +302,7 @@
         insert_kernel,
         [((half, *place), bf16), ((half - far, *place), f32), ((kinds * rows + 2 * height, length), f32)],
         [vmem] * 3,
-        (place_rows, sums, tiles_near),
+        (place_rows, sums, tiles),
         place_scratch,
         2 * rows * pixels * kinds * length,
         8 << 20,
@@ -336,7 +332,7 @@
             functools.partial(project_kernel, places),
             [((batches, height, pixels), f32)],
             [vmem] * (4 + len(base)),
-            (route, tiles_near, *columns, *base),
+            (route, tiles, *columns, *base),
             [
                 pltpu.SMEM((crossed, batches), i32),
                 pltpu.VMEM((half * height, length), bf16),

time: 29.9 us -> 29.9 us (level)
  no operation moved by 1% of the time
where the time goes in v18:
time: 29.9 us; the launch traced here: 29.7 us
  starting transfers between devices  15.2 us (51%)
  Pallas kernels  11 us (37%)
  waiting for transfers between devices  1.84 us (6%)
  between operations  0.78 us (3%)
  local copies, waits for them, and re-layouts  0.68 us (2%)
    ppermute x11, starting transfers between devices, swap(): lax.ppermute(array, 'slab', [(i, i ^ offset) for i in range(devices)])  15.2 us
    pallas_call x6, Pallas kernels, call(): pl.pallas_call(kernel, out_shape=tuple((jax.ShapeDtypeStruct(s, t) for s,...  11 us
    ppermute x11, waiting for transfers between devices, swap(): lax.ppermute(array, 'slab', [(i, i ^ offset) for i in range(devices)])  1.84 us
    slice x1, local copies, waits for them, and re-layouts, on_device(): return (scores.reshape(count), total[0:1], total[1:2])  0.66 us
  transfers between devices with their start and end apart: 11, of which 3 were waited for; matrix products, arithmetic and copies ran while one was open for 0% of the time, Pallas kernels for 37%

profile of v18, /device:TPU:0, one launch (start us, length us, event | category | flops | bytes accessed | tf_op | source)
XLA Modules:
  0.0 29.7 jit_solution(15394732827754632163)
XLA Ops:
  0.6 4.1 %collective-permute-start = (bf16[1,32,512]{2,1,0:T(8,128)(2,1)}, bf16[1,32,512]{2,1,0:T(8,128)(2,1)S(1)}, u32[]{:S(2)}, u32[]{:S(2)}) collective-permute-start(bf16[1,32,512]{2,1,0:T(8,128)(2,1)} %param.8), channel_id=1, source_target_pairs={{0,8},{1,9},{2,10},{3,11},{4,12},{5,13},{6,14},{7,15},{8,0},{9,1},... | collective-permute-start | bytes 98312 | tf_op jit(solution)/shard_map/ppermute | solution.py:236
  4.7 2.9 %sums.1 = (bf16[1024,256]{1,0:T(8,128)(2,1)S(1)}, f32[128,32,256]{2,1,0:T(8,128)S(1)}, bf16[128,32,256]{2,1,0:T(8,128)(2,1)S(1)}, f32[32,256]{1,0:T(8,128)S(1)},...) custom-call(s32[8,16]{1,0:T(8,128)} %bitcast.19, s32[8,16]{1,0:T(8,128)} %bitcast.20, ...), custom_call_target="tpu_custom_call" | custom-call | bytes 10485760 | tf_op jit(solution)/shard_map/sums/pallas_call | solution.py:248
  7.7 0.0 copy-start.1
  7.7 3.7 %insert.1 = (bf16[8,2,32,512]{3,2,1,0:T(8,128)(2,1)S(1)}, f32[4,2,32,512]{3,2,1,0:T(8,128)S(1)}, f32[8256,512]{1,0:T(8,128)S(1)}) custom-call(s32[16,16]{1,0:T(8,128)S(1)} %get-tuple-element.24.place_vmem, bf16[1024,256]{1,0:T(8,128)(2,1)S(1)} %get-tuple-element.25.sums_ref, bf16[8,512,256]{2,1,0:T(8,128)(2,1)S(1)} %copy-done), custom_call_target="tpu_custom_call" | custom-call | flops 2147483648 | bytes 8388608 | tf_op jit(solution)/shard_map/insert/pallas_call | solution.py:248
  11.4 0.0 collective-permute-done
  11.4 0.0 copy-done.1
  11.4 0.1 collective-permute-start.1
  11.5 1.6 %collective-permute-start.6 = (bf16[2,32,512]{2,1,0:T(8,128)(2,1)S(1)}, bf16[2,32,512]{2,1,0:T(8,128)(2,1)S(1)}, u32[]{:S(2)}, u32[]{:S(2)}) collective-permute-start(bf16[2,32,512]{2,1,0:T(8,128)(2,1)S(1)} %pad_maximum_fusion), channel_id=1, source_target_pairs={{0,2},{1,3},{2,0},{3,1},{4,6},{5,7},{6,4},{7,5},{8,10},{9,11},{10,... | collective-permute-start | bytes 196616 | tf_op jit(solution)/shard_map/ppermute | solution.py:236
  13.0 0.3 %collective-permute-done.1.mate_ref = bf16[8,2,32,512]{3,2,1,0:T(8,128)(2,1)S(1)} collective-permute-done((bf16[8,2,32,512]{3,2,1,0:T(8,128)(2,1)S(1)}, bf16[8,2,32,512]{3,2,1,0:T(8,128)(2,1)S(1)}, u32[]{:S(2)}, u32[]{:S(2)}) %collective-permute-start.1) | collective-permute-done | bytes 524320 | tf_op jit(solution)/shard_map/ppermute | solution.py:236
  13.4 0.1 add_convert_fusion
  13.4 1.6 %collective-permute-start.2 = (bf16[2,2,32,512]{3,2,1,0:T(8,128)(2,1)S(1)}, bf16[2,2,32,512]{3,2,1,0:T(8,128)(2,1)S(1)}, u32[]{:S(2)}, u32[]{:S(2)}) collective-permute-start(bf16[2,2,32,512]{3,2,1,0:T(8,128)(2,1)S(1)} %get-tuple-element.46), channel_id=1, source_target_pairs={{0,2},{1,3},{2,0},{3,1},{4,6},{5,7},{6,4},{7,5},{8,10},{9,11},{10,... | collective-permute-start | bytes 393224 | tf_op jit(solution)/shard_map/ppermute | solution.py:236
  15.0 1.1 %near.1 = f32[4,2,32,512]{3,2,1,0:T(8,128)S(1)} custom-call(s32[16,16]{1,0:T(8,128)S(1)} %get-tuple-element.24.place_vmem, f32[8256,512]{1,0:T(8,128)S(1)} %get-tuple-element.26.parts_ref, bf16[8,2,32,512]{3,2,1,0:T(8,128)(2,1)S(1)} %collective-permute-done.1.mate_ref), custom_call_target="tpu_custom_call" | custom-call | tf_op jit(solution)/shard_map/near/pallas_call | solution.py:248
  16.1 0.0 collective-permute-done.6
  16.1 0.1 collective-permute-start.7
  16.2 1.3 %collective-permute-start.5 = (bf16[2,2,32,512]{3,2,1,0:T(8,128)(2,1)S(1)}, bf16[2,2,32,512]{3,2,1,0:T(8,128)(2,1)S(1)}, u32[]{:S(2)}, u32[]{:S(2)}) collective-permute-start(bf16[2,2,32,512]{3,2,1,0:T(8,128)(2,1)S(1)} %get-tuple-element.45), channel_id=1, source_target_pairs={{0,2},{1,3},{2,0},{3,1},{4,6},{5,7},{6,4},{7,5},{8,10},{9,11},{10,... | collective-permute-start | bytes 393224 | tf_op jit(solution)/shard_map/ppermute | solution.py:236
  17.6 1.6 %collective-permute-start.8 = (bf16[4,32,512]{2,1,0:T(8,128)(2,1)S(1)}, bf16[4,32,512]{2,1,0:T(8,128)(2,1)S(1)}, u32[]{:S(2)}, u32[]{:S(2)}) collective-permute-start(bf16[4,32,512]{2,1,0:T(8,128)(2,1)S(1)} %constant_dynamic-update-slice_fusion.refs_0_), channel_id=1, source_target_pairs={{0,4},{1,5},{2,6},{3,7},{4,0},{5,1},{6,2},{7,3},{8,12},{9,13},{10,... | collective-permute-start | bytes 393224 | tf_op jit(solution)/shard_map/ppermute | solution.py:236
  19.1 0.0 collective-permute-done.2
  19.2 1.5 %collective-permute-start.3 = (bf16[2,32,512]{2,1,0:T(8,128)(2,1)S(1)}, bf16[2,32,512]{2,1,0:T(8,128)(2,1)S(1)}, u32[]{:S(2)}, u32[]{:S(2)}) collective-permute-start(bf16[2,32,512]{2,1,0:T(8,128)(2,1)S(1)} %get-tuple-element.48), channel_id=1, source_target_pairs={{0,12},{1,13},{2,14},{3,15},{4,8},{5,9},{6,10},{7,11},{8,4},{9,5},... | collective-permute-start | bytes 196616 | tf_op jit(solution)/shard_map/ppermute | solution.py:236
  20.7 0.0 collective-permute-done.7.refs_1_
  20.7 0.9 %project.2.refs_2_ = f32[16,32,256]{2,1,0:T(8,128)S(1)} custom-call(s32[8,16]{1,0:T(8,128)S(1)} %get-tuple-element.32.route_vmem, bf16[8,512,256]{2,1,0:T(8,128)(2,1)S(1)} %copy-done, bf16[4,32,512]{2,1,0:T(8,128)(2,1)S(1)} %constant_dynamic-update-slice_fusion.refs_0_, bf16[4,32,512]{2,1,0:T(8,128)(2,1)S(1)} %collective-permute-done.7.refs_1_), custom_call_target="tpu_custom_call" | custom-call | tf_op jit(solution)/shard_map/project/pallas_call | solution.py:248
  21.6 0.5 %collective-permute-done.5 = bf16[2,2,32,512]{3,2,1,0:T(8,128)(2,1)S(1)} collective-permute-done((bf16[2,2,32,512]{3,2,1,0:T(8,128)(2,1)S(1)}, bf16[2,2,32,512]{3,2,1,0:T(8,128)(2,1)S(1)}, u32[]{:S(2)}, u32[]{:S(2)}) %collective-permute-start.5) | collective-permute-done | bytes 131104 | tf_op jit(solution)/shard_map/ppermute | solution.py:236
  22.1 1.1 %collective-permute-start.4 = (bf16[2,32,512]{2,1,0:T(8,128)(2,1)S(1)}, bf16[2,32,512]{2,1,0:T(8,128)(2,1)S(1)}, u32[]{:S(2)}, u32[]{:S(2)}) collective-permute-start(bf16[2,32,512]{2,1,0:T(8,128)(2,1)S(1)} %get-tuple-element.47), channel_id=1, source_target_pairs={{0,8},{1,9},{2,10},{3,11},{4,12},{5,13},{6,14},{7,15},{8,0},{9,1},... | collective-permute-start | bytes 196616 | tf_op jit(solution)/shard_map/ppermute | solution.py:236
  23.2 0.0 collective-permute-done.8.refs_0_
  23.2 0.0 collective-permute-start.9
  23.2 2.3 %collective-permute-start.10 = (bf16[2,32,512]{2,1,0:T(8,128)(2,1)S(1)}, bf16[2,32,512]{2,1,0:T(8,128)(2,1)S(1)}, u32[]{:S(2)}, u32[]{:S(2)}) collective-permute-start(bf16[2,32,512]{2,1,0:T(8,128)(2,1)S(1)} %fusion.9), channel_id=1, source_target_pairs={{0,4},{1,5},{2,6},{3,7},{4,0},{5,1},{6,2},{7,3},{8,12},{9,13},{10,... | collective-permute-start | bytes 196616 | tf_op jit(solution)/shard_map/ppermute | solution.py:236
  25.6 0.0 collective-permute-done.9.refs_1_
  25.6 0.9 %project.3.proj_ref = f32[16,32,256]{2,1,0:T(8,128)S(1)} custom-call(s32[8,16]{1,0:T(8,128)S(1)} %get-tuple-element.31.route_vmem, bf16[8,512,256]{2,1,0:T(8,128)(2,1)S(1)} %copy-done, bf16[4,32,512]{2,1,0:T(8,128)(2,1)S(1)} %collective-permute-done.8.refs_0_, bf16[4,32,512]{2,1,0:T(8,128)(2,1)S(1)} %collective-permute-done.9.refs_1_, ...), custom_call_target="tpu_custom_call" | custom-call | tf_op jit(solution)/shard_map/project/pallas_call | solution.py:248
  26.5 1.5 %scores.1 = f32[1,128]{1,0:T(1,128)} custom-call(f32[32,256]{1,0:T(8,128)S(1)} %get-tuple-element.30.noise_ref, f32[16,32,256]{2,1,0:T(8,128)S(1)} %project.3.proj_ref, f32[128,32,256]{2,1,0:T(8,128)S(1)} %get-tuple-element.39.wave_ref, bf16[128,32,256]{2,1,0:T(8,128)(2,1)S(1)} %get-tuple-element.40.images_ref), custom_call_target="tpu_custom_call" | custom-call | tf_op jit(solution)/shard_map/scores/pallas_call | solution.py:248
  28.0 0.0 collective-permute-done.4
  28.0 0.0 collective-permute-done.3
  28.0 1.0 %collective-permute-done.10 = bf16[2,32,512]{2,1,0:T(8,128)(2,1)S(1)} collective-permute-done((bf16[2,32,512]{2,1,0:T(8,128)(2,1)S(1)}, bf16[2,32,512]{2,1,0:T(8,128)(2,1)S(1)}, u32[]{:S(2)}, u32[]{:S(2)}) %collective-permute-start.10) | collective-permute-done | bytes 65568 | tf_op jit(solution)/shard_map/ppermute | solution.py:236
  29.0 0.7 %fusion.10 = (f32[1,32,512]{2,1,0:T(8,128)}, f32[1,32,512]{2,1,0:T(8,128)}) fusion(f32[2,32,512]{2,1,0:T(8,128)S(1)} %fusion.3), kind=kLoop, calls=%fused_computation.19 | loop fusion | bytes 262144 | tf_op jit(solution)/shard_map/slice | solution.py:381
  (8 shorter events, 0.1 us)
Async XLA Ops:
  0.6 7.0 %copy-start = (bf16[8,512,256]{2,1,0:T(8,128)(2,1)S(1)}, bf16[8,512,256]{2,1,0:T(8,128)(2,1)}, u32[]{:S(2)}) copy-start(bf16[8,512,256]{2,1,0:T(8,128)(2,1)} %tiles_ref.5) | copy-start | bytes 6291460
  0.6 10.7 %collective-permute-start = (bf16[1,32,512]{2,1,0:T(8,128)(2,1)}, bf16[1,32,512]{2,1,0:T(8,128)(2,1)S(1)}, u32[]{:S(2)}, u32[]{:S(2)}) collective-permute-start(bf16[1,32,512]{2,1,0:T(8,128)(2,1)} %param.8), channel_id=1, source_target_pairs={{0,8},{1,9},{2,10},{3,11},{4,12},{5,13},{6,14},{7,15},{8,0},{9,1},... | collective-permute-start | bytes 98312 | tf_op jit(solution)/shard_map/ppermute | solution.py:236
  7.7 3.7 %copy-start.1 = (bf16[1,32,512]{2,1,0:T(8,128)(2,1)S(1)}, bf16[1,32,512]{2,1,0:T(8,128)(2,1)}, u32[]{:S(2)}) copy-start(bf16[1,32,512]{2,1,0:T(8,128)(2,1)} %param.8) | copy-start | bytes 98308
  11.4 2.0 %collective-permute-start.1 = (bf16[8,2,32,512]{3,2,1,0:T(8,128)(2,1)S(1)}, bf16[8,2,32,512]{3,2,1,0:T(8,128)(2,1)S(1)}, u32[]{:S(2)}, u32[]{:S(2)}) collective-permute-start(bf16[8,2,32,512]{3,2,1,0:T(8,128)(2,1)S(1)} %get-tuple-element.28), channel_id=1, source_target_pairs={{0,1},{1,0},{2,3},{3,2},{4,5},{5,4},{6,7},{7,6},{8,9},{9,8},{10,11... | collective-permute-start | bytes 1572872 | tf_op jit(solution)/shard_map/ppermute | solution.py:236
  11.5 4.7 %collective-permute-start.6 = (bf16[2,32,512]{2,1,0:T(8,128)(2,1)S(1)}, bf16[2,32,512]{2,1,0:T(8,128)(2,1)S(1)}, u32[]{:S(2)}, u32[]{:S(2)}) collective-permute-start(bf16[2,32,512]{2,1,0:T(8,128)(2,1)S(1)} %pad_maximum_fusion), channel_id=1, source_target_pairs={{0,2},{1,3},{2,0},{3,1},{4,6},{5,7},{6,4},{7,5},{8,10},{9,11},{10,... | collective-permute-start | bytes 196616 | tf_op jit(solution)/shard_map/ppermute | solution.py:236
  13.4 5.7 %collective-permute-start.2 = (bf16[2,2,32,512]{3,2,1,0:T(8,128)(2,1)S(1)}, bf16[2,2,32,512]{3,2,1,0:T(8,128)(2,1)S(1)}, u32[]{:S(2)}, u32[]{:S(2)}) collective-permute-start(bf16[2,2,32,512]{3,2,1,0:T(8,128)(2,1)S(1)} %get-tuple-element.46), channel_id=1, source_target_pairs={{0,2},{1,3},{2,0},{3,1},{4,6},{5,7},{6,4},{7,5},{8,10},{9,11},{10,... | collective-permute-start | bytes 393224 | tf_op jit(solution)/shard_map/ppermute | solution.py:236
  16.1 4.6 %collective-permute-start.7 = (bf16[4,32,512]{2,1,0:T(8,128)(2,1)S(1)}, bf16[4,32,512]{2,1,0:T(8,128)(2,1)S(1)}, u32[]{:S(2)}, u32[]{:S(2)}) collective-permute-start(bf16[4,32,512]{2,1,0:T(8,128)(2,1)S(1)} %constant_dynamic-update-slice_fusion.refs_0_), channel_id=1, source_target_pairs={{0,1},{1,0},{2,3},{3,2},{4,5},{5,4},{6,7},{7,6},{8,9},{9,8},{10,11... | collective-permute-start | bytes 393224 | tf_op jit(solution)/shard_map/ppermute | solution.py:236
  16.2 5.9 %collective-permute-start.5 = (bf16[2,2,32,512]{3,2,1,0:T(8,128)(2,1)S(1)}, bf16[2,2,32,512]{3,2,1,0:T(8,128)(2,1)S(1)}, u32[]{:S(2)}, u32[]{:S(2)}) collective-permute-start(bf16[2,2,32,512]{3,2,1,0:T(8,128)(2,1)S(1)} %get-tuple-element.45), channel_id=1, source_target_pairs={{0,2},{1,3},{2,0},{3,1},{4,6},{5,7},{6,4},{7,5},{8,10},{9,11},{10,... | collective-permute-start | bytes 393224 | tf_op jit(solution)/shard_map/ppermute | solution.py:236
  17.6 5.7 %collective-permute-start.8 = (bf16[4,32,512]{2,1,0:T(8,128)(2,1)S(1)}, bf16[4,32,512]{2,1,0:T(8,128)(2,1)S(1)}, u32[]{:S(2)}, u32[]{:S(2)}) collective-permute-start(bf16[4,32,512]{2,1,0:T(8,128)(2,1)S(1)} %constant_dynamic-update-slice_fusion.refs_0_), channel_id=1, source_target_pairs={{0,4},{1,5},{2,6},{3,7},{4,0},{5,1},{6,2},{7,3},{8,12},{9,13},{10,... | collective-permute-start | bytes 393224 | tf_op jit(solution)/shard_map/ppermute | solution.py:236
  19.2 8.9 %collective-permute-start.3 = (bf16[2,32,512]{2,1,0:T(8,128)(2,1)S(1)}, bf16[2,32,512]{2,1,0:T(8,128)(2,1)S(1)}, u32[]{:S(2)}, u32[]{:S(2)}) collective-permute-start(bf16[2,32,512]{2,1,0:T(8,128)(2,1)S(1)} %get-tuple-element.48), channel_id=1, source_target_pairs={{0,12},{1,13},{2,14},{3,15},{4,8},{5,9},{6,10},{7,11},{8,4},{9,5},... | collective-permute-start | bytes 196616 | tf_op jit(solution)/shard_map/ppermute | solution.py:236
  22.1 5.9 %collective-permute-start.4 = (bf16[2,32,512]{2,1,0:T(8,128)(2,1)S(1)}, bf16[2,32,512]{2,1,0:T(8,128)(2,1)S(1)}, u32[]{:S(2)}, u32[]{:S(2)}) collective-permute-start(bf16[2,32,512]{2,1,0:T(8,128)(2,1)S(1)} %get-tuple-element.47), channel_id=1, source_target_pairs={{0,8},{1,9},{2,10},{3,11},{4,12},{5,13},{6,14},{7,15},{8,0},{9,1},... | collective-permute-start | bytes 196616 | tf_op jit(solution)/shard_map/ppermute | solution.py:236
  23.2 2.4 %collective-permute-start.9 = (bf16[4,32,512]{2,1,0:T(8,128)(2,1)S(1)}, bf16[4,32,512]{2,1,0:T(8,128)(2,1)S(1)}, u32[]{:S(2)}, u32[]{:S(2)}) collective-permute-start(bf16[4,32,512]{2,1,0:T(8,128)(2,1)S(1)} %collective-permute-done.8.refs_0_), channel_id=1, source_target_pairs={{0,1},{1,0},{2,3},{3,2},{4,5},{5,4},{6,7},{7,6},{8,9},{9,8},{10,11... | collective-permute-start | bytes 393224 | tf_op jit(solution)/shard_map/ppermute | solution.py:236
  23.2 5.8 %collective-permute-start.10 = (bf16[2,32,512]{2,1,0:T(8,128)(2,1)S(1)}, bf16[2,32,512]{2,1,0:T(8,128)(2,1)S(1)}, u32[]{:S(2)}, u32[]{:S(2)}) collective-permute-start(bf16[2,32,512]{2,1,0:T(8,128)(2,1)S(1)} %fusion.9), channel_id=1, source_target_pairs={{0,4},{1,5},{2,6},{3,7},{4,0},{5,1},{6,2},{7,3},{8,12},{9,13},{10,... | collective-permute-start | bytes 196616 | tf_op jit(solution)/shard_map/ppermute | solution.py:236

commit v19 on v17

--- a/solution.py
+++ b/solution.py
@@ -149,7 +149,7 @@
     lax.fori_loop(0, ref.shape[0], step, 0)
 
 
-def insert_kernel(place_vmem, sums_ref, tiles_ref, send_ref, far_ref, parts_ref, place_ref, sems):
+def insert_kernel(far, cut, place_vmem, sums_ref, tiles_ref, send_ref, far_ref, parts_ref, place_ref, sems):
     (started,) = copies([(place_vmem, place_ref)], sems)
     kinds = tiles_ref.shape[0]
     rows = sums_ref.shape[0]
@@ -161,14 +161,19 @@
         )
     started.wait()
     fill(send_ref, 0, place_ref, parts_ref)
-    devices = place_ref.shape[0]
-    fill(far_ref, devices - far_ref.shape[0], place_ref, parts_ref)
-
-
-def near_kernel(place_vmem, parts_ref, mate_ref, near_ref, place_ref, sems):
+    half, size = place_ref.shape[0] // 2, far - cut
+    for x in range(far_ref.shape[0] // size):
+        fill(far_ref.at[pl.ds(x * size, size)], half + (x + 1) * far + cut, place_ref, parts_ref)
+
+
+def near_kernel(cut, place_vmem, parts_ref, mate_ref, later_ref, near_ref, place_ref, sems):
     (started,) = copies([(place_vmem, place_ref)], sems)
     started.wait()
-    fill(near_ref, place_ref.shape[0] // 2, place_ref, parts_ref, mate_ref)
+    half, far = place_ref.shape[0] // 2, near_ref.shape[0]
+    for x in range(later_ref.shape[0] // cut):
+        mates = mate_ref.at[pl.ds((x + 1) * far, cut)]
+        fill(later_ref.at[pl.ds(x * cut, cut)], half + (x + 1) * far, place_ref, parts_ref, mates)
+    fill(near_ref, half, place_ref, parts_ref, mate_ref)
 
 
 def project_kernel(places, route_vmem, tiles_ref, *refs):
@@ -302,9 +307,10 @@
 
     place = (2, height, length)
     place_scratch = [pltpu.SMEM((devices, blocks), i32), pltpu.SemaphoreType.DMA((1,))]
+    cut = max(1, far // 2)
     send, keep, parts = call(
-        insert_kernel,
-        [((half, *place), bf16), ((half - far, *place), f32), ((kinds * rows + 2 * height, length), f32)],
+        functools.partial(insert_kernel, far, cut),
+        [((half, *place), bf16), (((wide - 1) * (far - cut), *place), f32), ((kinds * rows + 2 * height, length), f32)],
         [vmem] * 3,
         (place_rows, sums, tiles_near),
         place_scratch,
@@ -314,15 +320,21 @@
     )
     send, gathered = lax.optimization_barrier((send, gathered))
     mate = swap(send, 1)
-    def along_x(start, stop):
-        return (keep[start:stop] + mate[far + start : far + stop].astype(f32)).astype(bf16)
-
-    cut = max(1, far // 2)
-    main = [along_x(x * far + cut, (x + 1) * far) for x in range(wide - 1)]
-    later = [along_x(x * far, x * far + cut) for x in range(wide - 1)]
-    (near,) = call(
-        near_kernel, [((far, *place), f32)], [vmem] * 3, (place_rows, parts, mate), place_scratch, 0, 0, "near"
-    )
+    main = []
+    for x in range(wide - 1):
+        came = mate[(x + 1) * far + cut : (x + 2) * far].astype(f32)
+        main.append((keep[x * (far - cut) : (x + 1) * (far - cut)] + came).astype(bf16))
+    later, near = call(
+        functools.partial(near_kernel, cut),
+        [(((wide - 1) * cut, *place), bf16), ((far, *place), f32)],
+        [vmem] * 3,
+        (place_rows, parts, mate),
+        place_scratch,
+        0,
+        0,
+        "near",
+    )
+    later = [later[x * cut : (x + 1) * cut] for x in range(wide - 1)]
     for offset in offsets[1:-1]:
         came, _ = lax.optimization_barrier((swap(gathered, offset), near))
         gathered = jnp.concatenate([gathered, came], axis=0)

time: 29.9 us -> 29.7 us (level)
  starting transfers between devices: 15 us -> 14.6 us
    ppermute x11, starting transfers between devices: 15 us -> 14.6 us  [swap(): lax.ppermute(array, 'slab', [(i, i ^ offset) for i in range(devices)])]
  transfers between devices with their start and end apart: 11 -> 11, of which waited for: 3 -> 3; matrix products, arithmetic and copies ran while one was open for 0% -> 0% of each run, Pallas kernels for 37% -> 38%
where the time goes in v19:
time: 29.7 us; the launch traced here: 29.5 us
  starting transfers between devices  14.6 us (49%)
  Pallas kernels  11.1 us (37%)
  waiting for transfers between devices  2.26 us (8%)
  between operations  0.76 us (3%)
  local copies, waits for them, and re-layouts  0.68 us (2%)
    ppermute x11, starting transfers between devices, swap(): lax.ppermute(array, 'slab', [(i, i ^ offset) for i in range(devices)])  14.6 us
    pallas_call x6, Pallas kernels, call(): pl.pallas_call(kernel, out_shape=tuple((jax.ShapeDtypeStruct(s, t) for s,...  11.1 us
    ppermute x11, waiting for transfers between devices, swap(): lax.ppermute(array, 'slab', [(i, i ^ offset) for i in range(devices)])  2.26 us
    slice x1, local copies, waits for them, and re-layouts, on_device(): return (scores.reshape(count), total[0:1], total[1:2])  0.66 us
  transfers between devices with their start and end apart: 11, of which 3 were waited for; matrix products, arithmetic and copies ran while one was open for 0% of the time, Pallas kernels for 38%

profile of v19, /device:TPU:0, one launch (start us, length us, event | category | flops | bytes accessed | tf_op | source)
XLA Modules:
  0.0 29.5 jit_solution(5506044354077337513)
XLA Ops:
  0.6 4.1 %collective-permute-start = (bf16[1,32,512]{2,1,0:T(8,128)(2,1)}, bf16[1,32,512]{2,1,0:T(8,128)(2,1)S(1)}, u32[]{:S(2)}, u32[]{:S(2)}) collective-permute-start(bf16[1,32,512]{2,1,0:T(8,128)(2,1)} %param.8), channel_id=1, source_target_pairs={{0,8},{1,9},{2,10},{3,11},{4,12},{5,13},{6,14},{7,15},{8,0},{9,1},... | collective-permute-start | bytes 98312 | tf_op jit(solution)/shard_map/ppermute | solution.py:244
  4.7 2.9 %sums.1 = (bf16[1024,256]{1,0:T(8,128)(2,1)S(1)}, f32[128,32,256]{2,1,0:T(8,128)S(1)}, bf16[8,512,256]{2,1,0:T(8,128)(2,1)S(1)}, bf16[128,32,256]{2,1,0:T(8,128)...) custom-call(s32[8,16]{1,0:T(8,128)} %bitcast.17, ...), custom_call_target="tpu_custom_call" | custom-call | bytes 10485760 | tf_op jit(solution)/shard_map/sums/pallas_call | solution.py:256
  7.7 0.0 copy-start
  7.7 3.5 %insert.1 = (bf16[8,2,32,512]{3,2,1,0:T(8,128)(2,1)S(1)}, f32[2,2,32,512]{3,2,1,0:T(8,128)S(1)}, f32[8256,512]{1,0:T(8,128)S(1)}) custom-call(s32[16,16]{1,0:T(8,128)S(1)} %get-tuple-element.27.place_vmem, bf16[1024,256]{1,0:T(8,128)(2,1)S(1)} %get-tuple-element.28.sums_ref, bf16[8,512,256]{2,1,0:T(8,128)(2,1)S(1)} %get-tuple-element.29.tiles_ref), custom_call_target="tpu_custom_call" | custom-call | flops 2147483648 | bytes 8388608 | tf_op jit(solution)/shard_map/insert/pallas_call | solution.py:256
  11.1 0.0 collective-permute-done
  11.2 0.0 copy-done
  11.2 0.1 collective-permute-start.1
  11.3 1.6 %collective-permute-start.6 = (bf16[2,32,512]{2,1,0:T(8,128)(2,1)S(1)}, bf16[2,32,512]{2,1,0:T(8,128)(2,1)S(1)}, u32[]{:S(2)}, u32[]{:S(2)}) collective-permute-start(bf16[2,32,512]{2,1,0:T(8,128)(2,1)S(1)} %pad_maximum_fusion), channel_id=1, source_target_pairs={{0,2},{1,3},{2,0},{3,1},{4,6},{5,7},{6,4},{7,5},{8,10},{9,11},{10,... | collective-permute-start | bytes 196616 | tf_op jit(solution)/shard_map/ppermute | solution.py:244
  12.8 0.3 %collective-permute-done.1.mate_ref = bf16[8,2,32,512]{3,2,1,0:T(8,128)(2,1)S(1)} collective-permute-done((bf16[8,2,32,512]{3,2,1,0:T(8,128)(2,1)S(1)}, bf16[8,2,32,512]{3,2,1,0:T(8,128)(2,1)S(1)}, u32[]{:S(2)}, u32[]{:S(2)}) %collective-permute-start.1) | collective-permute-done | bytes 524320 | tf_op jit(solution)/shard_map/ppermute | solution.py:244
  13.2 1.6 %collective-permute-start.2 = (bf16[2,2,32,512]{3,2,1,0:T(8,128)(2,1)S(1)}, bf16[2,2,32,512]{3,2,1,0:T(8,128)(2,1)S(1)}, u32[]{:S(2)}, u32[]{:S(2)}) collective-permute-start(bf16[2,2,32,512]{3,2,1,0:T(8,128)(2,1)S(1)} %add_convert_fusion), channel_id=1, source_target_pairs={{0,2},{1,3},{2,0},{3,1},{4,6},{5,7},{6,4},{7,5},{8,10},{9,11},{10,... | collective-permute-start | bytes 393224 | tf_op jit(solution)/shard_map/ppermute | solution.py:244
  14.8 1.3 %near.1 = (bf16[2,2,32,512]{3,2,1,0:T(8,128)(2,1)S(1)}, f32[4,2,32,512]{3,2,1,0:T(8,128)S(1)}) custom-call(s32[16,16]{1,0:T(8,128)S(1)} %get-tuple-element.27.place_vmem, f32[8256,512]{1,0:T(8,128)S(1)} %get-tuple-element.30.parts_ref, bf16[8,2,32,512]{3,2,1,0:T(8,128)(2,1)S(1)} %collective-permute-done.1.mate_ref), custom_call_target="tpu_custom_call" | custom-call | tf_op jit(solution)/shard_map/near/pallas_call | solution.py:256
  16.1 0.0 collective-permute-done.6
  16.1 0.1 collective-permute-start.7
  16.2 1.1 %collective-permute-start.5 = (bf16[2,2,32,512]{3,2,1,0:T(8,128)(2,1)S(1)}, bf16[2,2,32,512]{3,2,1,0:T(8,128)(2,1)S(1)}, u32[]{:S(2)}, u32[]{:S(2)}) collective-permute-start(bf16[2,2,32,512]{3,2,1,0:T(8,128)(2,1)S(1)} %get-tuple-element.37), channel_id=1, source_target_pairs={{0,2},{1,3},{2,0},{3,1},{4,6},{5,7},{6,4},{7,5},{8,10},{9,11},{10,... | collective-permute-start | bytes 393224 | tf_op jit(solution)/shard_map/ppermute | solution.py:244
  17.3 1.6 %collective-permute-start.8 = (bf16[4,32,512]{2,1,0:T(8,128)(2,1)S(1)}, bf16[4,32,512]{2,1,0:T(8,128)(2,1)S(1)}, u32[]{:S(2)}, u32[]{:S(2)}) collective-permute-start(bf16[4,32,512]{2,1,0:T(8,128)(2,1)S(1)} %constant_dynamic-update-slice_fusion.refs_0_), channel_id=1, source_target_pairs={{0,4},{1,5},{2,6},{3,7},{4,0},{5,1},{6,2},{7,3},{8,12},{9,13},{10,... | collective-permute-start | bytes 393224 | tf_op jit(solution)/shard_map/ppermute | solution.py:244
  18.9 0.0 collective-permute-done.2
  19.0 1.3 %collective-permute-start.3 = (bf16[2,32,512]{2,1,0:T(8,128)(2,1)S(1)}, bf16[2,32,512]{2,1,0:T(8,128)(2,1)S(1)}, u32[]{:S(2)}, u32[]{:S(2)}) collective-permute-start(bf16[2,32,512]{2,1,0:T(8,128)(2,1)S(1)} %get-tuple-element.52), channel_id=1, source_target_pairs={{0,12},{1,13},{2,14},{3,15},{4,8},{5,9},{6,10},{7,11},{8,4},{9,5},... | collective-permute-start | bytes 196616 | tf_op jit(solution)/shard_map/ppermute | solution.py:244
  20.2 0.0 collective-permute-done.7.refs_1_
  20.3 0.9 %project.2.refs_2_ = f32[16,32,256]{2,1,0:T(8,128)S(1)} custom-call(s32[8,16]{1,0:T(8,128)S(1)} %get-tuple-element.38.route_vmem, bf16[8,512,256]{2,1,0:T(8,128)(2,1)S(1)} %get-tuple-element.29.tiles_ref, bf16[4,32,512]{2,1,0:T(8,128)(2,1)S(1)} %constant_dynamic-update-slice_fusion.refs_0_, bf16[4,32,512]{2,1,0:T(8,128)(2,1)S(1)} %collective-permute-done.7.refs_1_), custom_call_target="tpu_custom_call" | custom-call | tf_op jit(solution)/shard_map/project/pallas_call | solution.py:256
  21.2 0.9 %collective-permute-done.5 = bf16[2,2,32,512]{3,2,1,0:T(8,128)(2,1)S(1)} collective-permute-done((bf16[2,2,32,512]{3,2,1,0:T(8,128)(2,1)S(1)}, bf16[2,2,32,512]{3,2,1,0:T(8,128)(2,1)S(1)}, u32[]{:S(2)}, u32[]{:S(2)}) %collective-permute-start.5) | collective-permute-done | bytes 131104 | tf_op jit(solution)/shard_map/ppermute | solution.py:244
  22.1 0.8 %collective-permute-start.4 = (bf16[2,32,512]{2,1,0:T(8,128)(2,1)S(1)}, bf16[2,32,512]{2,1,0:T(8,128)(2,1)S(1)}, u32[]{:S(2)}, u32[]{:S(2)}) collective-permute-start(bf16[2,32,512]{2,1,0:T(8,128)(2,1)S(1)} %get-tuple-element.51), channel_id=1, source_target_pairs={{0,8},{1,9},{2,10},{3,11},{4,12},{5,13},{6,14},{7,15},{8,0},{9,1},... | collective-permute-start | bytes 196616 | tf_op jit(solution)/shard_map/ppermute | solution.py:244
  22.9 0.0 collective-permute-done.8.refs_0_
  23.0 0.0 collective-permute-start.9
  23.0 2.4 %collective-permute-start.10 = (bf16[2,32,512]{2,1,0:T(8,128)(2,1)S(1)}, bf16[2,32,512]{2,1,0:T(8,128)(2,1)S(1)}, u32[]{:S(2)}, u32[]{:S(2)}) collective-permute-start(bf16[2,32,512]{2,1,0:T(8,128)(2,1)S(1)} %fusion.4), channel_id=1, source_target_pairs={{0,4},{1,5},{2,6},{3,7},{4,0},{5,1},{6,2},{7,3},{8,12},{9,13},{10,... | collective-permute-start | bytes 196616 | tf_op jit(solution)/shard_map/ppermute | solution.py:244
  25.4 0.0 collective-permute-done.9.refs_1_
  25.4 1.0 %project.3.proj_ref = f32[16,32,256]{2,1,0:T(8,128)S(1)} custom-call(s32[8,16]{1,0:T(8,128)S(1)} %get-tuple-element.36.route_vmem, bf16[8,512,256]{2,1,0:T(8,128)(2,1)S(1)} %get-tuple-element.29.tiles_ref, bf16[4,32,512]{2,1,0:T(8,128)(2,1)S(1)} %collective-permute-done.8.refs_0_, bf16[4,32,512]{2,1,0:T(8,128)(2,1)S(1)} %collective-permute-done.9.refs_1_, ...), custom_call_target="tpu_custom_call" | custom-call | tf_op jit(solution)/shard_map/project/pallas_call | solution.py:256
  26.4 1.5 %scores.1 = f32[1,128]{1,0:T(1,128)} custom-call(f32[32,256]{1,0:T(8,128)S(1)} %get-tuple-element.35.noise_ref, f32[16,32,256]{2,1,0:T(8,128)S(1)} %project.3.proj_ref, f32[128,32,256]{2,1,0:T(8,128)S(1)} %get-tuple-element.45.wave_ref, bf16[128,32,256]{2,1,0:T(8,128)(2,1)S(1)} %get-tuple-element.46.images_ref), custom_call_target="tpu_custom_call" | custom-call | tf_op jit(solution)/shard_map/scores/pallas_call | solution.py:256
  27.8 0.0 collective-permute-done.4
  27.8 0.0 collective-permute-done.3
  27.8 1.0 %collective-permute-done.10 = bf16[2,32,512]{2,1,0:T(8,128)(2,1)S(1)} collective-permute-done((bf16[2,32,512]{2,1,0:T(8,128)(2,1)S(1)}, bf16[2,32,512]{2,1,0:T(8,128)(2,1)S(1)}, u32[]{:S(2)}, u32[]{:S(2)}) %collective-permute-start.10) | collective-permute-done | bytes 65568 | tf_op jit(solution)/shard_map/ppermute | solution.py:244
  28.8 0.7 %fusion.5 = (f32[1,32,512]{2,1,0:T(8,128)}, f32[1,32,512]{2,1,0:T(8,128)}) fusion(f32[2,32,512]{2,1,0:T(8,128)S(1)} %fusion.1), kind=kLoop, calls=%fused_computation.13 | loop fusion | bytes 262144 | tf_op jit(solution)/shard_map/slice | solution.py:397
  (7 shorter events, 0.1 us)
Async XLA Ops:
  0.6 10.5 %collective-permute-start = (bf16[1,32,512]{2,1,0:T(8,128)(2,1)}, bf16[1,32,512]{2,1,0:T(8,128)(2,1)S(1)}, u32[]{:S(2)}, u32[]{:S(2)}) collective-permute-start(bf16[1,32,512]{2,1,0:T(8,128)(2,1)} %param.8), channel_id=1, source_target_pairs={{0,8},{1,9},{2,10},{3,11},{4,12},{5,13},{6,14},{7,15},{8,0},{9,1},... | collective-permute-start | bytes 98312 | tf_op jit(solution)/shard_map/ppermute | solution.py:244
  7.7 3.5 %copy-start = (bf16[1,32,512]{2,1,0:T(8,128)(2,1)S(1)}, bf16[1,32,512]{2,1,0:T(8,128)(2,1)}, u32[]{:S(2)}) copy-start(bf16[1,32,512]{2,1,0:T(8,128)(2,1)} %param.8) | copy-start | bytes 98308
  11.2 2.0 %collective-permute-start.1 = (bf16[8,2,32,512]{3,2,1,0:T(8,128)(2,1)S(1)}, bf16[8,2,32,512]{3,2,1,0:T(8,128)(2,1)S(1)}, u32[]{:S(2)}, u32[]{:S(2)}) collective-permute-start(bf16[8,2,32,512]{3,2,1,0:T(8,128)(2,1)S(1)} %get-tuple-element.32), channel_id=1, source_target_pairs={{0,1},{1,0},{2,3},{3,2},{4,5},{5,4},{6,7},{7,6},{8,9},{9,8},{10,11... | collective-permute-start | bytes 1572872 | tf_op jit(solution)/shard_map/ppermute | solution.py:244
  11.3 4.8 %collective-permute-start.6 = (bf16[2,32,512]{2,1,0:T(8,128)(2,1)S(1)}, bf16[2,32,512]{2,1,0:T(8,128)(2,1)S(1)}, u32[]{:S(2)}, u32[]{:S(2)}) collective-permute-start(bf16[2,32,512]{2,1,0:T(8,128)(2,1)S(1)} %pad_maximum_fusion), channel_id=1, source_target_pairs={{0,2},{1,3},{2,0},{3,1},{4,6},{5,7},{6,4},{7,5},{8,10},{9,11},{10,... | collective-permute-start | bytes 196616 | tf_op jit(solution)/shard_map/ppermute | solution.py:244
  13.2 5.7 %collective-permute-start.2 = (bf16[2,2,32,512]{3,2,1,0:T(8,128)(2,1)S(1)}, bf16[2,2,32,512]{3,2,1,0:T(8,128)(2,1)S(1)}, u32[]{:S(2)}, u32[]{:S(2)}) collective-permute-start(bf16[2,2,32,512]{3,2,1,0:T(8,128)(2,1)S(1)} %add_convert_fusion), channel_id=1, source_target_pairs={{0,2},{1,3},{2,0},{3,1},{4,6},{5,7},{6,4},{7,5},{8,10},{9,11},{10,... | collective-permute-start | bytes 393224 | tf_op jit(solution)/shard_map/ppermute | solution.py:244
  16.1 4.1 %collective-permute-start.7 = (bf16[4,32,512]{2,1,0:T(8,128)(2,1)S(1)}, bf16[4,32,512]{2,1,0:T(8,128)(2,1)S(1)}, u32[]{:S(2)}, u32[]{:S(2)}) collective-permute-start(bf16[4,32,512]{2,1,0:T(8,128)(2,1)S(1)} %constant_dynamic-update-slice_fusion.refs_0_), channel_id=1, source_target_pairs={{0,1},{1,0},{2,3},{3,2},{4,5},{5,4},{6,7},{7,6},{8,9},{9,8},{10,11... | collective-permute-start | bytes 393224 | tf_op jit(solution)/shard_map/ppermute | solution.py:244
  16.2 5.9 %collective-permute-start.5 = (bf16[2,2,32,512]{3,2,1,0:T(8,128)(2,1)S(1)}, bf16[2,2,32,512]{3,2,1,0:T(8,128)(2,1)S(1)}, u32[]{:S(2)}, u32[]{:S(2)}) collective-permute-start(bf16[2,2,32,512]{3,2,1,0:T(8,128)(2,1)S(1)} %get-tuple-element.37), channel_id=1, source_target_pairs={{0,2},{1,3},{2,0},{3,1},{4,6},{5,7},{6,4},{7,5},{8,10},{9,11},{10,... | collective-permute-start | bytes 393224 | tf_op jit(solution)/shard_map/ppermute | solution.py:244
  17.3 5.6 %collective-permute-start.8 = (bf16[4,32,512]{2,1,0:T(8,128)(2,1)S(1)}, bf16[4,32,512]{2,1,0:T(8,128)(2,1)S(1)}, u32[]{:S(2)}, u32[]{:S(2)}) collective-permute-start(bf16[4,32,512]{2,1,0:T(8,128)(2,1)S(1)} %constant_dynamic-update-slice_fusion.refs_0_), channel_id=1, source_target_pairs={{0,4},{1,5},{2,6},{3,7},{4,0},{5,1},{6,2},{7,3},{8,12},{9,13},{10,... | collective-permute-start | bytes 393224 | tf_op jit(solution)/shard_map/ppermute | solution.py:244
  19.0 8.9 %collective-permute-start.3 = (bf16[2,32,512]{2,1,0:T(8,128)(2,1)S(1)}, bf16[2,32,512]{2,1,0:T(8,128)(2,1)S(1)}, u32[]{:S(2)}, u32[]{:S(2)}) collective-permute-start(bf16[2,32,512]{2,1,0:T(8,128)(2,1)S(1)} %get-tuple-element.52), channel_id=1, source_target_pairs={{0,12},{1,13},{2,14},{3,15},{4,8},{5,9},{6,10},{7,11},{8,4},{9,5},... | collective-permute-start | bytes 196616 | tf_op jit(solution)/shard_map/ppermute | solution.py:244
  22.1 5.7 %collective-permute-start.4 = (bf16[2,32,512]{2,1,0:T(8,128)(2,1)S(1)}, bf16[2,32,512]{2,1,0:T(8,128)(2,1)S(1)}, u32[]{:S(2)}, u32[]{:S(2)}) collective-permute-start(bf16[2,32,512]{2,1,0:T(8,128)(2,1)S(1)} %get-tuple-element.51), channel_id=1, source_target_pairs={{0,8},{1,9},{2,10},{3,11},{4,12},{5,13},{6,14},{7,15},{8,0},{9,1},... | collective-permute-start | bytes 196616 | tf_op jit(solution)/shard_map/ppermute | solution.py:244
  23.0 2.4 %collective-permute-start.9 = (bf16[4,32,512]{2,1,0:T(8,128)(2,1)S(1)}, bf16[4,32,512]{2,1,0:T(8,128)(2,1)S(1)}, u32[]{:S(2)}, u32[]{:S(2)}) collective-permute-start(bf16[4,32,512]{2,1,0:T(8,128)(2,1)S(1)} %collective-permute-done.8.refs_0_), channel_id=1, source_target_pairs={{0,1},{1,0},{2,3},{3,2},{4,5},{5,4},{6,7},{7,6},{8,9},{9,8},{10,11... | collective-permute-start | bytes 393224 | tf_op jit(solution)/shard_map/ppermute | solution.py:244
  23.0 5.8 %collective-permute-start.10 = (bf16[2,32,512]{2,1,0:T(8,128)(2,1)S(1)}, bf16[2,32,512]{2,1,0:T(8,128)(2,1)S(1)}, u32[]{:S(2)}, u32[]{:S(2)}) collective-permute-start(bf16[2,32,512]{2,1,0:T(8,128)(2,1)S(1)} %fusion.4), channel_id=1, source_target_pairs={{0,4},{1,5},{2,6},{3,7},{4,0},{5,1},{6,2},{7,3},{8,12},{9,13},{10,... | collective-permute-start | bytes 196616 | tf_op jit(solution)/shard_map/ppermute | solution.py:244

commit v20 on v17

--- a/solution.py
+++ b/solution.py
@@ -146,7 +146,7 @@
         ref[slot] = acc.astype(ref.dtype)
         return carry
 
-    lax.fori_loop(0, ref.shape[0], step, 0)
+    lax.fori_loop(0, ref.shape[0], step, 0, unroll=2)
 
 
 def insert_kernel(place_vmem, sums_ref, tiles_ref, send_ref, far_ref, parts_ref, place_ref, sems):

time: 29.9 us -> 29.8 us (level)
  no operation moved by 1% of the time
where the time goes in v20:
time: 29.8 us; the launch traced here: 29.6 us
  starting transfers between devices  15 us (50%)
  Pallas kernels  11 us (37%)
  waiting for transfers between devices  2.01 us (7%)
  between operations  0.76 us (3%)
  local copies, waits for them, and re-layouts  0.68 us (2%)
    ppermute x11, starting transfers between devices, swap(): lax.ppermute(array, 'slab', [(i, i ^ offset) for i in range(devices)])  15 us
    pallas_call x6, Pallas kernels, call(): pl.pallas_call(kernel, out_shape=tuple((jax.ShapeDtypeStruct(s, t) for s,...  11 us
    ppermute x11, waiting for transfers between devices, swap(): lax.ppermute(array, 'slab', [(i, i ^ offset) for i in range(devices)])  2.01 us
    slice x1, local copies, waits for them, and re-layouts, on_device(): return (scores.reshape(count), total[0:1], total[1:2])  0.66 us
  transfers between devices with their start and end apart: 11, of which 3 were waited for; matrix products, arithmetic and copies ran while one was open for 0% of the time, Pallas kernels for 37%

profile of v20, /device:TPU:0, one launch (start us, length us, event | category | flops | bytes accessed | tf_op | source)
XLA Modules:
  0.0 29.6 jit_solution(17978931208494102241)
XLA Ops:
  0.6 4.1 %collective-permute-start = (bf16[1,32,512]{2,1,0:T(8,128)(2,1)}, bf16[1,32,512]{2,1,0:T(8,128)(2,1)S(1)}, u32[]{:S(2)}, u32[]{:S(2)}) collective-permute-start(bf16[1,32,512]{2,1,0:T(8,128)(2,1)} %param.8), channel_id=1, source_target_pairs={{0,8},{1,9},{2,10},{3,11},{4,12},{5,13},{6,14},{7,15},{8,0},{9,1},... | collective-permute-start | bytes 98312 | tf_op jit(solution)/shard_map/ppermute | solution.py:239
  4.7 2.9 %sums.1 = (bf16[1024,256]{1,0:T(8,128)(2,1)S(1)}, f32[128,32,256]{2,1,0:T(8,128)S(1)}, bf16[8,512,256]{2,1,0:T(8,128)(2,1)S(1)}, bf16[128,32,256]{2,1,0:T(8,128)...) custom-call(s32[8,16]{1,0:T(8,128)} %bitcast.19, ...), custom_call_target="tpu_custom_call" | custom-call | bytes 10485760 | tf_op jit(solution)/shard_map/sums/pallas_call | solution.py:251
  7.7 0.0 copy-start
  7.7 3.6 %insert.1 = (bf16[8,2,32,512]{3,2,1,0:T(8,128)(2,1)S(1)}, f32[4,2,32,512]{3,2,1,0:T(8,128)S(1)}, f32[8256,512]{1,0:T(8,128)S(1)}) custom-call(s32[16,16]{1,0:T(8,128)S(1)} %get-tuple-element.25.place_vmem, bf16[1024,256]{1,0:T(8,128)(2,1)S(1)} %get-tuple-element.26.sums_ref, bf16[8,512,256]{2,1,0:T(8,128)(2,1)S(1)} %get-tuple-element.27.tiles_ref), custom_call_target="tpu_custom_call" | custom-call | flops 2147483648 | bytes 8388608 | tf_op jit(solution)/shard_map/insert/pallas_call | solution.py:251
  11.3 0.0 collective-permute-done
  11.3 0.0 copy-done
  11.3 0.1 collective-permute-start.1
  11.4 1.6 %collective-permute-start.6 = (bf16[2,32,512]{2,1,0:T(8,128)(2,1)S(1)}, bf16[2,32,512]{2,1,0:T(8,128)(2,1)S(1)}, u32[]{:S(2)}, u32[]{:S(2)}) collective-permute-start(bf16[2,32,512]{2,1,0:T(8,128)(2,1)S(1)} %pad_maximum_fusion), channel_id=1, source_target_pairs={{0,2},{1,3},{2,0},{3,1},{4,6},{5,7},{6,4},{7,5},{8,10},{9,11},{10,... | collective-permute-start | bytes 196616 | tf_op jit(solution)/shard_map/ppermute | solution.py:239
  12.9 0.3 %collective-permute-done.1.mate_ref = bf16[8,2,32,512]{3,2,1,0:T(8,128)(2,1)S(1)} collective-permute-done((bf16[8,2,32,512]{3,2,1,0:T(8,128)(2,1)S(1)}, bf16[8,2,32,512]{3,2,1,0:T(8,128)(2,1)S(1)}, u32[]{:S(2)}, u32[]{:S(2)}) %collective-permute-start.1) | collective-permute-done | bytes 524320 | tf_op jit(solution)/shard_map/ppermute | solution.py:239
  13.3 0.1 add_convert_fusion
  13.4 1.6 %collective-permute-start.2 = (bf16[2,2,32,512]{3,2,1,0:T(8,128)(2,1)S(1)}, bf16[2,2,32,512]{3,2,1,0:T(8,128)(2,1)S(1)}, u32[]{:S(2)}, u32[]{:S(2)}) collective-permute-start(bf16[2,2,32,512]{3,2,1,0:T(8,128)(2,1)S(1)} %get-tuple-element.48), channel_id=1, source_target_pairs={{0,2},{1,3},{2,0},{3,1},{4,6},{5,7},{6,4},{7,5},{8,10},{9,11},{10,... | collective-permute-start | bytes 393224 | tf_op jit(solution)/shard_map/ppermute | solution.py:239
  14.9 1.1 %near.1 = f32[4,2,32,512]{3,2,1,0:T(8,128)S(1)} custom-call(s32[16,16]{1,0:T(8,128)S(1)} %get-tuple-element.25.place_vmem, f32[8256,512]{1,0:T(8,128)S(1)} %get-tuple-element.28.parts_ref, bf16[8,2,32,512]{3,2,1,0:T(8,128)(2,1)S(1)} %collective-permute-done.1.mate_ref), custom_call_target="tpu_custom_call" | custom-call | tf_op jit(solution)/shard_map/near/pallas_call | solution.py:251
  16.0 0.0 collective-permute-done.6
  16.1 0.1 collective-permute-start.7
  16.1 1.3 %collective-permute-start.5 = (bf16[2,2,32,512]{3,2,1,0:T(8,128)(2,1)S(1)}, bf16[2,2,32,512]{3,2,1,0:T(8,128)(2,1)S(1)}, u32[]{:S(2)}, u32[]{:S(2)}) collective-permute-start(bf16[2,2,32,512]{3,2,1,0:T(8,128)(2,1)S(1)} %get-tuple-element.47), channel_id=1, source_target_pairs={{0,2},{1,3},{2,0},{3,1},{4,6},{5,7},{6,4},{7,5},{8,10},{9,11},{10,... | collective-permute-start | bytes 393224 | tf_op jit(solution)/shard_map/ppermute | solution.py:239
  17.5 1.6 %collective-permute-start.8 = (bf16[4,32,512]{2,1,0:T(8,128)(2,1)S(1)}, bf16[4,32,512]{2,1,0:T(8,128)(2,1)S(1)}, u32[]{:S(2)}, u32[]{:S(2)}) collective-permute-start(bf16[4,32,512]{2,1,0:T(8,128)(2,1)S(1)} %constant_dynamic-update-slice_fusion.refs_0_), channel_id=1, source_target_pairs={{0,4},{1,5},{2,6},{3,7},{4,0},{5,1},{6,2},{7,3},{8,12},{9,13},{10,... | collective-permute-start | bytes 393224 | tf_op jit(solution)/shard_map/ppermute | solution.py:239
  19.0 0.0 collective-permute-done.2
  19.1 1.3 %collective-permute-start.3 = (bf16[2,32,512]{2,1,0:T(8,128)(2,1)S(1)}, bf16[2,32,512]{2,1,0:T(8,128)(2,1)S(1)}, u32[]{:S(2)}, u32[]{:S(2)}) collective-permute-start(bf16[2,32,512]{2,1,0:T(8,128)(2,1)S(1)} %get-tuple-element.50), channel_id=1, source_target_pairs={{0,12},{1,13},{2,14},{3,15},{4,8},{5,9},{6,10},{7,11},{8,4},{9,5},... | collective-permute-start | bytes 196616 | tf_op jit(solution)/shard_map/ppermute | solution.py:239
  20.4 0.0 collective-permute-done.7.refs_1_
  20.4 0.9 %project.2.refs_2_ = f32[16,32,256]{2,1,0:T(8,128)S(1)} custom-call(s32[8,16]{1,0:T(8,128)S(1)} %get-tuple-element.34.route_vmem, bf16[8,512,256]{2,1,0:T(8,128)(2,1)S(1)} %get-tuple-element.27.tiles_ref, bf16[4,32,512]{2,1,0:T(8,128)(2,1)S(1)} %constant_dynamic-update-slice_fusion.refs_0_, bf16[4,32,512]{2,1,0:T(8,128)(2,1)S(1)} %collective-permute-done.7.refs_1_), custom_call_target="tpu_custom_call" | custom-call | tf_op jit(solution)/shard_map/project/pallas_call | solution.py:251
  21.4 0.7 %collective-permute-done.5 = bf16[2,2,32,512]{3,2,1,0:T(8,128)(2,1)S(1)} collective-permute-done((bf16[2,2,32,512]{3,2,1,0:T(8,128)(2,1)S(1)}, bf16[2,2,32,512]{3,2,1,0:T(8,128)(2,1)S(1)}, u32[]{:S(2)}, u32[]{:S(2)}) %collective-permute-start.5) | collective-permute-done | bytes 131104 | tf_op jit(solution)/shard_map/ppermute | solution.py:239
  22.1 1.1 %collective-permute-start.4 = (bf16[2,32,512]{2,1,0:T(8,128)(2,1)S(1)}, bf16[2,32,512]{2,1,0:T(8,128)(2,1)S(1)}, u32[]{:S(2)}, u32[]{:S(2)}) collective-permute-start(bf16[2,32,512]{2,1,0:T(8,128)(2,1)S(1)} %get-tuple-element.49), channel_id=1, source_target_pairs={{0,8},{1,9},{2,10},{3,11},{4,12},{5,13},{6,14},{7,15},{8,0},{9,1},... | collective-permute-start | bytes 196616 | tf_op jit(solution)/shard_map/ppermute | solution.py:239
  23.1 0.0 collective-permute-done.8.refs_0_
  23.1 0.0 collective-permute-start.9
  23.1 2.3 %collective-permute-start.10 = (bf16[2,32,512]{2,1,0:T(8,128)(2,1)S(1)}, bf16[2,32,512]{2,1,0:T(8,128)(2,1)S(1)}, u32[]{:S(2)}, u32[]{:S(2)}) collective-permute-start(bf16[2,32,512]{2,1,0:T(8,128)(2,1)S(1)} %fusion.9), channel_id=1, source_target_pairs={{0,4},{1,5},{2,6},{3,7},{4,0},{5,1},{6,2},{7,3},{8,12},{9,13},{10,... | collective-permute-start | bytes 196616 | tf_op jit(solution)/shard_map/ppermute | solution.py:239
  25.5 0.0 collective-permute-done.9.refs_1_
  25.5 1.0 %project.3.proj_ref = f32[16,32,256]{2,1,0:T(8,128)S(1)} custom-call(s32[8,16]{1,0:T(8,128)S(1)} %get-tuple-element.33.route_vmem, bf16[8,512,256]{2,1,0:T(8,128)(2,1)S(1)} %get-tuple-element.27.tiles_ref, bf16[4,32,512]{2,1,0:T(8,128)(2,1)S(1)} %collective-permute-done.8.refs_0_, bf16[4,32,512]{2,1,0:T(8,128)(2,1)S(1)} %collective-permute-done.9.refs_1_, ...), custom_call_target="tpu_custom_call" | custom-call | tf_op jit(solution)/shard_map/project/pallas_call | solution.py:251
  26.5 1.5 %scores.1 = f32[1,128]{1,0:T(1,128)} custom-call(f32[32,256]{1,0:T(8,128)S(1)} %get-tuple-element.32.noise_ref, f32[16,32,256]{2,1,0:T(8,128)S(1)} %project.3.proj_ref, f32[128,32,256]{2,1,0:T(8,128)S(1)} %get-tuple-element.41.wave_ref, bf16[128,32,256]{2,1,0:T(8,128)(2,1)S(1)} %get-tuple-element.42.images_ref), custom_call_target="tpu_custom_call" | custom-call | tf_op jit(solution)/shard_map/scores/pallas_call | solution.py:251
  28.0 0.0 collective-permute-done.4
  28.0 0.0 collective-permute-done.3
  28.0 0.9 %collective-permute-done.10 = bf16[2,32,512]{2,1,0:T(8,128)(2,1)S(1)} collective-permute-done((bf16[2,32,512]{2,1,0:T(8,128)(2,1)S(1)}, bf16[2,32,512]{2,1,0:T(8,128)(2,1)S(1)}, u32[]{:S(2)}, u32[]{:S(2)}) %collective-permute-start.10) | collective-permute-done | bytes 65568 | tf_op jit(solution)/shard_map/ppermute | solution.py:239
  29.0 0.7 %fusion.10 = (f32[1,32,512]{2,1,0:T(8,128)}, f32[1,32,512]{2,1,0:T(8,128)}) fusion(f32[2,32,512]{2,1,0:T(8,128)S(1)} %fusion.3), kind=kLoop, calls=%fused_computation.19 | loop fusion | bytes 262144 | tf_op jit(solution)/shard_map/slice | solution.py:385
  (6 shorter events, 0.1 us)
Async XLA Ops:
  0.6 10.6 %collective-permute-start = (bf16[1,32,512]{2,1,0:T(8,128)(2,1)}, bf16[1,32,512]{2,1,0:T(8,128)(2,1)S(1)}, u32[]{:S(2)}, u32[]{:S(2)}) collective-permute-start(bf16[1,32,512]{2,1,0:T(8,128)(2,1)} %param.8), channel_id=1, source_target_pairs={{0,8},{1,9},{2,10},{3,11},{4,12},{5,13},{6,14},{7,15},{8,0},{9,1},... | collective-permute-start | bytes 98312 | tf_op jit(solution)/shard_map/ppermute | solution.py:239
  7.7 3.6 %copy-start = (bf16[1,32,512]{2,1,0:T(8,128)(2,1)S(1)}, bf16[1,32,512]{2,1,0:T(8,128)(2,1)}, u32[]{:S(2)}) copy-start(bf16[1,32,512]{2,1,0:T(8,128)(2,1)} %param.8) | copy-start | bytes 98308
  11.3 2.0 %collective-permute-start.1 = (bf16[8,2,32,512]{3,2,1,0:T(8,128)(2,1)S(1)}, bf16[8,2,32,512]{3,2,1,0:T(8,128)(2,1)S(1)}, u32[]{:S(2)}, u32[]{:S(2)}) collective-permute-start(bf16[8,2,32,512]{3,2,1,0:T(8,128)(2,1)S(1)} %get-tuple-element.30), channel_id=1, source_target_pairs={{0,1},{1,0},{2,3},{3,2},{4,5},{5,4},{6,7},{7,6},{8,9},{9,8},{10,11... | collective-permute-start | bytes 1572872 | tf_op jit(solution)/shard_map/ppermute | solution.py:239
  11.4 4.7 %collective-permute-start.6 = (bf16[2,32,512]{2,1,0:T(8,128)(2,1)S(1)}, bf16[2,32,512]{2,1,0:T(8,128)(2,1)S(1)}, u32[]{:S(2)}, u32[]{:S(2)}) collective-permute-start(bf16[2,32,512]{2,1,0:T(8,128)(2,1)S(1)} %pad_maximum_fusion), channel_id=1, source_target_pairs={{0,2},{1,3},{2,0},{3,1},{4,6},{5,7},{6,4},{7,5},{8,10},{9,11},{10,... | collective-permute-start | bytes 196616 | tf_op jit(solution)/shard_map/ppermute | solution.py:239
  13.4 5.7 %collective-permute-start.2 = (bf16[2,2,32,512]{3,2,1,0:T(8,128)(2,1)S(1)}, bf16[2,2,32,512]{3,2,1,0:T(8,128)(2,1)S(1)}, u32[]{:S(2)}, u32[]{:S(2)}) collective-permute-start(bf16[2,2,32,512]{3,2,1,0:T(8,128)(2,1)S(1)} %get-tuple-element.48), channel_id=1, source_target_pairs={{0,2},{1,3},{2,0},{3,1},{4,6},{5,7},{6,4},{7,5},{8,10},{9,11},{10,... | collective-permute-start | bytes 393224 | tf_op jit(solution)/shard_map/ppermute | solution.py:239
  16.1 4.4 %collective-permute-start.7 = (bf16[4,32,512]{2,1,0:T(8,128)(2,1)S(1)}, bf16[4,32,512]{2,1,0:T(8,128)(2,1)S(1)}, u32[]{:S(2)}, u32[]{:S(2)}) collective-permute-start(bf16[4,32,512]{2,1,0:T(8,128)(2,1)S(1)} %constant_dynamic-update-slice_fusion.refs_0_), channel_id=1, source_target_pairs={{0,1},{1,0},{2,3},{3,2},{4,5},{5,4},{6,7},{7,6},{8,9},{9,8},{10,11... | collective-permute-start | bytes 393224 | tf_op jit(solution)/shard_map/ppermute | solution.py:239
  16.1 5.9 %collective-permute-start.5 = (bf16[2,2,32,512]{3,2,1,0:T(8,128)(2,1)S(1)}, bf16[2,2,32,512]{3,2,1,0:T(8,128)(2,1)S(1)}, u32[]{:S(2)}, u32[]{:S(2)}) collective-permute-start(bf16[2,2,32,512]{3,2,1,0:T(8,128)(2,1)S(1)} %get-tuple-element.47), channel_id=1, source_target_pairs={{0,2},{1,3},{2,0},{3,1},{4,6},{5,7},{6,4},{7,5},{8,10},{9,11},{10,... | collective-permute-start | bytes 393224 | tf_op jit(solution)/shard_map/ppermute | solution.py:239
  17.5 5.7 %collective-permute-start.8 = (bf16[4,32,512]{2,1,0:T(8,128)(2,1)S(1)}, bf16[4,32,512]{2,1,0:T(8,128)(2,1)S(1)}, u32[]{:S(2)}, u32[]{:S(2)}) collective-permute-start(bf16[4,32,512]{2,1,0:T(8,128)(2,1)S(1)} %constant_dynamic-update-slice_fusion.refs_0_), channel_id=1, source_target_pairs={{0,4},{1,5},{2,6},{3,7},{4,0},{5,1},{6,2},{7,3},{8,12},{9,13},{10,... | collective-permute-start | bytes 393224 | tf_op jit(solution)/shard_map/ppermute | solution.py:239
  19.1 8.9 %collective-permute-start.3 = (bf16[2,32,512]{2,1,0:T(8,128)(2,1)S(1)}, bf16[2,32,512]{2,1,0:T(8,128)(2,1)S(1)}, u32[]{:S(2)}, u32[]{:S(2)}) collective-permute-start(bf16[2,32,512]{2,1,0:T(8,128)(2,1)S(1)} %get-tuple-element.50), channel_id=1, source_target_pairs={{0,12},{1,13},{2,14},{3,15},{4,8},{5,9},{6,10},{7,11},{8,4},{9,5},... | collective-permute-start | bytes 196616 | tf_op jit(solution)/shard_map/ppermute | solution.py:239
  22.1 5.9 %collective-permute-start.4 = (bf16[2,32,512]{2,1,0:T(8,128)(2,1)S(1)}, bf16[2,32,512]{2,1,0:T(8,128)(2,1)S(1)}, u32[]{:S(2)}, u32[]{:S(2)}) collective-permute-start(bf16[2,32,512]{2,1,0:T(8,128)(2,1)S(1)} %get-tuple-element.49), channel_id=1, source_target_pairs={{0,8},{1,9},{2,10},{3,11},{4,12},{5,13},{6,14},{7,15},{8,0},{9,1},... | collective-permute-start | bytes 196616 | tf_op jit(solution)/shard_map/ppermute | solution.py:239
  23.1 2.4 %collective-permute-start.9 = (bf16[4,32,512]{2,1,0:T(8,128)(2,1)S(1)}, bf16[4,32,512]{2,1,0:T(8,128)(2,1)S(1)}, u32[]{:S(2)}, u32[]{:S(2)}) collective-permute-start(bf16[4,32,512]{2,1,0:T(8,128)(2,1)S(1)} %collective-permute-done.8.refs_0_), channel_id=1, source_target_pairs={{0,1},{1,0},{2,3},{3,2},{4,5},{5,4},{6,7},{7,6},{8,9},{9,8},{10,11... | collective-permute-start | bytes 393224 | tf_op jit(solution)/shard_map/ppermute | solution.py:239
  23.1 5.8 %collective-permute-start.10 = (bf16[2,32,512]{2,1,0:T(8,128)(2,1)S(1)}, bf16[2,32,512]{2,1,0:T(8,128)(2,1)S(1)}, u32[]{:S(2)}, u32[]{:S(2)}) collective-permute-start(bf16[2,32,512]{2,1,0:T(8,128)(2,1)S(1)} %fusion.9), channel_id=1, source_target_pairs={{0,4},{1,5},{2,6},{3,7},{4,0},{5,1},{6,2},{7,3},{8,12},{9,13},{10,... | collective-permute-start | bytes 196616 | tf_op jit(solution)/shard_map/ppermute | solution.py:239
